TPU v7x, 768 devices: a whole 4x8x12 slice. The times are simulated.
768 devices in a mesh: pair: 192 (over z, y_hi, x, core), virt: 4 (over y_lo).
Axes of the slice: x: 4, y: 8 (y_hi: 2, y_lo: 4; y = y_hi * 4 + y_lo), z: 12, core: 2. Of those that a mesh axis runs over, the one named last changes fastest.
Arguments:
- amplitudes: bfloat16 [768, 1600, 200], P('pair', 'virt'), may hold values from -6 to 6
- integrals: bfloat16 [768, 1600, 200], P('pair', 'virt'), may hold values from -6 to 6
- ladder_slab: bfloat16 [16, 1600, 200], P(None, 'virt'), may hold values from -0.4375 to 0.4375
- pair_list: int32 [768, 2], P('pair'), may hold values from 0 to 199, as said below
- mirror_slot: int32 [768], P('pair'), may hold values from 0 to 3, as said below
- occ_irrep: int32 [200], replicated, may hold values from 0 to 7
- occ_energy: float32 [200], replicated, may hold values from -2 to -0.5
- virt_energy: bfloat16 [1600], P('virt'), may hold values from 0.29882812 to 3
Outputs:
- new_amplitudes: bfloat16 [768, 1600, 200], P('pair', 'virt')
Inputs may be any that keep to these rules, and one draw needn't show every extreme that they name: `pair_list`: each row is (i, j) with i != j. The pair at slot s of index d of pair has its mirror (j, i) at index (d + 96) mod 192, slot mirror_slot of that row; the mirror of the mirror is the pair itself. `mirror_slot`: on each index of pair the slots of the mirrors form a permutation of 0 to 3.
All inputs are finite; a program needn't handle non-finite values.
Results may differ from a plain program's by a relative error of at most 0.005.
Values may be sent and summed in bfloat16 or wider, within the bound.
No kernel may reach another device: no remote copies, remote signals or barrier semaphores. Data moves between devices by JAX's collectives and lax.ppermute only.
A program may use at most 128 MiB of HBM per device.

v0:
```python
import jax
import jax.numpy as jnp
from jax import lax
from jax.sharding import PartitionSpec as P


def from_behind(value, axis, steps):
    count = lax.axis_size(axis)
    pairs = [(source, (source + steps) % count) for source in range(count)]
    return lax.ppermute(value, axis, pairs)


def on_device(
    amplitudes, integrals, ladder_slab, pair_list, mirror_slot, occ_irrep, occ_energy, virt_energy
):
    pair_count, slab_rows, width = amplitudes.shape
    local_blocks = slab_rows // width
    slab_all, energy_all = (
        lax.all_gather(ladder_slab, "virt", axis=1, tiled=True),
        lax.all_gather(virt_energy, "virt", axis=0, tiled=True),
    )
    aux_depth = slab_all.shape[0]
    irrep_count = slab_all.shape[1] // width
    slab_blocks = slab_all.reshape(aux_depth, irrep_count, width, width)
    energy_blocks = energy_all.astype(jnp.float32).reshape(irrep_count, width)
    pair_irrep = jnp.bitwise_xor(occ_irrep[pair_list[:, 0]], occ_irrep[pair_list[:, 1]])
    virt_index = lax.axis_index("virt")
    pieces = []
    for block_slot in range(local_blocks):
        start = block_slot * width
        amp_tile = amplitudes[:, start : start + width, :]
        half_done = jnp.einsum(
            "qac,pcd->pqad",
            ladder_slab[:, start : start + width, :],
            amp_tile,
            preferred_element_type=jnp.float32,
        ).astype(jnp.bfloat16)
        partner = jnp.bitwise_xor(virt_index * local_blocks + block_slot, pair_irrep)
        right_slab = slab_blocks[:, partner]
        ladder_sum = jnp.einsum(
            "pqad,qpbd->pab", half_done, right_slab, preferred_element_type=jnp.float32
        )
        pieces.append(
            (integrals[:, start : start + width, :].astype(jnp.float32) + ladder_sum).astype(
                jnp.bfloat16
            )
        )
    residual = jnp.concatenate(pieces, axis=1)
    mirrored = from_behind(residual, "pair", lax.axis_size("pair") // 2)
    mirrored = mirrored[mirror_slot]
    mirror_tiles = []
    all_blocks = lax.all_gather(mirrored, "virt", axis=1, tiled=True).reshape(
        pair_count, irrep_count, width, width
    )
    for block_slot in range(local_blocks):
        block_index = jnp.bitwise_xor(virt_index * local_blocks + block_slot, pair_irrep)
        mirror_tiles.append(
            jnp.take_along_axis(all_blocks, block_index[:, None, None, None], axis=1)[:, 0]
        )
    pair_energy = occ_energy[pair_list[:, 0]] + occ_energy[pair_list[:, 1]]
    results = []
    for block_slot in range(local_blocks):
        start = block_slot * width
        partner = jnp.bitwise_xor(virt_index * local_blocks + block_slot, pair_irrep)
        symmetric = pieces[block_slot].astype(jnp.float32) + jnp.swapaxes(
            mirror_tiles[block_slot], 1, 2
        ).astype(jnp.float32)
        own_energy = virt_energy[start : start + width].astype(jnp.float32)
        far_energy = energy_blocks[partner]
        denominator = (
            pair_energy[:, None, None] - own_energy[None, :, None] - far_energy[:, None, :]
        )
        results.append(
            (
                amplitudes[:, start : start + width, :].astype(jnp.float32)
                + symmetric / denominator
            ).astype(jnp.bfloat16)
        )
    return jnp.concatenate(results, axis=1)


def solution(mesh):
    return jax.shard_map(
        on_device,
        mesh=mesh,
        in_specs=(
            P("pair", "virt", None),
            P("pair", "virt", None),
            P(None, "virt", None),
            P("pair", None),
            P("pair"),
            P(),
            P(),
            P("virt"),
        ),
        out_specs=P("pair", "virt", None),
        check_vma=False,
    )
```

profile of v0, /device:TPU:56, one launch (start us, length us, event | category | flops | bytes accessed | tf_op | source)
XLA Modules:
  0.0 439.0 jit_solution(3848931196716880930)
XLA Ops:
  6.5 0.0 copy-start
  6.5 0.0 all-gather.4.cloned.1.call-start
  6.5 0.7 all-gather.4.cloned.1.call-update
  7.3 0.0 all-gather.6.cloned.1.call-start
  7.3 0.8 fusion.81
  8.1 0.0 copy-done
  8.1 0.6 gather_fusion
  8.7 0.6 gather_fusion.1
  9.4 243.1 %all-gather.4.cloned.1.call-done = bf16[16,1600,200]{2,1,0:T(8,128)(2,1)} async-done(((bf16[16,400,200]{2,1,0:T(8,128)(2,1)}), bf16[16,1600,200]{2,1,0:T(8,128)(2,1)}) %all-gather.4.cloned.1.call-update) | async-done | bytes 10240016 | tf_op jit(solution)/shard_map/all_gather | solution.py:19
  252.5 8.5 %gather_fusion.3 = bf16[4,16,200,200]{3,2,1,0:T(8,128)(2,1)} fusion(bf16[16,8,200,200]{3,2,1,0:T(8,128)(2,1)} %bitcast.159, s32[1024]{0:T(1024)S(1)} %pad_clamp_fusion.1), kind=kCustom, calls=%fused_computation.5 | custom fusion | bytes 10240016 | tf_op jit(solution)/shard_map/gather | solution.py:39
  261.0 0.0 copy-start.2
  261.0 8.5 %gather_fusion.2 = bf16[4,16,200,200]{3,2,1,0:T(8,128)(2,1)} fusion(bf16[16,8,200,200]{3,2,1,0:T(8,128)(2,1)} %bitcast.160, s32[1024]{0:T(1024)S(1)} %pad_clamp_fusion.2), kind=kCustom, calls=%fused_computation.4 | custom fusion | bytes 10240016 | tf_op jit(solution)/shard_map/gather | solution.py:39
  269.5 0.0 copy-done.2
  269.5 7.4 %fusion.55 = bf16[4,200,200]{2,1,0:T(8,128)(2,1)} fusion(bf16[4,16,200,200]{3,2,1,0:T(8,128)(2,1)} %gather_fusion.3, bf16[16,400,200]{2,1,0:T(8,128)(2,1)S(1)} %copy-done.2, bf16[4,400,200]{2,1,0:T(8,128)(2,1)} %param.11, bf16[4,400,200]{2,1,0:T(8,128)(2,1)} %param.10), kind=kOutput, calls=%fused_computation.30 | convolution fusion | flops 2051040000 | bytes 9331200 | tf_op jit(solution)/shard_map/pqad,qpbd->pab/dot_general | solution.py:40
  276.9 0.0 copy-start.7
  276.9 0.0 copy-start.6
  276.9 0.0 copy-start.1
  276.9 7.4 %fusion.48 = bf16[4,200,200]{2,1,0:T(8,128)(2,1)} fusion(bf16[4,16,200,200]{3,2,1,0:T(8,128)(2,1)} %gather_fusion.2, bf16[16,400,200]{2,1,0:T(8,128)(2,1)S(1)} %copy-done.2, bf16[4,400,200]{2,1,0:T(8,128)(2,1)} %param.11, bf16[4,400,200]{2,1,0:T(8,128)(2,1)} %param.10), kind=kOutput, calls=%fused_computation.29 | convolution fusion | flops 2051040000 | bytes 9331200 | tf_op jit(solution)/shard_map/pqad,qpbd->pab/dot_general | solution.py:40
  284.3 0.0 copy-start.3
  284.3 0.0 copy-start.4
  284.3 0.0 copy-start.5
  284.3 1.4 pad_maximum_fusion
  285.7 10.8 %collective-permute-start = (bf16[4,400,200]{2,1,0:T(8,128)(2,1)S(1)}, bf16[4,400,200]{2,1,0:T(8,128)(2,1)S(1)}, u32[]{:S(2)}, u32[]{:S(2)}) collective-permute-start(bf16[4,400,200]{2,1,0:T(8,128)(2,1)S(1)} %pad_maximum_fusion), channel_id=1, source_target_pairs={{0,384},{4,388},{8,392},{12,396},{16,400},{20,404},{24,408},{28,41... | collective-permute-start | bytes 1920008 | tf_op jit(solution)/shard_map/ppermute | solution.py:10
  296.5 0.0 copy-done.7
  296.5 52.4 %collective-permute-done = bf16[4,400,200]{2,1,0:T(8,128)(2,1)S(1)} collective-permute-done((bf16[4,400,200]{2,1,0:T(8,128)(2,1)S(1)}, bf16[4,400,200]{2,1,0:T(8,128)(2,1)S(1)}, u32[]{:S(2)}, u32[]{:S(2)}) %collective-permute-start) | collective-permute-done | bytes 640032 | tf_op jit(solution)/shard_map/ppermute | solution.py:10
  348.9 1.5 gather_fusion.4
  350.4 0.0 all-gather.6.cloned.1.call-update
  350.4 1.3 dynamic-slice
  352.3 0.0 copy-done.6
  352.3 0.2 dynamic-update-slice
  352.6 8.1 %all-reduce = bf16[1600]{0:T(1024)(128)(2,1)S(1)} all-reduce(bf16[1600]{0:T(1024)(128)(2,1)S(1)} %dynamic-update-slice), channel_id=1, replica_groups=mesh['pair'=192,'virt'=4] {'virt'}, use_global_device_ids=true, to_apply=%add | all-reduce | flops 1600 | bytes 6400
  360.7 0.1 reshape.196
  360.8 0.6 gather_fusion.8
  361.3 0.6 gather_fusion.7
  361.9 0.0 copy-done.1
  361.9 0.6 gather_fusion.5
  362.5 0.6 gather_fusion.6
  363.3 0.1 slice_convert_fusion.1
  363.3 0.1 broadcast_subtract_fusion.1
  363.4 61.8 %all-gather.6.cloned.1.call-done = bf16[4,1600,200]{2,1,0:T(8,128)(2,1)} async-done(((bf16[4,400,200]{2,1,0:T(8,128)(2,1)}), bf16[4,1600,200]{2,1,0:T(8,128)(2,1)}) %all-gather.6.cloned.1.call-update) | async-done | bytes 2560016 | tf_op jit(solution)/shard_map/all_gather | solution.py:52
  425.2 2.5 gather_fusion.10
  427.8 0.2 copy.10
  428.0 2.5 gather_fusion.9
  430.5 0.2 copy.9
  430.7 0.0 copy-done.3
  430.7 0.0 copy-done.4
  430.7 0.0 copy-done.5
  430.7 1.5 fusion.69
  (16 shorter events, 0.1 us)
Async XLA Ops:
  6.5 1.5 copy-start
  6.5 246.0 %all-gather.4.cloned.1.call-start = ((), (), s32[]{:S(2)}) async-start(), calls=%async_computation | async-start | bytes 16384000 | tf_op jit(solution)/shard_map/all_gather | solution.py:19
  7.3 418.0 %all-gather.6.cloned.1.call-start = ((), (), s32[]{:S(2)}) async-start(), calls=%async_computation.1 | async-start | bytes 4096000 | tf_op jit(solution)/shard_map/all_gather | solution.py:52
  261.0 8.5 %copy-start.2 = (bf16[16,400,200]{2,1,0:T(8,128)(2,1)S(1)}, bf16[16,400,200]{2,1,0:T(8,128)(2,1)}, u32[]{:S(2)}) copy-start(bf16[16,400,200]{2,1,0:T(8,128)(2,1)} %param.12) | copy-start | bytes 7680004
  276.9 19.6 %copy-start.7 = (s32[4]{0:T(128)S(1)}, s32[4]{0:T(128)}, u32[]{:S(2)}) copy-start(s32[4]{0:T(128)} %param.14) | copy-start | bytes 52
  276.9 75.4 %copy-start.6 = (bf16[400]{0:T(512)(128)(2,1)S(1)}, bf16[400]{0:T(512)(128)(2,1)}, u32[]{:S(2)}) copy-start(bf16[400]{0:T(512)(128)(2,1)} %param.17) | copy-start | bytes 2404
  276.9 85.0 %copy-start.1 = (f32[200]{0:T(256)S(1)}, f32[200]{0:T(256)}, u32[]{:S(2)}) copy-start(f32[200]{0:T(256)} %param.16) | copy-start | bytes 2404
  284.3 146.4 %copy-start.3 = (bf16[4,200,200]{2,1,0:T(8,128)(2,1)S(1)}, bf16[4,200,200]{2,1,0:T(8,128)(2,1)}, u32[]{:S(2)}) copy-start(bf16[4,200,200]{2,1,0:T(8,128)(2,1)} %fusion.55) | copy-start | bytes 960004
  284.3 146.4 %copy-start.4 = (bf16[4,200,200]{2,1,0:T(8,128)(2,1)S(1)}, bf16[4,200,200]{2,1,0:T(8,128)(2,1)}, u32[]{:S(2)}) copy-start(bf16[4,200,200]{2,1,0:T(8,128)(2,1)} %fusion.48) | copy-start | bytes 960004
  284.3 146.4 %copy-start.5 = (bf16[4,400,200]{2,1,0:T(8,128)(2,1)S(1)}, bf16[4,400,200]{2,1,0:T(8,128)(2,1)}, u32[]{:S(2)}) copy-start(bf16[4,400,200]{2,1,0:T(8,128)(2,1)} %param.10) | copy-start | bytes 1920004
  285.7 63.2 %collective-permute-start = (bf16[4,400,200]{2,1,0:T(8,128)(2,1)S(1)}, bf16[4,400,200]{2,1,0:T(8,128)(2,1)S(1)}, u32[]{:S(2)}, u32[]{:S(2)}) collective-permute-start(bf16[4,400,200]{2,1,0:T(8,128)(2,1)S(1)} %pad_maximum_fusion), channel_id=1, source_target_pairs={{0,384},{4,388},{8,392},{12,396},{16,400},{20,404},{24,408},{28,41... | collective-permute-start | bytes 1920008 | tf_op jit(solution)/shard_map/ppermute | solution.py:10
Sparse Core Ops, SparseCore 0:
  9.7 242.7 all-gather.3
  350.5 74.6 all-gather.5
where the time goes:
time: 439 us
  waiting for transfers between devices  358 us (82%)
  local copies, waits for them, and re-layouts  29.2 us (7%)
  matrix products  14.7 us (3%)
  between operations  14.2 us (3%)
  starting transfers between devices  10.8 us (2%)
  blocking collectives  8.09 us (2%)
    all_gather x1, waiting for transfers between devices, on_device(): lax.all_gather(ladder_slab, 'virt', axis=1, tiled=True)  243 us
    all_gather x1, waiting for transfers between devices, on_device(): lax.all_gather(mirrored, 'virt', axis=1, tiled=True)  61.8 us
    ppermute x1, waiting for transfers between devices, from_behind(): return lax.ppermute(value, axis, pairs)  52.4 us
    gather x2, local copies, waits for them, and re-layouts, on_device(): right_slab = slab_blocks[:, partner]  17 us
    dot_general x2, matrix products, on_device(): jnp.einsum('pqad,qpbd->pab', half_done, right_slab, preferred_element_typ...  14.7 us
    ppermute x1, starting transfers between devices, from_behind(): return lax.ppermute(value, axis, pairs)  10.8 us
  transfers between devices with their start and end apart: 3, of which 3 were waited for; matrix products, arithmetic and copies ran while one was open for 1% of the time, Pallas kernels for 0%

commit v1 on v0

v1 whole, which is shorter than its diff:
```python
import functools

import jax
import jax.numpy as jnp
from jax import lax
from jax.experimental import pallas as pl
from jax.experimental.pallas import tpu as pltpu
from jax.sharding import PartitionSpec as P

W = 200
NQ = 16
DEEP = NQ * W
TALL = 208
PIECE = 160
UNIT = 4 * PIECE
BF = jnp.bfloat16
F32 = jnp.float32
VMEM_LIMIT = 56 * 1024 * 1024


def permute(value, move):
    layers, halves, width, cores, lines = lax.axis_size("pair") // 16, 2, 4, 2, 4
    pairs = []
    for z in range(layers):
        for y in range(halves * lines):
            for x in range(width):
                for core in range(cores):
                    ends = []
                    for tz, ty, tx, tc in ((z, y, x, core), move(z, y, x, core)):
                        tz, ty, tx, tc = tz % layers, ty % (halves * lines), tx % width, tc % cores
                        pair = ((tz * halves + ty // lines) * width + tx) * cores + tc
                        ends.append(pair * lines + ty % lines)
                    pairs.append(tuple(ends))
    return lax.ppermute(value, ("pair", "virt"), pairs)


def along_y(value):
    return permute(value, lambda z, y, x, core: (z, y + 1 - 2 * core, x, core))


def swap_cores(value):
    return permute(value, lambda z, y, x, core: (z, y, x, 1 - core))


def to_mirror(value):
    half = lax.axis_size("pair") // 32
    return permute(value, lambda z, y, x, core: (z + half, y, x, core))


def params(*semantics):
    return pltpu.CompilerParams(
        dimension_semantics=semantics, vmem_limit_bytes=VMEM_LIMIT
    )


def pack_kernel(order_ref, slab_ref, energy_ref, out_ref):
    for q in range(NQ):
        out_ref[0:W, q * W : (q + 1) * W] = slab_ref[q, 0]
    out_ref[W:TALL, 0:W] = jnp.broadcast_to(energy_ref[0], (TALL - W, W))
    out_ref[W:TALL, W:DEEP] = jnp.zeros((TALL - W, DEEP - W), BF)


def pack_slab(slab, energy, block):
    return pl.pallas_call(
        pack_kernel,
        out_shape=jax.ShapeDtypeStruct((TALL, DEEP), BF),
        grid_spec=pltpu.PrefetchScalarGridSpec(
            num_scalar_prefetch=1,
            grid=(1,),
            in_specs=[
                pl.BlockSpec((NQ, 1, W, W), lambda i, order: (0, order[0], 0, 0)),
                pl.BlockSpec((1, 1, W), lambda i, order: (order[0], 0, 0)),
            ],
            out_specs=pl.BlockSpec((TALL, DEEP), lambda i, order: (0, 0)),
        ),
        compiler_params=params("arbitrary"),
        cost_estimate=pl.CostEstimate(flops=0, bytes_accessed=3_000_000, transcendentals=0),
    )(block, slab, energy)


def half_kernel(slab_ref, amp_ref, out_ref):
    for q in range(NQ):
        out_ref[0, 0, :, q * W : (q + 1) * W] = jnp.dot(
            slab_ref[q, 0], amp_ref[0, 0], preferred_element_type=F32
        ).astype(BF)


def first_half(slab, amplitudes):
    pairs = amplitudes.shape[0]
    return pl.pallas_call(
        half_kernel,
        out_shape=jax.ShapeDtypeStruct((pairs, 2, W, DEEP), BF),
        grid=(2, pairs),
        in_specs=[
            pl.BlockSpec((NQ, 1, W, W), lambda b, p: (0, b, 0, 0)),
            pl.BlockSpec((1, 1, W, W), lambda b, p: (p, b, 0, 0)),
        ],
        out_specs=pl.BlockSpec((1, 1, W, DEEP), lambda b, p: (p, b, 0, 0)),
        compiler_params=params("arbitrary", "arbitrary"),
        cost_estimate=pl.CostEstimate(
            flops=2 * pairs * 2 * NQ * W**3, bytes_accessed=18_000_000, transcendentals=0
        ),
    )(slab, amplitudes)


def put_tile(unit_ref, block, tile):
    unit_ref[block * W : (block + 1) * W, :] = tile[:, 0:128]
    unit_ref[2 * W : 3 * W, block * 64 : (block + 1) * 64] = tile[:, 128:192]
    base = 3 * W + 16 * block
    for c in range(13):
        rows = min(16, W - 16 * c)
        unit_ref[base : base + rows, 8 * c : 8 * c + 8] = tile[16 * c : 16 * c + rows, 192:200]


def get_tile(unit, block):
    base = 3 * W + 16 * block
    tail = [
        unit[base : base + min(16, W - 16 * c), 8 * c : 8 * c + 8] for c in range(13)
    ]
    return jnp.concatenate(
        [
            unit[block * W : (block + 1) * W, :],
            unit[2 * W : 3 * W, block * 64 : (block + 1) * 64],
            jnp.concatenate(tail, axis=0),
        ],
        axis=1,
    )


def ladder_kernel(first, source_ref, half_ref, int_ref, *refs):
    sources, (out_ref, far_ref, right, unit, sems) = refs[:8], refs[8:]
    pair, block = pl.program_id(0), pl.program_id(1)
    step, steps = pair * 2 + block, pl.num_programs(0) * 2
    slot = lax.rem(step, 2)

    def fetch(at, into):
        for r in range(8):

            @pl.when(source_ref[first * 2 + at] == r)
            def _():
                pltpu.make_async_copy(sources[r], right.at[into], sems.at[into]).start()

    @pl.when(step == 0)
    def _():
        fetch(0, 0)
        unit[...] = jnp.zeros_like(unit)

    @pl.when(step + 1 < steps)
    def _():
        fetch(step + 1, 1 - slot)

    pltpu.make_async_copy(sources[0], right.at[slot], sems.at[slot]).wait()
    ladder = lax.dot_general(
        half_ref[0, 0],
        right[slot, 0:W, :],
        (((1,), (1,)), ((), ())),
        preferred_element_type=F32,
    )
    tile = int_ref[0, 0].astype(F32) + ladder
    far_ref[0, 0] = right[slot, W:TALL, 0:W].astype(F32)

    @pl.when(block == 0)
    def _():
        put_tile(unit, 0, tile)

    @pl.when(block == 1)
    def _():
        put_tile(unit, 1, tile)
        for j in range(4):
            out_ref[j, 0] = unit[j * PIECE : (j + 1) * PIECE, :].astype(BF)


def residual_units(first, count, source, half_done, integrals, blocks):
    return pl.pallas_call(
        functools.partial(ladder_kernel, first),
        out_shape=(
            jax.ShapeDtypeStruct((4, count, PIECE, 128), BF),
            jax.ShapeDtypeStruct((count, 2, TALL - W, W), F32),
        ),
        grid_spec=pltpu.PrefetchScalarGridSpec(
            num_scalar_prefetch=1,
            grid=(count, 2),
            in_specs=[
                pl.BlockSpec((1, 1, W, DEEP), lambda p, b, s: (first + p, b, 0, 0)),
                pl.BlockSpec((1, 1, W, W), lambda p, b, s: (first + p, b, 0, 0)),
            ]
            + [pl.BlockSpec(memory_space=pl.ANY)] * 8,
            out_specs=[
                pl.BlockSpec((4, 1, PIECE, 128), lambda p, b, s: (0, p, 0, 0)),
                pl.BlockSpec((1, 1, TALL - W, W), lambda p, b, s: (p, b, 0, 0)),
            ],
            scratch_shapes=[
                pltpu.VMEM((2, TALL, DEEP), BF),
                pltpu.VMEM((UNIT, 128), F32),
                pltpu.SemaphoreType.DMA((2,)),
            ],
        ),
        compiler_params=params("arbitrary", "arbitrary"),
        cost_estimate=pl.CostEstimate(
            flops=4 * count * NQ * W**3, bytes_accessed=count * 2 * 2_700_000, transcendentals=0
        ),
    )(source, half_done, integrals, *blocks)


def update_kernel(
    slot_ref, flip_ref, pair_ref, amp_ref, own_a, own_b, far_a, far_b, mir_a, mir_b, near_ref, out_ref
):
    p = pl.program_id(0)

    def unit(low, high, use_low):
        rows = [jnp.where(use_low, low[j, 0].astype(F32), high[j, 0].astype(F32)) for j in range(4)]
        return jnp.concatenate(rows, axis=0)

    own = unit(own_a, own_b, p < 2)
    other = unit(mir_a, mir_b, slot_ref[p] < 2)
    straight = flip_ref[p] == 0
    tiles = [get_tile(other, b) for b in range(2)]
    for b in range(2):
        mirror = jnp.where(straight, tiles[b], tiles[1 - b])
        square = jnp.pad(mirror, ((0, 56), (0, 56)))
        symmetric = get_tile(own, b) + square.T[0:W, 0:W]
        far = jnp.where(p < 2, far_a[0, b, 0:1, :], far_b[0, b, 0:1, :])
        denominator = pair_ref[p] - near_ref[b] - far
        out_ref[0, b] = (amp_ref[0, b].astype(F32) + symmetric / denominator).astype(BF)


def update(slot, flip, pair_energy, amplitudes, own_a, own_b, far_a, far_b, mir_a, mir_b, near):
    pairs = amplitudes.shape[0]
    low = lambda p, s, f, e: (0, jnp.minimum(p, 1), 0, 0)
    high = lambda p, s, f, e: (0, jnp.maximum(p - 2, 0), 0, 0)
    low_far = lambda p, s, f, e: (jnp.minimum(p, 1), 0, 0, 0)
    high_far = lambda p, s, f, e: (jnp.maximum(p - 2, 0), 0, 0, 0)
    pick = lambda p, s, f, e: (0, jnp.bitwise_and(s[p], 1), 0, 0)
    own = lambda p, s, f, e: (p, 0, 0, 0)
    unit = (4, 1, PIECE, 128)
    return pl.pallas_call(
        update_kernel,
        out_shape=jax.ShapeDtypeStruct((pairs, 2, W, W), BF),
        grid_spec=pltpu.PrefetchScalarGridSpec(
            num_scalar_prefetch=3,
            grid=(pairs,),
            in_specs=[
                pl.BlockSpec((1, 2, W, W), own),
                pl.BlockSpec(unit, low),
                pl.BlockSpec(unit, high),
                pl.BlockSpec((1, 2, TALL - W, W), low_far),
                pl.BlockSpec((1, 2, TALL - W, W), high_far),
                pl.BlockSpec(unit, pick),
                pl.BlockSpec(unit, pick),
                pl.BlockSpec((2, W, 1), lambda p, s, f, e: (0, 0, 0)),
            ],
            out_specs=pl.BlockSpec((1, 2, W, W), own),
        ),
        compiler_params=params("arbitrary"),
    )(slot, flip, pair_energy, amplitudes, own_a, own_b, far_a, far_b, mir_a, mir_b, near)


def across_virt(units, step):
    scattered = lax.all_to_all(units, "virt", 0, 0, tiled=True)
    index = jnp.bitwise_xor(jnp.arange(4, dtype=jnp.int32)[:, None], step[None, :])
    chosen = scattered[index, jnp.arange(units.shape[1], dtype=jnp.int32)[None, :]]
    return lax.all_to_all(chosen, "virt", 0, 0, tiled=True)


def on_device(
    amplitudes, integrals, ladder_slab, pair_list, mirror_slot, occ_irrep, occ_energy, virt_energy
):
    pairs = amplitudes.shape[0]
    amp = amplitudes.reshape(pairs, 2, W, W)
    ints = integrals.reshape(pairs, 2, W, W)
    slab = ladder_slab.reshape(NQ, 2, W, W)
    energy = virt_energy.reshape(2, 1, W)
    core = lax.rem(lax.axis_index("pair"), 2).astype(jnp.int32)
    virt = lax.axis_index("virt").astype(jnp.int32)

    one, two = pack_slab(slab, energy, core[None]), pack_slab(slab, energy, 1 - core[None])
    near_one = along_y(one)
    near_two = along_y(two)
    far_one = along_y(near_one)
    half_done = first_half(slab, amp)
    blocks = (
        one,
        two,
        near_one,
        near_two,
        swap_cores(near_one),
        swap_cores(near_two),
        far_one,
        swap_cores(far_one),
    )

    irrep = jnp.bitwise_xor(occ_irrep[pair_list[:, 0]], occ_irrep[pair_list[:, 1]])
    step, flip = jnp.right_shift(irrep, 1), jnp.bitwise_and(irrep, 1)
    apart = jnp.bitwise_and(jnp.bitwise_xor(virt, step) - virt, 3)[:, None]
    second = (jnp.bitwise_xor(jnp.arange(2)[None, :], flip[:, None]) != core).astype(jnp.int32)
    mine = 2 + second
    theirs = 5 - second
    source = jnp.where(
        apart == 0,
        second,
        jnp.where(apart == 2, 6 + second, jnp.where(apart == 3 - 2 * core, mine, theirs)),
    ).reshape(-1)

    unit_a, far_a = residual_units(0, 2, source, half_done, ints, blocks)
    unit_b, far_b = residual_units(2, 2, source, half_done, ints, blocks)
    slots = jnp.arange(pairs, dtype=jnp.int32)
    mirror_step = jnp.sum(
        jnp.where(mirror_slot[:, None] == slots[None, :], step[:, None], 0), axis=0
    )
    mir_a = to_mirror(unit_a)
    mir_b = to_mirror(across_virt(unit_b, step[2:4]))
    mir_a = across_virt(mir_a, mirror_step[0:2])
    pair_energy = occ_energy[pair_list[:, 0]] + occ_energy[pair_list[:, 1]]
    near = virt_energy.astype(F32).reshape(2, W, 1)
    new = update(
        mirror_slot, flip, pair_energy, amp, unit_a, unit_b, far_a, far_b, mir_a, mir_b, near
    )
    return new.reshape(amplitudes.shape)


def solution(mesh):
    return jax.shard_map(
        on_device,
        mesh=mesh,
        in_specs=(
            P("pair", "virt", None),
            P("pair", "virt", None),
            P(None, "virt", None),
            P("pair", None),
            P("pair"),
            P(),
            P(),
            P("virt"),
        ),
        out_specs=P("pair", "virt", None),
        check_vma=False,
    )
```

time: 439 us -> 191 us (0.44)
  the two profiles are of different devices: /device:TPU:56 before, /device:TPU:120 now
where the time goes in v1:
time: 191 us; the launch traced here: 190 us
  waiting for transfers between devices  78.9 us (41%)
  starting transfers between devices  62.1 us (33%)
  Pallas kernels  38.7 us (20%)
  local copies, waits for them, and re-layouts  9 us (5%)
    ppermute x8, waiting for transfers between devices, permute(): return lax.ppermute(value, ('pair', 'virt'), pairs)  68.1 us
    ppermute x8, starting transfers between devices, permute(): return lax.ppermute(value, ('pair', 'virt'), pairs)  37.8 us
    pallas_call x2, Pallas kernels, residual_units(): pl.pallas_call(functools.partial(ladder_kernel, first), out_shape=(jax.Sh...  16.5 us
    all_to_all x2, starting transfers between devices, across_virt(): scattered = lax.all_to_all(units, 'virt', 0, 0, tiled=True)  12.6 us
    all_to_all x2, starting transfers between devices, across_virt(): return lax.all_to_all(chosen, 'virt', 0, 0, tiled=True)  11.6 us
    pallas_call x1, Pallas kernels, first_half(): pl.pallas_call(half_kernel, out_shape=jax.ShapeDtypeStruct((pairs, 2, W,...  10.2 us
    all_to_all x2, waiting for transfers between devices, across_virt(): scattered = lax.all_to_all(units, 'virt', 0, 0, tiled=True)  6.08 us
    pallas_call x2, Pallas kernels, pack_slab(): pl.pallas_call(pack_kernel, out_shape=jax.ShapeDtypeStruct((TALL, DEEP),...  6 us
  transfers between devices with their start and end apart: 12, of which 7 were waited for; matrix products, arithmetic and copies ran while one was open for 4% of the time, Pallas kernels for 11%

profile of v1, /device:TPU:120, one launch (start us, length us, event | category | flops | bytes accessed | tf_op | source)
XLA Modules:
  0.0 190.1 jit_solution(3197958673221336078)
XLA Ops:
  0.0 1.4 reshape.195.energy_ref
  1.4 3.0 %shard_map.83.refs_0_ = bf16[208,3200]{1,0:T(8,128)(2,1)} custom-call(s32[1]{0:T(128)} %bitcast.5.order_ref, bf16[16,2,200,200]{3,2,1,0:T(8,128)(2,1)} %bitcast.16, bf16[2,1,200]{2,1,0:T(2,128)(2,1)} %reshape.195.energy_ref), custom_call_target="tpu_custom_call" | custom-call | bytes 3000000 | tf_op jit(solution)/shard_map/pallas_call | solution.py:64
  4.3 1.9 %collective-permute-start = (bf16[208,3200]{1,0:T(8,128)(2,1)}, bf16[208,3200]{1,0:T(8,128)(2,1)S(1)}, u32[]{:S(2)}, u32[]{:S(2)}) collective-permute-start(bf16[208,3200]{1,0:T(8,128)(2,1)} %shard_map.83.refs_0_), channel_id=1, source_target_pairs={{0,1},{4,39},{8,9},{12,47},{16,17},{20,55},{24,25},{28,63},{1,2},{... | collective-permute-start | bytes 3993608 | tf_op jit(solution)/shard_map/ppermute | solution.py:34
  6.3 3.0 %shard_map.84.refs_1_ = bf16[208,3200]{1,0:T(8,128)(2,1)} custom-call(s32[1]{0:T(128)S(6)} %sub.27.order_ref, bf16[16,2,200,200]{3,2,1,0:T(8,128)(2,1)} %bitcast.17, bf16[2,1,200]{2,1,0:T(2,128)(2,1)} %reshape.195.energy_ref), custom_call_target="tpu_custom_call" | custom-call | bytes 3000000 | tf_op jit(solution)/shard_map/pallas_call | solution.py:64
  9.3 3.2 %collective-permute-start.1 = (bf16[208,3200]{1,0:T(8,128)(2,1)}, bf16[208,3200]{1,0:T(8,128)(2,1)S(1)}, u32[]{:S(2)}, u32[]{:S(2)}) collective-permute-start(bf16[208,3200]{1,0:T(8,128)(2,1)} %shard_map.84.refs_1_), channel_id=1, source_target_pairs={{0,1},{4,39},{8,9},{12,47},{16,17},{20,55},{24,25},{28,63},{1,2},{... | collective-permute-start | bytes 3993608 | tf_op jit(solution)/shard_map/ppermute | solution.py:34
  12.5 11.7 %collective-permute-done.refs_2_ = bf16[208,3200]{1,0:T(8,128)(2,1)S(1)} collective-permute-done((bf16[208,3200]{1,0:T(8,128)(2,1)}, bf16[208,3200]{1,0:T(8,128)(2,1)S(1)}, u32[]{:S(2)}, u32[]{:S(2)}) %collective-permute-start) | collective-permute-done | bytes 1331232 | tf_op jit(solution)/shard_map/ppermute | solution.py:34
  24.2 3.1 %collective-permute-start.4 = (bf16[208,3200]{1,0:T(8,128)(2,1)S(1)}, bf16[208,3200]{1,0:T(8,128)(2,1)}, u32[]{:S(2)}, u32[]{:S(2)}) collective-permute-start(bf16[208,3200]{1,0:T(8,128)(2,1)S(1)} %collective-permute-done.refs_2_), channel_id=1, source_target_pairs={{0,1},{4,39},{8,9},{12,47},{16,17},{20,55},{24,25},{28,63},{1,2},{... | collective-permute-start | bytes 3993608 | tf_op jit(solution)/shard_map/ppermute | solution.py:34
  27.4 1.9 %collective-permute-start.2 = (bf16[208,3200]{1,0:T(8,128)(2,1)S(1)}, bf16[208,3200]{1,0:T(8,128)(2,1)}, u32[]{:S(2)}, u32[]{:S(2)}) collective-permute-start(bf16[208,3200]{1,0:T(8,128)(2,1)S(1)} %collective-permute-done.refs_2_), channel_id=1, source_target_pairs={{0,4},{4,0},{8,12},{12,8},{16,20},{20,16},{24,28},{28,24},{1,5},{5... | collective-permute-start | bytes 3993608 | tf_op jit(solution)/shard_map/ppermute | solution.py:34
  29.3 9.2 %collective-permute-done.1.refs_3_ = bf16[208,3200]{1,0:T(8,128)(2,1)S(1)} collective-permute-done((bf16[208,3200]{1,0:T(8,128)(2,1)}, bf16[208,3200]{1,0:T(8,128)(2,1)S(1)}, u32[]{:S(2)}, u32[]{:S(2)}) %collective-permute-start.1) | collective-permute-done | bytes 1331232 | tf_op jit(solution)/shard_map/ppermute | solution.py:34
  38.5 1.9 %collective-permute-start.3 = (bf16[208,3200]{1,0:T(8,128)(2,1)S(1)}, bf16[208,3200]{1,0:T(8,128)(2,1)}, u32[]{:S(2)}, u32[]{:S(2)}) collective-permute-start(bf16[208,3200]{1,0:T(8,128)(2,1)S(1)} %collective-permute-done.1.refs_3_), channel_id=1, source_target_pairs={{0,4},{4,0},{8,12},{12,8},{16,20},{20,16},{24,28},{28,24},{1,5},{5... | collective-permute-start | bytes 3993608 | tf_op jit(solution)/shard_map/ppermute | solution.py:34
  40.4 12.4 %collective-permute-done.4.refs_6_ = bf16[208,3200]{1,0:T(8,128)(2,1)} collective-permute-done((bf16[208,3200]{1,0:T(8,128)(2,1)S(1)}, bf16[208,3200]{1,0:T(8,128)(2,1)}, u32[]{:S(2)}, u32[]{:S(2)}) %collective-permute-start.4) | collective-permute-done | bytes 1331232 | tf_op jit(solution)/shard_map/ppermute | solution.py:34
  52.9 1.9 %collective-permute-start.5 = (bf16[208,3200]{1,0:T(8,128)(2,1)}, bf16[208,3200]{1,0:T(8,128)(2,1)}, u32[]{:S(2)}, u32[]{:S(2)}) collective-permute-start(bf16[208,3200]{1,0:T(8,128)(2,1)} %collective-permute-done.4.refs_6_), channel_id=1, source_target_pairs={{0,4},{4,0},{8,12},{12,8},{16,20},{20,16},{24,28},{28,24},{1,5},{5... | collective-permute-start | bytes 3993608 | tf_op jit(solution)/shard_map/ppermute | solution.py:34
  54.8 0.6 gather_fusion
  55.5 0.6 gather_fusion.1
  56.1 0.1 broadcast_in_dim.68
  56.2 0.1 broadcast_in_dim.69
  56.3 0.1 fusion.6
  56.4 0.1 reshape.148
  56.5 0.1 broadcast_in_dim.70
  56.5 0.1 broadcast_in_dim.71
  56.6 0.1 broadcast_in_dim.72
  56.7 0.1 broadcast_in_dim.73
  56.8 10.2 %shard_map.82.half_ref = bf16[4,2,200,3200]{3,2,1,0:T(8,128)(2,1)} custom-call(bf16[16,2,200,200]{3,2,1,0:T(8,128)(2,1)} %bitcast.18, bf16[4,2,200,200]{3,2,1,0:T(8,128)(2,1)} %bitcast.19), custom_call_target="tpu_custom_call" | custom-call | flops 2048000000 | bytes 18000000 | tf_op jit(solution)/shard_map/pallas_call | solution.py:90
  67.0 0.5 select_select_fusion.source_ref
  67.5 8.3 %shard_map.86 = (bf16[4,2,160,128]{3,2,1,0:T(8,128)(2,1)}, f32[2,2,8,200]{3,2,1,0:T(8,128)}) custom-call(s32[8]{0:T(128)} %select_select_fusion.source_ref, bf16[4,2,200,3200]{3,2,1,0:T(8,128)(2,1)} %shard_map.82.half_ref, bf16[4,2,200,200]{3,2,1,0:T(8,128)(2,1)} %bitcast.21, bf16[208,3200]{1,0:T(8,128)(2,1)} %shard_map.83.refs_0_, ...), custom_call_target="tpu_custom_call" | custom-call | flops 1024000000 | bytes 10800000 | tf_op jit(solution)/shard_map/pallas_call | solution.py:174
  75.8 7.5 %all-to-all-start.2 = ((bf16[4,2,160,128]{3,2,1,0:T(8,128)(2,1)}), bf16[4,2,160,128]{3,2,1,0:T(8,128)(2,1)S(1)}, u32[]{:S(2)}, u32[]{:S(2)}) async-start(bf16[4,2,160,128]{3,2,1,0:T(8,128)(2,1)} %get-tuple-element.10.own_b), calls=%async_computation.2 | async-start | bytes 655360 | tf_op jit(solution)/shard_map/all_to_all | solution.py:259
  83.4 8.2 %shard_map.85 = (bf16[4,2,160,128]{3,2,1,0:T(8,128)(2,1)}, f32[2,2,8,200]{3,2,1,0:T(8,128)}) custom-call(s32[8]{0:T(128)} %select_select_fusion.source_ref, bf16[4,2,200,3200]{3,2,1,0:T(8,128)(2,1)} %shard_map.82.half_ref, bf16[4,2,200,200]{3,2,1,0:T(8,128)(2,1)} %bitcast.22, bf16[208,3200]{1,0:T(8,128)(2,1)} %shard_map.83.refs_0_, ...), custom_call_target="tpu_custom_call" | custom-call | flops 1024000000 | bytes 10800000 | tf_op jit(solution)/shard_map/pallas_call | solution.py:174
  91.6 14.2 %collective-permute-start.6 = (bf16[4,2,160,128]{3,2,1,0:T(8,128)(2,1)}, bf16[4,2,160,128]{3,2,1,0:T(8,128)(2,1)}, u32[]{:S(2)}, u32[]{:S(2)}) collective-permute-start(bf16[4,2,160,128]{3,2,1,0:T(8,128)(2,1)} %get-tuple-element.9.own_a), channel_id=1, source_target_pairs={{0,384},{4,388},{8,392},{12,396},{16,400},{20,404},{24,408},{28,41... | collective-permute-start | bytes 983048 | tf_op jit(solution)/shard_map/ppermute | solution.py:34
  105.9 22.7 %collective-permute-done.6 = bf16[4,2,160,128]{3,2,1,0:T(8,128)(2,1)} collective-permute-done((bf16[4,2,160,128]{3,2,1,0:T(8,128)(2,1)}, bf16[4,2,160,128]{3,2,1,0:T(8,128)(2,1)}, u32[]{:S(2)}, u32[]{:S(2)}) %collective-permute-start.6) | collective-permute-done | bytes 327712 | tf_op jit(solution)/shard_map/ppermute | solution.py:34
  128.6 5.1 %all-to-all-start = ((bf16[4,2,160,128]{3,2,1,0:T(8,128)(2,1)}), bf16[4,2,160,128]{3,2,1,0:T(8,128)(2,1)S(1)}, u32[]{:S(2)}, u32[]{:S(2)}) async-start(bf16[4,2,160,128]{3,2,1,0:T(8,128)(2,1)} %collective-permute-done.6), calls=%async_computation | async-start | bytes 655360 | tf_op jit(solution)/shard_map/all_to_all | solution.py:259
  133.7 0.1 slice.17
  133.8 0.1 reshape.189
  133.9 1.3 gather_fusion.5
  135.2 6.1 %all-to-all-done = bf16[4,2,160,128]{3,2,1,0:T(8,128)(2,1)S(1)} async-done(((bf16[4,2,160,128]{3,2,1,0:T(8,128)(2,1)}), bf16[4,2,160,128]{3,2,1,0:T(8,128)(2,1)S(1)}, u32[]{:S(2)}, u32[]{:S(2)}) %all-to-all-start) | async-done | bytes 327712 | tf_op jit(solution)/shard_map/all_to_all | solution.py:259
  141.2 5.8 %all-to-all-start.3 = ((bf16[4,2,160,128]{3,2,1,0:T(8,128)(2,1)}), bf16[4,2,160,128]{3,2,1,0:T(8,128)(2,1)S(1)}, u32[]{:S(2)}, u32[]{:S(2)}) async-start(bf16[4,2,160,128]{3,2,1,0:T(8,128)(2,1)} %bitcast.7), calls=%async_computation.3 | async-start | bytes 655360 | tf_op jit(solution)/shard_map/all_to_all | solution.py:262
  147.1 0.1 select_reduce_fusion
  147.2 0.1 reshape.183
  147.3 1.3 gather_fusion.4
  148.6 4.7 %all-to-all-done.3 = bf16[4,2,160,128]{3,2,1,0:T(8,128)(2,1)S(1)} async-done(((bf16[4,2,160,128]{3,2,1,0:T(8,128)(2,1)}), bf16[4,2,160,128]{3,2,1,0:T(8,128)(2,1)S(1)}, u32[]{:S(2)}, u32[]{:S(2)}) %all-to-all-start.3) | async-done | bytes 327712 | tf_op jit(solution)/shard_map/all_to_all | solution.py:262
  153.3 5.8 %all-to-all-start.1 = ((bf16[4,2,160,128]{3,2,1,0:T(8,128)(2,1)}), bf16[4,2,160,128]{3,2,1,0:T(8,128)(2,1)S(1)}, u32[]{:S(2)}, u32[]{:S(2)}) async-start(bf16[4,2,160,128]{3,2,1,0:T(8,128)(2,1)} %bitcast.6), calls=%async_computation.1 | async-start | bytes 655360 | tf_op jit(solution)/shard_map/all_to_all | solution.py:262
  159.1 9.5 %collective-permute-start.7 = (bf16[4,2,160,128]{3,2,1,0:T(8,128)(2,1)S(1)}, bf16[4,2,160,128]{3,2,1,0:T(8,128)(2,1)S(1)}, u32[]{:S(2)}, u32[]{:S(2)}) collective-permute-start(bf16[4,2,160,128]{3,2,1,0:T(8,128)(2,1)S(1)} %all-to-all-done.3), channel_id=1, source_target_pairs={{0,384},{4,388},{8,392},{12,396},{16,400},{20,404},{24,408},{28,41... | collective-permute-start | bytes 983048 | tf_op jit(solution)/shard_map/ppermute | solution.py:34
  168.7 0.6 gather_fusion.2
  169.3 0.6 gather_fusion.3
  170.0 0.9 reshape.196.near_ref
  170.9 0.5 add.45.pair_ref
  171.4 12.0 %collective-permute-done.7.mir_b = bf16[4,2,160,128]{3,2,1,0:T(8,128)(2,1)S(1)} collective-permute-done((bf16[4,2,160,128]{3,2,1,0:T(8,128)(2,1)S(1)}, bf16[4,2,160,128]{3,2,1,0:T(8,128)(2,1)S(1)}, u32[]{:S(2)}, u32[]{:S(2)}) %collective-permute-start.7) | collective-permute-done | bytes 327712 | tf_op jit(solution)/shard_map/ppermute | solution.py:34
  183.4 0.7 copy-done.5
  184.1 6.0 %shard_map.87 = bf16[4,2,200,200]{3,2,1,0:T(8,128)(2,1)} custom-call(s32[4]{0:T(128)} %slot_ref.1, s32[4]{0:T(128)} %copy-done.7, f32[4]{0:T(128)} %add.45.pair_ref, bf16[4,2,200,200]{3,2,1,0:T(8,128)(2,1)} %bitcast.20, bf16[4,2,160,128]{3,2,1,0:T(8,128)(2,1)} %get-tuple-element.9.own_a, bf16[4,2,160,128]{3,2,1,0:T(8,128)(2,1)} %get-tuple-element.10.own_b, ...), custom_call_target="tpu_custom_call" | custom-call | tf_op jit(solution)/shard_map/pallas_call | solution.py:236
  (31 shorter events, 0.1 us)
Async XLA Ops:
  0.0 54.8 %copy-start = (s32[200]{0:T(256)S(1)}, s32[200]{0:T(256)}, u32[]{:S(2)}) copy-start(s32[200]{0:T(256)} %param.13) | copy-start | bytes 2404
  4.3 19.9 %collective-permute-start = (bf16[208,3200]{1,0:T(8,128)(2,1)}, bf16[208,3200]{1,0:T(8,128)(2,1)S(1)}, u32[]{:S(2)}, u32[]{:S(2)}) collective-permute-start(bf16[208,3200]{1,0:T(8,128)(2,1)} %shard_map.83.refs_0_), channel_id=1, source_target_pairs={{0,1},{4,39},{8,9},{12,47},{16,17},{20,55},{24,25},{28,63},{1,2},{... | collective-permute-start | bytes 3993608 | tf_op jit(solution)/shard_map/ppermute | solution.py:34
  6.2 21.1 %copy-start.8 = (s32[4,2]{0,1:T(2,128)S(1)}, s32[4,2]{0,1:T(2,128)}, u32[]{:S(2)}) copy-start(s32[4,2]{0,1:T(2,128)} %param.11) | copy-start | bytes 100
  9.3 29.2 %collective-permute-start.1 = (bf16[208,3200]{1,0:T(8,128)(2,1)}, bf16[208,3200]{1,0:T(8,128)(2,1)S(1)}, u32[]{:S(2)}, u32[]{:S(2)}) collective-permute-start(bf16[208,3200]{1,0:T(8,128)(2,1)} %shard_map.84.refs_1_), channel_id=1, source_target_pairs={{0,1},{4,39},{8,9},{12,47},{16,17},{20,55},{24,25},{28,63},{1,2},{... | collective-permute-start | bytes 3993608 | tf_op jit(solution)/shard_map/ppermute | solution.py:34
  24.2 42.8 %copy-start.2 = (bf16[208,3200]{1,0:T(8,128)(2,1)}, bf16[208,3200]{1,0:T(8,128)(2,1)S(1)}, u32[]{:S(2)}) copy-start(bf16[208,3200]{1,0:T(8,128)(2,1)S(1)} %collective-permute-done.refs_2_) | copy-start | bytes 3993604
  24.2 28.6 %collective-permute-start.4 = (bf16[208,3200]{1,0:T(8,128)(2,1)S(1)}, bf16[208,3200]{1,0:T(8,128)(2,1)}, u32[]{:S(2)}, u32[]{:S(2)}) collective-permute-start(bf16[208,3200]{1,0:T(8,128)(2,1)S(1)} %collective-permute-done.refs_2_), channel_id=1, source_target_pairs={{0,1},{4,39},{8,9},{12,47},{16,17},{20,55},{24,25},{28,63},{1,2},{... | collective-permute-start | bytes 3993608 | tf_op jit(solution)/shard_map/ppermute | solution.py:34
  27.4 40.1 %collective-permute-start.2 = (bf16[208,3200]{1,0:T(8,128)(2,1)S(1)}, bf16[208,3200]{1,0:T(8,128)(2,1)}, u32[]{:S(2)}, u32[]{:S(2)}) collective-permute-start(bf16[208,3200]{1,0:T(8,128)(2,1)S(1)} %collective-permute-done.refs_2_), channel_id=1, source_target_pairs={{0,4},{4,0},{8,12},{12,8},{16,20},{20,16},{24,28},{28,24},{1,5},{5... | collective-permute-start | bytes 3993608 | tf_op jit(solution)/shard_map/ppermute | solution.py:34
  38.5 28.5 %copy-start.3 = (bf16[208,3200]{1,0:T(8,128)(2,1)}, bf16[208,3200]{1,0:T(8,128)(2,1)S(1)}, u32[]{:S(2)}) copy-start(bf16[208,3200]{1,0:T(8,128)(2,1)S(1)} %collective-permute-done.1.refs_3_) | copy-start | bytes 3993604
  38.5 29.0 %collective-permute-start.3 = (bf16[208,3200]{1,0:T(8,128)(2,1)S(1)}, bf16[208,3200]{1,0:T(8,128)(2,1)}, u32[]{:S(2)}, u32[]{:S(2)}) collective-permute-start(bf16[208,3200]{1,0:T(8,128)(2,1)S(1)} %collective-permute-done.1.refs_3_), channel_id=1, source_target_pairs={{0,4},{4,0},{8,12},{12,8},{16,20},{20,16},{24,28},{28,24},{1,5},{5... | collective-permute-start | bytes 3993608 | tf_op jit(solution)/shard_map/ppermute | solution.py:34
  52.9 14.7 %collective-permute-start.5 = (bf16[208,3200]{1,0:T(8,128)(2,1)}, bf16[208,3200]{1,0:T(8,128)(2,1)}, u32[]{:S(2)}, u32[]{:S(2)}) collective-permute-start(bf16[208,3200]{1,0:T(8,128)(2,1)} %collective-permute-done.4.refs_6_), channel_id=1, source_target_pairs={{0,4},{4,0},{8,12},{12,8},{16,20},{20,16},{24,28},{28,24},{1,5},{5... | collective-permute-start | bytes 3993608 | tf_op jit(solution)/shard_map/ppermute | solution.py:34
  56.3 10.7 %copy-start.7 = (s32[4]{0:T(128)}, s32[4]{0:T(128)S(1)}, u32[]{:S(2)}) copy-start(s32[4]{0:T(128)S(1)} %broadcast_and_fusion.flip_ref) | copy-start | bytes 52
  75.8 52.8 %all-to-all-start.2 = ((bf16[4,2,160,128]{3,2,1,0:T(8,128)(2,1)}), bf16[4,2,160,128]{3,2,1,0:T(8,128)(2,1)S(1)}, u32[]{:S(2)}, u32[]{:S(2)}) async-start(bf16[4,2,160,128]{3,2,1,0:T(8,128)(2,1)} %get-tuple-element.10.own_b), calls=%async_computation.2 | async-start | bytes 655360 | tf_op jit(solution)/shard_map/all_to_all | solution.py:259
  91.6 55.5 %copy-start.9 = (s32[4]{0:T(128)S(1)}, s32[4]{0:T(128)}, u32[]{:S(2)}) copy-start(s32[4]{0:T(128)} %slot_ref.1) | copy-start | bytes 52
  91.6 36.9 %collective-permute-start.6 = (bf16[4,2,160,128]{3,2,1,0:T(8,128)(2,1)}, bf16[4,2,160,128]{3,2,1,0:T(8,128)(2,1)}, u32[]{:S(2)}, u32[]{:S(2)}) collective-permute-start(bf16[4,2,160,128]{3,2,1,0:T(8,128)(2,1)} %get-tuple-element.9.own_a), channel_id=1, source_target_pairs={{0,384},{4,388},{8,392},{12,396},{16,400},{20,404},{24,408},{28,41... | collective-permute-start | bytes 983048 | tf_op jit(solution)/shard_map/ppermute | solution.py:34
  128.6 12.7 %all-to-all-start = ((bf16[4,2,160,128]{3,2,1,0:T(8,128)(2,1)}), bf16[4,2,160,128]{3,2,1,0:T(8,128)(2,1)S(1)}, u32[]{:S(2)}, u32[]{:S(2)}) async-start(bf16[4,2,160,128]{3,2,1,0:T(8,128)(2,1)} %collective-permute-done.6), calls=%async_computation | async-start | bytes 655360 | tf_op jit(solution)/shard_map/all_to_all | solution.py:259
  133.7 35.0 %copy-start.1 = (f32[200]{0:T(256)S(1)}, f32[200]{0:T(256)}, u32[]{:S(2)}) copy-start(f32[200]{0:T(256)} %param.14) | copy-start | bytes 2404
  141.2 12.1 %all-to-all-start.3 = ((bf16[4,2,160,128]{3,2,1,0:T(8,128)(2,1)}), bf16[4,2,160,128]{3,2,1,0:T(8,128)(2,1)S(1)}, u32[]{:S(2)}, u32[]{:S(2)}) async-start(bf16[4,2,160,128]{3,2,1,0:T(8,128)(2,1)} %bitcast.7), calls=%async_computation.3 | async-start | bytes 655360 | tf_op jit(solution)/shard_map/all_to_all | solution.py:262
  147.1 22.9 %copy-start.6 = (bf16[400]{0:T(512)(128)(2,1)S(1)}, bf16[400]{0:T(512)(128)(2,1)}, u32[]{:S(2)}) copy-start(bf16[400]{0:T(512)(128)(2,1)} %param.15) | copy-start | bytes 2404
  153.3 18.1 %all-to-all-start.1 = ((bf16[4,2,160,128]{3,2,1,0:T(8,128)(2,1)}), bf16[4,2,160,128]{3,2,1,0:T(8,128)(2,1)S(1)}, u32[]{:S(2)}, u32[]{:S(2)}) async-start(bf16[4,2,160,128]{3,2,1,0:T(8,128)(2,1)} %bitcast.6), calls=%async_computation.1 | async-start | bytes 655360 | tf_op jit(solution)/shard_map/all_to_all | solution.py:262
  159.1 24.3 %collective-permute-start.7 = (bf16[4,2,160,128]{3,2,1,0:T(8,128)(2,1)S(1)}, bf16[4,2,160,128]{3,2,1,0:T(8,128)(2,1)S(1)}, u32[]{:S(2)}, u32[]{:S(2)}) collective-permute-start(bf16[4,2,160,128]{3,2,1,0:T(8,128)(2,1)S(1)} %all-to-all-done.3), channel_id=1, source_target_pairs={{0,384},{4,388},{8,392},{12,396},{16,400},{20,404},{24,408},{28,41... | collective-permute-start | bytes 983048 | tf_op jit(solution)/shard_map/ppermute | solution.py:34
  171.4 12.0 %copy-start.4 = (bf16[4,2,160,128]{3,2,1,0:T(8,128)(2,1)}, bf16[4,2,160,128]{3,2,1,0:T(8,128)(2,1)S(1)}, u32[]{:S(2)}) copy-start(bf16[4,2,160,128]{3,2,1,0:T(8,128)(2,1)S(1)} %all-to-all-done.1.mir_a) | copy-start | bytes 983044
  183.4 0.7 copy-start.5

commit v2 on v1

v2 whole, which is shorter than its diff:
```python
import functools

import jax
import jax.numpy as jnp
from jax import lax
from jax.experimental import pallas as pl
from jax.experimental.pallas import tpu as pltpu
from jax.sharding import PartitionSpec as P

W = 200
NQ = 16
DEEP = NQ * W
TALL = 208
PIECE = 160
UNIT = 4 * PIECE
BF = jnp.bfloat16
F32 = jnp.float32
VMEM_LIMIT = 56 * 1024 * 1024


def permute(value, move):
    layers, halves, width, cores, lines = lax.axis_size("pair") // 16, 2, 4, 2, 4
    pairs = []
    for z in range(layers):
        for y in range(halves * lines):
            for x in range(width):
                for core in range(cores):
                    ends = []
                    for tz, ty, tx, tc in ((z, y, x, core), move(z, y, x, core)):
                        tz, ty, tx, tc = tz % layers, ty % (halves * lines), tx % width, tc % cores
                        pair = ((tz * halves + ty // lines) * width + tx) * cores + tc
                        ends.append(pair * lines + ty % lines)
                    pairs.append(tuple(ends))
    return lax.ppermute(value, ("pair", "virt"), pairs)


def along_y(value):
    return permute(value, lambda z, y, x, core: (z, y + 1 - 2 * core, x, core))


def swap_cores(value):
    return permute(value, lambda z, y, x, core: (z, y, x, 1 - core))


def to_mirror(value):
    half = lax.axis_size("pair") // 32
    return permute(value, lambda z, y, x, core: (z + half, y, x, core))


def together(*values):
    return lax.optimization_barrier(values)


def params(*semantics):
    return pltpu.CompilerParams(
        dimension_semantics=semantics, vmem_limit_bytes=VMEM_LIMIT
    )


def pack_kernel(order_ref, slab_ref, energy_ref, out_ref):
    for q in range(NQ):
        out_ref[0:W, q * W : (q + 1) * W] = slab_ref[q, 0]
    both = jnp.broadcast_to(energy_ref[...].reshape(1, 2 * W), (TALL - W, 2 * W))
    out_ref[W:TALL, 0:W] = jnp.where(order_ref[0] == 0, both[:, 0:W], both[:, W : 2 * W])
    out_ref[W:TALL, W:DEEP] = jnp.zeros((TALL - W, DEEP - W), BF)


def pack_slab(slab, energy, block):
    return pl.pallas_call(
        pack_kernel,
        out_shape=jax.ShapeDtypeStruct((TALL, DEEP), BF),
        grid_spec=pltpu.PrefetchScalarGridSpec(
            num_scalar_prefetch=1,
            grid=(1,),
            in_specs=[
                pl.BlockSpec((NQ, 1, W, W), lambda i, order: (0, order[0], 0, 0)),
                pl.BlockSpec((2 * W,), lambda i, order: (0,)),
            ],
            out_specs=pl.BlockSpec((TALL, DEEP), lambda i, order: (0, 0)),
        ),
        compiler_params=params("arbitrary"),
        cost_estimate=pl.CostEstimate(flops=0, bytes_accessed=3_000_000, transcendentals=0),
    )(block, slab, energy)


def half_kernel(slab_ref, amp_ref, out_ref):
    for q in range(NQ):
        out_ref[0, :, q * W : (q + 1) * W] = jnp.dot(
            slab_ref[q, 0], amp_ref[0, 0], preferred_element_type=F32
        ).astype(BF)


def first_half(slab, amplitudes, block):
    pairs = amplitudes.shape[0]
    return pl.pallas_call(
        half_kernel,
        out_shape=jax.ShapeDtypeStruct((pairs, W, DEEP), BF),
        grid=(pairs,),
        in_specs=[
            pl.BlockSpec((NQ, 1, W, W), lambda p: (0, block, 0, 0)),
            pl.BlockSpec((1, 1, W, W), lambda p: (p, block, 0, 0)),
        ],
        out_specs=pl.BlockSpec((1, W, DEEP), lambda p: (p, 0, 0)),
        compiler_params=params("arbitrary"),
        cost_estimate=pl.CostEstimate(
            flops=2 * pairs * NQ * W**3, bytes_accessed=9_000_000, transcendentals=0
        ),
    )(slab, amplitudes)


def put_tile(unit_ref, block, tile):
    unit_ref[block * W : (block + 1) * W, :] = tile[:, 0:128]
    unit_ref[2 * W : 3 * W, block * 64 : (block + 1) * 64] = tile[:, 128:192]
    base = 3 * W + 16 * block
    for c in range(13):
        rows = min(16, W - 16 * c)
        unit_ref[base : base + rows, 8 * c : 8 * c + 8] = tile[16 * c : 16 * c + rows, 192:200]


def get_tile(unit, block):
    base = 3 * W + 16 * block
    tail = [
        unit[base : base + min(16, W - 16 * c), 8 * c : 8 * c + 8] for c in range(13)
    ]
    return jnp.concatenate(
        [
            unit[block * W : (block + 1) * W, :],
            unit[2 * W : 3 * W, block * 64 : (block + 1) * 64],
            jnp.concatenate(tail, axis=0),
        ],
        axis=1,
    )


def ladder_kernel(first, count, source_ref, int_ref, half_zero, half_one, *refs):
    sources, (out_ref, own_ref, far_ref, right, left, unit, sems) = refs[:8], refs[8:]
    halves = (half_zero, half_one)

    for t in range(2 * count):
        pltpu.make_async_copy(halves[t % 2].at[first + t // 2], left.at[t], sems.at[0, t]).start()
        for r in range(8):

            @pl.when(source_ref[first * 2 + t] == r)
            def _():
                pltpu.make_async_copy(sources[r], right.at[t], sems.at[1, t]).start()

    unit[3 * W : UNIT, :] = jnp.zeros((UNIT - 3 * W, 128), F32)
    for t in range(2 * count):
        pair, block = t // 2, t % 2
        pltpu.make_async_copy(halves[0].at[first], left.at[t], sems.at[0, t]).wait()
        pltpu.make_async_copy(sources[0], right.at[t], sems.at[1, t]).wait()
        ladder = lax.dot_general(
            left[t], right[t, 0:W, :], (((1,), (1,)), ((), ())), preferred_element_type=F32
        )
        tile = int_ref[pair, block].astype(F32) + ladder
        own_ref[pair, block] = tile.astype(BF)
        far_ref[pair, block] = right[t, W:TALL, 0:W].astype(F32)
        put_tile(unit, block, tile)
        if block == 1:
            for j in range(4):
                out_ref[j, pair] = unit[j * PIECE : (j + 1) * PIECE, :].astype(BF)


def residual_units(first, count, source, halves, integrals, blocks):
    return pl.pallas_call(
        functools.partial(ladder_kernel, first, count),
        out_shape=(
            jax.ShapeDtypeStruct((4, count, PIECE, 128), BF),
            jax.ShapeDtypeStruct((count, 2, W, W), BF),
            jax.ShapeDtypeStruct((count, 2, TALL - W, W), F32),
        ),
        grid_spec=pltpu.PrefetchScalarGridSpec(
            num_scalar_prefetch=1,
            grid=(1,),
            in_specs=[pl.BlockSpec((count, 2, W, W), lambda i, s: (first // count, 0, 0, 0))]
            + [pl.BlockSpec(memory_space=pl.ANY)] * 10,
            out_specs=[
                pl.BlockSpec((4, count, PIECE, 128), lambda i, s: (0, 0, 0, 0)),
                pl.BlockSpec((count, 2, W, W), lambda i, s: (0, 0, 0, 0)),
                pl.BlockSpec((count, 2, TALL - W, W), lambda i, s: (0, 0, 0, 0)),
            ],
            scratch_shapes=[
                pltpu.VMEM((2 * count, TALL, DEEP), BF),
                pltpu.VMEM((2 * count, W, DEEP), BF),
                pltpu.VMEM((UNIT, 128), F32),
                pltpu.SemaphoreType.DMA((2, 2 * count)),
            ],
        ),
        compiler_params=params("arbitrary"),
        cost_estimate=pl.CostEstimate(
            flops=4 * count * NQ * W**3, bytes_accessed=count * 2 * 2_700_000, transcendentals=0
        ),
    )(source, integrals, *halves, *blocks)


def update_kernel(
    slot_ref, flip_ref, pair_ref, amp_ref, own_a, own_b, far_a, far_b, mir_a, mir_b, near_ref, out_ref
):
    p = pl.program_id(0)
    low = slot_ref[p] < 2
    other = jnp.concatenate(
        [jnp.where(low, mir_a[j, 0].astype(F32), mir_b[j, 0].astype(F32)) for j in range(4)], axis=0
    )
    straight = flip_ref[p] == 0
    tiles = [get_tile(other, b) for b in range(2)]
    for b in range(2):
        mirror = jnp.where(straight, tiles[b], tiles[1 - b])
        square = jnp.pad(mirror, ((0, 56), (0, 56)))
        own = jnp.where(p < 2, own_a[0, b].astype(F32), own_b[0, b].astype(F32))
        symmetric = own + square.T[0:W, 0:W]
        far = jnp.where(p < 2, far_a[0, b, 0:1, :], far_b[0, b, 0:1, :])
        denominator = pair_ref[p] - near_ref[b] - far
        out_ref[0, b] = (amp_ref[0, b].astype(F32) + symmetric / denominator).astype(BF)


def update(slot, flip, pair_energy, amplitudes, own_a, own_b, far_a, far_b, mir_a, mir_b, near):
    pairs = amplitudes.shape[0]
    low = lambda p, s, f, e: (jnp.minimum(p, 1), 0, 0, 0)
    high = lambda p, s, f, e: (jnp.maximum(p - 2, 0), 0, 0, 0)
    pick = lambda p, s, f, e: (0, jnp.bitwise_and(s[p], 1), 0, 0)
    own = lambda p, s, f, e: (p, 0, 0, 0)
    return pl.pallas_call(
        update_kernel,
        out_shape=jax.ShapeDtypeStruct((pairs, 2, W, W), BF),
        grid_spec=pltpu.PrefetchScalarGridSpec(
            num_scalar_prefetch=3,
            grid=(pairs,),
            in_specs=[
                pl.BlockSpec((1, 2, W, W), own),
                pl.BlockSpec((1, 2, W, W), low),
                pl.BlockSpec((1, 2, W, W), high),
                pl.BlockSpec((1, 2, TALL - W, W), low),
                pl.BlockSpec((1, 2, TALL - W, W), high),
                pl.BlockSpec((4, 1, PIECE, 128), pick),
                pl.BlockSpec((4, 1, PIECE, 128), pick),
                pl.BlockSpec((2, W, 1), lambda p, s, f, e: (0, 0, 0)),
            ],
            out_specs=pl.BlockSpec((1, 2, W, W), own),
        ),
        compiler_params=params("arbitrary"),
    )(slot, flip, pair_energy, amplitudes, own_a, own_b, far_a, far_b, mir_a, mir_b, near)


def across_virt(units, step):
    scattered = lax.all_to_all(units, "virt", 0, 0, tiled=True)
    index = jnp.bitwise_xor(jnp.arange(4, dtype=jnp.int32)[:, None], step[None, :])
    chosen = scattered[index, jnp.arange(units.shape[1], dtype=jnp.int32)[None, :]]
    return lax.all_to_all(chosen, "virt", 0, 0, tiled=True)


def on_device(
    amplitudes, integrals, ladder_slab, pair_list, mirror_slot, occ_irrep, occ_energy, virt_energy
):
    pairs = amplitudes.shape[0]
    amp = amplitudes.reshape(pairs, 2, W, W)
    ints = integrals.reshape(pairs, 2, W, W)
    slab = ladder_slab.reshape(NQ, 2, W, W)
    core = lax.rem(lax.axis_index("pair"), 2).astype(jnp.int32)
    virt = lax.axis_index("virt").astype(jnp.int32)

    irrep = jnp.bitwise_xor(occ_irrep[pair_list[:, 0]], occ_irrep[pair_list[:, 1]])
    step, flip = jnp.right_shift(irrep, 1), jnp.bitwise_and(irrep, 1)
    apart = jnp.bitwise_and(jnp.bitwise_xor(virt, step) - virt, 3)[:, None]
    second = (jnp.bitwise_xor(jnp.arange(2)[None, :], flip[:, None]) != core).astype(jnp.int32)
    mine = 2 + second
    theirs = 5 - second
    source = jnp.where(
        apart == 0,
        second,
        jnp.where(apart == 2, 6 + second, jnp.where(apart == 3 - 2 * core, mine, theirs)),
    ).reshape(-1)
    slots = jnp.arange(pairs, dtype=jnp.int32)
    mirror_step = jnp.sum(
        jnp.where(mirror_slot[:, None] == slots[None, :], step[:, None], 0), axis=0
    )
    pair_energy = occ_energy[pair_list[:, 0]] + occ_energy[pair_list[:, 1]]
    near = virt_energy.astype(F32).reshape(2, W, 1)

    one = pack_slab(slab, virt_energy, core[None])
    two = pack_slab(slab, virt_energy, 1 - core[None])
    near_one = along_y(one)
    near_two = along_y(two)
    half_zero = first_half(slab, amp, 0)
    near_one, half_zero, source, near = together(near_one, half_zero, source, near)
    far_one = along_y(near_one)
    swapped_one = swap_cores(near_one)
    half_one = first_half(slab, amp, 1)
    near_two, half_one, flip, mirror_step, pair_energy, step = together(
        near_two, half_one, flip, mirror_step, pair_energy, step
    )
    swapped_two = swap_cores(near_two)
    blocks = (
        one, two, near_one, near_two, swapped_one, swapped_two, far_one, swap_cores(far_one)
    )
    halves = (half_zero, half_one)

    unit_a, own_a, far_a = residual_units(0, 2, source, halves, ints, blocks)
    unit_a, source = together(unit_a, source)
    mir_a = to_mirror(unit_a)
    unit_b, own_b, far_b = residual_units(2, 2, source, halves, ints, blocks)
    crossed_b = across_virt(unit_b, step[2:4])
    mir_a, crossed_b = together(mir_a, crossed_b)
    mir_b = to_mirror(crossed_b)
    mir_a = across_virt(mir_a, mirror_step[0:2])
    new = update(
        mirror_slot, flip, pair_energy, amp, own_a, own_b, far_a, far_b, mir_a, mir_b, near
    )
    return new.reshape(amplitudes.shape)


def solution(mesh):
    return jax.shard_map(
        on_device,
        mesh=mesh,
        in_specs=(
            P("pair", "virt", None),
            P("pair", "virt", None),
            P(None, "virt", None),
            P("pair", None),
            P("pair"),
            P(),
            P(),
            P("virt"),
        ),
        out_specs=P("pair", "virt", None),
        check_vma=False,
    )
```

time: 191 us -> 183 us (0.958)
  the two profiles are of different devices: /device:TPU:120 before, /device:TPU:14 now
where the time goes in v2:
time: 183 us; the launch traced here: 182 us
  starting transfers between devices  74.5 us (41%)
  waiting for transfers between devices  56.6 us (31%)
  Pallas kernels  40.2 us (22%)
  local copies, waits for them, and re-layouts  8.86 us (5%)
    ppermute x8, starting transfers between devices, permute(): return lax.ppermute(value, ('pair', 'virt'), pairs)  53.9 us
    ppermute x8, waiting for transfers between devices, permute(): return lax.ppermute(value, ('pair', 'virt'), pairs)  41.7 us
    pallas_call x2, Pallas kernels, residual_units(): pl.pallas_call(functools.partial(ladder_kernel, first, count), out_shape=...  16.9 us
    all_to_all x2, waiting for transfers between devices, across_virt(): scattered = lax.all_to_all(units, 'virt', 0, 0, tiled=True)  14.9 us
    pallas_call x2, Pallas kernels, first_half(): pl.pallas_call(half_kernel, out_shape=jax.ShapeDtypeStruct((pairs, W, DEE...  11.9 us
    all_to_all x2, starting transfers between devices, across_virt(): scattered = lax.all_to_all(units, 'virt', 0, 0, tiled=True)  10.8 us
    all_to_all x2, starting transfers between devices, across_virt(): return lax.all_to_all(chosen, 'virt', 0, 0, tiled=True)  9.9 us
    pallas_call x2, Pallas kernels, pack_slab(): pl.pallas_call(pack_kernel, out_shape=jax.ShapeDtypeStruct((TALL, DEEP),...  6.03 us
  transfers between devices with their start and end apart: 12, of which 8 were waited for; matrix products, arithmetic and copies ran while one was open for 3% of the time, Pallas kernels for 8%

profile of v2, /device:TPU:14, one launch (start us, length us, event | category | flops | bytes accessed | tf_op | source)
XLA Modules:
  0.0 181.8 jit_solution(18192693874128187748)
XLA Ops:
  0.0 3.0 %shard_map.84.refs_0_ = bf16[208,3200]{1,0:T(8,128)(2,1)} custom-call(s32[1]{0:T(128)} %bitcast.order_ref, bf16[16,2,200,200]{3,2,1,0:T(8,128)(2,1)} %bitcast.16, bf16[400]{0:T(512)(128)(2,1)} %energy_ref.3), custom_call_target="tpu_custom_call" | custom-call | bytes 3000000 | tf_op jit(solution)/shard_map/pallas_call | solution.py:69
  3.0 3.5 %collective-permute-start.1 = (bf16[208,3200]{1,0:T(8,128)(2,1)}, bf16[208,3200]{1,0:T(8,128)(2,1)S(1)}, u32[]{:S(2)}, u32[]{:S(2)}) collective-permute-start(bf16[208,3200]{1,0:T(8,128)(2,1)} %shard_map.84.refs_0_), channel_id=1, source_target_pairs={{0,1},{4,39},{8,9},{12,47},{16,17},{20,55},{24,25},{28,63},{1,2},{... | collective-permute-start | bytes 3993608 | tf_op jit(solution)/shard_map/ppermute | solution.py:34
  6.5 3.0 %shard_map.82.refs_1_ = bf16[208,3200]{1,0:T(8,128)(2,1)} custom-call(s32[1]{0:T(128)S(6)} %sub.24.order_ref, bf16[16,2,200,200]{3,2,1,0:T(8,128)(2,1)} %bitcast.17, bf16[400]{0:T(512)(128)(2,1)} %energy_ref.3), custom_call_target="tpu_custom_call" | custom-call | bytes 3000000 | tf_op jit(solution)/shard_map/pallas_call | solution.py:69
  9.5 3.5 %collective-permute-start = (bf16[208,3200]{1,0:T(8,128)(2,1)}, bf16[208,3200]{1,0:T(8,128)(2,1)S(1)}, u32[]{:S(2)}, u32[]{:S(2)}) collective-permute-start(bf16[208,3200]{1,0:T(8,128)(2,1)} %shard_map.82.refs_1_), channel_id=1, source_target_pairs={{0,1},{4,39},{8,9},{12,47},{16,17},{20,55},{24,25},{28,63},{1,2},{... | collective-permute-start | bytes 3993608 | tf_op jit(solution)/shard_map/ppermute | solution.py:34
  13.1 0.6 gather_fusion
  13.7 0.6 gather_fusion.1
  14.4 0.1 broadcast_in_dim.71
  14.4 0.1 broadcast_in_dim.72
  14.6 0.1 broadcast_in_dim.74
  14.8 0.1 broadcast_in_dim.76
  14.9 0.1 reshape.145
  15.0 6.0 %shard_map.85.half_zero = bf16[4,200,3200]{2,1,0:T(8,128)(2,1)} custom-call(bf16[16,2,200,200]{3,2,1,0:T(8,128)(2,1)} %bitcast.18, bf16[4,2,200,200]{3,2,1,0:T(8,128)(2,1)} %bitcast.20), custom_call_target="tpu_custom_call" | custom-call | flops 1024000000 | bytes 9000000 | tf_op jit(solution)/shard_map/pallas_call | solution.py:95
  21.0 0.5 select_select_fusion.source_ref
  21.5 0.1 reshape.147
  21.6 1.3 collective-permute-done.1.refs_2_
  22.9 3.5 %collective-permute-start.4 = (bf16[208,3200]{1,0:T(8,128)(2,1)S(1)}, bf16[208,3200]{1,0:T(8,128)(2,1)}, u32[]{:S(2)}, u32[]{:S(2)}) collective-permute-start(bf16[208,3200]{1,0:T(8,128)(2,1)S(1)} %collective-permute-done.1.refs_2_), channel_id=1, source_target_pairs={{0,1},{4,39},{8,9},{12,47},{16,17},{20,55},{24,25},{28,63},{1,2},{... | collective-permute-start | bytes 3993608 | tf_op jit(solution)/shard_map/ppermute | solution.py:34
  26.4 0.6 gather_fusion.2
  27.0 0.6 gather_fusion.3
  27.7 0.5 add.45.pair_ref
  28.2 5.9 %shard_map.83.half_one = bf16[4,200,3200]{2,1,0:T(8,128)(2,1)} custom-call(bf16[16,2,200,200]{3,2,1,0:T(8,128)(2,1)} %bitcast.19, bf16[4,2,200,200]{3,2,1,0:T(8,128)(2,1)} %bitcast.21), custom_call_target="tpu_custom_call" | custom-call | flops 1024000000 | bytes 9000000 | tf_op jit(solution)/shard_map/pallas_call | solution.py:95
  34.2 0.1 select_reduce_fusion
  34.3 1.9 %collective-permute-start.2 = (bf16[208,3200]{1,0:T(8,128)(2,1)S(1)}, bf16[208,3200]{1,0:T(8,128)(2,1)S(1)}, u32[]{:S(2)}, u32[]{:S(2)}) collective-permute-start(bf16[208,3200]{1,0:T(8,128)(2,1)S(1)} %collective-permute-done.1.refs_2_), channel_id=1, source_target_pairs={{0,4},{4,0},{8,12},{12,8},{16,20},{20,16},{24,28},{28,24},{1,5},{5... | collective-permute-start | bytes 3993608 | tf_op jit(solution)/shard_map/ppermute | solution.py:34
  36.2 1.0 collective-permute-done.refs_3_
  37.2 1.9 %collective-permute-start.3 = (bf16[208,3200]{1,0:T(8,128)(2,1)S(1)}, bf16[208,3200]{1,0:T(8,128)(2,1)S(1)}, u32[]{:S(2)}, u32[]{:S(2)}) collective-permute-start(bf16[208,3200]{1,0:T(8,128)(2,1)S(1)} %collective-permute-done.refs_3_), channel_id=1, source_target_pairs={{0,4},{4,0},{8,12},{12,8},{16,20},{20,16},{24,28},{28,24},{1,5},{5... | collective-permute-start | bytes 3993608 | tf_op jit(solution)/shard_map/ppermute | solution.py:34
  39.1 12.4 %collective-permute-done.4.refs_6_ = bf16[208,3200]{1,0:T(8,128)(2,1)} collective-permute-done((bf16[208,3200]{1,0:T(8,128)(2,1)S(1)}, bf16[208,3200]{1,0:T(8,128)(2,1)}, u32[]{:S(2)}, u32[]{:S(2)}) %collective-permute-start.4) | collective-permute-done | bytes 1331232 | tf_op jit(solution)/shard_map/ppermute | solution.py:34
  51.5 1.9 %collective-permute-start.5 = (bf16[208,3200]{1,0:T(8,128)(2,1)}, bf16[208,3200]{1,0:T(8,128)(2,1)S(1)}, u32[]{:S(2)}, u32[]{:S(2)}) collective-permute-start(bf16[208,3200]{1,0:T(8,128)(2,1)} %collective-permute-done.4.refs_6_), channel_id=1, source_target_pairs={{0,4},{4,0},{8,12},{12,8},{16,20},{20,16},{24,28},{28,24},{1,5},{5... | collective-permute-start | bytes 3993608 | tf_op jit(solution)/shard_map/ppermute | solution.py:34
  53.5 3.2 %collective-permute-done.5.refs_7_ = bf16[208,3200]{1,0:T(8,128)(2,1)S(1)} collective-permute-done((bf16[208,3200]{1,0:T(8,128)(2,1)}, bf16[208,3200]{1,0:T(8,128)(2,1)S(1)}, u32[]{:S(2)}, u32[]{:S(2)}) %collective-permute-start.5) | collective-permute-done | bytes 1331232 | tf_op jit(solution)/shard_map/ppermute | solution.py:34
  56.7 1.1 copy-done.6
  57.8 8.7 %shard_map.86 = (bf16[4,2,160,128]{3,2,1,0:T(8,128)(2,1)}, bf16[2,2,200,200]{3,2,1,0:T(8,128)(2,1)}, f32[2,2,8,200]{3,2,1,0:T(8,128)}) custom-call(s32[8]{0:T(128)} %select_select_fusion.source_ref, bf16[4,2,200,200]{3,2,1,0:T(8,128)(2,1)} %bitcast.23, bf16[4,200,3200]{2,1,0:T(8,128)(2,1)} %shard_map.85.half_zero, bf16[4,200,3200]{2,1,0:T(8,128)(2,1)} %shard_map.83.half_one, ...), custom_call_target="tpu_custom_call" | custom-call | flops 1024000000 | bytes 10800000 | tf_op jit(solution)/shard_map/pallas_call | solution.py:165
  66.5 8.1 %shard_map.87 = (bf16[4,2,160,128]{3,2,1,0:T(8,128)(2,1)}, bf16[2,2,200,200]{3,2,1,0:T(8,128)(2,1)}, f32[2,2,8,200]{3,2,1,0:T(8,128)}) custom-call(s32[8]{0:T(128)} %select_select_fusion.source_ref, bf16[4,2,200,200]{3,2,1,0:T(8,128)(2,1)} %bitcast.24, bf16[4,200,3200]{2,1,0:T(8,128)(2,1)} %shard_map.85.half_zero, bf16[4,200,3200]{2,1,0:T(8,128)(2,1)} %shard_map.83.half_one, ...), custom_call_target="tpu_custom_call" | custom-call | flops 1024000000 | bytes 10800000 | tf_op jit(solution)/shard_map/pallas_call | solution.py:165
  74.6 5.7 %all-to-all-start = ((bf16[4,2,160,128]{3,2,1,0:T(8,128)(2,1)}), bf16[4,2,160,128]{3,2,1,0:T(8,128)(2,1)S(1)}, u32[]{:S(2)}, u32[]{:S(2)}) async-start(bf16[4,2,160,128]{3,2,1,0:T(8,128)(2,1)} %get-tuple-element.39), calls=%async_computation | async-start | bytes 655360 | tf_op jit(solution)/shard_map/all_to_all | solution.py:245
  80.4 0.1 reshape.180
  80.5 8.3 %all-to-all-done = bf16[4,2,160,128]{3,2,1,0:T(8,128)(2,1)S(1)} async-done(((bf16[4,2,160,128]{3,2,1,0:T(8,128)(2,1)}), bf16[4,2,160,128]{3,2,1,0:T(8,128)(2,1)S(1)}, u32[]{:S(2)}, u32[]{:S(2)}) %all-to-all-start) | async-done | bytes 327712 | tf_op jit(solution)/shard_map/all_to_all | solution.py:245
  88.8 1.3 gather_fusion.4
  90.1 5.7 %all-to-all-start.1 = ((bf16[4,2,160,128]{3,2,1,0:T(8,128)(2,1)}), bf16[4,2,160,128]{3,2,1,0:T(8,128)(2,1)S(1)}, u32[]{:S(2)}, u32[]{:S(2)}) async-start(bf16[4,2,160,128]{3,2,1,0:T(8,128)(2,1)} %bitcast.6), calls=%async_computation.1 | async-start | bytes 655360 | tf_op jit(solution)/shard_map/all_to_all | solution.py:248
  95.8 14.5 %collective-permute-start.6 = (bf16[4,2,160,128]{3,2,1,0:T(8,128)(2,1)S(1)}, bf16[4,2,160,128]{3,2,1,0:T(8,128)(2,1)}, u32[]{:S(2)}, u32[]{:S(2)}) collective-permute-start(bf16[4,2,160,128]{3,2,1,0:T(8,128)(2,1)S(1)} %copy-done.13), channel_id=1, source_target_pairs={{0,384},{4,388},{8,392},{12,396},{16,400},{20,404},{24,408},{28,41... | collective-permute-start | bytes 983048 | tf_op jit(solution)/shard_map/ppermute | solution.py:34
  110.3 5.8 %collective-permute-done.6 = bf16[4,2,160,128]{3,2,1,0:T(8,128)(2,1)} collective-permute-done((bf16[4,2,160,128]{3,2,1,0:T(8,128)(2,1)S(1)}, bf16[4,2,160,128]{3,2,1,0:T(8,128)(2,1)}, u32[]{:S(2)}, u32[]{:S(2)}) %collective-permute-start.6) | collective-permute-done | bytes 327712 | tf_op jit(solution)/shard_map/ppermute | solution.py:34
  116.0 5.1 %all-to-all-start.2 = ((bf16[4,2,160,128]{3,2,1,0:T(8,128)(2,1)}), bf16[4,2,160,128]{3,2,1,0:T(8,128)(2,1)S(1)}, u32[]{:S(2)}, u32[]{:S(2)}) async-start(bf16[4,2,160,128]{3,2,1,0:T(8,128)(2,1)} %collective-permute-done.6), calls=%async_computation.2 | async-start | bytes 655360 | tf_op jit(solution)/shard_map/all_to_all | solution.py:245
  121.1 0.1 reshape.186
  121.2 6.6 %all-to-all-done.2 = bf16[4,2,160,128]{3,2,1,0:T(8,128)(2,1)S(1)} async-done(((bf16[4,2,160,128]{3,2,1,0:T(8,128)(2,1)}), bf16[4,2,160,128]{3,2,1,0:T(8,128)(2,1)S(1)}, u32[]{:S(2)}, u32[]{:S(2)}) %all-to-all-start.2) | async-done | bytes 327712 | tf_op jit(solution)/shard_map/all_to_all | solution.py:245
  127.9 1.3 gather_fusion.5
  129.2 4.2 %all-to-all-start.3 = ((bf16[4,2,160,128]{3,2,1,0:T(8,128)(2,1)}), bf16[4,2,160,128]{3,2,1,0:T(8,128)(2,1)S(1)}, u32[]{:S(2)}, u32[]{:S(2)}) async-start(bf16[4,2,160,128]{3,2,1,0:T(8,128)(2,1)} %bitcast.7), calls=%async_computation.3 | async-start | bytes 655360 | tf_op jit(solution)/shard_map/all_to_all | solution.py:248
  133.4 23.3 %collective-permute-start.7 = (bf16[4,2,160,128]{3,2,1,0:T(8,128)(2,1)S(1)}, bf16[4,2,160,128]{3,2,1,0:T(8,128)(2,1)S(1)}, u32[]{:S(2)}, u32[]{:S(2)}) collective-permute-start(bf16[4,2,160,128]{3,2,1,0:T(8,128)(2,1)S(1)} %all-to-all-done.1), channel_id=1, source_target_pairs={{0,384},{4,388},{8,392},{12,396},{16,400},{20,404},{24,408},{28,41... | collective-permute-start | bytes 983048 | tf_op jit(solution)/shard_map/ppermute | solution.py:34
  156.6 0.8 copy.10.near_ref
  157.5 18.0 %collective-permute-done.7.mir_b = bf16[4,2,160,128]{3,2,1,0:T(8,128)(2,1)S(1)} collective-permute-done((bf16[4,2,160,128]{3,2,1,0:T(8,128)(2,1)S(1)}, bf16[4,2,160,128]{3,2,1,0:T(8,128)(2,1)S(1)}, u32[]{:S(2)}, u32[]{:S(2)}) %collective-permute-start.7) | collective-permute-done | bytes 327712 | tf_op jit(solution)/shard_map/ppermute | solution.py:34
  175.5 0.7 copy-done.8
  176.2 0.1 copy-done.7
  176.3 5.5 %shard_map.88 = bf16[4,2,200,200]{3,2,1,0:T(8,128)(2,1)} custom-call(s32[4]{0:T(128)} %slot_ref.1, s32[4]{0:T(128)} %copy-done.10, f32[4]{0:T(128)} %add.45.pair_ref, bf16[4,2,200,200]{3,2,1,0:T(8,128)(2,1)} %bitcast.22, bf16[2,2,200,200]{3,2,1,0:T(8,128)(2,1)} %get-tuple-element.32.own_a, bf16[2,2,200,200]{3,2,1,0:T(8,128)(2,1)} %get-tuple-element.35.own_b, ...), custom_call_target="tpu_custom_call" | custom-call | tf_op jit(solution)/shard_map/pallas_call | solution.py:222
  (40 shorter events, 0.4 us)
Async XLA Ops:
  0.0 13.1 %copy-start = (s32[200]{0:T(256)S(1)}, s32[200]{0:T(256)}, u32[]{:S(2)}) copy-start(s32[200]{0:T(256)} %param.13) | copy-start | bytes 2404
  3.0 19.9 %collective-permute-start.1 = (bf16[208,3200]{1,0:T(8,128)(2,1)}, bf16[208,3200]{1,0:T(8,128)(2,1)S(1)}, u32[]{:S(2)}, u32[]{:S(2)}) collective-permute-start(bf16[208,3200]{1,0:T(8,128)(2,1)} %shard_map.84.refs_0_), channel_id=1, source_target_pairs={{0,1},{4,39},{8,9},{12,47},{16,17},{20,55},{24,25},{28,63},{1,2},{... | collective-permute-start | bytes 3993608 | tf_op jit(solution)/shard_map/ppermute | solution.py:34
  6.5 6.5 %copy-start.11 = (s32[4,2]{0,1:T(2,128)S(1)}, s32[4,2]{0,1:T(2,128)}, u32[]{:S(2)}) copy-start(s32[4,2]{0,1:T(2,128)} %param.11) | copy-start | bytes 100
  9.5 27.6 %collective-permute-start = (bf16[208,3200]{1,0:T(8,128)(2,1)}, bf16[208,3200]{1,0:T(8,128)(2,1)S(1)}, u32[]{:S(2)}, u32[]{:S(2)}) collective-permute-start(bf16[208,3200]{1,0:T(8,128)(2,1)} %shard_map.82.refs_1_), channel_id=1, source_target_pairs={{0,1},{4,39},{8,9},{12,47},{16,17},{20,55},{24,25},{28,63},{1,2},{... | collective-permute-start | bytes 3993608 | tf_op jit(solution)/shard_map/ppermute | solution.py:34
  14.9 6.1 %copy-start.10 = (s32[4]{0:T(128)}, s32[4]{0:T(128)S(1)}, u32[]{:S(2)}) copy-start(s32[4]{0:T(128)S(1)} %broadcast_and_fusion.flip_ref) | copy-start | bytes 52
  15.0 6.5 %copy-start.9 = (bf16[400]{0:T(512)(128)(2,1)S(1)}, bf16[400]{0:T(512)(128)(2,1)}, u32[]{:S(2)}) copy-start(bf16[400]{0:T(512)(128)(2,1)} %energy_ref.3) | copy-start | bytes 2404
  15.0 11.4 %copy-start.1 = (f32[200]{0:T(256)S(1)}, f32[200]{0:T(256)}, u32[]{:S(2)}) copy-start(f32[200]{0:T(256)} %param.14) | copy-start | bytes 2404
  22.9 11.4 %copy-start.2 = (bf16[208,3200]{1,0:T(8,128)(2,1)}, bf16[208,3200]{1,0:T(8,128)(2,1)S(1)}, u32[]{:S(2)}) copy-start(bf16[208,3200]{1,0:T(8,128)(2,1)S(1)} %collective-permute-done.1.refs_2_) | copy-start | bytes 3993604
  22.9 28.6 %collective-permute-start.4 = (bf16[208,3200]{1,0:T(8,128)(2,1)S(1)}, bf16[208,3200]{1,0:T(8,128)(2,1)}, u32[]{:S(2)}, u32[]{:S(2)}) collective-permute-start(bf16[208,3200]{1,0:T(8,128)(2,1)S(1)} %collective-permute-done.1.refs_2_), channel_id=1, source_target_pairs={{0,1},{4,39},{8,9},{12,47},{16,17},{20,55},{24,25},{28,63},{1,2},{... | collective-permute-start | bytes 3993608 | tf_op jit(solution)/shard_map/ppermute | solution.py:34
  28.2 5.9 %copy-start.12 = (s32[4]{0:T(128)S(1)}, s32[4]{0:T(128)}, u32[]{:S(2)}) copy-start(s32[4]{0:T(128)} %slot_ref.1) | copy-start | bytes 52
  34.3 19.2 %collective-permute-start.2 = (bf16[208,3200]{1,0:T(8,128)(2,1)S(1)}, bf16[208,3200]{1,0:T(8,128)(2,1)S(1)}, u32[]{:S(2)}, u32[]{:S(2)}) collective-permute-start(bf16[208,3200]{1,0:T(8,128)(2,1)S(1)} %collective-permute-done.1.refs_2_), channel_id=1, source_target_pairs={{0,4},{4,0},{8,12},{12,8},{16,20},{20,16},{24,28},{28,24},{1,5},{5... | collective-permute-start | bytes 3993608 | tf_op jit(solution)/shard_map/ppermute | solution.py:34
  37.2 19.5 %copy-start.3 = (bf16[208,3200]{1,0:T(8,128)(2,1)}, bf16[208,3200]{1,0:T(8,128)(2,1)S(1)}, u32[]{:S(2)}) copy-start(bf16[208,3200]{1,0:T(8,128)(2,1)S(1)} %collective-permute-done.refs_3_) | copy-start | bytes 3993604
  37.2 16.3 %collective-permute-start.3 = (bf16[208,3200]{1,0:T(8,128)(2,1)S(1)}, bf16[208,3200]{1,0:T(8,128)(2,1)S(1)}, u32[]{:S(2)}, u32[]{:S(2)}) collective-permute-start(bf16[208,3200]{1,0:T(8,128)(2,1)S(1)} %collective-permute-done.refs_3_), channel_id=1, source_target_pairs={{0,4},{4,0},{8,12},{12,8},{16,20},{20,16},{24,28},{28,24},{1,5},{5... | collective-permute-start | bytes 3993608 | tf_op jit(solution)/shard_map/ppermute | solution.py:34
  51.5 5.2 %collective-permute-start.5 = (bf16[208,3200]{1,0:T(8,128)(2,1)}, bf16[208,3200]{1,0:T(8,128)(2,1)S(1)}, u32[]{:S(2)}, u32[]{:S(2)}) collective-permute-start(bf16[208,3200]{1,0:T(8,128)(2,1)} %collective-permute-done.4.refs_6_), channel_id=1, source_target_pairs={{0,4},{4,0},{8,12},{12,8},{16,20},{20,16},{24,28},{28,24},{1,5},{5... | collective-permute-start | bytes 3993608 | tf_op jit(solution)/shard_map/ppermute | solution.py:34
  53.5 3.2 %copy-start.4 = (bf16[208,3200]{1,0:T(8,128)(2,1)}, bf16[208,3200]{1,0:T(8,128)(2,1)S(1)}, u32[]{:S(2)}) copy-start(bf16[208,3200]{1,0:T(8,128)(2,1)S(1)} %collective-permute-done.2.refs_4_) | copy-start | bytes 3993604
  53.5 3.2 %copy-start.5 = (bf16[208,3200]{1,0:T(8,128)(2,1)}, bf16[208,3200]{1,0:T(8,128)(2,1)S(1)}, u32[]{:S(2)}) copy-start(bf16[208,3200]{1,0:T(8,128)(2,1)S(1)} %collective-permute-done.3.refs_5_) | copy-start | bytes 3993604
  56.7 1.1 copy-start.6
  74.6 21.2 %copy-start.13 = (bf16[4,2,160,128]{3,2,1,0:T(8,128)(2,1)S(1)}, bf16[4,2,160,128]{3,2,1,0:T(8,128)(2,1)}, u32[]{:S(2)}) copy-start(bf16[4,2,160,128]{3,2,1,0:T(8,128)(2,1)} %get-tuple-element.38) | copy-start | bytes 983044
  74.6 14.1 %all-to-all-start = ((bf16[4,2,160,128]{3,2,1,0:T(8,128)(2,1)}), bf16[4,2,160,128]{3,2,1,0:T(8,128)(2,1)S(1)}, u32[]{:S(2)}, u32[]{:S(2)}) async-start(bf16[4,2,160,128]{3,2,1,0:T(8,128)(2,1)} %get-tuple-element.39), calls=%async_computation | async-start | bytes 655360 | tf_op jit(solution)/shard_map/all_to_all | solution.py:245
  90.1 26.0 %all-to-all-start.1 = ((bf16[4,2,160,128]{3,2,1,0:T(8,128)(2,1)}), bf16[4,2,160,128]{3,2,1,0:T(8,128)(2,1)S(1)}, u32[]{:S(2)}, u32[]{:S(2)}) async-start(bf16[4,2,160,128]{3,2,1,0:T(8,128)(2,1)} %bitcast.6), calls=%async_computation.1 | async-start | bytes 655360 | tf_op jit(solution)/shard_map/all_to_all | solution.py:248
  95.8 20.2 %collective-permute-start.6 = (bf16[4,2,160,128]{3,2,1,0:T(8,128)(2,1)S(1)}, bf16[4,2,160,128]{3,2,1,0:T(8,128)(2,1)}, u32[]{:S(2)}, u32[]{:S(2)}) collective-permute-start(bf16[4,2,160,128]{3,2,1,0:T(8,128)(2,1)S(1)} %copy-done.13), channel_id=1, source_target_pairs={{0,384},{4,388},{8,392},{12,396},{16,400},{20,404},{24,408},{28,41... | collective-permute-start | bytes 983048 | tf_op jit(solution)/shard_map/ppermute | solution.py:34
  116.0 11.8 %all-to-all-start.2 = ((bf16[4,2,160,128]{3,2,1,0:T(8,128)(2,1)}), bf16[4,2,160,128]{3,2,1,0:T(8,128)(2,1)S(1)}, u32[]{:S(2)}, u32[]{:S(2)}) async-start(bf16[4,2,160,128]{3,2,1,0:T(8,128)(2,1)} %collective-permute-done.6), calls=%async_computation.2 | async-start | bytes 655360 | tf_op jit(solution)/shard_map/all_to_all | solution.py:245
  129.2 46.3 %all-to-all-start.3 = ((bf16[4,2,160,128]{3,2,1,0:T(8,128)(2,1)}), bf16[4,2,160,128]{3,2,1,0:T(8,128)(2,1)S(1)}, u32[]{:S(2)}, u32[]{:S(2)}) async-start(bf16[4,2,160,128]{3,2,1,0:T(8,128)(2,1)} %bitcast.7), calls=%async_computation.3 | async-start | bytes 655360 | tf_op jit(solution)/shard_map/all_to_all | solution.py:248
  133.4 42.1 %collective-permute-start.7 = (bf16[4,2,160,128]{3,2,1,0:T(8,128)(2,1)S(1)}, bf16[4,2,160,128]{3,2,1,0:T(8,128)(2,1)S(1)}, u32[]{:S(2)}, u32[]{:S(2)}) collective-permute-start(bf16[4,2,160,128]{3,2,1,0:T(8,128)(2,1)S(1)} %all-to-all-done.1), channel_id=1, source_target_pairs={{0,384},{4,388},{8,392},{12,396},{16,400},{20,404},{24,408},{28,41... | collective-permute-start | bytes 983048 | tf_op jit(solution)/shard_map/ppermute | solution.py:34
  175.5 0.7 copy-start.8
  175.5 0.8 copy-start.7

commit v3 on v2

--- a/solution.py
+++ b/solution.py
@@ -15,7 +15,7 @@
 UNIT = 4 * PIECE
 BF = jnp.bfloat16
 F32 = jnp.float32
-VMEM_LIMIT = 56 * 1024 * 1024
+VMEM_LIMIT = 20 * 1024 * 1024
 
 
 def permute(value, move):
@@ -84,8 +84,9 @@
 
 
 def half_kernel(slab_ref, amp_ref, out_ref):
+    p = pl.program_id(0)
     for q in range(NQ):
-        out_ref[0, :, q * W : (q + 1) * W] = jnp.dot(
+        out_ref[p, :, q * W : (q + 1) * W] = jnp.dot(
             slab_ref[q, 0], amp_ref[0, 0], preferred_element_type=F32
         ).astype(BF)
 
@@ -94,13 +95,13 @@
     pairs = amplitudes.shape[0]
     return pl.pallas_call(
         half_kernel,
-        out_shape=jax.ShapeDtypeStruct((pairs, W, DEEP), BF),
+        out_shape=pltpu.VMEM((pairs, W, DEEP), BF),
         grid=(pairs,),
         in_specs=[
             pl.BlockSpec((NQ, 1, W, W), lambda p: (0, block, 0, 0)),
             pl.BlockSpec((1, 1, W, W), lambda p: (p, block, 0, 0)),
         ],
-        out_specs=pl.BlockSpec((1, W, DEEP), lambda p: (p, 0, 0)),
+        out_specs=pl.BlockSpec(memory_space=pltpu.VMEM),
         compiler_params=params("arbitrary"),
         cost_estimate=pl.CostEstimate(
             flops=2 * pairs * NQ * W**3, bytes_accessed=9_000_000, transcendentals=0
@@ -132,93 +133,96 @@
     )
 
 
-def ladder_kernel(first, count, source_ref, int_ref, half_zero, half_one, *refs):
-    sources, (out_ref, own_ref, far_ref, right, left, unit, sems) = refs[:8], refs[8:]
-    halves = (half_zero, half_one)
-
-    for t in range(2 * count):
-        pltpu.make_async_copy(halves[t % 2].at[first + t // 2], left.at[t], sems.at[0, t]).start()
-        for r in range(8):
-
-            @pl.when(source_ref[first * 2 + t] == r)
-            def _():
-                pltpu.make_async_copy(sources[r], right.at[t], sems.at[1, t]).start()
+def ladder_kernel(source_ref, int_ref, *refs):
+    halves, sources, (low_ref, high_ref, late_ref, own_ref, far_ref, unit, sums) = (
+        refs[:2], refs[2:10], refs[10:]
+    )
+    pairs = int_ref.shape[0]
+
+    @pl.loop(0, pairs)
+    def _(p):
+        for block in range(2):
+            for r in range(8):
+
+                @pl.when(source_ref[2 * p + block] == r)
+                def _():
+                    sums[2 * p + block] = lax.dot_general(
+                        halves[block][p],
+                        sources[r][0:W, :],
+                        (((1,), (1,)), ((), ())),
+                        preferred_element_type=F32,
+                    )
+                    far_ref[p, block] = sources[r][W:TALL, 0:W].astype(F32)
 
     unit[3 * W : UNIT, :] = jnp.zeros((UNIT - 3 * W, 128), F32)
-    for t in range(2 * count):
-        pair, block = t // 2, t % 2
-        pltpu.make_async_copy(halves[0].at[first], left.at[t], sems.at[0, t]).wait()
-        pltpu.make_async_copy(sources[0], right.at[t], sems.at[1, t]).wait()
-        ladder = lax.dot_general(
-            left[t], right[t, 0:W, :], (((1,), (1,)), ((), ())), preferred_element_type=F32
-        )
-        tile = int_ref[pair, block].astype(F32) + ladder
-        own_ref[pair, block] = tile.astype(BF)
-        far_ref[pair, block] = right[t, W:TALL, 0:W].astype(F32)
-        put_tile(unit, block, tile)
-        if block == 1:
-            for j in range(4):
-                out_ref[j, pair] = unit[j * PIECE : (j + 1) * PIECE, :].astype(BF)
-
-
-def residual_units(first, count, source, halves, integrals, blocks):
+    for p in range(pairs):
+        for block in range(2):
+            tile = int_ref[p, block].astype(F32) + sums[2 * p + block]
+            own_ref[p, block] = tile.astype(BF)
+            put_tile(unit, block, tile)
+        for j in range(4):
+            piece = unit[j * PIECE : (j + 1) * PIECE, :].astype(BF)
+            if p >= 2:
+                late_ref[j, p - 2] = piece
+            elif j < 2:
+                low_ref[j, p] = piece
+            else:
+                high_ref[j - 2, p] = piece
+
+
+def residual_units(source, halves, integrals, blocks):
+    pairs = integrals.shape[0]
+    whole = pl.BlockSpec(memory_space=pltpu.VMEM)
+    held = [pltpu.with_memory_space_constraint(x, pltpu.VMEM) for x in (*halves, *blocks)]
     return pl.pallas_call(
-        functools.partial(ladder_kernel, first, count),
+        ladder_kernel,
         out_shape=(
-            jax.ShapeDtypeStruct((4, count, PIECE, 128), BF),
-            jax.ShapeDtypeStruct((count, 2, W, W), BF),
-            jax.ShapeDtypeStruct((count, 2, TALL - W, W), F32),
-        ),
-        grid_spec=pltpu.PrefetchScalarGridSpec(
-            num_scalar_prefetch=1,
-            grid=(1,),
-            in_specs=[pl.BlockSpec((count, 2, W, W), lambda i, s: (first // count, 0, 0, 0))]
-            + [pl.BlockSpec(memory_space=pl.ANY)] * 10,
-            out_specs=[
-                pl.BlockSpec((4, count, PIECE, 128), lambda i, s: (0, 0, 0, 0)),
-                pl.BlockSpec((count, 2, W, W), lambda i, s: (0, 0, 0, 0)),
-                pl.BlockSpec((count, 2, TALL - W, W), lambda i, s: (0, 0, 0, 0)),
-            ],
-            scratch_shapes=[
-                pltpu.VMEM((2 * count, TALL, DEEP), BF),
-                pltpu.VMEM((2 * count, W, DEEP), BF),
-                pltpu.VMEM((UNIT, 128), F32),
-                pltpu.SemaphoreType.DMA((2, 2 * count)),
-            ],
-        ),
-        compiler_params=params("arbitrary"),
+            jax.ShapeDtypeStruct((2, 2, PIECE, 128), BF),
+            jax.ShapeDtypeStruct((2, 2, PIECE, 128), BF),
+            jax.ShapeDtypeStruct((4, 2, PIECE, 128), BF),
+            jax.ShapeDtypeStruct((pairs, 2, W, W), BF),
+            jax.ShapeDtypeStruct((pairs, 2, TALL - W, W), F32),
+        ),
+        in_specs=[pl.BlockSpec(memory_space=pltpu.SMEM)] + [whole] * 11,
+        out_specs=[whole] * 5,
+        scratch_shapes=[
+            pltpu.VMEM((UNIT, 128), F32),
+            pltpu.VMEM((2 * pairs, W, W), F32),
+        ],
+        compiler_params=params(),
         cost_estimate=pl.CostEstimate(
-            flops=4 * count * NQ * W**3, bytes_accessed=count * 2 * 2_700_000, transcendentals=0
-        ),
-    )(source, integrals, *halves, *blocks)
+            flops=4 * pairs * NQ * W**3, bytes_accessed=5_000_000, transcendentals=0
+        ),
+    )(source, integrals, *held)
 
 
 def update_kernel(
-    slot_ref, flip_ref, pair_ref, amp_ref, own_a, own_b, far_a, far_b, mir_a, mir_b, near_ref, out_ref
+    slot_ref, flip_ref, pair_ref, amp_ref, own_ref, far_ref, mir_a, low_b, high_b, near_ref, out_ref
 ):
     p = pl.program_id(0)
-    low = slot_ref[p] < 2
+    first = slot_ref[p] < 2
+    mir_b = (low_b.at[0, 0], low_b.at[1, 0], high_b.at[0, 0], high_b.at[1, 0])
     other = jnp.concatenate(
-        [jnp.where(low, mir_a[j, 0].astype(F32), mir_b[j, 0].astype(F32)) for j in range(4)], axis=0
+        [
+            jnp.where(first, mir_a[j, 0].astype(F32), mir_b[j][...].astype(F32))
+            for j in range(4)
+        ],
+        axis=0,
     )
     straight = flip_ref[p] == 0
     tiles = [get_tile(other, b) for b in range(2)]
     for b in range(2):
         mirror = jnp.where(straight, tiles[b], tiles[1 - b])
         square = jnp.pad(mirror, ((0, 56), (0, 56)))
-        own = jnp.where(p < 2, own_a[0, b].astype(F32), own_b[0, b].astype(F32))
-        symmetric = own + square.T[0:W, 0:W]
-        far = jnp.where(p < 2, far_a[0, b, 0:1, :], far_b[0, b, 0:1, :])
-        denominator = pair_ref[p] - near_ref[b] - far
+        symmetric = own_ref[0, b].astype(F32) + square.T[0:W, 0:W]
+        denominator = pair_ref[p] - near_ref[b] - far_ref[0, b, 0:1, :]
         out_ref[0, b] = (amp_ref[0, b].astype(F32) + symmetric / denominator).astype(BF)
 
 
-def update(slot, flip, pair_energy, amplitudes, own_a, own_b, far_a, far_b, mir_a, mir_b, near):
+def update(slot, flip, pair_energy, amplitudes, own, far, mir_a, low_b, high_b, near):
     pairs = amplitudes.shape[0]
-    low = lambda p, s, f, e: (jnp.minimum(p, 1), 0, 0, 0)
-    high = lambda p, s, f, e: (jnp.maximum(p - 2, 0), 0, 0, 0)
     pick = lambda p, s, f, e: (0, jnp.bitwise_and(s[p], 1), 0, 0)
-    own = lambda p, s, f, e: (p, 0, 0, 0)
+    here = lambda p, s, f, e: (p, 0, 0, 0)
     return pl.pallas_call(
         update_kernel,
         out_shape=jax.ShapeDtypeStruct((pairs, 2, W, W), BF),
@@ -226,26 +230,27 @@
             num_scalar_prefetch=3,
             grid=(pairs,),
             in_specs=[
-                pl.BlockSpec((1, 2, W, W), own),
-                pl.BlockSpec((1, 2, W, W), low),
-                pl.BlockSpec((1, 2, W, W), high),
-                pl.BlockSpec((1, 2, TALL - W, W), low),
-                pl.BlockSpec((1, 2, TALL - W, W), high),
+                pl.BlockSpec((1, 2, W, W), here),
+                pl.BlockSpec((1, 2, W, W), here),
+                pl.BlockSpec((1, 2, TALL - W, W), here),
                 pl.BlockSpec((4, 1, PIECE, 128), pick),
-                pl.BlockSpec((4, 1, PIECE, 128), pick),
+                pl.BlockSpec((2, 1, PIECE, 128), pick),
+                pl.BlockSpec((2, 1, PIECE, 128), pick),
                 pl.BlockSpec((2, W, 1), lambda p, s, f, e: (0, 0, 0)),
             ],
-            out_specs=pl.BlockSpec((1, 2, W, W), own),
+            out_specs=pl.BlockSpec((1, 2, W, W), here),
         ),
         compiler_params=params("arbitrary"),
-    )(slot, flip, pair_energy, amplitudes, own_a, own_b, far_a, far_b, mir_a, mir_b, near)
-
-
-def across_virt(units, step):
-    scattered = lax.all_to_all(units, "virt", 0, 0, tiled=True)
+    )(slot, flip, pair_energy, amplitudes, own, far, mir_a, low_b, high_b, near)
+
+
+def exchange(units):
+    return lax.all_to_all(units, "virt", 0, 0, tiled=True)
+
+
+def reorder(scattered, step):
     index = jnp.bitwise_xor(jnp.arange(4, dtype=jnp.int32)[:, None], step[None, :])
-    chosen = scattered[index, jnp.arange(units.shape[1], dtype=jnp.int32)[None, :]]
-    return lax.all_to_all(chosen, "virt", 0, 0, tiled=True)
+    return scattered[index, jnp.arange(scattered.shape[1], dtype=jnp.int32)[None, :]]
 
 
 def on_device(
@@ -294,16 +299,17 @@
     )
     halves = (half_zero, half_one)
 
-    unit_a, own_a, far_a = residual_units(0, 2, source, halves, ints, blocks)
-    unit_a, source = together(unit_a, source)
-    mir_a = to_mirror(unit_a)
-    unit_b, own_b, far_b = residual_units(2, 2, source, halves, ints, blocks)
-    crossed_b = across_virt(unit_b, step[2:4])
-    mir_a, crossed_b = together(mir_a, crossed_b)
-    mir_b = to_mirror(crossed_b)
-    mir_a = across_virt(mir_a, mirror_step[0:2])
+    low_a, high_a, unit_b, own, far = residual_units(source, halves, ints, blocks)
+    low_a, scattered_b = together(to_mirror(low_a), exchange(unit_b))
+    crossed_b = exchange(reorder(scattered_b, step[2:4]))
+    high_a, crossed_b = together(to_mirror(high_a), crossed_b)
+    low_b, scattered_a = together(
+        to_mirror(crossed_b[0:2]), exchange(jnp.concatenate([low_a, high_a], axis=0))
+    )
+    crossed_a = exchange(reorder(scattered_a, mirror_step[0:2]))
+    high_b = to_mirror(crossed_b[2:4])
     new = update(
-        mirror_slot, flip, pair_energy, amp, own_a, own_b, far_a, far_b, mir_a, mir_b, near
+        mirror_slot, flip, pair_energy, amp, own, far, crossed_a, low_b, high_b, near
     )
     return new.reshape(amplitudes.shape)
 

time: 183 us -> 174 us (0.951)
  the two profiles are of different devices: /device:TPU:14 before, /device:TPU:122 now
where the time goes in v3:
time: 174 us; the launch traced here: 173 us
  starting transfers between devices  80.2 us (46%)
  waiting for transfers between devices  57.3 us (33%)
  Pallas kernels  21.1 us (12%)
  local copies, waits for them, and re-layouts  13.6 us (8%)
    ppermute x10, waiting for transfers between devices, permute(): return lax.ppermute(value, ('pair', 'virt'), pairs)  57.3 us
    ppermute x10, starting transfers between devices, permute(): return lax.ppermute(value, ('pair', 'virt'), pairs)  57.2 us
    all_to_all x4, starting transfers between devices, exchange(): return lax.all_to_all(units, 'virt', 0, 0, tiled=True)  23 us
    pallas_call x1, Pallas kernels, residual_units(): pl.pallas_call(ladder_kernel, out_shape=(jax.ShapeDtypeStruct((2, 2, PIEC...  8.99 us
    unnamed x30, local copies, waits for them, and re-layouts  7.39 us
    pallas_call x2, Pallas kernels, first_half(): pl.pallas_call(half_kernel, out_shape=pltpu.VMEM((pairs, W, DEEP), BF), g...  5.7 us
  transfers between devices with their start and end apart: 14, of which 8 were waited for; matrix products, arithmetic and copies ran while one was open for 2% of the time, Pallas kernels for 4%

profile of v3, /device:TPU:122, one launch (start us, length us, event | category | flops | bytes accessed | tf_op | source)
XLA Modules:
  0.0 173.4 jit_solution(18321063140327700350)
XLA Ops:
  0.0 1.9 %copy-done.1 = bf16[16,400,200]{2,1,0:T(8,128)(2,1)S(1)} copy-done((bf16[16,400,200]{2,1,0:T(8,128)(2,1)S(1)}, bf16[16,400,200]{2,1,0:T(8,128)(2,1)}, u32[]{:S(2)}) %copy-start.1) | copy-done | bytes 2560024
  1.9 0.7 copy-done.8
  2.6 1.5 shard_map.84.refs_2_
  4.2 1.9 %collective-permute-start.1 = (bf16[208,3200]{1,0:T(8,128)(2,1)}, bf16[208,3200]{1,0:T(8,128)(2,1)}, u32[]{:S(2)}, u32[]{:S(2)}) collective-permute-start(bf16[208,3200]{1,0:T(8,128)(2,1)} %shard_map.84.refs_2_), channel_id=1, source_target_pairs={{0,1},{4,39},{8,9},{12,47},{16,17},{20,55},{24,25},{28,63},{1,2},{... | collective-permute-start | bytes 3993608 | tf_op jit(solution)/shard_map/ppermute | solution.py:34
  6.1 1.5 shard_map.82.refs_3_
  7.7 3.2 %collective-permute-start = (bf16[208,3200]{1,0:T(8,128)(2,1)}, bf16[208,3200]{1,0:T(8,128)(2,1)}, u32[]{:S(2)}, u32[]{:S(2)}) collective-permute-start(bf16[208,3200]{1,0:T(8,128)(2,1)} %shard_map.82.refs_3_), channel_id=1, source_target_pairs={{0,1},{4,39},{8,9},{12,47},{16,17},{20,55},{24,25},{28,63},{1,2},{... | collective-permute-start | bytes 3993608 | tf_op jit(solution)/shard_map/ppermute | solution.py:34
  10.9 0.6 gather_fusion
  11.6 0.6 gather_fusion.1
  12.3 0.1 broadcast_in_dim.72
  12.5 0.1 broadcast_in_dim.74
  12.6 0.1 broadcast_in_dim.76
  12.8 0.1 reshape.145
  12.9 1.2 copy-done.4
  14.1 2.8 %shard_map.85.refs_0_ = bf16[4,200,3200]{2,1,0:T(8,128)(2,1)S(1)} custom-call(bf16[16,2,200,200]{3,2,1,0:T(8,128)(2,1)S(1)} %bitcast.18, bf16[4,2,200,200]{3,2,1,0:T(8,128)(2,1)S(1)} %bitcast.22), custom_call_target="tpu_custom_call" | custom-call | flops 1024000000 | bytes 9000000 | tf_op jit(solution)/shard_map/pallas_call | solution.py:96
  16.9 2.3 %copy-done.3 = bf16[4,200,3200]{2,1,0:T(8,128)(2,1)} copy-done((bf16[4,200,3200]{2,1,0:T(8,128)(2,1)}, bf16[4,200,3200]{2,1,0:T(8,128)(2,1)S(1)}, u32[]{:S(2)}) %copy-start.3) | copy-done | bytes 5120024
  19.2 0.1 reshape.147
  19.3 4.9 %collective-permute-done.1.refs_4_ = bf16[208,3200]{1,0:T(8,128)(2,1)} collective-permute-done((bf16[208,3200]{1,0:T(8,128)(2,1)}, bf16[208,3200]{1,0:T(8,128)(2,1)}, u32[]{:S(2)}, u32[]{:S(2)}) %collective-permute-start.1) | collective-permute-done | bytes 1331232 | tf_op jit(solution)/shard_map/ppermute | solution.py:34
  24.2 3.1 %collective-permute-start.4 = (bf16[208,3200]{1,0:T(8,128)(2,1)}, bf16[208,3200]{1,0:T(8,128)(2,1)}, u32[]{:S(2)}, u32[]{:S(2)}) collective-permute-start(bf16[208,3200]{1,0:T(8,128)(2,1)} %collective-permute-done.1.refs_4_), channel_id=1, source_target_pairs={{0,1},{4,39},{8,9},{12,47},{16,17},{20,55},{24,25},{28,63},{1,2},{... | collective-permute-start | bytes 3993608 | tf_op jit(solution)/shard_map/ppermute | solution.py:34
  27.3 0.6 gather_fusion.2
  28.0 0.6 gather_fusion.3
  28.6 1.3 copy-done.5
  29.9 2.9 %shard_map.83.refs_1_ = bf16[4,200,3200]{2,1,0:T(8,128)(2,1)S(1)} custom-call(bf16[16,2,200,200]{3,2,1,0:T(8,128)(2,1)S(1)} %bitcast.19, bf16[4,2,200,200]{3,2,1,0:T(8,128)(2,1)S(1)} %bitcast.23), custom_call_target="tpu_custom_call" | custom-call | flops 1024000000 | bytes 9000000 | tf_op jit(solution)/shard_map/pallas_call | solution.py:96
  32.8 0.1 select_reduce_fusion
  32.9 1.9 %collective-permute-start.2 = (bf16[208,3200]{1,0:T(8,128)(2,1)}, bf16[208,3200]{1,0:T(8,128)(2,1)S(1)}, u32[]{:S(2)}, u32[]{:S(2)}) collective-permute-start(bf16[208,3200]{1,0:T(8,128)(2,1)} %collective-permute-done.1.refs_4_), channel_id=1, source_target_pairs={{0,4},{4,0},{8,12},{12,8},{16,20},{20,16},{24,28},{28,24},{1,5},{5... | collective-permute-start | bytes 3993608 | tf_op jit(solution)/shard_map/ppermute | solution.py:34
  34.8 3.7 %collective-permute-done.refs_5_ = bf16[208,3200]{1,0:T(8,128)(2,1)} collective-permute-done((bf16[208,3200]{1,0:T(8,128)(2,1)}, bf16[208,3200]{1,0:T(8,128)(2,1)}, u32[]{:S(2)}, u32[]{:S(2)}) %collective-permute-start) | collective-permute-done | bytes 1331232 | tf_op jit(solution)/shard_map/ppermute | solution.py:34
  38.4 1.9 %collective-permute-start.3 = (bf16[208,3200]{1,0:T(8,128)(2,1)}, bf16[208,3200]{1,0:T(8,128)(2,1)S(1)}, u32[]{:S(2)}, u32[]{:S(2)}) collective-permute-start(bf16[208,3200]{1,0:T(8,128)(2,1)} %collective-permute-done.refs_5_), channel_id=1, source_target_pairs={{0,4},{4,0},{8,12},{12,8},{16,20},{20,16},{24,28},{28,24},{1,5},{5... | collective-permute-start | bytes 3993608 | tf_op jit(solution)/shard_map/ppermute | solution.py:34
  40.4 12.3 %collective-permute-done.4.refs_8_ = bf16[208,3200]{1,0:T(8,128)(2,1)} collective-permute-done((bf16[208,3200]{1,0:T(8,128)(2,1)}, bf16[208,3200]{1,0:T(8,128)(2,1)}, u32[]{:S(2)}, u32[]{:S(2)}) %collective-permute-start.4) | collective-permute-done | bytes 1331232 | tf_op jit(solution)/shard_map/ppermute | solution.py:34
  52.7 1.9 %collective-permute-start.5 = (bf16[208,3200]{1,0:T(8,128)(2,1)}, bf16[208,3200]{1,0:T(8,128)(2,1)S(1)}, u32[]{:S(2)}, u32[]{:S(2)}) collective-permute-start(bf16[208,3200]{1,0:T(8,128)(2,1)} %collective-permute-done.4.refs_8_), channel_id=1, source_target_pairs={{0,4},{4,0},{8,12},{12,8},{16,20},{20,16},{24,28},{28,24},{1,5},{5... | collective-permute-start | bytes 3993608 | tf_op jit(solution)/shard_map/ppermute | solution.py:34
  54.6 3.2 %collective-permute-done.5.refs_9_ = bf16[208,3200]{1,0:T(8,128)(2,1)S(1)} collective-permute-done((bf16[208,3200]{1,0:T(8,128)(2,1)}, bf16[208,3200]{1,0:T(8,128)(2,1)S(1)}, u32[]{:S(2)}, u32[]{:S(2)}) %collective-permute-start.5) | collective-permute-done | bytes 1331232 | tf_op jit(solution)/shard_map/ppermute | solution.py:34
  57.9 9.0 %shard_map.86 = (bf16[2,2,160,128]{3,2,1,0:T(8,128)(2,1)S(1)}, bf16[2,2,160,128]{3,2,1,0:T(8,128)(2,1)S(1)}, bf16[4,2,160,128]{3,2,1,0:T(8,128)(2,1)}, bf16[4,2,...) custom-call(s32[8]{0:T(128)S(1)} %select_select_fusion.source_ref, bf16[4,2,200,200]{3,2,1,0:T(8,128)(2,1)S(1)} %bitcast.25, ...), custom_call_target="tpu_custom_call" | custom-call | flops 2048000000 | bytes 5000000 | tf_op jit(solution)/shard_map/pallas_call | solution.py:177
  66.9 7.6 %all-to-all-start = ((bf16[4,2,160,128]{3,2,1,0:T(8,128)(2,1)}), bf16[4,2,160,128]{3,2,1,0:T(8,128)(2,1)S(1)}, u32[]{:S(2)}, u32[]{:S(2)}) async-start(bf16[4,2,160,128]{3,2,1,0:T(8,128)(2,1)} %get-tuple-element.37), calls=%async_computation | async-start | bytes 655360 | tf_op jit(solution)/shard_map/all_to_all | solution.py:248
  74.5 14.2 %collective-permute-start.7 = (bf16[2,2,160,128]{3,2,1,0:T(8,128)(2,1)S(1)}, bf16[2,2,160,128]{3,2,1,0:T(8,128)(2,1)S(1)}, u32[]{:S(2)}, u32[]{:S(2)}) collective-permute-start(bf16[2,2,160,128]{3,2,1,0:T(8,128)(2,1)S(1)} %get-tuple-element.36), channel_id=1, source_target_pairs={{0,384},{4,388},{8,392},{12,396},{16,400},{20,404},{24,408},{28,41... | collective-permute-start | bytes 491528 | tf_op jit(solution)/shard_map/ppermute | solution.py:34
  88.7 0.1 reshape.180
  88.8 10.2 %collective-permute-done.7 = bf16[2,2,160,128]{3,2,1,0:T(8,128)(2,1)S(1)} collective-permute-done((bf16[2,2,160,128]{3,2,1,0:T(8,128)(2,1)S(1)}, bf16[2,2,160,128]{3,2,1,0:T(8,128)(2,1)S(1)}, u32[]{:S(2)}, u32[]{:S(2)}) %collective-permute-start.7) | collective-permute-done | bytes 163872 | tf_op jit(solution)/shard_map/ppermute | solution.py:34
  99.0 1.3 gather_fusion.4
  100.3 5.1 %all-to-all-start.1 = ((bf16[4,2,160,128]{3,2,1,0:T(8,128)(2,1)}), bf16[4,2,160,128]{3,2,1,0:T(8,128)(2,1)S(1)}, u32[]{:S(2)}, u32[]{:S(2)}) async-start(bf16[4,2,160,128]{3,2,1,0:T(8,128)(2,1)} %bitcast.6), calls=%async_computation.1 | async-start | bytes 655360 | tf_op jit(solution)/shard_map/all_to_all | solution.py:248
  105.4 9.8 %collective-permute-start.6 = (bf16[2,2,160,128]{3,2,1,0:T(8,128)(2,1)S(1)}, bf16[2,2,160,128]{3,2,1,0:T(8,128)(2,1)S(1)}, u32[]{:S(2)}, u32[]{:S(2)}) collective-permute-start(bf16[2,2,160,128]{3,2,1,0:T(8,128)(2,1)S(1)} %get-tuple-element.35), channel_id=1, source_target_pairs={{0,384},{4,388},{8,392},{12,396},{16,400},{20,404},{24,408},{28,41... | collective-permute-start | bytes 491528 | tf_op jit(solution)/shard_map/ppermute | solution.py:34
  115.2 8.6 %collective-permute-done.6 = bf16[2,2,160,128]{3,2,1,0:T(8,128)(2,1)S(1)} collective-permute-done((bf16[2,2,160,128]{3,2,1,0:T(8,128)(2,1)S(1)}, bf16[2,2,160,128]{3,2,1,0:T(8,128)(2,1)S(1)}, u32[]{:S(2)}, u32[]{:S(2)}) %collective-permute-start.6) | collective-permute-done | bytes 163872 | tf_op jit(solution)/shard_map/ppermute | solution.py:34
  123.8 0.8 pad_maximum_fusion
  124.6 5.2 %all-to-all-start.2 = ((bf16[4,2,160,128]{3,2,1,0:T(8,128)(2,1)}), bf16[4,2,160,128]{3,2,1,0:T(8,128)(2,1)S(1)}, u32[]{:S(2)}, u32[]{:S(2)}) async-start(bf16[4,2,160,128]{3,2,1,0:T(8,128)(2,1)} %pad_maximum_fusion), calls=%async_computation.2 | async-start | bytes 655360 | tf_op jit(solution)/shard_map/all_to_all | solution.py:248
  129.8 9.6 %collective-permute-start.8 = (bf16[2,2,160,128]{3,2,1,0:T(8,128)(2,1)S(1)}, bf16[2,2,160,128]{3,2,1,0:T(8,128)(2,1)S(1)}, u32[]{:S(2)}, u32[]{:S(2)}) collective-permute-start(bf16[2,2,160,128]{3,2,1,0:T(8,128)(2,1)S(1)} %get-tuple-element.51), channel_id=1, source_target_pairs={{0,384},{4,388},{8,392},{12,396},{16,400},{20,404},{24,408},{28,41... | collective-permute-start | bytes 491528 | tf_op jit(solution)/shard_map/ppermute | solution.py:34
  139.6 7.1 %collective-permute-done.8.low_b = bf16[2,2,160,128]{3,2,1,0:T(8,128)(2,1)S(1)} collective-permute-done((bf16[2,2,160,128]{3,2,1,0:T(8,128)(2,1)S(1)}, bf16[2,2,160,128]{3,2,1,0:T(8,128)(2,1)S(1)}, u32[]{:S(2)}, u32[]{:S(2)}) %collective-permute-start.8) | collective-permute-done | bytes 163872 | tf_op jit(solution)/shard_map/ppermute | solution.py:34
  146.7 1.3 gather_fusion.5
  148.0 5.1 %all-to-all-start.3 = ((bf16[4,2,160,128]{3,2,1,0:T(8,128)(2,1)}), bf16[4,2,160,128]{3,2,1,0:T(8,128)(2,1)S(1)}, u32[]{:S(2)}, u32[]{:S(2)}) async-start(bf16[4,2,160,128]{3,2,1,0:T(8,128)(2,1)} %bitcast.7), calls=%async_computation.3 | async-start | bytes 655360 | tf_op jit(solution)/shard_map/all_to_all | solution.py:248
  153.1 9.6 %collective-permute-start.9 = (bf16[2,2,160,128]{3,2,1,0:T(8,128)(2,1)S(1)}, bf16[2,2,160,128]{3,2,1,0:T(8,128)(2,1)S(1)}, u32[]{:S(2)}, u32[]{:S(2)}) collective-permute-start(bf16[2,2,160,128]{3,2,1,0:T(8,128)(2,1)S(1)} %get-tuple-element.50), channel_id=1, source_target_pairs={{0,384},{4,388},{8,392},{12,396},{16,400},{20,404},{24,408},{28,41... | collective-permute-start | bytes 491528 | tf_op jit(solution)/shard_map/ppermute | solution.py:34
  162.7 0.1 copy.10.near_ref
  162.8 7.3 %collective-permute-done.9.high_b = bf16[2,2,160,128]{3,2,1,0:T(8,128)(2,1)S(1)} collective-permute-done((bf16[2,2,160,128]{3,2,1,0:T(8,128)(2,1)S(1)}, bf16[2,2,160,128]{3,2,1,0:T(8,128)(2,1)S(1)}, u32[]{:S(2)}, u32[]{:S(2)}) %collective-permute-start.9) | collective-permute-done | bytes 163872 | tf_op jit(solution)/shard_map/ppermute | solution.py:34
  170.1 3.3 %shard_map.87 = bf16[4,2,200,200]{3,2,1,0:T(8,128)(2,1)} custom-call(s32[4]{0:T(128)S(1)} %copy-done.10, s32[4]{0:T(128)S(1)} %broadcast_and_fusion.flip_ref, f32[4]{0:T(128)S(1)} %add.45.pair_ref, bf16[4,2,200,200]{3,2,1,0:T(8,128)(2,1)S(1)} %bitcast.24, bf16[4,2,200,200]{3,2,1,0:T(8,128)(2,1)S(1)} %get-tuple-element.33.own_ref, ...), custom_call_target="tpu_custom_call" | custom-call | tf_op jit(solution)/shard_map/pallas_call | solution.py:226
  (48 shorter events, 0.6 us)
Async XLA Ops:
  0.0 10.9 %copy-start = (s32[200]{0:T(256)S(1)}, s32[200]{0:T(256)}, u32[]{:S(2)}) copy-start(s32[200]{0:T(256)} %param.13) | copy-start | bytes 2404
  0.0 1.9 %copy-start.1 = (bf16[16,400,200]{2,1,0:T(8,128)(2,1)S(1)}, bf16[16,400,200]{2,1,0:T(8,128)(2,1)}, u32[]{:S(2)}) copy-start(bf16[16,400,200]{2,1,0:T(8,128)(2,1)} %param.10) | copy-start | bytes 7680004
  1.9 0.7 copy-start.8
  2.6 3.5 %copy-start.9 = (bf16[400]{0:T(512)(128)(2,1)S(1)}, bf16[400]{0:T(512)(128)(2,1)}, u32[]{:S(2)}) copy-start(bf16[400]{0:T(512)(128)(2,1)} %energy_ref.3) | copy-start | bytes 2404
  4.2 20.0 %collective-permute-start.1 = (bf16[208,3200]{1,0:T(8,128)(2,1)}, bf16[208,3200]{1,0:T(8,128)(2,1)}, u32[]{:S(2)}, u32[]{:S(2)}) collective-permute-start(bf16[208,3200]{1,0:T(8,128)(2,1)} %shard_map.84.refs_2_), channel_id=1, source_target_pairs={{0,1},{4,39},{8,9},{12,47},{16,17},{20,55},{24,25},{28,63},{1,2},{... | collective-permute-start | bytes 3993608 | tf_op jit(solution)/shard_map/ppermute | solution.py:34
  6.1 4.8 %copy-start.12 = (s32[4,2]{0,1:T(2,128)S(1)}, s32[4,2]{0,1:T(2,128)}, u32[]{:S(2)}) copy-start(s32[4,2]{0,1:T(2,128)} %param.11) | copy-start | bytes 100
  6.1 6.8 %copy-start.2 = (bf16[16,400,200]{2,1,0:T(8,128)(2,1)S(1)}, bf16[16,400,200]{2,1,0:T(8,128)(2,1)}, u32[]{:S(2)}) copy-start(bf16[16,400,200]{2,1,0:T(8,128)(2,1)} %param.10) | copy-start | bytes 7680004
  7.7 30.8 %collective-permute-start = (bf16[208,3200]{1,0:T(8,128)(2,1)}, bf16[208,3200]{1,0:T(8,128)(2,1)}, u32[]{:S(2)}, u32[]{:S(2)}) collective-permute-start(bf16[208,3200]{1,0:T(8,128)(2,1)} %shard_map.82.refs_3_), channel_id=1, source_target_pairs={{0,1},{4,39},{8,9},{12,47},{16,17},{20,55},{24,25},{28,63},{1,2},{... | collective-permute-start | bytes 3993608 | tf_op jit(solution)/shard_map/ppermute | solution.py:34
  12.9 1.2 copy-start.4
  14.1 13.3 %copy-start.11 = (f32[200]{0:T(256)S(1)}, f32[200]{0:T(256)}, u32[]{:S(2)}) copy-start(f32[200]{0:T(256)} %param.14) | copy-start | bytes 2404
  16.9 2.3 %copy-start.3 = (bf16[4,200,3200]{2,1,0:T(8,128)(2,1)}, bf16[4,200,3200]{2,1,0:T(8,128)(2,1)S(1)}, u32[]{:S(2)}) copy-start(bf16[4,200,3200]{2,1,0:T(8,128)(2,1)S(1)} %shard_map.85.refs_0_) | copy-start | bytes 15360004
  24.2 28.5 %collective-permute-start.4 = (bf16[208,3200]{1,0:T(8,128)(2,1)}, bf16[208,3200]{1,0:T(8,128)(2,1)}, u32[]{:S(2)}, u32[]{:S(2)}) collective-permute-start(bf16[208,3200]{1,0:T(8,128)(2,1)} %collective-permute-done.1.refs_4_), channel_id=1, source_target_pairs={{0,1},{4,39},{8,9},{12,47},{16,17},{20,55},{24,25},{28,63},{1,2},{... | collective-permute-start | bytes 3993608 | tf_op jit(solution)/shard_map/ppermute | solution.py:34
  28.6 29.3 %slice-start = ((s8[5120000]{0:T(1024)(128)(4,1)}), s8[4194304]{0:T(1024)(128)(4,1)S(1)}, s32[]{:S(2)}) async-start(s8[5120000]{0:T(1024)(128)(4,1)} %bitcast.20), calls=%async_computation.4 | async-start | bytes 8388608
  28.6 1.3 copy-start.5
  29.9 2.9 %copy-start.10 = (s32[4]{0:T(128)S(1)}, s32[4]{0:T(128)}, u32[]{:S(2)}) copy-start(s32[4]{0:T(128)} %slot_ref.1) | copy-start | bytes 52
  29.9 28.0 %slice-start.1 = ((s8[5120000]{0:T(1024)(128)(4,1)}), s8[925696]{0:T(1024)(128)(4,1)S(1)}, s32[]{:S(2)}) async-start(s8[5120000]{0:T(1024)(128)(4,1)} %bitcast.20), calls=%async_computation.5 | async-start | bytes 1851392
  29.9 28.0 %copy-start.7 = (bf16[4,400,200]{2,1,0:T(8,128)(2,1)S(1)}, bf16[4,400,200]{2,1,0:T(8,128)(2,1)}, u32[]{:S(2)}) copy-start(bf16[4,400,200]{2,1,0:T(8,128)(2,1)} %param.9) | copy-start | bytes 1920004
  32.9 21.8 %collective-permute-start.2 = (bf16[208,3200]{1,0:T(8,128)(2,1)}, bf16[208,3200]{1,0:T(8,128)(2,1)S(1)}, u32[]{:S(2)}, u32[]{:S(2)}) collective-permute-start(bf16[208,3200]{1,0:T(8,128)(2,1)} %collective-permute-done.1.refs_4_), channel_id=1, source_target_pairs={{0,4},{4,0},{8,12},{12,8},{16,20},{20,16},{24,28},{28,24},{1,5},{5... | collective-permute-start | bytes 3993608 | tf_op jit(solution)/shard_map/ppermute | solution.py:34
  38.4 16.2 %collective-permute-start.3 = (bf16[208,3200]{1,0:T(8,128)(2,1)}, bf16[208,3200]{1,0:T(8,128)(2,1)S(1)}, u32[]{:S(2)}, u32[]{:S(2)}) collective-permute-start(bf16[208,3200]{1,0:T(8,128)(2,1)} %collective-permute-done.refs_5_), channel_id=1, source_target_pairs={{0,4},{4,0},{8,12},{12,8},{16,20},{20,16},{24,28},{28,24},{1,5},{5... | collective-permute-start | bytes 3993608 | tf_op jit(solution)/shard_map/ppermute | solution.py:34
  52.7 5.2 %collective-permute-start.5 = (bf16[208,3200]{1,0:T(8,128)(2,1)}, bf16[208,3200]{1,0:T(8,128)(2,1)S(1)}, u32[]{:S(2)}, u32[]{:S(2)}) collective-permute-start(bf16[208,3200]{1,0:T(8,128)(2,1)} %collective-permute-done.4.refs_8_), channel_id=1, source_target_pairs={{0,4},{4,0},{8,12},{12,8},{16,20},{20,16},{24,28},{28,24},{1,5},{5... | collective-permute-start | bytes 3993608 | tf_op jit(solution)/shard_map/ppermute | solution.py:34
  66.9 32.2 %all-to-all-start = ((bf16[4,2,160,128]{3,2,1,0:T(8,128)(2,1)}), bf16[4,2,160,128]{3,2,1,0:T(8,128)(2,1)S(1)}, u32[]{:S(2)}, u32[]{:S(2)}) async-start(bf16[4,2,160,128]{3,2,1,0:T(8,128)(2,1)} %get-tuple-element.37), calls=%async_computation | async-start | bytes 655360 | tf_op jit(solution)/shard_map/all_to_all | solution.py:248
  74.5 24.5 %collective-permute-start.7 = (bf16[2,2,160,128]{3,2,1,0:T(8,128)(2,1)S(1)}, bf16[2,2,160,128]{3,2,1,0:T(8,128)(2,1)S(1)}, u32[]{:S(2)}, u32[]{:S(2)}) collective-permute-start(bf16[2,2,160,128]{3,2,1,0:T(8,128)(2,1)S(1)} %get-tuple-element.36), channel_id=1, source_target_pairs={{0,384},{4,388},{8,392},{12,396},{16,400},{20,404},{24,408},{28,41... | collective-permute-start | bytes 491528 | tf_op jit(solution)/shard_map/ppermute | solution.py:34
  100.3 23.5 %all-to-all-start.1 = ((bf16[4,2,160,128]{3,2,1,0:T(8,128)(2,1)}), bf16[4,2,160,128]{3,2,1,0:T(8,128)(2,1)S(1)}, u32[]{:S(2)}, u32[]{:S(2)}) async-start(bf16[4,2,160,128]{3,2,1,0:T(8,128)(2,1)} %bitcast.6), calls=%async_computation.1 | async-start | bytes 655360 | tf_op jit(solution)/shard_map/all_to_all | solution.py:248
  105.4 18.4 %collective-permute-start.6 = (bf16[2,2,160,128]{3,2,1,0:T(8,128)(2,1)S(1)}, bf16[2,2,160,128]{3,2,1,0:T(8,128)(2,1)S(1)}, u32[]{:S(2)}, u32[]{:S(2)}) collective-permute-start(bf16[2,2,160,128]{3,2,1,0:T(8,128)(2,1)S(1)} %get-tuple-element.35), channel_id=1, source_target_pairs={{0,384},{4,388},{8,392},{12,396},{16,400},{20,404},{24,408},{28,41... | collective-permute-start | bytes 491528 | tf_op jit(solution)/shard_map/ppermute | solution.py:34
  124.6 45.6 %copy-start.6 = (bf16[4,400,200]{2,1,0:T(8,128)(2,1)S(1)}, bf16[4,400,200]{2,1,0:T(8,128)(2,1)}, u32[]{:S(2)}) copy-start(bf16[4,400,200]{2,1,0:T(8,128)(2,1)} %param.8) | copy-start | bytes 1920004
  124.6 22.1 %all-to-all-start.2 = ((bf16[4,2,160,128]{3,2,1,0:T(8,128)(2,1)}), bf16[4,2,160,128]{3,2,1,0:T(8,128)(2,1)S(1)}, u32[]{:S(2)}, u32[]{:S(2)}) async-start(bf16[4,2,160,128]{3,2,1,0:T(8,128)(2,1)} %pad_maximum_fusion), calls=%async_computation.2 | async-start | bytes 655360 | tf_op jit(solution)/shard_map/all_to_all | solution.py:248
  129.8 16.8 %collective-permute-start.8 = (bf16[2,2,160,128]{3,2,1,0:T(8,128)(2,1)S(1)}, bf16[2,2,160,128]{3,2,1,0:T(8,128)(2,1)S(1)}, u32[]{:S(2)}, u32[]{:S(2)}) collective-permute-start(bf16[2,2,160,128]{3,2,1,0:T(8,128)(2,1)S(1)} %get-tuple-element.51), channel_id=1, source_target_pairs={{0,384},{4,388},{8,392},{12,396},{16,400},{20,404},{24,408},{28,41... | collective-permute-start | bytes 491528 | tf_op jit(solution)/shard_map/ppermute | solution.py:34
  148.0 22.2 %all-to-all-start.3 = ((bf16[4,2,160,128]{3,2,1,0:T(8,128)(2,1)}), bf16[4,2,160,128]{3,2,1,0:T(8,128)(2,1)S(1)}, u32[]{:S(2)}, u32[]{:S(2)}) async-start(bf16[4,2,160,128]{3,2,1,0:T(8,128)(2,1)} %bitcast.7), calls=%async_computation.3 | async-start | bytes 655360 | tf_op jit(solution)/shard_map/all_to_all | solution.py:248
  153.1 17.1 %collective-permute-start.9 = (bf16[2,2,160,128]{3,2,1,0:T(8,128)(2,1)S(1)}, bf16[2,2,160,128]{3,2,1,0:T(8,128)(2,1)S(1)}, u32[]{:S(2)}, u32[]{:S(2)}) collective-permute-start(bf16[2,2,160,128]{3,2,1,0:T(8,128)(2,1)S(1)} %get-tuple-element.50), channel_id=1, source_target_pairs={{0,384},{4,388},{8,392},{12,396},{16,400},{20,404},{24,408},{28,41... | collective-permute-start | bytes 491528 | tf_op jit(solution)/shard_map/ppermute | solution.py:34

commit v4 on v3

v4 whole, which is shorter than its diff:
```python
import jax
import jax.numpy as jnp
from jax import lax
from jax.experimental import pallas as pl
from jax.experimental.pallas import tpu as pltpu
from jax.sharding import PartitionSpec as P

W = 200
NQ = 16
DEEP = NQ * W
TALL = 208
PART = 1664
PIECE = 160
UNIT = 4 * PIECE
BF = jnp.bfloat16
F32 = jnp.float32
VMEM_LIMIT = 20 * 1024 * 1024


def permute(value, move):
    layers, halves, width, cores, lines = lax.axis_size("pair") // 16, 2, 4, 2, 4
    pairs = []
    for z in range(layers):
        for y in range(halves * lines):
            for x in range(width):
                for core in range(cores):
                    ends = []
                    for tz, ty, tx, tc in ((z, y, x, core), move(z, y, x, core)):
                        tz, ty, tx, tc = tz % layers, ty % (halves * lines), tx % width, tc % cores
                        pair = ((tz * halves + ty // lines) * width + tx) * cores + tc
                        ends.append(pair * lines + ty % lines)
                    pairs.append(tuple(ends))
    return lax.ppermute(value, ("pair", "virt"), pairs)


def along_y(value):
    return permute(value, lambda z, y, x, core: (z, y + 1 - 2 * core, x, core))


def along_x(value):
    return permute(value, lambda z, y, x, core: (z, y, x + 1 - 2 * core, core))


def swap_cores(value):
    return permute(value, lambda z, y, x, core: (z, y, x, 1 - core))


def to_mirror(value):
    half = lax.axis_size("pair") // 32
    return permute(value, lambda z, y, x, core: (z + half, y, x, core))


def exchange(units):
    return lax.all_to_all(units, "virt", 0, 0, tiled=True)


def reorder(scattered, step):
    index = jnp.bitwise_xor(jnp.arange(4, dtype=jnp.int32)[:, None], step[None, :])
    return scattered[index, jnp.arange(scattered.shape[1], dtype=jnp.int32)[None, :]]


def together(*values):
    return lax.optimization_barrier(values)


def params(*semantics):
    return pltpu.CompilerParams(
        dimension_semantics=semantics or None, vmem_limit_bytes=VMEM_LIMIT
    )


def cost(flops, moved):
    return pl.CostEstimate(flops=flops, bytes_accessed=moved, transcendentals=0)


def in_vmem(*values):
    return [pltpu.with_memory_space_constraint(x, pltpu.VMEM) for x in values]


WHOLE = pl.BlockSpec(memory_space=pltpu.VMEM)
SCALARS = pl.BlockSpec(memory_space=pltpu.SMEM)


def pack_kernel(order_ref, slab_ref, energy_ref, out_ref):
    for q in range(NQ):
        out_ref[0:W, q * W : (q + 1) * W] = slab_ref[q, 0]
    both = jnp.broadcast_to(energy_ref[...].reshape(1, 2 * W), (TALL - W, 2 * W))
    out_ref[W:TALL, 0:W] = jnp.where(order_ref[0] == 0, both[:, 0:W], both[:, W : 2 * W])
    out_ref[W:TALL, W:DEEP] = jnp.zeros((TALL - W, DEEP - W), BF)


def pack_slab(slab, energy, block):
    return pl.pallas_call(
        pack_kernel,
        out_shape=jax.ShapeDtypeStruct((TALL, DEEP), BF),
        grid_spec=pltpu.PrefetchScalarGridSpec(
            num_scalar_prefetch=1,
            grid=(1,),
            in_specs=[
                pl.BlockSpec((NQ, 1, W, W), lambda i, order: (0, order[0], 0, 0)),
                pl.BlockSpec((2 * W,), lambda i, order: (0,)),
            ],
            out_specs=pl.BlockSpec((TALL, DEEP), lambda i, order: (0, 0)),
        ),
        compiler_params=params("arbitrary"),
        cost_estimate=cost(0, 3_000_000),
    )(block, slab, energy)


def put_tile(unit_ref, block, tile):
    unit_ref[block * W : (block + 1) * W, :] = tile[:, 0:128]
    unit_ref[2 * W : 3 * W, block * 64 : (block + 1) * 64] = tile[:, 128:192]
    base = 3 * W + 16 * block
    for c in range(13):
        rows = min(16, W - 16 * c)
        unit_ref[base : base + rows, 8 * c : 8 * c + 8] = tile[16 * c : 16 * c + rows, 192:200]


def get_tile(unit, block):
    base = 3 * W + 16 * block
    tail = [
        unit[base : base + min(16, W - 16 * c), 8 * c : 8 * c + 8] for c in range(13)
    ]
    return jnp.concatenate(
        [
            unit[block * W : (block + 1) * W, :],
            unit[2 * W : 3 * W, block * 64 : (block + 1) * 64],
            jnp.concatenate(tail, axis=0),
        ],
        axis=1,
    )


def whole_unit(j, *refs):
    pieces = [ref[i, j].astype(F32) for ref in refs for i in range(ref.shape[0])]
    return jnp.concatenate(pieces, axis=0)


def turned(tile):
    return jnp.pad(tile, ((0, 56), (0, 56))).T[0:W, 0:W]


def tiles_kernel(pick_ref, amp_ref, int_ref, *refs):
    *outs, unit = refs
    unit[3 * W : UNIT, :] = jnp.zeros((UNIT - 3 * W, 128), F32)
    j = pl.program_id(0)
    for kind, ref in enumerate((amp_ref, int_ref)):
        for block in range(2):
            put_tile(unit, block, ref[0, block].astype(F32))
        for i in range(4):
            piece = unit[i * PIECE : (i + 1) * PIECE, :].astype(BF)
            if len(outs) == 2:
                outs[kind][i, j] = piece
            else:
                outs[0][i, 2 * kind + j] = piece


def pack_tiles(pick, amplitudes, integrals, arrays):
    tile = pl.BlockSpec((1, 2, W, W), lambda j, pick: (pick[j], 0, 0, 0))
    shape = (4, 4 // arrays, PIECE, 128)
    return pl.pallas_call(
        tiles_kernel,
        out_shape=[jax.ShapeDtypeStruct(shape, BF)] * arrays,
        grid_spec=pltpu.PrefetchScalarGridSpec(
            num_scalar_prefetch=1,
            grid=(2,),
            in_specs=[tile, tile],
            out_specs=[pl.BlockSpec(shape, lambda j, pick: (0, 0, 0, 0))] * arrays,
            scratch_shapes=[pltpu.VMEM((UNIT, 128), F32)],
        ),
        compiler_params=params("arbitrary"),
        cost_estimate=cost(0, 1_500_000),
    )(pick, amplitudes, integrals)


def half_kernel(flip_ref, slab_ref, amp_ref, add_ref, cross_ref, half_ref, int_ref):
    @pl.loop(0, 2)
    def _(j):
        straight = flip_ref[j] == 0

        def sums(ref, at):
            local, cross = whole_unit(j, ref), whole_unit(at, cross_ref)
            tiles = [get_tile(cross, b) for b in range(2)]
            return [
                get_tile(local, b) + turned(jnp.where(straight, tiles[b], tiles[1 - b]))
                for b in range(2)
            ]

        for b, tile in enumerate(sums(add_ref, 2 + j)):
            int_ref[2 * j + b] = tile
        for b, tile in enumerate(sums(amp_ref, j)):
            both = tile.astype(BF)
            for q in range(NQ):
                half_ref[2 * j + b, :, q * W : (q + 1) * W] = jnp.dot(
                    slab_ref[q, b], both, preferred_element_type=F32
                ).astype(BF)


def first_half(flip, slab, amp, add, cross):
    return pl.pallas_call(
        half_kernel,
        out_shape=(pltpu.VMEM((4, W, DEEP), BF), pltpu.VMEM((4, W, W), F32)),
        in_specs=[SCALARS] + [WHOLE] * 4,
        out_specs=[WHOLE, WHOLE],
        compiler_params=params(),
        cost_estimate=cost(8 * NQ * W**3, 4_000_000),
    )(flip, slab, amp, add, cross)


def ladder_kernel(source_ref, core_ref, half_ref, int_ref, *refs):
    full, (near, near_x, far, far_x), (out_ref, low_ref, high_ref, table_ref, unit, sums) = (
        refs[:6], refs[6:10], refs[10:]
    )
    even = core_ref[0] == 0
    odd = core_ref[0] != 0
    split = ((even, near, far), (even, near_x, far_x), (odd, far, near), (odd, far_x, near_x))
    dims = (((1,), (1,)), ((), ()))

    @pl.loop(0, 4)
    def _(t):
        for r in range(6):

            @pl.when(source_ref[t] == r)
            def _():
                sums[t] = lax.dot_general(
                    half_ref[t], full[r][0:W, :], dims, preferred_element_type=F32
                )

        for r, (on, low, high) in enumerate(split):

            @pl.when(jnp.logical_and(on, source_ref[t] == 6 + r % 2))
            def _():
                sums[t] = lax.dot_general(
                    half_ref[t, :, 0:PART], low[0:W, :], dims, preferred_element_type=F32
                ) + lax.dot_general(
                    half_ref[t, :, PART:DEEP],
                    high[0:W, 2 * PART - DEEP : PART],
                    dims,
                    preferred_element_type=F32,
                )

    for r in range(6):
        table_ref[r] = full[r][W:TALL, 0:W].astype(F32)
    for r, (on, low, _) in enumerate(split):

        @pl.when(on)
        def _():
            table_ref[6 + r % 2] = low[W:TALL, 0:W].astype(F32)

    unit[3 * W : UNIT, :] = jnp.zeros((UNIT - 3 * W, 128), F32)
    for j in range(2):
        for b in range(2):
            put_tile(unit, b, int_ref[2 * j + b] + sums[2 * j + b])
        for i in range(4):
            piece = unit[i * PIECE : (i + 1) * PIECE, :].astype(BF)
            out_ref[i, j] = piece
            (low_ref if i < 2 else high_ref)[i % 2, j] = piece


def symmetric_units(source, core, half_done, integrals, full, parts):
    return pl.pallas_call(
        ladder_kernel,
        out_shape=(
            jax.ShapeDtypeStruct((4, 2, PIECE, 128), BF),
            jax.ShapeDtypeStruct((2, 2, PIECE, 128), BF),
            jax.ShapeDtypeStruct((2, 2, PIECE, 128), BF),
            jax.ShapeDtypeStruct((8, TALL - W, W), F32),
        ),
        in_specs=[SCALARS, SCALARS] + [WHOLE] * 12,
        out_specs=[WHOLE] * 4,
        scratch_shapes=[pltpu.VMEM((UNIT, 128), F32), pltpu.VMEM((4, W, W), F32)],
        compiler_params=params(),
        cost_estimate=cost(8 * NQ * W**3, 3_000_000),
    )(source, core, *in_vmem(half_done, integrals, *full, *parts))


def update_kernel(
    kept_ref, at_ref, flip_ref, source_ref, pair_ref,
    amp_ref, cross_ref, low_ref, high_ref, table_ref, near_ref, out_ref
):
    p = pl.program_id(0)

    def finish(block, symmetric):
        far = table_ref[source_ref[2 * p + block], 0:1, :]
        denominator = pair_ref[p] - near_ref[block] - far
        old = amp_ref[0, block].astype(F32)
        out_ref[0, block] = (old + symmetric / denominator).astype(BF)

    @pl.when(kept_ref[p] == 1)
    def _():
        unit = whole_unit(0, cross_ref)
        tiles = [get_tile(unit, b) for b in range(2)]
        straight = flip_ref[p] == 0
        for b in range(2):
            finish(b, turned(jnp.where(straight, tiles[b], tiles[1 - b])))

    @pl.when(kept_ref[p] == 0)
    def _():
        unit = whole_unit(0, low_ref, high_ref)
        for b in range(2):
            finish(b, get_tile(unit, b))


def update(kept, at, flip, source, pair_energy, amplitudes, cross, low, high, table, near):
    pairs = amplitudes.shape[0]
    pick = lambda p, k, a, f, s, e: (0, a[p], 0, 0)
    here = lambda p, k, a, f, s, e: (p, 0, 0, 0)
    fixed = lambda p, k, a, f, s, e: (0, 0, 0)
    return pl.pallas_call(
        update_kernel,
        out_shape=jax.ShapeDtypeStruct((pairs, 2, W, W), BF),
        grid_spec=pltpu.PrefetchScalarGridSpec(
            num_scalar_prefetch=5,
            grid=(pairs,),
            in_specs=[
                pl.BlockSpec((1, 2, W, W), here),
                pl.BlockSpec((4, 1, PIECE, 128), pick),
                pl.BlockSpec((2, 1, PIECE, 128), pick),
                pl.BlockSpec((2, 1, PIECE, 128), pick),
                pl.BlockSpec((8, TALL - W, W), fixed),
                pl.BlockSpec((2, W, 1), fixed),
            ],
            out_specs=pl.BlockSpec((1, 2, W, W), here),
        ),
        compiler_params=params("arbitrary"),
    )(kept, at, flip, source, pair_energy, amplitudes, cross, low, high, table, near)


def on_device(
    amplitudes, integrals, ladder_slab, pair_list, mirror_slot, occ_irrep, occ_energy, virt_energy
):
    pairs = amplitudes.shape[0]
    amp = amplitudes.reshape(pairs, 2, W, W)
    ints = integrals.reshape(pairs, 2, W, W)
    slab = ladder_slab.reshape(NQ, 2, W, W)
    place = lax.axis_index("pair").astype(jnp.int32)
    virt = lax.axis_index("virt").astype(jnp.int32)
    core = jnp.bitwise_and(place, 1)
    parity = jnp.bitwise_and(jnp.right_shift(place, 1), 1)
    upper = (place >= lax.axis_size("pair") // 2).astype(jnp.int32)

    slots = jnp.arange(pairs, dtype=jnp.int32)
    label = jnp.where(upper == 0, slots, mirror_slot)
    kept = (jnp.right_shift(label, 1) == upper).astype(jnp.int32)
    at = jnp.bitwise_and(label, 1)

    def among(values, group):
        chosen = label[:, None] == jnp.arange(2, dtype=jnp.int32)[None, :] + 2 * group
        return jnp.sum(jnp.where(chosen, values[:, None], 0), axis=0)

    keep, send = among(slots, upper), among(slots, 1 - upper)

    one = pack_slab(slab, virt_energy, parity[None])
    y_one = along_y(one)
    sent_amp, sent_int = pack_tiles(send, amp, ints, 2)
    local_amp = to_mirror(sent_amp)
    scattered = exchange(pack_tiles(keep, amp, ints, 1)[0])

    irrep = jnp.bitwise_xor(occ_irrep[pair_list[:, 0]], occ_irrep[pair_list[:, 1]])
    step, flip = jnp.right_shift(irrep, 1), jnp.bitwise_and(irrep, 1)
    keep_step, keep_flip = among(step, upper), among(flip, upper)
    pair_energy = occ_energy[pair_list[:, 0]] + occ_energy[pair_list[:, 1]]
    near = virt_energy.astype(F32).reshape(2, W, 1)

    def sources(step, flip):
        apart = jnp.bitwise_and(jnp.bitwise_xor(virt, step) - virt, 3)[:, None]
        second = (jnp.bitwise_xor(jnp.arange(2)[None, :], flip[:, None]) != parity).astype(jnp.int32)
        side = jnp.where(apart == 3 - 2 * core, 2, 4)
        start = jnp.where(apart == 0, 0, jnp.where(apart == 2, 6, side))
        return (start + second).reshape(-1)

    y_one, local_amp, scattered, sent_int = together(y_one, local_amp, scattered, sent_int)
    x_one = along_x(y_one)
    y_far = along_y(lax.dynamic_slice(y_one, (0, core * (DEEP - PART)), (TALL, PART)))
    local_int = to_mirror(sent_int)
    cross = exchange(reorder(scattered, jnp.concatenate([keep_step, keep_step])))
    swapped = swap_cores(y_one)
    two = pack_slab(slab, virt_energy, 1 - parity[None])
    x_far = along_x(y_far)
    x_one, local_int, two, cross = together(x_one, local_int, two, cross)
    full = (one, two, y_one, x_one, swapped, swap_cores(x_one))
    parts = (y_far, x_far, swap_cores(y_far), swap_cores(x_far))

    half_done, both_ints = first_half(keep_flip, slab, local_amp, local_int, cross)
    result, low, high, table = symmetric_units(
        sources(keep_step, keep_flip), core[None], half_done, both_ints, full, parts
    )
    low, scattered = together(to_mirror(low), exchange(result))
    crossed = exchange(reorder(scattered, keep_step))
    high = to_mirror(high)
    new = update(
        kept, at, flip, sources(step, flip), pair_energy, amp, crossed, low, high, table, near
    )
    return new.reshape(amplitudes.shape)


def solution(mesh):
    return jax.shard_map(
        on_device,
        mesh=mesh,
        in_specs=(
            P("pair", "virt", None),
            P("pair", "virt", None),
            P(None, "virt", None),
            P("pair", None),
            P("pair"),
            P(),
            P(),
            P("virt"),
        ),
        out_specs=P("pair", "virt", None),
        check_vma=False,
    )
```

time: 174 us -> 171 us (0.983)
  the two profiles are of different devices: /device:TPU:122 before, /device:TPU:72 now
where the time goes in v4:
time: 171 us; the launch traced here: 170 us
  starting transfers between devices  89.5 us (52%)
  waiting for transfers between devices  44.6 us (26%)
  Pallas kernels  17.9 us (10%)
  local copies, waits for them, and re-layouts  17 us (10%)
    ppermute x12, starting transfers between devices, permute(): return lax.ppermute(value, ('pair', 'virt'), pairs)  66.2 us
    ppermute x12, waiting for transfers between devices, permute(): return lax.ppermute(value, ('pair', 'virt'), pairs)  44.6 us
    all_to_all x4, starting transfers between devices, exchange(): return lax.all_to_all(units, 'virt', 0, 0, tiled=True)  23.3 us
    unnamed x44, local copies, waits for them, and re-layouts  8.72 us
    pallas_call x1, Pallas kernels, symmetric_units(): pl.pallas_call(ladder_kernel, out_shape=(jax.ShapeDtypeStruct((4, 2, PIEC...  6.82 us
    pallas_call x1, Pallas kernels, first_half(): pl.pallas_call(half_kernel, out_shape=(pltpu.VMEM((4, W, DEEP), BF), pltp...  5.06 us
    gather x2, local copies, waits for them, and re-layouts, reorder(): scattered[index, jnp.arange(scattered.shape[1], dtype=jnp.int32)[None, :]]  4.02 us
  transfers between devices with their start and end apart: 16, of which 5 were waited for; matrix products, arithmetic and copies ran while one was open for 4% of the time, Pallas kernels for 4%

profile of v4, /device:TPU:72, one launch (start us, length us, event | category | flops | bytes accessed | tf_op | source)
XLA Modules:
  0.0 169.8 jit_solution(12908537896528018813)
XLA Ops:
  0.0 1.9 %copy-done.1 = bf16[16,400,200]{2,1,0:T(8,128)(2,1)S(1)} copy-done((bf16[16,400,200]{2,1,0:T(8,128)(2,1)S(1)}, bf16[16,400,200]{2,1,0:T(8,128)(2,1)}, u32[]{:S(2)}) %copy-start.1) | copy-done | bytes 2560024
  1.9 0.7 copy-done.15
  2.6 0.5 shard_map.82.refs_0_
  3.1 3.6 %collective-permute-start = (bf16[208,3200]{1,0:T(8,128)(2,1)S(1)}, bf16[208,3200]{1,0:T(8,128)(2,1)}, u32[]{:S(2)}, u32[]{:S(2)}) collective-permute-start(bf16[208,3200]{1,0:T(8,128)(2,1)S(1)} %shard_map.82.refs_0_), channel_id=1, source_target_pairs={{0,1},{4,39},{8,9},{12,47},{16,17},{20,55},{24,25},{28,63},{1,2},{... | collective-permute-start | bytes 3993608 | tf_op jit(solution)/shard_map/ppermute | solution.py:33
  6.8 0.6 gather_fusion
  7.4 0.6 gather_fusion.1
  8.1 0.1 fusion.2
  8.2 0.9 shard_map.84
  9.2 0.8 copy-done.10
  10.0 6.5 %all-to-all-start = ((bf16[4,4,160,128]{3,2,1,0:T(8,128)(2,1)}), bf16[4,4,160,128]{3,2,1,0:T(8,128)(2,1)}, u32[]{:S(2)}, u32[]{:S(2)}) async-start(bf16[4,4,160,128]{3,2,1,0:T(8,128)(2,1)} %copy-done.10), calls=%async_computation | async-start | bytes 1310720 | tf_op jit(solution)/shard_map/all_to_all | solution.py:54
  16.5 0.9 shard_map.83
  17.5 0.7 copy-done.17
  18.2 14.2 %collective-permute-start.1 = (bf16[4,2,160,128]{3,2,1,0:T(8,128)(2,1)S(1)}, bf16[4,2,160,128]{3,2,1,0:T(8,128)(2,1)S(1)}, u32[]{:S(2)}, u32[]{:S(2)}) collective-permute-start(bf16[4,2,160,128]{3,2,1,0:T(8,128)(2,1)S(1)} %get-tuple-element.23), channel_id=1, source_target_pairs={{0,384},{4,388},{8,392},{12,396},{16,400},{20,404},{24,408},{28,41... | collective-permute-start | bytes 983048 | tf_op jit(solution)/shard_map/ppermute | solution.py:33
  32.4 21.4 %collective-permute-done.1.amp_ref = bf16[4,2,160,128]{3,2,1,0:T(8,128)(2,1)S(1)} collective-permute-done((bf16[4,2,160,128]{3,2,1,0:T(8,128)(2,1)S(1)}, bf16[4,2,160,128]{3,2,1,0:T(8,128)(2,1)S(1)}, u32[]{:S(2)}, u32[]{:S(2)}) %collective-permute-start.1) | collective-permute-done | bytes 327712 | tf_op jit(solution)/shard_map/ppermute | solution.py:33
  53.8 0.7 copy-done.11
  54.5 3.4 %collective-permute-start.2 = (bf16[208,3200]{1,0:T(8,128)(2,1)}, bf16[208,3200]{1,0:T(8,128)(2,1)}, u32[]{:S(2)}, u32[]{:S(2)}) collective-permute-start(bf16[208,3200]{1,0:T(8,128)(2,1)} %collective-permute-done.refs_2_), channel_id=1, source_target_pairs={{0,8},{4,28},{8,16},{12,4},{16,24},{20,12},{24,0},{28,20},{1,9},{5... | collective-permute-start | bytes 3993608 | tf_op jit(solution)/shard_map/ppermute | solution.py:33
  58.0 0.1 reshape.214
  58.1 2.7 %gather_fusion.4 = bf16[16,160,128]{2,1,0:T(8,128)(2,1)} fusion(bf16[4,4,160,128]{3,2,1,0:T(8,128)(2,1)} %all-to-all-done, s32[16]{0:T(128)S(1)} %reshape.214), kind=kCustom, calls=%fused_computation.4 | custom fusion | bytes 1310848 | tf_op jit(solution)/shard_map/gather | solution.py:59
  60.8 5.2 %all-to-all-start.1 = ((bf16[4,4,160,128]{3,2,1,0:T(8,128)(2,1)}), bf16[4,4,160,128]{3,2,1,0:T(8,128)(2,1)}, u32[]{:S(2)}, u32[]{:S(2)}) async-start(bf16[4,4,160,128]{3,2,1,0:T(8,128)(2,1)} %bitcast.24), calls=%async_computation.1 | async-start | bytes 1310720 | tf_op jit(solution)/shard_map/all_to_all | solution.py:54
  66.0 1.2 constant_dynamic-slice_fusion
  67.2 3.4 %collective-permute-start.6 = (bf16[208,1664]{1,0:T(8,128)(2,1)S(1)}, bf16[208,1664]{1,0:T(8,128)(2,1)}, u32[]{:S(2)}, u32[]{:S(2)}) collective-permute-start(bf16[208,1664]{1,0:T(8,128)(2,1)S(1)} %constant_dynamic-slice_fusion), channel_id=1, source_target_pairs={{0,1},{4,39},{8,9},{12,47},{16,17},{20,55},{24,25},{28,63},{1,2},{... | collective-permute-start | bytes 2076680 | tf_op jit(solution)/shard_map/ppermute | solution.py:33
  70.6 9.7 %collective-permute-start.3 = (bf16[4,2,160,128]{3,2,1,0:T(8,128)(2,1)S(1)}, bf16[4,2,160,128]{3,2,1,0:T(8,128)(2,1)S(1)}, u32[]{:S(2)}, u32[]{:S(2)}) collective-permute-start(bf16[4,2,160,128]{3,2,1,0:T(8,128)(2,1)S(1)} %copy-done.18), channel_id=1, source_target_pairs={{0,384},{4,388},{8,392},{12,396},{16,400},{20,404},{24,408},{28,41... | collective-permute-start | bytes 983048 | tf_op jit(solution)/shard_map/ppermute | solution.py:33
  80.4 4.3 %collective-permute-done.6.refs_6_ = bf16[208,1664]{1,0:T(8,128)(2,1)} collective-permute-done((bf16[208,1664]{1,0:T(8,128)(2,1)S(1)}, bf16[208,1664]{1,0:T(8,128)(2,1)}, u32[]{:S(2)}, u32[]{:S(2)}) %collective-permute-start.6) | collective-permute-done | bytes 692256 | tf_op jit(solution)/shard_map/ppermute | solution.py:33
  84.7 1.9 %collective-permute-start.7 = (bf16[208,1664]{1,0:T(8,128)(2,1)}, bf16[208,1664]{1,0:T(8,128)(2,1)}, u32[]{:S(2)}, u32[]{:S(2)}) collective-permute-start(bf16[208,1664]{1,0:T(8,128)(2,1)} %collective-permute-done.6.refs_6_), channel_id=1, source_target_pairs={{0,8},{4,28},{8,16},{12,4},{16,24},{20,12},{24,0},{28,20},{1,9},{5... | collective-permute-start | bytes 2076680 | tf_op jit(solution)/shard_map/ppermute | solution.py:33
  86.6 0.5 shard_map.85.refs_1_
  87.1 1.1 copy-done.7
  88.2 4.4 %collective-permute-start.4 = (bf16[208,3200]{1,0:T(8,128)(2,1)}, bf16[208,3200]{1,0:T(8,128)(2,1)}, u32[]{:S(2)}, u32[]{:S(2)}) collective-permute-start(bf16[208,3200]{1,0:T(8,128)(2,1)} %collective-permute-done.refs_2_), channel_id=1, source_target_pairs={{0,4},{4,0},{8,12},{12,8},{16,20},{20,16},{24,28},{28,24},{1,5},{5... | collective-permute-start | bytes 3993608 | tf_op jit(solution)/shard_map/ppermute | solution.py:33
  92.6 2.0 %collective-permute-done.3.add_ref = bf16[4,2,160,128]{3,2,1,0:T(8,128)(2,1)S(1)} collective-permute-done((bf16[4,2,160,128]{3,2,1,0:T(8,128)(2,1)S(1)}, bf16[4,2,160,128]{3,2,1,0:T(8,128)(2,1)S(1)}, u32[]{:S(2)}, u32[]{:S(2)}) %collective-permute-start.3) | collective-permute-done | bytes 327712 | tf_op jit(solution)/shard_map/ppermute | solution.py:33
  94.6 0.7 copy-done.13
  95.4 1.9 %collective-permute-start.5 = (bf16[208,3200]{1,0:T(8,128)(2,1)}, bf16[208,3200]{1,0:T(8,128)(2,1)}, u32[]{:S(2)}, u32[]{:S(2)}) collective-permute-start(bf16[208,3200]{1,0:T(8,128)(2,1)} %collective-permute-done.2.refs_3_), channel_id=1, source_target_pairs={{0,4},{4,0},{8,12},{12,8},{16,20},{20,16},{24,28},{28,24},{1,5},{5... | collective-permute-start | bytes 3993608 | tf_op jit(solution)/shard_map/ppermute | solution.py:33
  97.3 2.4 %collective-permute-start.8 = (bf16[208,1664]{1,0:T(8,128)(2,1)}, bf16[208,1664]{1,0:T(8,128)(2,1)}, u32[]{:S(2)}, u32[]{:S(2)}) collective-permute-start(bf16[208,1664]{1,0:T(8,128)(2,1)} %collective-permute-done.6.refs_6_), channel_id=1, source_target_pairs={{0,4},{4,0},{8,12},{12,8},{16,20},{20,16},{24,28},{28,24},{1,5},{5... | collective-permute-start | bytes 2076680 | tf_op jit(solution)/shard_map/ppermute | solution.py:33
  99.7 1.9 %collective-permute-start.9 = (bf16[208,1664]{1,0:T(8,128)(2,1)}, bf16[208,1664]{1,0:T(8,128)(2,1)}, u32[]{:S(2)}, u32[]{:S(2)}) collective-permute-start(bf16[208,1664]{1,0:T(8,128)(2,1)} %collective-permute-done.7.refs_7_), channel_id=1, source_target_pairs={{0,4},{4,0},{8,12},{12,8},{16,20},{20,16},{24,28},{28,24},{1,5},{5... | collective-permute-start | bytes 2076680 | tf_op jit(solution)/shard_map/ppermute | solution.py:33
  101.7 0.1 add.98.source_ref
  101.8 1.0 copy-done.12
  102.8 1.0 copy-done.14
  103.8 5.1 %shard_map.86 = (bf16[4,200,3200]{2,1,0:T(8,128)(2,1)S(1)}, f32[4,200,200]{2,1,0:T(8,128)S(1)}) custom-call(s32[2]{0:T(128)S(1)} %get-tuple-element.42.flip_ref, bf16[16,2,200,200]{3,2,1,0:T(8,128)(2,1)S(1)} %bitcast.18, bf16[4,2,160,128]{3,2,1,0:T(8,128)(2,1)S(1)} %copy-done.12, bf16[4,2,160,128]{3,2,1,0:T(8,128)(2,1)S(1)} %copy-done.14, ...), custom_call_target="tpu_custom_call" | custom-call | flops 1024000000 | bytes 4000000 | tf_op jit(solution)/shard_map/pallas_call | solution.py:200
  108.9 6.8 %shard_map.87 = (bf16[4,2,160,128]{3,2,1,0:T(8,128)(2,1)}, bf16[2,2,160,128]{3,2,1,0:T(8,128)(2,1)S(1)}, bf16[2,2,160,128]{3,2,1,0:T(8,128)(2,1)S(1)}, f32[8,8,200]{2,1,0:T(8,128)S(1)}) custom-call(s32[4]{0:T(128)S(1)} %add.98.source_ref, s32[1]{0:T(128)} %bitcast.3.core_ref, bf16[4,200,3200]{2,1,0:T(8,128)(2,1)S(1)} %get-tuple-element.31.half_ref, ...), custom_call_target="tpu_custom_call" | custom-call | flops 1024000000 | bytes 3000000 | tf_op jit(solution)/shard_map/pallas_call | solution.py:261
  115.7 6.5 %all-to-all-start.2 = ((bf16[4,2,160,128]{3,2,1,0:T(8,128)(2,1)}), bf16[4,2,160,128]{3,2,1,0:T(8,128)(2,1)S(1)}, u32[]{:S(2)}, u32[]{:S(2)}) async-start(bf16[4,2,160,128]{3,2,1,0:T(8,128)(2,1)} %get-tuple-element.36), calls=%async_computation.2 | async-start | bytes 655360 | tf_op jit(solution)/shard_map/all_to_all | solution.py:54
  122.2 9.7 %collective-permute-start.10 = (bf16[2,2,160,128]{3,2,1,0:T(8,128)(2,1)S(1)}, bf16[2,2,160,128]{3,2,1,0:T(8,128)(2,1)S(1)}, u32[]{:S(2)}, u32[]{:S(2)}) collective-permute-start(bf16[2,2,160,128]{3,2,1,0:T(8,128)(2,1)S(1)} %get-tuple-element.35), channel_id=1, source_target_pairs={{0,384},{4,388},{8,392},{12,396},{16,400},{20,404},{24,408},{28,41... | collective-permute-start | bytes 491528 | tf_op jit(solution)/shard_map/ppermute | solution.py:33
  132.0 10.9 %collective-permute-done.10.low_ref = bf16[2,2,160,128]{3,2,1,0:T(8,128)(2,1)S(1)} collective-permute-done((bf16[2,2,160,128]{3,2,1,0:T(8,128)(2,1)S(1)}, bf16[2,2,160,128]{3,2,1,0:T(8,128)(2,1)S(1)}, u32[]{:S(2)}, u32[]{:S(2)}) %collective-permute-start.10) | collective-permute-done | bytes 163872 | tf_op jit(solution)/shard_map/ppermute | solution.py:33
  143.0 1.3 gather_fusion.5
  144.3 5.1 %all-to-all-start.3 = ((bf16[4,2,160,128]{3,2,1,0:T(8,128)(2,1)}), bf16[4,2,160,128]{3,2,1,0:T(8,128)(2,1)S(1)}, u32[]{:S(2)}, u32[]{:S(2)}) async-start(bf16[4,2,160,128]{3,2,1,0:T(8,128)(2,1)} %bitcast.8), calls=%async_computation.3 | async-start | bytes 655360 | tf_op jit(solution)/shard_map/all_to_all | solution.py:54
  149.4 0.6 gather_fusion.2
  150.0 0.6 gather_fusion.3
  150.7 0.2 reshape.226.near_ref
  151.0 9.6 %collective-permute-start.11 = (bf16[2,2,160,128]{3,2,1,0:T(8,128)(2,1)S(1)}, bf16[2,2,160,128]{3,2,1,0:T(8,128)(2,1)S(1)}, u32[]{:S(2)}, u32[]{:S(2)}) collective-permute-start(bf16[2,2,160,128]{3,2,1,0:T(8,128)(2,1)S(1)} %get-tuple-element.39), channel_id=1, source_target_pairs={{0,384},{4,388},{8,392},{12,396},{16,400},{20,404},{24,408},{28,41... | collective-permute-start | bytes 491528 | tf_op jit(solution)/shard_map/ppermute | solution.py:33
  160.6 5.9 %collective-permute-done.11.high_ref = bf16[2,2,160,128]{3,2,1,0:T(8,128)(2,1)S(1)} collective-permute-done((bf16[2,2,160,128]{3,2,1,0:T(8,128)(2,1)S(1)}, bf16[2,2,160,128]{3,2,1,0:T(8,128)(2,1)S(1)}, u32[]{:S(2)}, u32[]{:S(2)}) %collective-permute-start.11) | collective-permute-done | bytes 163872 | tf_op jit(solution)/shard_map/ppermute | solution.py:33
  166.5 3.2 %shard_map.88 = bf16[4,2,200,200]{3,2,1,0:T(8,128)(2,1)} custom-call(s32[4]{0:T(128)S(1)} %compare_convert_fusion.1.kept_ref, s32[4]{0:T(128)S(1)} %get-tuple-element.47.at_ref, s32[4]{0:T(128)S(1)} %get-tuple-element.49.flip_ref, s32[8]{0:T(128)S(1)} %add.92.source_ref, f32[4]{0:T(128)S(1)} %add.93.pair_ref, bf16[4,2,200,200]{3,2,1,0:T(8,128)(2,1)S(1)} %bitcast.21, ...), custom_call_target="tpu_custom_call" | custom-call | tf_op jit(solution)/shard_map/pallas_call | solution.py:309
  (60 shorter events, 0.5 us)
Async XLA Ops:
  0.0 6.8 %copy-start = (s32[200]{0:T(256)S(1)}, s32[200]{0:T(256)}, u32[]{:S(2)}) copy-start(s32[200]{0:T(256)} %param.13) | copy-start | bytes 2404
  0.0 1.9 %copy-start.1 = (bf16[16,400,200]{2,1,0:T(8,128)(2,1)S(1)}, bf16[16,400,200]{2,1,0:T(8,128)(2,1)}, u32[]{:S(2)}) copy-start(bf16[16,400,200]{2,1,0:T(8,128)(2,1)} %param.10) | copy-start | bytes 7680004
  1.9 0.7 copy-start.15
  2.6 4.1 %copy-start.20 = (s32[4,2]{0,1:T(2,128)S(1)}, s32[4,2]{0,1:T(2,128)}, u32[]{:S(2)}) copy-start(s32[4,2]{0,1:T(2,128)} %param.11) | copy-start | bytes 100
  2.6 5.5 %copy-start.21 = (s32[4]{0:T(128)S(1)}, s32[4]{0:T(128)}, u32[]{:S(2)}) copy-start(s32[4]{0:T(128)} %param.12) | copy-start | bytes 52
  2.6 5.6 %copy-start.9 = (bf16[4,400,200]{2,1,0:T(8,128)(2,1)S(1)}, bf16[4,400,200]{2,1,0:T(8,128)(2,1)}, u32[]{:S(2)}) copy-start(bf16[4,400,200]{2,1,0:T(8,128)(2,1)} %param.9) | copy-start | bytes 1920004
  3.1 6.1 %copy-start.5 = (bf16[208,3200]{1,0:T(8,128)(2,1)}, bf16[208,3200]{1,0:T(8,128)(2,1)S(1)}, u32[]{:S(2)}) copy-start(bf16[208,3200]{1,0:T(8,128)(2,1)S(1)} %shard_map.82.refs_0_) | copy-start | bytes 3993604
  3.1 5.1 %copy-start.3 = (bf16[4,400,200]{2,1,0:T(8,128)(2,1)S(1)}, bf16[4,400,200]{2,1,0:T(8,128)(2,1)}, u32[]{:S(2)}) copy-start(bf16[4,400,200]{2,1,0:T(8,128)(2,1)} %param.8) | copy-start | bytes 1920004
  3.1 51.4 %collective-permute-start = (bf16[208,3200]{1,0:T(8,128)(2,1)S(1)}, bf16[208,3200]{1,0:T(8,128)(2,1)}, u32[]{:S(2)}, u32[]{:S(2)}) collective-permute-start(bf16[208,3200]{1,0:T(8,128)(2,1)S(1)} %shard_map.82.refs_0_), channel_id=1, source_target_pairs={{0,1},{4,39},{8,9},{12,47},{16,17},{20,55},{24,25},{28,63},{1,2},{... | collective-permute-start | bytes 3993608 | tf_op jit(solution)/shard_map/ppermute | solution.py:33
  9.2 0.8 copy-start.10
  10.0 44.5 %all-to-all-start = ((bf16[4,4,160,128]{3,2,1,0:T(8,128)(2,1)}), bf16[4,4,160,128]{3,2,1,0:T(8,128)(2,1)}, u32[]{:S(2)}, u32[]{:S(2)}) async-start(bf16[4,4,160,128]{3,2,1,0:T(8,128)(2,1)} %copy-done.10), calls=%async_computation | async-start | bytes 1310720 | tf_op jit(solution)/shard_map/all_to_all | solution.py:54
  17.5 0.7 copy-start.17
  18.2 35.6 %collective-permute-start.1 = (bf16[4,2,160,128]{3,2,1,0:T(8,128)(2,1)S(1)}, bf16[4,2,160,128]{3,2,1,0:T(8,128)(2,1)S(1)}, u32[]{:S(2)}, u32[]{:S(2)}) collective-permute-start(bf16[4,2,160,128]{3,2,1,0:T(8,128)(2,1)S(1)} %get-tuple-element.23), channel_id=1, source_target_pairs={{0,384},{4,388},{8,392},{12,396},{16,400},{20,404},{24,408},{28,41... | collective-permute-start | bytes 983048 | tf_op jit(solution)/shard_map/ppermute | solution.py:33
  53.8 0.7 copy-start.11
  54.5 40.8 %collective-permute-start.2 = (bf16[208,3200]{1,0:T(8,128)(2,1)}, bf16[208,3200]{1,0:T(8,128)(2,1)}, u32[]{:S(2)}, u32[]{:S(2)}) collective-permute-start(bf16[208,3200]{1,0:T(8,128)(2,1)} %collective-permute-done.refs_2_), channel_id=1, source_target_pairs={{0,8},{4,28},{8,16},{12,4},{16,24},{20,12},{24,0},{28,20},{1,9},{5... | collective-permute-start | bytes 3993608 | tf_op jit(solution)/shard_map/ppermute | solution.py:33
  58.1 28.5 %copy-start.2 = (bf16[16,400,200]{2,1,0:T(8,128)(2,1)S(1)}, bf16[16,400,200]{2,1,0:T(8,128)(2,1)}, u32[]{:S(2)}) copy-start(bf16[16,400,200]{2,1,0:T(8,128)(2,1)} %param.10) | copy-start | bytes 7680004
  60.8 25.8 %copy-start.16 = (bf16[400]{0:T(512)(128)(2,1)S(1)}, bf16[400]{0:T(512)(128)(2,1)}, u32[]{:S(2)}) copy-start(bf16[400]{0:T(512)(128)(2,1)} %energy_ref.3) | copy-start | bytes 2404
  60.8 34.5 %all-to-all-start.1 = ((bf16[4,4,160,128]{3,2,1,0:T(8,128)(2,1)}), bf16[4,4,160,128]{3,2,1,0:T(8,128)(2,1)}, u32[]{:S(2)}, u32[]{:S(2)}) async-start(bf16[4,4,160,128]{3,2,1,0:T(8,128)(2,1)} %bitcast.24), calls=%async_computation.1 | async-start | bytes 1310720 | tf_op jit(solution)/shard_map/all_to_all | solution.py:54
  66.0 4.6 %copy-start.18 = (bf16[4,2,160,128]{3,2,1,0:T(8,128)(2,1)S(1)}, bf16[4,2,160,128]{3,2,1,0:T(8,128)(2,1)}, u32[]{:S(2)}) copy-start(bf16[4,2,160,128]{3,2,1,0:T(8,128)(2,1)} %copy-done.17) | copy-start | bytes 983044
  67.2 17.4 %collective-permute-start.6 = (bf16[208,1664]{1,0:T(8,128)(2,1)S(1)}, bf16[208,1664]{1,0:T(8,128)(2,1)}, u32[]{:S(2)}, u32[]{:S(2)}) collective-permute-start(bf16[208,1664]{1,0:T(8,128)(2,1)S(1)} %constant_dynamic-slice_fusion), channel_id=1, source_target_pairs={{0,1},{4,39},{8,9},{12,47},{16,17},{20,55},{24,25},{28,63},{1,2},{... | collective-permute-start | bytes 2076680 | tf_op jit(solution)/shard_map/ppermute | solution.py:33
  70.6 24.0 %collective-permute-start.3 = (bf16[4,2,160,128]{3,2,1,0:T(8,128)(2,1)S(1)}, bf16[4,2,160,128]{3,2,1,0:T(8,128)(2,1)S(1)}, u32[]{:S(2)}, u32[]{:S(2)}) collective-permute-start(bf16[4,2,160,128]{3,2,1,0:T(8,128)(2,1)S(1)} %copy-done.18), channel_id=1, source_target_pairs={{0,384},{4,388},{8,392},{12,396},{16,400},{20,404},{24,408},{28,41... | collective-permute-start | bytes 983048 | tf_op jit(solution)/shard_map/ppermute | solution.py:33
  84.7 15.0 %collective-permute-start.7 = (bf16[208,1664]{1,0:T(8,128)(2,1)}, bf16[208,1664]{1,0:T(8,128)(2,1)}, u32[]{:S(2)}, u32[]{:S(2)}) collective-permute-start(bf16[208,1664]{1,0:T(8,128)(2,1)} %collective-permute-done.6.refs_6_), channel_id=1, source_target_pairs={{0,8},{4,28},{8,16},{12,4},{16,24},{20,12},{24,0},{28,20},{1,9},{5... | collective-permute-start | bytes 2076680 | tf_op jit(solution)/shard_map/ppermute | solution.py:33
  87.1 1.1 copy-start.7
  88.2 20.6 %collective-permute-start.4 = (bf16[208,3200]{1,0:T(8,128)(2,1)}, bf16[208,3200]{1,0:T(8,128)(2,1)}, u32[]{:S(2)}, u32[]{:S(2)}) collective-permute-start(bf16[208,3200]{1,0:T(8,128)(2,1)} %collective-permute-done.refs_2_), channel_id=1, source_target_pairs={{0,4},{4,0},{8,12},{12,8},{16,20},{20,16},{24,28},{28,24},{1,5},{5... | collective-permute-start | bytes 3993608 | tf_op jit(solution)/shard_map/ppermute | solution.py:33
  94.6 0.7 copy-start.13
  95.4 13.5 %collective-permute-start.5 = (bf16[208,3200]{1,0:T(8,128)(2,1)}, bf16[208,3200]{1,0:T(8,128)(2,1)}, u32[]{:S(2)}, u32[]{:S(2)}) collective-permute-start(bf16[208,3200]{1,0:T(8,128)(2,1)} %collective-permute-done.2.refs_3_), channel_id=1, source_target_pairs={{0,4},{4,0},{8,12},{12,8},{16,20},{20,16},{24,28},{28,24},{1,5},{5... | collective-permute-start | bytes 3993608 | tf_op jit(solution)/shard_map/ppermute | solution.py:33
  97.3 11.6 %collective-permute-start.8 = (bf16[208,1664]{1,0:T(8,128)(2,1)}, bf16[208,1664]{1,0:T(8,128)(2,1)}, u32[]{:S(2)}, u32[]{:S(2)}) collective-permute-start(bf16[208,1664]{1,0:T(8,128)(2,1)} %collective-permute-done.6.refs_6_), channel_id=1, source_target_pairs={{0,4},{4,0},{8,12},{12,8},{16,20},{20,16},{24,28},{28,24},{1,5},{5... | collective-permute-start | bytes 2076680 | tf_op jit(solution)/shard_map/ppermute | solution.py:33
  99.7 9.1 %collective-permute-start.9 = (bf16[208,1664]{1,0:T(8,128)(2,1)}, bf16[208,1664]{1,0:T(8,128)(2,1)}, u32[]{:S(2)}, u32[]{:S(2)}) collective-permute-start(bf16[208,1664]{1,0:T(8,128)(2,1)} %collective-permute-done.7.refs_7_), channel_id=1, source_target_pairs={{0,4},{4,0},{8,12},{12,8},{16,20},{20,16},{24,28},{28,24},{1,5},{5... | collective-permute-start | bytes 2076680 | tf_op jit(solution)/shard_map/ppermute | solution.py:33
  101.8 1.0 copy-start.12
  102.8 1.0 copy-start.14
  103.8 5.1 %copy-start.6 = (bf16[208,3200]{1,0:T(8,128)(2,1)S(1)}, bf16[208,3200]{1,0:T(8,128)(2,1)}, u32[]{:S(2)}) copy-start(bf16[208,3200]{1,0:T(8,128)(2,1)} %copy-done.5) | copy-start | bytes 3993604
  103.8 5.1 %copy-start.8 = (bf16[208,3200]{1,0:T(8,128)(2,1)S(1)}, bf16[208,3200]{1,0:T(8,128)(2,1)}, u32[]{:S(2)}) copy-start(bf16[208,3200]{1,0:T(8,128)(2,1)} %copy-done.7) | copy-start | bytes 3993604
  115.7 33.7 %copy-start.19 = (f32[200]{0:T(256)S(1)}, f32[200]{0:T(256)}, u32[]{:S(2)}) copy-start(f32[200]{0:T(256)} %param.14) | copy-start | bytes 2404
  115.7 27.2 %all-to-all-start.2 = ((bf16[4,2,160,128]{3,2,1,0:T(8,128)(2,1)}), bf16[4,2,160,128]{3,2,1,0:T(8,128)(2,1)S(1)}, u32[]{:S(2)}, u32[]{:S(2)}) async-start(bf16[4,2,160,128]{3,2,1,0:T(8,128)(2,1)} %get-tuple-element.36), calls=%async_computation.2 | async-start | bytes 655360 | tf_op jit(solution)/shard_map/all_to_all | solution.py:54
  122.2 44.3 %copy-start.4 = (bf16[4,400,200]{2,1,0:T(8,128)(2,1)S(1)}, bf16[4,400,200]{2,1,0:T(8,128)(2,1)}, u32[]{:S(2)}) copy-start(bf16[4,400,200]{2,1,0:T(8,128)(2,1)} %param.8) | copy-start | bytes 1920004
  122.2 20.7 %collective-permute-start.10 = (bf16[2,2,160,128]{3,2,1,0:T(8,128)(2,1)S(1)}, bf16[2,2,160,128]{3,2,1,0:T(8,128)(2,1)S(1)}, u32[]{:S(2)}, u32[]{:S(2)}) collective-permute-start(bf16[2,2,160,128]{3,2,1,0:T(8,128)(2,1)S(1)} %get-tuple-element.35), channel_id=1, source_target_pairs={{0,384},{4,388},{8,392},{12,396},{16,400},{20,404},{24,408},{28,41... | collective-permute-start | bytes 491528 | tf_op jit(solution)/shard_map/ppermute | solution.py:33
  144.3 22.2 %all-to-all-start.3 = ((bf16[4,2,160,128]{3,2,1,0:T(8,128)(2,1)}), bf16[4,2,160,128]{3,2,1,0:T(8,128)(2,1)S(1)}, u32[]{:S(2)}, u32[]{:S(2)}) async-start(bf16[4,2,160,128]{3,2,1,0:T(8,128)(2,1)} %bitcast.8), calls=%async_computation.3 | async-start | bytes 655360 | tf_op jit(solution)/shard_map/all_to_all | solution.py:54
  151.0 15.5 %collective-permute-start.11 = (bf16[2,2,160,128]{3,2,1,0:T(8,128)(2,1)S(1)}, bf16[2,2,160,128]{3,2,1,0:T(8,128)(2,1)S(1)}, u32[]{:S(2)}, u32[]{:S(2)}) collective-permute-start(bf16[2,2,160,128]{3,2,1,0:T(8,128)(2,1)S(1)} %get-tuple-element.39), channel_id=1, source_target_pairs={{0,384},{4,388},{8,392},{12,396},{16,400},{20,404},{24,408},{28,41... | collective-permute-start | bytes 491528 | tf_op jit(solution)/shard_map/ppermute | solution.py:33

commit v5 on v4

--- a/solution.py
+++ b/solution.py
@@ -61,6 +61,13 @@
 
 def together(*values):
     return lax.optimization_barrier(values)
+
+
+def as_unit(ready, work, *values):
+    def empty(*values):
+        return jax.tree.map(lambda x: jnp.zeros(x.shape, x.dtype), jax.eval_shape(work, *values))
+
+    return lax.cond(ready, work, empty, *values)
 
 
 def params(*semantics):
@@ -173,22 +180,22 @@
     )(pick, amplitudes, integrals)
 
 
-def half_kernel(flip_ref, slab_ref, amp_ref, add_ref, cross_ref, half_ref, int_ref):
+def half_kernel(flip_ref, slab_ref, local_ref, cross_ref, half_ref, int_ref):
     @pl.loop(0, 2)
     def _(j):
         straight = flip_ref[j] == 0
 
-        def sums(ref, at):
-            local, cross = whole_unit(j, ref), whole_unit(at, cross_ref)
+        def sums(at):
+            local, cross = whole_unit(at, local_ref), whole_unit(at, cross_ref)
             tiles = [get_tile(cross, b) for b in range(2)]
             return [
                 get_tile(local, b) + turned(jnp.where(straight, tiles[b], tiles[1 - b]))
                 for b in range(2)
             ]
 
-        for b, tile in enumerate(sums(add_ref, 2 + j)):
+        for b, tile in enumerate(sums(2 + j)):
             int_ref[2 * j + b] = tile
-        for b, tile in enumerate(sums(amp_ref, j)):
+        for b, tile in enumerate(sums(j)):
             both = tile.astype(BF)
             for q in range(NQ):
                 half_ref[2 * j + b, :, q * W : (q + 1) * W] = jnp.dot(
@@ -196,19 +203,19 @@
                 ).astype(BF)
 
 
-def first_half(flip, slab, amp, add, cross):
+def first_half(flip, slab, local, cross):
     return pl.pallas_call(
         half_kernel,
         out_shape=(pltpu.VMEM((4, W, DEEP), BF), pltpu.VMEM((4, W, W), F32)),
-        in_specs=[SCALARS] + [WHOLE] * 4,
+        in_specs=[SCALARS] + [WHOLE] * 3,
         out_specs=[WHOLE, WHOLE],
         compiler_params=params(),
         cost_estimate=cost(8 * NQ * W**3, 4_000_000),
-    )(flip, slab, amp, add, cross)
+    )(flip, slab, local, cross)
 
 
 def ladder_kernel(source_ref, core_ref, half_ref, int_ref, *refs):
-    full, (near, near_x, far, far_x), (out_ref, low_ref, high_ref, table_ref, unit, sums) = (
+    full, (near, near_x, far, far_x), (out_ref, table_ref, unit, sums) = (
         refs[:6], refs[6:10], refs[10:]
     )
     even = core_ref[0] == 0
@@ -252,9 +259,7 @@
         for b in range(2):
             put_tile(unit, b, int_ref[2 * j + b] + sums[2 * j + b])
         for i in range(4):
-            piece = unit[i * PIECE : (i + 1) * PIECE, :].astype(BF)
-            out_ref[i, j] = piece
-            (low_ref if i < 2 else high_ref)[i % 2, j] = piece
+            out_ref[i, j] = unit[i * PIECE : (i + 1) * PIECE, :].astype(BF)
 
 
 def symmetric_units(source, core, half_done, integrals, full, parts):
@@ -262,12 +267,10 @@
         ladder_kernel,
         out_shape=(
             jax.ShapeDtypeStruct((4, 2, PIECE, 128), BF),
-            jax.ShapeDtypeStruct((2, 2, PIECE, 128), BF),
-            jax.ShapeDtypeStruct((2, 2, PIECE, 128), BF),
             jax.ShapeDtypeStruct((8, TALL - W, W), F32),
         ),
         in_specs=[SCALARS, SCALARS] + [WHOLE] * 12,
-        out_specs=[WHOLE] * 4,
+        out_specs=[WHOLE] * 2,
         scratch_shapes=[pltpu.VMEM((UNIT, 128), F32), pltpu.VMEM((4, W, W), F32)],
         compiler_params=params(),
         cost_estimate=cost(8 * NQ * W**3, 3_000_000),
@@ -276,7 +279,7 @@
 
 def update_kernel(
     kept_ref, at_ref, flip_ref, source_ref, pair_ref,
-    amp_ref, cross_ref, low_ref, high_ref, table_ref, near_ref, out_ref
+    amp_ref, cross_ref, mirror_ref, table_ref, near_ref, out_ref
 ):
     p = pl.program_id(0)
 
@@ -296,12 +299,12 @@
 
     @pl.when(kept_ref[p] == 0)
     def _():
-        unit = whole_unit(0, low_ref, high_ref)
+        unit = whole_unit(0, mirror_ref)
         for b in range(2):
             finish(b, get_tile(unit, b))
 
 
-def update(kept, at, flip, source, pair_energy, amplitudes, cross, low, high, table, near):
+def update(kept, at, flip, source, pair_energy, amplitudes, cross, mirror, table, near):
     pairs = amplitudes.shape[0]
     pick = lambda p, k, a, f, s, e: (0, a[p], 0, 0)
     here = lambda p, k, a, f, s, e: (p, 0, 0, 0)
@@ -315,15 +318,14 @@
             in_specs=[
                 pl.BlockSpec((1, 2, W, W), here),
                 pl.BlockSpec((4, 1, PIECE, 128), pick),
-                pl.BlockSpec((2, 1, PIECE, 128), pick),
-                pl.BlockSpec((2, 1, PIECE, 128), pick),
+                pl.BlockSpec((4, 1, PIECE, 128), pick),
                 pl.BlockSpec((8, TALL - W, W), fixed),
                 pl.BlockSpec((2, W, 1), fixed),
             ],
             out_specs=pl.BlockSpec((1, 2, W, W), here),
         ),
         compiler_params=params("arbitrary"),
-    )(kept, at, flip, source, pair_energy, amplitudes, cross, low, high, table, near)
+    )(kept, at, flip, source, pair_energy, amplitudes, cross, mirror, table, near)
 
 
 def on_device(
@@ -350,11 +352,9 @@
 
     keep, send = among(slots, upper), among(slots, 1 - upper)
 
-    one = pack_slab(slab, virt_energy, parity[None])
-    y_one = along_y(one)
-    sent_amp, sent_int = pack_tiles(send, amp, ints, 2)
-    local_amp = to_mirror(sent_amp)
-    scattered = exchange(pack_tiles(keep, amp, ints, 1)[0])
+    sent = pack_tiles(send, amp, ints, 1)[0]
+    local = to_mirror(sent)
+    ready = pair_list[0, 0] >= 0
 
     irrep = jnp.bitwise_xor(occ_irrep[pair_list[:, 0]], occ_irrep[pair_list[:, 1]])
     step, flip = jnp.right_shift(irrep, 1), jnp.bitwise_and(irrep, 1)
@@ -369,27 +369,29 @@
         start = jnp.where(apart == 0, 0, jnp.where(apart == 2, 6, side))
         return (start + second).reshape(-1)
 
-    y_one, local_amp, scattered, sent_int = together(y_one, local_amp, scattered, sent_int)
-    x_one = along_x(y_one)
-    y_far = along_y(lax.dynamic_slice(y_one, (0, core * (DEEP - PART)), (TALL, PART)))
-    local_int = to_mirror(sent_int)
-    cross = exchange(reorder(scattered, jnp.concatenate([keep_step, keep_step])))
-    swapped = swap_cores(y_one)
+    def bring(slab, virt_energy, amp, ints):
+        one = pack_slab(slab, virt_energy, parity[None])
+        y_one = along_y(one)
+        scattered = exchange(pack_tiles(keep, amp, ints, 1)[0])
+        x_one = along_x(y_one)
+        y_far = along_y(lax.dynamic_slice(y_one, (0, core * (DEEP - PART)), (TALL, PART)))
+        cross = exchange(reorder(scattered, jnp.concatenate([keep_step, keep_step])))
+        return one, y_one, x_one, y_far, along_x(y_far), cross
+
+    one, y_one, x_one, y_far, x_far, cross = as_unit(ready, bring, slab, virt_energy, amp, ints)
+    y_one, x_one, y_far, x_far, cross, local = together(y_one, x_one, y_far, x_far, cross, local)
     two = pack_slab(slab, virt_energy, 1 - parity[None])
-    x_far = along_x(y_far)
-    x_one, local_int, two, cross = together(x_one, local_int, two, cross)
-    full = (one, two, y_one, x_one, swapped, swap_cores(x_one))
+    full = (one, two, y_one, x_one, swap_cores(y_one), swap_cores(x_one))
     parts = (y_far, x_far, swap_cores(y_far), swap_cores(x_far))
 
-    half_done, both_ints = first_half(keep_flip, slab, local_amp, local_int, cross)
-    result, low, high, table = symmetric_units(
+    half_done, both_ints = first_half(keep_flip, slab, local, cross)
+    result, table = symmetric_units(
         sources(keep_step, keep_flip), core[None], half_done, both_ints, full, parts
     )
-    low, scattered = together(to_mirror(low), exchange(result))
-    crossed = exchange(reorder(scattered, keep_step))
-    high = to_mirror(high)
+    mirrored = to_mirror(result)
+    crossed = as_unit(ready, lambda x: exchange(reorder(exchange(x), keep_step)), result)
     new = update(
-        kept, at, flip, sources(step, flip), pair_energy, amp, crossed, low, high, table, near
+        kept, at, flip, sources(step, flip), pair_energy, amp, crossed, mirrored, table, near
     )
     return new.reshape(amplitudes.shape)
 

time: 171 us -> 152 us (0.89)
  the two profiles are of different devices: /device:TPU:72 before, /device:TPU:80 now
where the time goes in v5:
time: 152 us; the launch traced here: 151 us
  starting transfers between devices  53.8 us (35%)
  waiting for transfers between devices  51.4 us (34%)
  Pallas kernels  22 us (14%)
  blocking collectives  12.9 us (8%)
  local copies, waits for them, and re-layouts  9.15 us (6%)
    ppermute x10, waiting for transfers between devices, permute(): return lax.ppermute(value, ('pair', 'virt'), pairs)  44.2 us
    ppermute x10, starting transfers between devices, permute(): return lax.ppermute(value, ('pair', 'virt'), pairs)  38.4 us
    all_to_all x3, starting transfers between devices, exchange(): return lax.all_to_all(units, 'virt', 0, 0, tiled=True)  15.4 us
    all_to_all x1, blocking collectives, exchange(): return lax.all_to_all(units, 'virt', 0, 0, tiled=True)  12.9 us
    all_to_all x3, waiting for transfers between devices, exchange(): return lax.all_to_all(units, 'virt', 0, 0, tiled=True)  7.14 us
    pallas_call x1, Pallas kernels, symmetric_units(): pl.pallas_call(ladder_kernel, out_shape=(jax.ShapeDtypeStruct((4, 2, PIEC...  6.21 us
    pallas_call x1, Pallas kernels, first_half(): pl.pallas_call(half_kernel, out_shape=(pltpu.VMEM((4, W, DEEP), BF), pltp...  4.97 us
    pallas_call x2, Pallas kernels, pack_slab(): pl.pallas_call(pack_kernel, out_shape=jax.ShapeDtypeStruct((TALL, DEEP),...  4.02 us
  transfers between devices with their start and end apart: 13, of which 5 were waited for; matrix products, arithmetic and copies ran while one was open for 4% of the time, Pallas kernels for 7%

profile of v5, /device:TPU:80, one launch (start us, length us, event | category | flops | bytes accessed | tf_op | source)
XLA Modules:
  0.0 151.2 jit_solution(6959386699052461014)
XLA Ops:
  0.0 0.8 fusion.8
  0.8 0.6 gather_fusion.2
  1.4 0.6 gather_fusion.3
  2.1 0.1 select_reduce_fusion.3
  2.2 1.9 %shard_map.82 = bf16[4,4,160,128]{3,2,1,0:T(8,128)(2,1)S(1)} custom-call(s32[2]{0:T(128)S(1)} %get-tuple-element.88.pick_ref, bf16[4,2,200,200]{3,2,1,0:T(8,128)(2,1)S(1)} %bitcast.21, bf16[4,2,200,200]{3,2,1,0:T(8,128)(2,1)} %bitcast.24), custom_call_target="tpu_custom_call" | custom-call | bytes 1500000 | tf_op jit(solution)/shard_map/pallas_call | solution.py:168
  4.1 14.9 %collective-permute-start.4 = (bf16[4,4,160,128]{3,2,1,0:T(8,128)(2,1)S(1)}, bf16[4,4,160,128]{3,2,1,0:T(8,128)(2,1)S(1)}, u32[]{:S(2)}, u32[]{:S(2)}) collective-permute-start(bf16[4,4,160,128]{3,2,1,0:T(8,128)(2,1)S(1)} %shard_map.82), channel_id=1, source_target_pairs={{0,384},{4,388},{8,392},{12,396},{16,400},{20,404},{24,408},{28,41... | collective-permute-start | bytes 1966088 | tf_op jit(solution)/shard_map/ppermute | solution.py:33
  19.0 0.5 slice.13
  20.2 72.2 %conditional.2 = (bf16[208,3200]{1,0:T(8,128)(2,1)S(1)}, bf16[208,3200]{1,0:T(8,128)(2,1)}, bf16[208,3200]{1,0:T(8,128)(2,1)}, bf16[208,1664]{1,0:T(8,128)(2,1)}...) conditional(s32[]{:T(128)} %bitcast.6, () %tuple.21, (s32[]{:T(128)}, ...), branch_computations={%region_2.3_spmd, %region_3.5_spmd} | conditional | flops 166 | bytes 40525132 | solution.py:70
  20.2 0.0 copy-start.9
  20.2 2.0 %branch_1_fun.2 = bf16[208,3200]{1,0:T(8,128)(2,1)S(1)} custom-call(s32[1]{0:T(128)} %bitcast.order_ref, bf16[16,2,200,200]{3,2,1,0:T(8,128)(2,1)} %get-tuple-element.36.slab_ref, bf16[400]{0:T(512)(128)(2,1)S(1)} %get-tuple-element.37.energy_ref), custom_call_target="tpu_custom_call" | custom-call | bytes 3000000 | tf_op jit(solution)/shard_map/cond/branch_1_fun/pallas_call | solution.py:100
  22.2 3.5 %collective-permute-start = (bf16[208,3200]{1,0:T(8,128)(2,1)S(1)}, bf16[208,3200]{1,0:T(8,128)(2,1)}, u32[]{:S(2)}, u32[]{:S(2)}) collective-permute-start(bf16[208,3200]{1,0:T(8,128)(2,1)S(1)} %branch_1_fun.2), channel_id=1, source_target_pairs={{0,1},{4,39},{8,9},{12,47},{16,17},{20,55},{24,25},{28,63},{1,2},{... | collective-permute-start | bytes 3993608 | tf_op jit(solution)/shard_map/cond/branch_1_fun/ppermute | solution.py:33
  25.7 1.8 %branch_1_fun.3 = bf16[4,4,160,128]{3,2,1,0:T(8,128)(2,1)} custom-call(s32[2]{0:T(128)S(1)} %select_reduce_fusion.pick_ref, bf16[4,2,200,200]{3,2,1,0:T(8,128)(2,1)S(1)} %get-tuple-element.41.amp_ref, bf16[4,2,200,200]{3,2,1,0:T(8,128)(2,1)S(1)} %copy-done.9), custom_call_target="tpu_custom_call" | custom-call | bytes 1500000 | tf_op jit(solution)/shard_map/cond/branch_1_fun/pallas_call | solution.py:168
  27.5 6.4 %all-to-all-start = ((bf16[4,4,160,128]{3,2,1,0:T(8,128)(2,1)}), bf16[4,4,160,128]{3,2,1,0:T(8,128)(2,1)S(1)}, u32[]{:S(2)}, u32[]{:S(2)}) async-start(bf16[4,4,160,128]{3,2,1,0:T(8,128)(2,1)} %branch_1_fun.3), calls=%async_computation | async-start | bytes 1310720 | tf_op jit(solution)/shard_map/cond/branch_1_fun/all_to_all | solution.py:54
  33.9 18.7 %collective-permute-done = bf16[208,3200]{1,0:T(8,128)(2,1)} collective-permute-done((bf16[208,3200]{1,0:T(8,128)(2,1)S(1)}, bf16[208,3200]{1,0:T(8,128)(2,1)}, u32[]{:S(2)}, u32[]{:S(2)}) %collective-permute-start) | collective-permute-done | bytes 1331232 | tf_op jit(solution)/shard_map/cond/branch_1_fun/ppermute | solution.py:33
  52.5 2.0 %constant_dynamic-slice_fusion = bf16[208,1664]{1,0:T(8,128)(2,1)} fusion(bf16[208,3200]{1,0:T(8,128)(2,1)} %collective-permute-done, s32[]{:T(128)S(6)} %select_n.92), kind=kLoop, calls=%fused_computation.12 | loop fusion | bytes 1384452 | tf_op jit(solution)/shard_map/cond/branch_1_fun/dynamic_slice | solution.py:377
  54.5 2.0 %collective-permute-start.2 = (bf16[208,1664]{1,0:T(8,128)(2,1)}, bf16[208,1664]{1,0:T(8,128)(2,1)}, u32[]{:S(2)}, u32[]{:S(2)}) collective-permute-start(bf16[208,1664]{1,0:T(8,128)(2,1)} %constant_dynamic-slice_fusion), channel_id=1, source_target_pairs={{0,1},{4,39},{8,9},{12,47},{16,17},{20,55},{24,25},{28,63},{1,2},{... | collective-permute-start | bytes 2076680 | tf_op jit(solution)/shard_map/cond/branch_1_fun/ppermute | solution.py:33
  56.6 3.4 %collective-permute-start.1 = (bf16[208,3200]{1,0:T(8,128)(2,1)}, bf16[208,3200]{1,0:T(8,128)(2,1)}, u32[]{:S(2)}, u32[]{:S(2)}) collective-permute-start(bf16[208,3200]{1,0:T(8,128)(2,1)} %collective-permute-done), channel_id=1, source_target_pairs={{0,8},{4,28},{8,16},{12,4},{16,24},{20,12},{24,0},{28,20},{1,9},{5... | collective-permute-start | bytes 3993608 | tf_op jit(solution)/shard_map/cond/branch_1_fun/ppermute | solution.py:33
  60.0 0.1 pad_add_fusion
  60.1 0.1 reshape.189
  60.2 1.5 gather_fusion
  61.7 4.7 %all-to-all-start.1 = ((bf16[4,4,160,128]{3,2,1,0:T(8,128)(2,1)}), bf16[4,4,160,128]{3,2,1,0:T(8,128)(2,1)}, u32[]{:S(2)}, u32[]{:S(2)}) async-start(bf16[4,4,160,128]{3,2,1,0:T(8,128)(2,1)} %bitcast.26), calls=%async_computation.1 | async-start | bytes 1310720 | tf_op jit(solution)/shard_map/cond/branch_1_fun/all_to_all | solution.py:54
  66.4 11.3 %collective-permute-done.2 = bf16[208,1664]{1,0:T(8,128)(2,1)} collective-permute-done((bf16[208,1664]{1,0:T(8,128)(2,1)}, bf16[208,1664]{1,0:T(8,128)(2,1)}, u32[]{:S(2)}, u32[]{:S(2)}) %collective-permute-start.2) | collective-permute-done | bytes 692256 | tf_op jit(solution)/shard_map/cond/branch_1_fun/ppermute | solution.py:33
  77.7 4.0 %collective-permute-start.3 = (bf16[208,1664]{1,0:T(8,128)(2,1)}, bf16[208,1664]{1,0:T(8,128)(2,1)}, u32[]{:S(2)}, u32[]{:S(2)}) collective-permute-start(bf16[208,1664]{1,0:T(8,128)(2,1)} %collective-permute-done.2), channel_id=1, source_target_pairs={{0,8},{4,28},{8,16},{12,4},{16,24},{20,12},{24,0},{28,20},{1,9},{5... | collective-permute-start | bytes 2076680 | tf_op jit(solution)/shard_map/cond/branch_1_fun/ppermute | solution.py:33
  81.8 10.5 %collective-permute-done.3 = bf16[208,1664]{1,0:T(8,128)(2,1)} collective-permute-done((bf16[208,1664]{1,0:T(8,128)(2,1)}, bf16[208,1664]{1,0:T(8,128)(2,1)}, u32[]{:S(2)}, u32[]{:S(2)}) %collective-permute-start.3) | collective-permute-done | bytes 692256 | tf_op jit(solution)/shard_map/cond/branch_1_fun/ppermute | solution.py:33
  92.4 0.8 copy-done.3
  93.2 1.9 %collective-permute-start.5 = (bf16[208,3200]{1,0:T(8,128)(2,1)}, bf16[208,3200]{1,0:T(8,128)(2,1)S(1)}, u32[]{:S(2)}, u32[]{:S(2)}) collective-permute-start(bf16[208,3200]{1,0:T(8,128)(2,1)} %get-tuple-element.72.refs_2_), channel_id=1, source_target_pairs={{0,4},{4,0},{8,12},{12,8},{16,20},{20,16},{24,28},{28,24},{1,5},{5... | collective-permute-start | bytes 3993608 | tf_op jit(solution)/shard_map/ppermute | solution.py:33
  95.1 2.4 %collective-permute-start.6 = (bf16[208,3200]{1,0:T(8,128)(2,1)}, bf16[208,3200]{1,0:T(8,128)(2,1)}, u32[]{:S(2)}, u32[]{:S(2)}) collective-permute-start(bf16[208,3200]{1,0:T(8,128)(2,1)} %get-tuple-element.73.refs_3_), channel_id=1, source_target_pairs={{0,4},{4,0},{8,12},{12,8},{16,20},{20,16},{24,28},{28,24},{1,5},{5... | collective-permute-start | bytes 3993608 | tf_op jit(solution)/shard_map/ppermute | solution.py:33
  97.5 1.9 %collective-permute-start.7 = (bf16[208,1664]{1,0:T(8,128)(2,1)}, bf16[208,1664]{1,0:T(8,128)(2,1)S(1)}, u32[]{:S(2)}, u32[]{:S(2)}) collective-permute-start(bf16[208,1664]{1,0:T(8,128)(2,1)} %get-tuple-element.74.refs_6_), channel_id=1, source_target_pairs={{0,4},{4,0},{8,12},{12,8},{16,20},{20,16},{24,28},{28,24},{1,5},{5... | collective-permute-start | bytes 2076680 | tf_op jit(solution)/shard_map/ppermute | solution.py:33
  99.5 2.4 %collective-permute-start.8 = (bf16[208,1664]{1,0:T(8,128)(2,1)}, bf16[208,1664]{1,0:T(8,128)(2,1)}, u32[]{:S(2)}, u32[]{:S(2)}) collective-permute-start(bf16[208,1664]{1,0:T(8,128)(2,1)} %get-tuple-element.75.refs_7_), channel_id=1, source_target_pairs={{0,4},{4,0},{8,12},{12,8},{16,20},{20,16},{24,28},{28,24},{1,5},{5... | collective-permute-start | bytes 2076680 | tf_op jit(solution)/shard_map/ppermute | solution.py:33
  101.9 0.1 fusion.6
  102.0 0.1 add.98.source_ref
  102.1 2.0 %shard_map.84.refs_1_ = bf16[208,3200]{1,0:T(8,128)(2,1)S(1)} custom-call(s32[1]{0:T(128)} %bitcast.10.order_ref, bf16[16,2,200,200]{3,2,1,0:T(8,128)(2,1)} %bitcast.19, bf16[400]{0:T(512)(128)(2,1)S(1)} %copy-done.10), custom_call_target="tpu_custom_call" | custom-call | bytes 3000000 | tf_op jit(solution)/shard_map/pallas_call | solution.py:100
  104.1 0.6 copy-done.6
  104.7 5.0 %shard_map.83 = (bf16[4,200,3200]{2,1,0:T(8,128)(2,1)S(1)}, f32[4,200,200]{2,1,0:T(8,128)S(1)}) custom-call(s32[2]{0:T(128)S(1)} %get-tuple-element.79.flip_ref, bf16[16,2,200,200]{3,2,1,0:T(8,128)(2,1)S(1)} %bitcast.20, bf16[4,4,160,128]{3,2,1,0:T(8,128)(2,1)S(1)} %copy-done.4, bf16[4,4,160,128]{3,2,1,0:T(8,128)(2,1)} %get-tuple-element.68.cross_ref), custom_call_target="tpu_custom_call" | custom-call | flops 1024000000 | bytes 4000000 | tf_op jit(solution)/shard_map/pallas_call | solution.py:207
  109.7 6.2 %shard_map.85 = (bf16[4,2,160,128]{3,2,1,0:T(8,128)(2,1)}, f32[8,8,200]{2,1,0:T(8,128)S(1)}) custom-call(s32[4]{0:T(128)S(1)} %add.98.source_ref, s32[1]{0:T(128)} %bitcast.7.core_ref, bf16[4,200,3200]{2,1,0:T(8,128)(2,1)S(1)} %get-tuple-element.69.half_ref, f32[4,200,200]{2,1,0:T(8,128)S(1)} %get-tuple-element.70.int_ref, ...), custom_call_target="tpu_custom_call" | custom-call | flops 1024000000 | bytes 3000000 | tf_op jit(solution)/shard_map/pallas_call | solution.py:266
  115.9 1.9 %collective-permute-start.9 = (bf16[4,2,160,128]{3,2,1,0:T(8,128)(2,1)}, bf16[4,2,160,128]{3,2,1,0:T(8,128)(2,1)S(1)}, u32[]{:S(2)}, u32[]{:S(2)}) collective-permute-start(bf16[4,2,160,128]{3,2,1,0:T(8,128)(2,1)} %get-tuple-element.76), channel_id=1, source_target_pairs={{0,384},{4,388},{8,392},{12,396},{16,400},{20,404},{24,408},{28,41... | collective-permute-start | bytes 983048 | tf_op jit(solution)/shard_map/ppermute | solution.py:33
  117.8 0.6 gather_fusion.4
  118.5 0.6 gather_fusion.5
  119.1 0.2 reshape.233.near_ref
  119.3 0.1 add.92.source_ref
  119.4 24.9 %conditional.3 = (bf16[4,2,160,128]{3,2,1,0:T(8,128)(2,1)S(1)}) conditional(s32[]{:T(128)} %bitcast.6, () %tuple.20, (bf16[4,2,160,128]{3,2,1,0:T(8,128)(2,1)}, s32[2]{0:T(128)S(1)}) %tuple.24), branch_computations={%region_6.7_spmd, %region_7.8_spmd} | conditional | flops 72 | bytes 2293968 | solution.py:70
  119.4 4.2 %all-to-all-start.2 = ((bf16[4,2,160,128]{3,2,1,0:T(8,128)(2,1)}), bf16[4,2,160,128]{3,2,1,0:T(8,128)(2,1)S(1)}, u32[]{:S(2)}, u32[]{:S(2)}) async-start(bf16[4,2,160,128]{3,2,1,0:T(8,128)(2,1)} %get-tuple-element.44), calls=%async_computation.2 | async-start | bytes 655360 | tf_op jit(solution)/shard_map/cond/branch_1_fun/all_to_all | solution.py:54
  123.7 0.1 reshape.195
  123.7 7.1 %all-to-all-done.2 = bf16[4,2,160,128]{3,2,1,0:T(8,128)(2,1)S(1)} async-done(((bf16[4,2,160,128]{3,2,1,0:T(8,128)(2,1)}), bf16[4,2,160,128]{3,2,1,0:T(8,128)(2,1)S(1)}, u32[]{:S(2)}, u32[]{:S(2)}) %all-to-all-start.2) | async-done | bytes 327712 | tf_op jit(solution)/shard_map/cond/branch_1_fun/all_to_all | solution.py:54
  130.9 0.6 gather_fusion.1
  131.5 12.9 %all_to_all.16 = bf16[4,2,160,128]{3,2,1,0:T(8,128)(2,1)S(1)} all-to-all(bf16[4,2,160,128]{3,2,1,0:T(8,128)(2,1)S(1)} %bitcast.27), channel_id=1, replica_groups=mesh['pair'=192,'virt'=4] {'virt'}, dimensions={0} | all-to-all | bytes 655360 | tf_op jit(solution)/shard_map/cond/branch_1_fun/all_to_all | solution.py:54
  144.4 3.7 %collective-permute-done.9.mirror_ref = bf16[4,2,160,128]{3,2,1,0:T(8,128)(2,1)S(1)} collective-permute-done((bf16[4,2,160,128]{3,2,1,0:T(8,128)(2,1)}, bf16[4,2,160,128]{3,2,1,0:T(8,128)(2,1)S(1)}, u32[]{:S(2)}, u32[]{:S(2)}) %collective-permute-start.9) | collective-permute-done | bytes 327712 | tf_op jit(solution)/shard_map/ppermute | solution.py:33
  148.0 3.2 %shard_map.86 = bf16[4,2,200,200]{3,2,1,0:T(8,128)(2,1)} custom-call(s32[4]{0:T(128)S(1)} %compare_convert_fusion.1.kept_ref, s32[4]{0:T(128)S(1)} %get-tuple-element.83.at_ref, s32[4]{0:T(128)S(1)} %get-tuple-element.85.flip_ref, s32[8]{0:T(128)S(1)} %add.92.source_ref, f32[4]{0:T(128)S(1)} %add.93.pair_ref, bf16[4,2,200,200]{3,2,1,0:T(8,128)(2,1)S(1)} %bitcast.23, ...), custom_call_target="tpu_custom_call" | custom-call | tf_op jit(solution)/shard_map/pallas_call | solution.py:312
  (40 shorter events, 0.2 us)
Async XLA Ops:
  0.0 0.8 copy-start
  0.0 2.2 %copy-start.7 = (bf16[4,400,200]{2,1,0:T(8,128)(2,1)S(1)}, bf16[4,400,200]{2,1,0:T(8,128)(2,1)}, u32[]{:S(2)}) copy-start(bf16[4,400,200]{2,1,0:T(8,128)(2,1)} %param.12) | copy-start | bytes 1920004
  1.4 17.5 %copy-start.11 = (s32[4,2]{0,1:T(2,128)S(1)}, s32[4,2]{0,1:T(2,128)}, u32[]{:S(2)}) copy-start(s32[4,2]{0,1:T(2,128)} %param.15) | copy-start | bytes 100
  1.4 18.7 %copy-start.10 = (bf16[400]{0:T(512)(128)(2,1)S(1)}, bf16[400]{0:T(512)(128)(2,1)}, u32[]{:S(2)}) copy-start(bf16[400]{0:T(512)(128)(2,1)} %energy_ref.1) | copy-start | bytes 2404
  4.1 88.3 %collective-permute-start.4 = (bf16[4,4,160,128]{3,2,1,0:T(8,128)(2,1)S(1)}, bf16[4,4,160,128]{3,2,1,0:T(8,128)(2,1)S(1)}, u32[]{:S(2)}, u32[]{:S(2)}) collective-permute-start(bf16[4,4,160,128]{3,2,1,0:T(8,128)(2,1)S(1)} %shard_map.82), channel_id=1, source_target_pairs={{0,384},{4,388},{8,392},{12,396},{16,400},{20,404},{24,408},{28,41... | collective-permute-start | bytes 1966088 | tf_op jit(solution)/shard_map/ppermute | solution.py:33
  20.2 5.5 %copy-start.9 = (bf16[4,2,200,200]{3,2,1,0:T(8,128)(2,1)S(1)}, bf16[4,2,200,200]{3,2,1,0:T(8,128)(2,1)}, u32[]{:S(2)}) copy-start(bf16[4,2,200,200]{3,2,1,0:T(8,128)(2,1)} %get-tuple-element.42.int_ref) | copy-start | bytes 1920004 | tf_op jit(solution)/shard_map/cond
  22.2 5.3 %copy-start.1 = (bf16[208,3200]{1,0:T(8,128)(2,1)}, bf16[208,3200]{1,0:T(8,128)(2,1)S(1)}, u32[]{:S(2)}) copy-start(bf16[208,3200]{1,0:T(8,128)(2,1)S(1)} %branch_1_fun.2) | copy-start | bytes 3993604 | tf_op jit(solution)/shard_map/cond
  22.2 30.4 %collective-permute-start = (bf16[208,3200]{1,0:T(8,128)(2,1)S(1)}, bf16[208,3200]{1,0:T(8,128)(2,1)}, u32[]{:S(2)}, u32[]{:S(2)}) collective-permute-start(bf16[208,3200]{1,0:T(8,128)(2,1)S(1)} %branch_1_fun.2), channel_id=1, source_target_pairs={{0,1},{4,39},{8,9},{12,47},{16,17},{20,55},{24,25},{28,63},{1,2},{... | collective-permute-start | bytes 3993608 | tf_op jit(solution)/shard_map/cond/branch_1_fun/ppermute | solution.py:33
  27.5 32.7 %all-to-all-start = ((bf16[4,4,160,128]{3,2,1,0:T(8,128)(2,1)}), bf16[4,4,160,128]{3,2,1,0:T(8,128)(2,1)S(1)}, u32[]{:S(2)}, u32[]{:S(2)}) async-start(bf16[4,4,160,128]{3,2,1,0:T(8,128)(2,1)} %branch_1_fun.3), calls=%async_computation | async-start | bytes 1310720 | tf_op jit(solution)/shard_map/cond/branch_1_fun/all_to_all | solution.py:54
  54.5 37.8 %copy-start.2 = (bf16[208,3200]{1,0:T(8,128)(2,1)S(1)}, bf16[208,3200]{1,0:T(8,128)(2,1)}, u32[]{:S(2)}) copy-start(bf16[208,3200]{1,0:T(8,128)(2,1)} %copy-done.1) | copy-start | bytes 3993604 | tf_op jit(solution)/shard_map/cond
  54.5 23.2 %collective-permute-start.2 = (bf16[208,1664]{1,0:T(8,128)(2,1)}, bf16[208,1664]{1,0:T(8,128)(2,1)}, u32[]{:S(2)}, u32[]{:S(2)}) collective-permute-start(bf16[208,1664]{1,0:T(8,128)(2,1)} %constant_dynamic-slice_fusion), channel_id=1, source_target_pairs={{0,1},{4,39},{8,9},{12,47},{16,17},{20,55},{24,25},{28,63},{1,2},{... | collective-permute-start | bytes 2076680 | tf_op jit(solution)/shard_map/cond/branch_1_fun/ppermute | solution.py:33
  56.6 25.2 %collective-permute-start.1 = (bf16[208,3200]{1,0:T(8,128)(2,1)}, bf16[208,3200]{1,0:T(8,128)(2,1)}, u32[]{:S(2)}, u32[]{:S(2)}) collective-permute-start(bf16[208,3200]{1,0:T(8,128)(2,1)} %collective-permute-done), channel_id=1, source_target_pairs={{0,8},{4,28},{8,16},{12,4},{16,24},{20,12},{24,0},{28,20},{1,9},{5... | collective-permute-start | bytes 3993608 | tf_op jit(solution)/shard_map/cond/branch_1_fun/ppermute | solution.py:33
  61.7 20.1 %all-to-all-start.1 = ((bf16[4,4,160,128]{3,2,1,0:T(8,128)(2,1)}), bf16[4,4,160,128]{3,2,1,0:T(8,128)(2,1)}, u32[]{:S(2)}, u32[]{:S(2)}) async-start(bf16[4,4,160,128]{3,2,1,0:T(8,128)(2,1)} %bitcast.26), calls=%async_computation.1 | async-start | bytes 1310720 | tf_op jit(solution)/shard_map/cond/branch_1_fun/all_to_all | solution.py:54
  77.7 14.6 %collective-permute-start.3 = (bf16[208,1664]{1,0:T(8,128)(2,1)}, bf16[208,1664]{1,0:T(8,128)(2,1)}, u32[]{:S(2)}, u32[]{:S(2)}) collective-permute-start(bf16[208,1664]{1,0:T(8,128)(2,1)} %collective-permute-done.2), channel_id=1, source_target_pairs={{0,8},{4,28},{8,16},{12,4},{16,24},{20,12},{24,0},{28,20},{1,9},{5... | collective-permute-start | bytes 2076680 | tf_op jit(solution)/shard_map/cond/branch_1_fun/ppermute | solution.py:33
  92.4 0.8 copy-start.3
  93.2 16.5 %collective-permute-start.5 = (bf16[208,3200]{1,0:T(8,128)(2,1)}, bf16[208,3200]{1,0:T(8,128)(2,1)S(1)}, u32[]{:S(2)}, u32[]{:S(2)}) collective-permute-start(bf16[208,3200]{1,0:T(8,128)(2,1)} %get-tuple-element.72.refs_2_), channel_id=1, source_target_pairs={{0,4},{4,0},{8,12},{12,8},{16,20},{20,16},{24,28},{28,24},{1,5},{5... | collective-permute-start | bytes 3993608 | tf_op jit(solution)/shard_map/ppermute | solution.py:33
  95.1 14.6 %collective-permute-start.6 = (bf16[208,3200]{1,0:T(8,128)(2,1)}, bf16[208,3200]{1,0:T(8,128)(2,1)}, u32[]{:S(2)}, u32[]{:S(2)}) collective-permute-start(bf16[208,3200]{1,0:T(8,128)(2,1)} %get-tuple-element.73.refs_3_), channel_id=1, source_target_pairs={{0,4},{4,0},{8,12},{12,8},{16,20},{20,16},{24,28},{28,24},{1,5},{5... | collective-permute-start | bytes 3993608 | tf_op jit(solution)/shard_map/ppermute | solution.py:33
  97.5 12.1 %collective-permute-start.7 = (bf16[208,1664]{1,0:T(8,128)(2,1)}, bf16[208,1664]{1,0:T(8,128)(2,1)S(1)}, u32[]{:S(2)}, u32[]{:S(2)}) collective-permute-start(bf16[208,1664]{1,0:T(8,128)(2,1)} %get-tuple-element.74.refs_6_), channel_id=1, source_target_pairs={{0,4},{4,0},{8,12},{12,8},{16,20},{20,16},{24,28},{28,24},{1,5},{5... | collective-permute-start | bytes 2076680 | tf_op jit(solution)/shard_map/ppermute | solution.py:33
  99.5 10.2 %collective-permute-start.8 = (bf16[208,1664]{1,0:T(8,128)(2,1)}, bf16[208,1664]{1,0:T(8,128)(2,1)}, u32[]{:S(2)}, u32[]{:S(2)}) collective-permute-start(bf16[208,1664]{1,0:T(8,128)(2,1)} %get-tuple-element.75.refs_7_), channel_id=1, source_target_pairs={{0,4},{4,0},{8,12},{12,8},{16,20},{20,16},{24,28},{28,24},{1,5},{5... | collective-permute-start | bytes 2076680 | tf_op jit(solution)/shard_map/ppermute | solution.py:33
  102.0 2.1 %copy-start.4 = (bf16[4,4,160,128]{3,2,1,0:T(8,128)(2,1)S(1)}, bf16[4,4,160,128]{3,2,1,0:T(8,128)(2,1)}, u32[]{:S(2)}) copy-start(bf16[4,4,160,128]{3,2,1,0:T(8,128)(2,1)} %copy-done.3) | copy-start | bytes 1966084
  102.0 2.6 %copy-start.6 = (bf16[16,400,200]{2,1,0:T(8,128)(2,1)S(1)}, bf16[16,400,200]{2,1,0:T(8,128)(2,1)}, u32[]{:S(2)}) copy-start(bf16[16,400,200]{2,1,0:T(8,128)(2,1)} %param.14) | copy-start | bytes 7680004
  109.7 8.1 %copy-start.5 = (f32[200]{0:T(256)S(1)}, f32[200]{0:T(256)}, u32[]{:S(2)}) copy-start(f32[200]{0:T(256)} %param.18) | copy-start | bytes 2404
  115.9 32.1 %collective-permute-start.9 = (bf16[4,2,160,128]{3,2,1,0:T(8,128)(2,1)}, bf16[4,2,160,128]{3,2,1,0:T(8,128)(2,1)S(1)}, u32[]{:S(2)}, u32[]{:S(2)}) collective-permute-start(bf16[4,2,160,128]{3,2,1,0:T(8,128)(2,1)} %get-tuple-element.76), channel_id=1, source_target_pairs={{0,384},{4,388},{8,392},{12,396},{16,400},{20,404},{24,408},{28,41... | collective-permute-start | bytes 983048 | tf_op jit(solution)/shard_map/ppermute | solution.py:33
  119.1 28.9 %copy-start.8 = (bf16[4,400,200]{2,1,0:T(8,128)(2,1)S(1)}, bf16[4,400,200]{2,1,0:T(8,128)(2,1)}, u32[]{:S(2)}) copy-start(bf16[4,400,200]{2,1,0:T(8,128)(2,1)} %param.12) | copy-start | bytes 1920004
  119.4 11.4 %all-to-all-start.2 = ((bf16[4,2,160,128]{3,2,1,0:T(8,128)(2,1)}), bf16[4,2,160,128]{3,2,1,0:T(8,128)(2,1)S(1)}, u32[]{:S(2)}, u32[]{:S(2)}) async-start(bf16[4,2,160,128]{3,2,1,0:T(8,128)(2,1)} %get-tuple-element.44), calls=%async_computation.2 | async-start | bytes 655360 | tf_op jit(solution)/shard_map/cond/branch_1_fun/all_to_all | solution.py:54

commit v6 on v5

--- a/solution.py
+++ b/solution.py
@@ -352,9 +352,10 @@
 
     keep, send = among(slots, upper), among(slots, 1 - upper)
 
-    sent = pack_tiles(send, amp, ints, 1)[0]
-    local = to_mirror(sent)
-    ready = pair_list[0, 0] >= 0
+    one = pack_slab(slab, virt_energy, parity[None])
+    y_one = along_y(one)
+    local = to_mirror(pack_tiles(send, amp, ints, 1)[0])
+    kept_tiles = pack_tiles(keep, amp, ints, 1)[0]
 
     irrep = jnp.bitwise_xor(occ_irrep[pair_list[:, 0]], occ_irrep[pair_list[:, 1]])
     step, flip = jnp.right_shift(irrep, 1), jnp.bitwise_and(irrep, 1)
@@ -369,29 +370,38 @@
         start = jnp.where(apart == 0, 0, jnp.where(apart == 2, 6, side))
         return (start + second).reshape(-1)
 
-    def bring(slab, virt_energy, amp, ints):
-        one = pack_slab(slab, virt_energy, parity[None])
-        y_one = along_y(one)
-        scattered = exchange(pack_tiles(keep, amp, ints, 1)[0])
+    keep_source, source = sources(keep_step, keep_flip), sources(step, flip)
+    ready = pair_list[0, 0] >= 0
+    (
+        y_one, kept_tiles, keep_step, keep_flip, pair_energy, near, keep_source, source
+    ) = together(
+        y_one, kept_tiles, keep_step, keep_flip, pair_energy, near, keep_source, source
+    )
+
+    def bring(y_one, kept_tiles, keep_step, slab, virt_energy):
+        scattered = exchange(kept_tiles)
         x_one = along_x(y_one)
         y_far = along_y(lax.dynamic_slice(y_one, (0, core * (DEEP - PART)), (TALL, PART)))
         cross = exchange(reorder(scattered, jnp.concatenate([keep_step, keep_step])))
-        return one, y_one, x_one, y_far, along_x(y_far), cross
-
-    one, y_one, x_one, y_far, x_far, cross = as_unit(ready, bring, slab, virt_energy, amp, ints)
-    y_one, x_one, y_far, x_far, cross, local = together(y_one, x_one, y_far, x_far, cross, local)
-    two = pack_slab(slab, virt_energy, 1 - parity[None])
-    full = (one, two, y_one, x_one, swap_cores(y_one), swap_cores(x_one))
-    parts = (y_far, x_far, swap_cores(y_far), swap_cores(x_far))
+        two = pack_slab(slab, virt_energy, 1 - parity[None])
+        return (
+            two, x_one, swap_cores(y_one), swap_cores(x_one),
+            y_far, along_x(y_far), swap_cores(y_far), cross,
+        )
+
+    brought = as_unit(ready, bring, y_one, kept_tiles, keep_step, slab, virt_energy)
+    two, x_one, y_swap, x_swap, y_far, x_far, y_far_swap, cross, local = together(*brought, local)
+    full = (one, two, y_one, x_one, y_swap, x_swap)
+    parts = (y_far, x_far, y_far_swap, swap_cores(x_far))
 
     half_done, both_ints = first_half(keep_flip, slab, local, cross)
     result, table = symmetric_units(
-        sources(keep_step, keep_flip), core[None], half_done, both_ints, full, parts
+        keep_source, core[None], half_done, both_ints, full, parts
     )
     mirrored = to_mirror(result)
     crossed = as_unit(ready, lambda x: exchange(reorder(exchange(x), keep_step)), result)
     new = update(
-        kept, at, flip, sources(step, flip), pair_energy, amp, crossed, mirrored, table, near
+        kept, at, flip, source, pair_energy, amp, crossed, mirrored, table, near
     )
     return new.reshape(amplitudes.shape)
 

time: 152 us -> 133 us (0.88)
  the two profiles are of different devices: /device:TPU:80 before, /device:TPU:56 now
where the time goes in v6:
time: 133 us; the launch traced here: 132 us
  starting transfers between devices  59.6 us (45%)
  waiting for transfers between devices  23.8 us (18%)
  Pallas kernels  23.3 us (18%)
  blocking collectives  12.5 us (9%)
  local copies, waits for them, and re-layouts  10.2 us (8%)
  other arithmetic  2.09 us (2%)
    ppermute x10, starting transfers between devices, permute(): return lax.ppermute(value, ('pair', 'virt'), pairs)  39.4 us
    all_to_all x3, starting transfers between devices, exchange(): return lax.all_to_all(units, 'virt', 0, 0, tiled=True)  20.1 us
    ppermute x10, waiting for transfers between devices, permute(): return lax.ppermute(value, ('pair', 'virt'), pairs)  13.2 us
    all_to_all x1, blocking collectives, exchange(): return lax.all_to_all(units, 'virt', 0, 0, tiled=True)  12.5 us
    all_to_all x3, waiting for transfers between devices, exchange(): return lax.all_to_all(units, 'virt', 0, 0, tiled=True)  10.5 us
    pallas_call x1, Pallas kernels, symmetric_units(): pl.pallas_call(ladder_kernel, out_shape=(jax.ShapeDtypeStruct((4, 2, PIEC...  6.58 us
    pallas_call x1, Pallas kernels, first_half(): pl.pallas_call(half_kernel, out_shape=(pltpu.VMEM((4, W, DEEP), BF), pltp...  6.07 us
    pallas_call x2, Pallas kernels, pack_slab(): pl.pallas_call(pack_kernel, out_shape=jax.ShapeDtypeStruct((TALL, DEEP),...  3.88 us
  transfers between devices with their start and end apart: 13, of which 4 were waited for; matrix products, arithmetic and copies ran while one was open for 9% of the time, Pallas kernels for 9%

profile of v6, /device:TPU:56, one launch (start us, length us, event | category | flops | bytes accessed | tf_op | source)
XLA Modules:
  0.0 132.4 jit_solution(3390963682538489172)
XLA Ops:
  0.0 2.0 %shard_map.82.refs_0_ = bf16[208,3200]{1,0:T(8,128)(2,1)S(1)} custom-call(s32[1]{0:T(128)} %bitcast.5.order_ref, bf16[16,2,200,200]{3,2,1,0:T(8,128)(2,1)} %bitcast.23, bf16[400]{0:T(512)(128)(2,1)} %energy_ref.1), custom_call_target="tpu_custom_call" | custom-call | bytes 3000000 | tf_op jit(solution)/shard_map/pallas_call | solution.py:100
  2.0 0.0 copy-start.1
  2.0 10.8 %collective-permute-start.6 = (bf16[208,3200]{1,0:T(8,128)(2,1)S(1)}, bf16[208,3200]{1,0:T(8,128)(2,1)}, u32[]{:S(2)}, u32[]{:S(2)}) collective-permute-start(bf16[208,3200]{1,0:T(8,128)(2,1)S(1)} %shard_map.82.refs_0_), channel_id=1, source_target_pairs={{0,1},{4,39},{8,9},{12,47},{16,17},{20,55},{24,25},{28,63},{1,2},{... | collective-permute-start | bytes 3993608 | tf_op jit(solution)/shard_map/ppermute | solution.py:33
  12.9 0.6 gather_fusion.2
  13.6 0.6 gather_fusion.3
  14.2 0.6 broadcast_and_fusion.1
  14.8 0.1 fusion.8
  14.9 1.8 %shard_map.84 = bf16[4,4,160,128]{3,2,1,0:T(8,128)(2,1)} custom-call(s32[2]{0:T(128)S(1)} %get-tuple-element.96.pick_ref, bf16[4,2,200,200]{3,2,1,0:T(8,128)(2,1)S(1)} %bitcast.18, bf16[4,2,200,200]{3,2,1,0:T(8,128)(2,1)S(1)} %bitcast.21), custom_call_target="tpu_custom_call" | custom-call | bytes 1500000 | tf_op jit(solution)/shard_map/pallas_call | solution.py:168
  16.7 6.4 %collective-permute-start.7 = (bf16[4,4,160,128]{3,2,1,0:T(8,128)(2,1)}, bf16[4,4,160,128]{3,2,1,0:T(8,128)(2,1)}, u32[]{:S(2)}, u32[]{:S(2)}) collective-permute-start(bf16[4,4,160,128]{3,2,1,0:T(8,128)(2,1)} %shard_map.84), channel_id=1, source_target_pairs={{0,384},{4,388},{8,392},{12,396},{16,400},{20,404},{24,408},{28,41... | collective-permute-start | bytes 1966088 | tf_op jit(solution)/shard_map/ppermute | solution.py:33
  23.1 0.6 gather_fusion.4
  23.8 0.6 gather_fusion.5
  24.4 0.7 reshape.188
  25.1 0.5 slice.13
  25.6 1.7 %shard_map.83 = bf16[4,4,160,128]{3,2,1,0:T(8,128)(2,1)} custom-call(s32[2]{0:T(128)S(1)} %get-tuple-element.95.pick_ref, bf16[4,2,200,200]{3,2,1,0:T(8,128)(2,1)S(1)} %bitcast.19, bf16[4,2,200,200]{3,2,1,0:T(8,128)(2,1)S(1)} %bitcast.22), custom_call_target="tpu_custom_call" | custom-call | bytes 1500000 | tf_op jit(solution)/shard_map/pallas_call | solution.py:168
  27.4 0.1 fusion.9
  27.4 0.7 add.95.source_ref
  28.1 0.6 add.98.source_ref
  29.4 0.6 add.92.pair_ref
  30.0 49.1 %conditional.2 = (bf16[208,3200]{1,0:T(8,128)(2,1)S(1)}, bf16[208,3200]{1,0:T(8,128)(2,1)}, bf16[208,3200]{1,0:T(8,128)(2,1)}, bf16[208,3200]{1,0:T(8,128)(2,1)}...) conditional(s32[]{:T(128)} %bitcast.9, () %tuple.23, ...), branch_computations={%region_3.4_spmd, %region_4.5_spmd} | conditional | flops 153 | bytes 33909204 | solution.py:70
  30.0 3.4 %collective-permute-start = (bf16[208,3200]{1,0:T(8,128)(2,1)}, bf16[208,3200]{1,0:T(8,128)(2,1)}, u32[]{:S(2)}, u32[]{:S(2)}) collective-permute-start(bf16[208,3200]{1,0:T(8,128)(2,1)} %get-tuple-element.29), channel_id=1, source_target_pairs={{0,8},{4,28},{8,16},{12,4},{16,24},{20,12},{24,0},{28,20},{1,9},{5... | collective-permute-start | bytes 3993608 | tf_op jit(solution)/shard_map/cond/branch_1_fun/ppermute | solution.py:33
  33.4 7.0 %all-to-all-start = ((bf16[4,4,160,128]{3,2,1,0:T(8,128)(2,1)}), bf16[4,4,160,128]{3,2,1,0:T(8,128)(2,1)S(1)}, u32[]{:S(2)}, u32[]{:S(2)}) async-start(bf16[4,4,160,128]{3,2,1,0:T(8,128)(2,1)} %get-tuple-element.31), calls=%async_computation | async-start | bytes 1310720 | tf_op jit(solution)/shard_map/cond/branch_1_fun/all_to_all | solution.py:54
  40.5 2.0 %constant_dynamic-slice_fusion = bf16[208,1664]{1,0:T(8,128)(2,1)} fusion(bf16[208,3200]{1,0:T(8,128)(2,1)} %get-tuple-element.29, s32[]{:T(128)S(6)} %select_n.91), kind=kLoop, calls=%fused_computation.11 | loop fusion | bytes 1384452 | tf_op jit(solution)/shard_map/cond/branch_1_fun/dynamic_slice | solution.py:384
  42.5 2.3 %collective-permute-start.3 = (bf16[208,1664]{1,0:T(8,128)(2,1)}, bf16[208,1664]{1,0:T(8,128)(2,1)}, u32[]{:S(2)}, u32[]{:S(2)}) collective-permute-start(bf16[208,1664]{1,0:T(8,128)(2,1)} %constant_dynamic-slice_fusion), channel_id=1, source_target_pairs={{0,1},{4,39},{8,9},{12,47},{16,17},{20,55},{24,25},{28,63},{1,2},{... | collective-permute-start | bytes 2076680 | tf_op jit(solution)/shard_map/cond/branch_1_fun/ppermute | solution.py:33
  44.7 1.9 %collective-permute-start.1 = (bf16[208,3200]{1,0:T(8,128)(2,1)}, bf16[208,3200]{1,0:T(8,128)(2,1)}, u32[]{:S(2)}, u32[]{:S(2)}) collective-permute-start(bf16[208,3200]{1,0:T(8,128)(2,1)} %get-tuple-element.29), channel_id=1, source_target_pairs={{0,4},{4,0},{8,12},{12,8},{16,20},{20,16},{24,28},{28,24},{1,5},{5... | collective-permute-start | bytes 3993608 | tf_op jit(solution)/shard_map/cond/branch_1_fun/ppermute | solution.py:33
  46.7 4.6 %collective-permute-done = bf16[208,3200]{1,0:T(8,128)(2,1)} collective-permute-done((bf16[208,3200]{1,0:T(8,128)(2,1)}, bf16[208,3200]{1,0:T(8,128)(2,1)}, u32[]{:S(2)}, u32[]{:S(2)}) %collective-permute-start) | collective-permute-done | bytes 1331232 | tf_op jit(solution)/shard_map/cond/branch_1_fun/ppermute | solution.py:33
  51.2 1.9 %collective-permute-start.2 = (bf16[208,3200]{1,0:T(8,128)(2,1)}, bf16[208,3200]{1,0:T(8,128)(2,1)}, u32[]{:S(2)}, u32[]{:S(2)}) collective-permute-start(bf16[208,3200]{1,0:T(8,128)(2,1)} %collective-permute-done), channel_id=1, source_target_pairs={{0,4},{4,0},{8,12},{12,8},{16,20},{20,16},{24,28},{28,24},{1,5},{5... | collective-permute-start | bytes 3993608 | tf_op jit(solution)/shard_map/cond/branch_1_fun/ppermute | solution.py:33
  53.2 0.1 pad_add_fusion
  53.3 0.1 reshape.190
  53.3 2.6 %all-to-all-done = bf16[4,4,160,128]{3,2,1,0:T(8,128)(2,1)S(1)} async-done(((bf16[4,4,160,128]{3,2,1,0:T(8,128)(2,1)}), bf16[4,4,160,128]{3,2,1,0:T(8,128)(2,1)S(1)}, u32[]{:S(2)}, u32[]{:S(2)}) %all-to-all-start) | async-done | bytes 655392 | tf_op jit(solution)/shard_map/cond/branch_1_fun/all_to_all | solution.py:54
  56.0 1.5 %gather_fusion = bf16[16,160,128]{2,1,0:T(8,128)(2,1)} fusion(bf16[4,4,160,128]{3,2,1,0:T(8,128)(2,1)S(1)} %all-to-all-done, s32[16]{0:T(128)S(1)} %reshape.190), kind=kCustom, calls=%fused_computation | custom fusion | bytes 1310848 | tf_op jit(solution)/shard_map/cond/branch_1_fun/gather | solution.py:59
  57.5 7.3 %all-to-all-start.1 = ((bf16[4,4,160,128]{3,2,1,0:T(8,128)(2,1)}), bf16[4,4,160,128]{3,2,1,0:T(8,128)(2,1)}, u32[]{:S(2)}, u32[]{:S(2)}) async-start(bf16[4,4,160,128]{3,2,1,0:T(8,128)(2,1)} %bitcast.1), calls=%async_computation.1 | async-start | bytes 1310720 | tf_op jit(solution)/shard_map/cond/branch_1_fun/all_to_all | solution.py:54
  64.7 1.9 %collective-permute-start.4 = (bf16[208,1664]{1,0:T(8,128)(2,1)}, bf16[208,1664]{1,0:T(8,128)(2,1)}, u32[]{:S(2)}, u32[]{:S(2)}) collective-permute-start(bf16[208,1664]{1,0:T(8,128)(2,1)} %collective-permute-done.3), channel_id=1, source_target_pairs={{0,8},{4,28},{8,16},{12,4},{16,24},{20,12},{24,0},{28,20},{1,9},{5... | collective-permute-start | bytes 2076680 | tf_op jit(solution)/shard_map/cond/branch_1_fun/ppermute | solution.py:33
  66.7 1.9 %collective-permute-start.5 = (bf16[208,1664]{1,0:T(8,128)(2,1)}, bf16[208,1664]{1,0:T(8,128)(2,1)}, u32[]{:S(2)}, u32[]{:S(2)}) collective-permute-start(bf16[208,1664]{1,0:T(8,128)(2,1)} %collective-permute-done.3), channel_id=1, source_target_pairs={{0,4},{4,0},{8,12},{12,8},{16,20},{20,16},{24,28},{28,24},{1,5},{5... | collective-permute-start | bytes 2076680 | tf_op jit(solution)/shard_map/cond/branch_1_fun/ppermute | solution.py:33
  68.6 1.9 %branch_1_fun.1 = bf16[208,3200]{1,0:T(8,128)(2,1)S(1)} custom-call(s32[1]{0:T(128)} %bitcast.order_ref, bf16[16,2,200,200]{3,2,1,0:T(8,128)(2,1)} %get-tuple-element.27.slab_ref, bf16[400]{0:T(512)(128)(2,1)S(1)} %get-tuple-element.28.energy_ref), custom_call_target="tpu_custom_call" | custom-call | bytes 3000000 | tf_op jit(solution)/shard_map/cond/branch_1_fun/pallas_call | solution.py:100
  70.5 8.6 %collective-permute-done.4 = bf16[208,1664]{1,0:T(8,128)(2,1)} collective-permute-done((bf16[208,1664]{1,0:T(8,128)(2,1)}, bf16[208,1664]{1,0:T(8,128)(2,1)}, u32[]{:S(2)}, u32[]{:S(2)}) %collective-permute-start.4) | collective-permute-done | bytes 692256 | tf_op jit(solution)/shard_map/cond/branch_1_fun/ppermute | solution.py:33
  79.2 1.9 %collective-permute-start.8 = (bf16[208,1664]{1,0:T(8,128)(2,1)}, bf16[208,1664]{1,0:T(8,128)(2,1)S(1)}, u32[]{:S(2)}, u32[]{:S(2)}) collective-permute-start(bf16[208,1664]{1,0:T(8,128)(2,1)} %get-tuple-element.88.refs_7_), channel_id=1, source_target_pairs={{0,4},{4,0},{8,12},{12,8},{16,20},{20,16},{24,28},{28,24},{1,5},{5... | collective-permute-start | bytes 2076680 | tf_op jit(solution)/shard_map/ppermute | solution.py:33
  81.1 6.1 %shard_map.85 = (bf16[4,200,3200]{2,1,0:T(8,128)(2,1)S(1)}, f32[4,200,200]{2,1,0:T(8,128)S(1)}) custom-call(s32[2]{0:T(128)S(1)} %get-tuple-element.67.flip_ref, bf16[16,2,200,200]{3,2,1,0:T(8,128)(2,1)} %bitcast.25, bf16[4,4,160,128]{3,2,1,0:T(8,128)(2,1)} %collective-permute-done.7.local_ref, bf16[4,4,160,128]{3,2,1,0:T(8,128)(2,1)} %get-tuple-element.80.cross_ref), custom_call_target="tpu_custom_call" | custom-call | flops 1024000000 | bytes 4000000 | tf_op jit(solution)/shard_map/pallas_call | solution.py:207
  87.2 6.6 %shard_map.86 = (bf16[4,2,160,128]{3,2,1,0:T(8,128)(2,1)}, f32[8,8,200]{2,1,0:T(8,128)S(1)}) custom-call(s32[4]{0:T(128)S(1)} %copy-done.5, s32[1]{0:T(128)} %bitcast.10.core_ref, bf16[4,200,3200]{2,1,0:T(8,128)(2,1)S(1)} %get-tuple-element.81.half_ref, f32[4,200,200]{2,1,0:T(8,128)S(1)} %get-tuple-element.82.int_ref, ...), custom_call_target="tpu_custom_call" | custom-call | flops 1024000000 | bytes 3000000 | tf_op jit(solution)/shard_map/pallas_call | solution.py:266
  93.8 7.0 %collective-permute-start.9 = (bf16[4,2,160,128]{3,2,1,0:T(8,128)(2,1)}, bf16[4,2,160,128]{3,2,1,0:T(8,128)(2,1)S(1)}, u32[]{:S(2)}, u32[]{:S(2)}) collective-permute-start(bf16[4,2,160,128]{3,2,1,0:T(8,128)(2,1)} %get-tuple-element.90), channel_id=1, source_target_pairs={{0,384},{4,388},{8,392},{12,396},{16,400},{20,404},{24,408},{28,41... | collective-permute-start | bytes 983048 | tf_op jit(solution)/shard_map/ppermute | solution.py:33
  100.8 0.8 copy.9.near_ref
  101.6 27.5 %conditional.3 = (bf16[4,2,160,128]{3,2,1,0:T(8,128)(2,1)S(1)}) conditional(s32[]{:T(128)} %bitcast.9, () %tuple.22, (bf16[4,2,160,128]{3,2,1,0:T(8,128)(2,1)}, s32[2]{0:T(128)}) %tuple.43), branch_computations={%region_6.7_spmd, %region_7.8_spmd} | conditional | flops 72 | bytes 2293968 | solution.py:70
  101.7 5.8 %all-to-all-start.2 = ((bf16[4,2,160,128]{3,2,1,0:T(8,128)(2,1)}), bf16[4,2,160,128]{3,2,1,0:T(8,128)(2,1)S(1)}, u32[]{:S(2)}, u32[]{:S(2)}) async-start(bf16[4,2,160,128]{3,2,1,0:T(8,128)(2,1)} %get-tuple-element.33), calls=%async_computation.2 | async-start | bytes 655360 | tf_op jit(solution)/shard_map/cond/branch_1_fun/all_to_all | solution.py:54
  107.5 0.6 fusion.5
  108.1 0.1 reshape.196
  108.2 7.9 %all-to-all-done.2 = bf16[4,2,160,128]{3,2,1,0:T(8,128)(2,1)S(1)} async-done(((bf16[4,2,160,128]{3,2,1,0:T(8,128)(2,1)}), bf16[4,2,160,128]{3,2,1,0:T(8,128)(2,1)S(1)}, u32[]{:S(2)}, u32[]{:S(2)}) %all-to-all-start.2) | async-done | bytes 327712 | tf_op jit(solution)/shard_map/cond/branch_1_fun/all_to_all | solution.py:54
  116.1 0.6 gather_fusion.1
  116.7 12.5 %all_to_all.16 = bf16[4,2,160,128]{3,2,1,0:T(8,128)(2,1)S(1)} all-to-all(bf16[4,2,160,128]{3,2,1,0:T(8,128)(2,1)S(1)} %bitcast.26), channel_id=1, replica_groups=mesh['pair'=192,'virt'=4] {'virt'}, dimensions={0} | all-to-all | bytes 655360 | tf_op jit(solution)/shard_map/cond/branch_1_fun/all_to_all | solution.py:54
  129.2 3.2 %shard_map.87 = bf16[4,2,200,200]{3,2,1,0:T(8,128)(2,1)} custom-call(s32[4]{0:T(128)S(1)} %compare_convert_fusion.1.kept_ref, s32[4]{0:T(128)S(1)} %copy-done.4, s32[4]{0:T(128)S(1)} %get-tuple-element.101.flip_ref, s32[8]{0:T(128)S(1)} %copy-done.3, f32[4]{0:T(128)S(1)} %copy-done.6, bf16[4,2,200,200]{3,2,1,0:T(8,128)(2,1)S(1)} %bitcast.20, ...), custom_call_target="tpu_custom_call" | custom-call | tf_op jit(solution)/shard_map/pallas_call | solution.py:312
  (43 shorter events, 0.1 us)
Async XLA Ops:
  0.0 12.9 %copy-start = (s32[200]{0:T(256)S(1)}, s32[200]{0:T(256)}, u32[]{:S(2)}) copy-start(s32[200]{0:T(256)} %param.17) | copy-start | bytes 2404
  0.0 12.8 %copy-start.12 = (s32[4,2]{0,1:T(2,128)S(1)}, s32[4,2]{0,1:T(2,128)}, u32[]{:S(2)}) copy-start(s32[4,2]{0,1:T(2,128)} %param.15) | copy-start | bytes 100
  0.0 14.2 %copy-start.13 = (s32[4]{0:T(128)S(1)}, s32[4]{0:T(128)}, u32[]{:S(2)}) copy-start(s32[4]{0:T(128)} %param.16) | copy-start | bytes 52
  0.0 14.9 %copy-start.2 = (bf16[4,400,200]{2,1,0:T(8,128)(2,1)S(1)}, bf16[4,400,200]{2,1,0:T(8,128)(2,1)}, u32[]{:S(2)}) copy-start(bf16[4,400,200]{2,1,0:T(8,128)(2,1)} %param.13) | copy-start | bytes 1920004
  2.0 12.9 %copy-start.1 = (bf16[4,400,200]{2,1,0:T(8,128)(2,1)S(1)}, bf16[4,400,200]{2,1,0:T(8,128)(2,1)}, u32[]{:S(2)}) copy-start(bf16[4,400,200]{2,1,0:T(8,128)(2,1)} %param.12) | copy-start | bytes 1920004
  2.0 28.0 %collective-permute-start.6 = (bf16[208,3200]{1,0:T(8,128)(2,1)S(1)}, bf16[208,3200]{1,0:T(8,128)(2,1)}, u32[]{:S(2)}, u32[]{:S(2)}) collective-permute-start(bf16[208,3200]{1,0:T(8,128)(2,1)S(1)} %shard_map.82.refs_0_), channel_id=1, source_target_pairs={{0,1},{4,39},{8,9},{12,47},{16,17},{20,55},{24,25},{28,63},{1,2},{... | collective-permute-start | bytes 3993608 | tf_op jit(solution)/shard_map/ppermute | solution.py:33
  13.6 9.6 %copy-start.7 = (f32[200]{0:T(256)S(1)}, f32[200]{0:T(256)}, u32[]{:S(2)}) copy-start(f32[200]{0:T(256)} %param.18) | copy-start | bytes 2404
  14.8 9.0 %copy-start.10 = (s32[4]{0:T(128)}, s32[4]{0:T(128)S(1)}, u32[]{:S(2)}) copy-start(s32[4]{0:T(128)S(1)} %get-tuple-element.100) | copy-start | bytes 52
  14.9 15.1 %copy-start.9 = (s32[2]{0:T(128)}, s32[2]{0:T(128)S(1)}, u32[]{:S(2)}) copy-start(s32[2]{0:T(128)S(1)} %get-tuple-element.70) | copy-start | bytes 28
  14.9 9.5 %copy-start.8 = (bf16[400]{0:T(512)(128)(2,1)S(1)}, bf16[400]{0:T(512)(128)(2,1)}, u32[]{:S(2)}) copy-start(bf16[400]{0:T(512)(128)(2,1)} %energy_ref.1) | copy-start | bytes 2404
  16.7 62.4 %collective-permute-start.7 = (bf16[4,4,160,128]{3,2,1,0:T(8,128)(2,1)}, bf16[4,4,160,128]{3,2,1,0:T(8,128)(2,1)}, u32[]{:S(2)}, u32[]{:S(2)}) collective-permute-start(bf16[4,4,160,128]{3,2,1,0:T(8,128)(2,1)} %shard_map.84), channel_id=1, source_target_pairs={{0,384},{4,388},{8,392},{12,396},{16,400},{20,404},{24,408},{28,41... | collective-permute-start | bytes 1966088 | tf_op jit(solution)/shard_map/ppermute | solution.py:33
  30.0 21.2 %collective-permute-start = (bf16[208,3200]{1,0:T(8,128)(2,1)}, bf16[208,3200]{1,0:T(8,128)(2,1)}, u32[]{:S(2)}, u32[]{:S(2)}) collective-permute-start(bf16[208,3200]{1,0:T(8,128)(2,1)} %get-tuple-element.29), channel_id=1, source_target_pairs={{0,8},{4,28},{8,16},{12,4},{16,24},{20,12},{24,0},{28,20},{1,9},{5... | collective-permute-start | bytes 3993608 | tf_op jit(solution)/shard_map/cond/branch_1_fun/ppermute | solution.py:33
  33.4 22.6 %all-to-all-start = ((bf16[4,4,160,128]{3,2,1,0:T(8,128)(2,1)}), bf16[4,4,160,128]{3,2,1,0:T(8,128)(2,1)S(1)}, u32[]{:S(2)}, u32[]{:S(2)}) async-start(bf16[4,4,160,128]{3,2,1,0:T(8,128)(2,1)} %get-tuple-element.31), calls=%async_computation | async-start | bytes 1310720 | tf_op jit(solution)/shard_map/cond/branch_1_fun/all_to_all | solution.py:54
  42.5 22.3 %collective-permute-start.3 = (bf16[208,1664]{1,0:T(8,128)(2,1)}, bf16[208,1664]{1,0:T(8,128)(2,1)}, u32[]{:S(2)}, u32[]{:S(2)}) collective-permute-start(bf16[208,1664]{1,0:T(8,128)(2,1)} %constant_dynamic-slice_fusion), channel_id=1, source_target_pairs={{0,1},{4,39},{8,9},{12,47},{16,17},{20,55},{24,25},{28,63},{1,2},{... | collective-permute-start | bytes 2076680 | tf_op jit(solution)/shard_map/cond/branch_1_fun/ppermute | solution.py:33
  44.7 25.8 %collective-permute-start.1 = (bf16[208,3200]{1,0:T(8,128)(2,1)}, bf16[208,3200]{1,0:T(8,128)(2,1)}, u32[]{:S(2)}, u32[]{:S(2)}) collective-permute-start(bf16[208,3200]{1,0:T(8,128)(2,1)} %get-tuple-element.29), channel_id=1, source_target_pairs={{0,4},{4,0},{8,12},{12,8},{16,20},{20,16},{24,28},{28,24},{1,5},{5... | collective-permute-start | bytes 3993608 | tf_op jit(solution)/shard_map/cond/branch_1_fun/ppermute | solution.py:33
  51.2 27.9 %collective-permute-start.2 = (bf16[208,3200]{1,0:T(8,128)(2,1)}, bf16[208,3200]{1,0:T(8,128)(2,1)}, u32[]{:S(2)}, u32[]{:S(2)}) collective-permute-start(bf16[208,3200]{1,0:T(8,128)(2,1)} %collective-permute-done), channel_id=1, source_target_pairs={{0,4},{4,0},{8,12},{12,8},{16,20},{20,16},{24,28},{28,24},{1,5},{5... | collective-permute-start | bytes 3993608 | tf_op jit(solution)/shard_map/cond/branch_1_fun/ppermute | solution.py:33
  57.5 21.7 %all-to-all-start.1 = ((bf16[4,4,160,128]{3,2,1,0:T(8,128)(2,1)}), bf16[4,4,160,128]{3,2,1,0:T(8,128)(2,1)}, u32[]{:S(2)}, u32[]{:S(2)}) async-start(bf16[4,4,160,128]{3,2,1,0:T(8,128)(2,1)} %bitcast.1), calls=%async_computation.1 | async-start | bytes 1310720 | tf_op jit(solution)/shard_map/cond/branch_1_fun/all_to_all | solution.py:54
  64.7 14.4 %collective-permute-start.4 = (bf16[208,1664]{1,0:T(8,128)(2,1)}, bf16[208,1664]{1,0:T(8,128)(2,1)}, u32[]{:S(2)}, u32[]{:S(2)}) collective-permute-start(bf16[208,1664]{1,0:T(8,128)(2,1)} %collective-permute-done.3), channel_id=1, source_target_pairs={{0,8},{4,28},{8,16},{12,4},{16,24},{20,12},{24,0},{28,20},{1,9},{5... | collective-permute-start | bytes 2076680 | tf_op jit(solution)/shard_map/cond/branch_1_fun/ppermute | solution.py:33
  66.7 12.5 %collective-permute-start.5 = (bf16[208,1664]{1,0:T(8,128)(2,1)}, bf16[208,1664]{1,0:T(8,128)(2,1)}, u32[]{:S(2)}, u32[]{:S(2)}) collective-permute-start(bf16[208,1664]{1,0:T(8,128)(2,1)} %collective-permute-done.3), channel_id=1, source_target_pairs={{0,4},{4,0},{8,12},{12,8},{16,20},{20,16},{24,28},{28,24},{1,5},{5... | collective-permute-start | bytes 2076680 | tf_op jit(solution)/shard_map/cond/branch_1_fun/ppermute | solution.py:33
  79.2 8.0 %copy-start.5 = (s32[4]{0:T(128)S(1)}, s32[4]{0:T(128)}, u32[]{:S(2)}) copy-start(s32[4]{0:T(128)} %add.95.source_ref) | copy-start | bytes 52
  79.2 8.0 %collective-permute-start.8 = (bf16[208,1664]{1,0:T(8,128)(2,1)}, bf16[208,1664]{1,0:T(8,128)(2,1)S(1)}, u32[]{:S(2)}, u32[]{:S(2)}) collective-permute-start(bf16[208,1664]{1,0:T(8,128)(2,1)} %get-tuple-element.88.refs_7_), channel_id=1, source_target_pairs={{0,4},{4,0},{8,12},{12,8},{16,20},{20,16},{24,28},{28,24},{1,5},{5... | collective-permute-start | bytes 2076680 | tf_op jit(solution)/shard_map/ppermute | solution.py:33
  87.2 13.6 %copy-start.11 = (s32[4]{0:T(128)S(1)}, s32[4]{0:T(128)}, u32[]{:S(2)}) copy-start(s32[4]{0:T(128)} %copy-done.10) | copy-start | bytes 52
  93.8 35.4 %copy-start.3 = (s32[8]{0:T(128)S(1)}, s32[8]{0:T(128)}, u32[]{:S(2)}) copy-start(s32[8]{0:T(128)} %add.98.source_ref) | copy-start | bytes 100
  93.8 35.4 %copy-start.4 = (s32[4]{0:T(128)S(1)}, s32[4]{0:T(128)}, u32[]{:S(2)}) copy-start(s32[4]{0:T(128)} %get-tuple-element.99.at_ref) | copy-start | bytes 52
  93.8 35.4 %copy-start.6 = (f32[4]{0:T(128)S(1)}, f32[4]{0:T(128)}, u32[]{:S(2)}) copy-start(f32[4]{0:T(128)} %add.92.pair_ref) | copy-start | bytes 52
  93.8 35.4 %collective-permute-start.9 = (bf16[4,2,160,128]{3,2,1,0:T(8,128)(2,1)}, bf16[4,2,160,128]{3,2,1,0:T(8,128)(2,1)S(1)}, u32[]{:S(2)}, u32[]{:S(2)}) collective-permute-start(bf16[4,2,160,128]{3,2,1,0:T(8,128)(2,1)} %get-tuple-element.90), channel_id=1, source_target_pairs={{0,384},{4,388},{8,392},{12,396},{16,400},{20,404},{24,408},{28,41... | collective-permute-start | bytes 983048 | tf_op jit(solution)/shard_map/ppermute | solution.py:33
  101.7 14.4 %all-to-all-start.2 = ((bf16[4,2,160,128]{3,2,1,0:T(8,128)(2,1)}), bf16[4,2,160,128]{3,2,1,0:T(8,128)(2,1)S(1)}, u32[]{:S(2)}, u32[]{:S(2)}) async-start(bf16[4,2,160,128]{3,2,1,0:T(8,128)(2,1)} %get-tuple-element.33), calls=%async_computation.2 | async-start | bytes 655360 | tf_op jit(solution)/shard_map/cond/branch_1_fun/all_to_all | solution.py:54

commit v7 on v6

--- a/solution.py
+++ b/solution.py
@@ -1,3 +1,5 @@
+import functools
+
 import jax
 import jax.numpy as jnp
 from jax import lax
@@ -54,11 +56,6 @@
     return lax.all_to_all(units, "virt", 0, 0, tiled=True)
 
 
-def reorder(scattered, step):
-    index = jnp.bitwise_xor(jnp.arange(4, dtype=jnp.int32)[:, None], step[None, :])
-    return scattered[index, jnp.arange(scattered.shape[1], dtype=jnp.int32)[None, :]]
-
-
 def together(*values):
     return lax.optimization_barrier(values)
 
@@ -86,6 +83,47 @@
 
 WHOLE = pl.BlockSpec(memory_space=pltpu.VMEM)
 SCALARS = pl.BlockSpec(memory_space=pltpu.SMEM)
+
+
+def reorder_kernel(step_ref, in_ref, out_ref):
+    for p in range(in_ref.shape[1]):
+        for v in range(4):
+            out_ref[v, p] = in_ref[jnp.bitwise_xor(step_ref[p % 2], v), p]
+
+
+def reorder(scattered, step):
+    return pl.pallas_call(
+        reorder_kernel,
+        out_shape=jax.ShapeDtypeStruct(scattered.shape, BF),
+        in_specs=[SCALARS, WHOLE],
+        out_specs=WHOLE,
+        compiler_params=params(),
+        cost_estimate=cost(0, 1_300_000),
+    )(step, scattered)
+
+
+def part_kernel(core_ref, in_ref, out_ref, sem):
+    for c in range(2):
+
+        @pl.when(core_ref[0] == c)
+        def _():
+            copy = pltpu.make_async_copy(
+                in_ref.at[:, pl.ds(c * (DEEP - PART), PART)], out_ref, sem
+            )
+            copy.start()
+            copy.wait()
+
+
+def part_of(core, block):
+    return pl.pallas_call(
+        part_kernel,
+        out_shape=jax.ShapeDtypeStruct((TALL, PART), BF),
+        in_specs=[SCALARS, pl.BlockSpec(memory_space=pl.ANY)],
+        out_specs=WHOLE,
+        scratch_shapes=[pltpu.SemaphoreType.DMA],
+        compiler_params=params(),
+        cost_estimate=cost(0, 1_400_000),
+    )(core, block)
 
 
 def pack_kernel(order_ref, slab_ref, energy_ref, out_ref):
@@ -147,32 +185,28 @@
     return jnp.pad(tile, ((0, 56), (0, 56))).T[0:W, 0:W]
 
 
-def tiles_kernel(pick_ref, amp_ref, int_ref, *refs):
-    *outs, unit = refs
+def tiles_kernel(turn, pick_ref, amp_ref, int_ref, out_ref, unit):
     unit[3 * W : UNIT, :] = jnp.zeros((UNIT - 3 * W, 128), F32)
     j = pl.program_id(0)
     for kind, ref in enumerate((amp_ref, int_ref)):
         for block in range(2):
-            put_tile(unit, block, ref[0, block].astype(F32))
+            tile = ref[0, block].astype(F32)
+            put_tile(unit, block, turned(tile) if turn else tile)
         for i in range(4):
-            piece = unit[i * PIECE : (i + 1) * PIECE, :].astype(BF)
-            if len(outs) == 2:
-                outs[kind][i, j] = piece
-            else:
-                outs[0][i, 2 * kind + j] = piece
-
-
-def pack_tiles(pick, amplitudes, integrals, arrays):
+            out_ref[i, 2 * kind + j] = unit[i * PIECE : (i + 1) * PIECE, :].astype(BF)
+
+
+def pack_tiles(pick, amplitudes, integrals, turn):
     tile = pl.BlockSpec((1, 2, W, W), lambda j, pick: (pick[j], 0, 0, 0))
-    shape = (4, 4 // arrays, PIECE, 128)
-    return pl.pallas_call(
-        tiles_kernel,
-        out_shape=[jax.ShapeDtypeStruct(shape, BF)] * arrays,
+    shape = (4, 4, PIECE, 128)
+    return pl.pallas_call(
+        functools.partial(tiles_kernel, turn),
+        out_shape=jax.ShapeDtypeStruct(shape, BF),
         grid_spec=pltpu.PrefetchScalarGridSpec(
             num_scalar_prefetch=1,
             grid=(2,),
             in_specs=[tile, tile],
-            out_specs=[pl.BlockSpec(shape, lambda j, pick: (0, 0, 0, 0))] * arrays,
+            out_specs=pl.BlockSpec(shape, lambda j, pick: (0, 0, 0, 0)),
             scratch_shapes=[pltpu.VMEM((UNIT, 128), F32)],
         ),
         compiler_params=params("arbitrary"),
@@ -180,101 +214,117 @@
     )(pick, amplitudes, integrals)
 
 
-def half_kernel(flip_ref, slab_ref, local_ref, cross_ref, half_ref, int_ref):
+def ladder_kernel(source_ref, flip_ref, core_ref, *refs):
+    slab_ref, local_ref, cross_ref, *refs = refs
+    full, (near, near_x, far, far_x), (out_ref, table_ref, *refs) = refs[:6], refs[6:10], refs[10:]
+    local, cross, slab, right, rows, half, unit, one_sem, slab_sem, right_sem, row_sem = refs
+    even, odd = core_ref[0] == 0, core_ref[0] != 0
+    split = ((even, near, far), (even, near_x, far_x), (odd, far, near), (odd, far_x, near_x))
+
+    copies = [
+        pltpu.make_async_copy(local_ref, local, one_sem.at[0]),
+        pltpu.make_async_copy(cross_ref, cross, one_sem.at[1]),
+        pltpu.make_async_copy(slab_ref.at[:, 0], slab.at[0], slab_sem.at[0]),
+        pltpu.make_async_copy(slab_ref.at[:, 1], slab.at[1], slab_sem.at[1]),
+    ]
+    for copy in copies:
+        copy.start()
+    for t in range(4):
+        for r in range(6):
+
+            @pl.when(source_ref[t] == r)
+            def _():
+                pltpu.make_async_copy(full[r], right.at[t], right_sem.at[t]).start()
+
+        for r, (on, low, high) in enumerate(split):
+
+            @pl.when(jnp.logical_and(on, source_ref[t] == 6 + r % 2))
+            def _():
+                pltpu.make_async_copy(
+                    low, right.at[t, :, pl.ds(0, PART)], right_sem.at[t]
+                ).start()
+                pltpu.make_async_copy(
+                    high.at[:, pl.ds(2 * PART - DEEP, DEEP - PART)],
+                    right.at[t, :, pl.ds(PART, DEEP - PART)],
+                    right_sem.at[t],
+                ).start()
+
+    corner = (pl.ds(TALL - 16, 16), pl.ds(0, 256))
+    for r in range(6):
+        pltpu.make_async_copy(full[r].at[corner], rows.at[r], row_sem.at[r]).start()
+    for r, (on, low, _) in enumerate(split):
+
+        @pl.when(on)
+        def _():
+            pltpu.make_async_copy(low.at[corner], rows.at[6 + r % 2], row_sem.at[6 + r % 2]).start()
+
+    copies[0].wait()
+    copies[1].wait()
+    unit[3 * W : UNIT, :] = jnp.zeros((UNIT - 3 * W, 128), F32)
+
     @pl.loop(0, 2)
     def _(j):
         straight = flip_ref[j] == 0
 
         def sums(at):
-            local, cross = whole_unit(at, local_ref), whole_unit(at, cross_ref)
-            tiles = [get_tile(cross, b) for b in range(2)]
+            here, there = whole_unit(at, local), whole_unit(at, cross)
+            tiles = [get_tile(there, b) for b in range(2)]
             return [
-                get_tile(local, b) + turned(jnp.where(straight, tiles[b], tiles[1 - b]))
-                for b in range(2)
+                get_tile(here, b) + jnp.where(straight, tiles[b], tiles[1 - b]) for b in range(2)
             ]
 
-        for b, tile in enumerate(sums(2 + j)):
-            int_ref[2 * j + b] = tile
-        for b, tile in enumerate(sums(j)):
-            both = tile.astype(BF)
+        amp, add = sums(j), sums(2 + j)
+        for b in range(2):
+            t = 2 * j + b
+
+            @pl.when(j == 0)
+            def _():
+                copies[2 + b].wait()
+
+            both = amp[b].astype(BF)
             for q in range(NQ):
-                half_ref[2 * j + b, :, q * W : (q + 1) * W] = jnp.dot(
-                    slab_ref[q, b], both, preferred_element_type=F32
+                half[:, q * W : (q + 1) * W] = jnp.dot(
+                    slab[b, q], both, preferred_element_type=F32
                 ).astype(BF)
-
-
-def first_half(flip, slab, local, cross):
-    return pl.pallas_call(
-        half_kernel,
-        out_shape=(pltpu.VMEM((4, W, DEEP), BF), pltpu.VMEM((4, W, W), F32)),
-        in_specs=[SCALARS] + [WHOLE] * 3,
-        out_specs=[WHOLE, WHOLE],
-        compiler_params=params(),
-        cost_estimate=cost(8 * NQ * W**3, 4_000_000),
-    )(flip, slab, local, cross)
-
-
-def ladder_kernel(source_ref, core_ref, half_ref, int_ref, *refs):
-    full, (near, near_x, far, far_x), (out_ref, table_ref, unit, sums) = (
-        refs[:6], refs[6:10], refs[10:]
-    )
-    even = core_ref[0] == 0
-    odd = core_ref[0] != 0
-    split = ((even, near, far), (even, near_x, far_x), (odd, far, near), (odd, far_x, near_x))
-    dims = (((1,), (1,)), ((), ()))
-
-    @pl.loop(0, 4)
-    def _(t):
-        for r in range(6):
-
-            @pl.when(source_ref[t] == r)
-            def _():
-                sums[t] = lax.dot_general(
-                    half_ref[t], full[r][0:W, :], dims, preferred_element_type=F32
-                )
-
-        for r, (on, low, high) in enumerate(split):
-
-            @pl.when(jnp.logical_and(on, source_ref[t] == 6 + r % 2))
-            def _():
-                sums[t] = lax.dot_general(
-                    half_ref[t, :, 0:PART], low[0:W, :], dims, preferred_element_type=F32
-                ) + lax.dot_general(
-                    half_ref[t, :, PART:DEEP],
-                    high[0:W, 2 * PART - DEEP : PART],
-                    dims,
-                    preferred_element_type=F32,
-                )
-
-    for r in range(6):
-        table_ref[r] = full[r][W:TALL, 0:W].astype(F32)
-    for r, (on, low, _) in enumerate(split):
-
-        @pl.when(on)
-        def _():
-            table_ref[6 + r % 2] = low[W:TALL, 0:W].astype(F32)
-
-    unit[3 * W : UNIT, :] = jnp.zeros((UNIT - 3 * W, 128), F32)
-    for j in range(2):
-        for b in range(2):
-            put_tile(unit, b, int_ref[2 * j + b] + sums[2 * j + b])
+            pltpu.make_async_copy(full[0], right.at[t], right_sem.at[t]).wait()
+            ladder = lax.dot_general(
+                half[...], right[t, 0:W, :], (((1,), (1,)), ((), ())), preferred_element_type=F32
+            )
+            put_tile(unit, b, add[b] + ladder)
         for i in range(4):
             out_ref[i, j] = unit[i * PIECE : (i + 1) * PIECE, :].astype(BF)
 
-
-def symmetric_units(source, core, half_done, integrals, full, parts):
+    for r in range(8):
+        pltpu.make_async_copy(full[0].at[corner], rows.at[r], row_sem.at[r]).wait()
+        table_ref[r] = rows[r].astype(F32)[8:16, 0:W]
+
+
+def symmetric_units(source, flip, core, slab, local, cross, full, parts):
+    dma = pltpu.SemaphoreType.DMA
     return pl.pallas_call(
         ladder_kernel,
         out_shape=(
             jax.ShapeDtypeStruct((4, 2, PIECE, 128), BF),
             jax.ShapeDtypeStruct((8, TALL - W, W), F32),
         ),
-        in_specs=[SCALARS, SCALARS] + [WHOLE] * 12,
+        in_specs=[SCALARS] * 3 + [pl.BlockSpec(memory_space=pl.ANY)] * 13,
         out_specs=[WHOLE] * 2,
-        scratch_shapes=[pltpu.VMEM((UNIT, 128), F32), pltpu.VMEM((4, W, W), F32)],
+        scratch_shapes=[
+            pltpu.VMEM((4, 4, PIECE, 128), BF),
+            pltpu.VMEM((4, 4, PIECE, 128), BF),
+            pltpu.VMEM((2, NQ, W, W), BF),
+            pltpu.VMEM((4, TALL, DEEP), BF),
+            pltpu.VMEM((8, 16, 256), BF),
+            pltpu.VMEM((W, DEEP), BF),
+            pltpu.VMEM((UNIT, 128), F32),
+            dma((2,)),
+            dma((2,)),
+            dma((4,)),
+            dma((8,)),
+        ],
         compiler_params=params(),
-        cost_estimate=cost(8 * NQ * W**3, 3_000_000),
-    )(source, core, *in_vmem(half_done, integrals, *full, *parts))
+        cost_estimate=cost(16 * NQ * W**3, 10_000_000),
+    )(source, flip, core, slab, local, cross, *full, *parts)
 
 
 def update_kernel(
@@ -285,7 +335,7 @@
 
     def finish(block, symmetric):
         far = table_ref[source_ref[2 * p + block], 0:1, :]
-        denominator = pair_ref[p] - near_ref[block] - far
+        denominator = pair_ref[p] - near_ref[block, :, 0:1] - far
         old = amp_ref[0, block].astype(F32)
         out_ref[0, block] = (old + symmetric / denominator).astype(BF)
 
@@ -320,7 +370,7 @@
                 pl.BlockSpec((4, 1, PIECE, 128), pick),
                 pl.BlockSpec((4, 1, PIECE, 128), pick),
                 pl.BlockSpec((8, TALL - W, W), fixed),
-                pl.BlockSpec((2, W, 1), fixed),
+                pl.BlockSpec((2, W, 128), fixed),
             ],
             out_specs=pl.BlockSpec((1, 2, W, W), here),
         ),
@@ -354,14 +404,14 @@
 
     one = pack_slab(slab, virt_energy, parity[None])
     y_one = along_y(one)
-    local = to_mirror(pack_tiles(send, amp, ints, 1)[0])
-    kept_tiles = pack_tiles(keep, amp, ints, 1)[0]
+    local = to_mirror(pack_tiles(send, amp, ints, False))
+    kept_tiles = pack_tiles(keep, amp, ints, True)
 
     irrep = jnp.bitwise_xor(occ_irrep[pair_list[:, 0]], occ_irrep[pair_list[:, 1]])
     step, flip = jnp.right_shift(irrep, 1), jnp.bitwise_and(irrep, 1)
     keep_step, keep_flip = among(step, upper), among(flip, upper)
     pair_energy = occ_energy[pair_list[:, 0]] + occ_energy[pair_list[:, 1]]
-    near = virt_energy.astype(F32).reshape(2, W, 1)
+    near = jnp.broadcast_to(virt_energy.astype(F32).reshape(2, W, 1), (2, W, 128))
 
     def sources(step, flip):
         apart = jnp.bitwise_and(jnp.bitwise_xor(virt, step) - virt, 3)[:, None]
@@ -381,22 +431,20 @@
     def bring(y_one, kept_tiles, keep_step, slab, virt_energy):
         scattered = exchange(kept_tiles)
         x_one = along_x(y_one)
-        y_far = along_y(lax.dynamic_slice(y_one, (0, core * (DEEP - PART)), (TALL, PART)))
-        cross = exchange(reorder(scattered, jnp.concatenate([keep_step, keep_step])))
+        y_far = along_y(part_of(core[None], y_one))
+        cross = exchange(reorder(scattered, keep_step))
         two = pack_slab(slab, virt_energy, 1 - parity[None])
+        x_far = along_x(y_far)
         return (
             two, x_one, swap_cores(y_one), swap_cores(x_one),
-            y_far, along_x(y_far), swap_cores(y_far), cross,
+            y_far, x_far, swap_cores(y_far), swap_cores(x_far), cross,
         )
 
     brought = as_unit(ready, bring, y_one, kept_tiles, keep_step, slab, virt_energy)
-    two, x_one, y_swap, x_swap, y_far, x_far, y_far_swap, cross, local = together(*brought, local)
+    two, x_one, y_swap, x_swap, *parts, cross, local = together(*brought, local)
     full = (one, two, y_one, x_one, y_swap, x_swap)
-    parts = (y_far, x_far, y_far_swap, swap_cores(x_far))
-
-    half_done, both_ints = first_half(keep_flip, slab, local, cross)
     result, table = symmetric_units(
-        keep_source, core[None], half_done, both_ints, full, parts
+        keep_source, keep_flip, core[None], slab, local, cross, full, parts
     )
     mirrored = to_mirror(result)
     crossed = as_unit(ready, lambda x: exchange(reorder(exchange(x), keep_step)), result)

time: 133 us -> 140 us (1.053)
  the two profiles are of different devices: /device:TPU:56 before, /device:TPU:64 now
where the time goes in v7:
time: 140 us; the launch traced here: 139 us
  starting transfers between devices  62.5 us (45%)
  Pallas kernels  28.7 us (20%)
  blocking collectives  25.9 us (18%)
  waiting for transfers between devices  17.3 us (12%)
  local copies, waits for them, and re-layouts  3.47 us (2%)
    ppermute x10, starting transfers between devices, permute(): return lax.ppermute(value, ('pair', 'virt'), pairs)  48.3 us
    all_to_all x2, blocking collectives, exchange(): return lax.all_to_all(units, 'virt', 0, 0, tiled=True)  25.9 us
    all_to_all x2, starting transfers between devices, exchange(): return lax.all_to_all(units, 'virt', 0, 0, tiled=True)  14.2 us
    pallas_call x1, Pallas kernels, symmetric_units(): pl.pallas_call(ladder_kernel, out_shape=(jax.ShapeDtypeStruct((4, 2, PIEC...  12.7 us
    all_to_all x2, waiting for transfers between devices, exchange(): return lax.all_to_all(units, 'virt', 0, 0, tiled=True)  10.8 us
    ppermute x10, waiting for transfers between devices, permute(): return lax.ppermute(value, ('pair', 'virt'), pairs)  6.47 us
    pallas_call x2, Pallas kernels, pack_slab(): pl.pallas_call(pack_kernel, out_shape=jax.ShapeDtypeStruct((TALL, DEEP),...  4.96 us
    pallas_call x2, Pallas kernels, pack_tiles(): pl.pallas_call(functools.partial(tiles_kernel, turn), out_shape=jax.Shape...  3.84 us
  transfers between devices with their start and end apart: 12, of which 3 were waited for; matrix products, arithmetic and copies ran while one was open for 3% of the time, Pallas kernels for 8%

profile of v7, /device:TPU:64, one launch (start us, length us, event | category | flops | bytes accessed | tf_op | source)
XLA Modules:
  0.0 139.0 jit_solution(3129117679885232536)
XLA Ops:
  0.0 2.0 %shard_map.82.refs_3_ = bf16[208,3200]{1,0:T(8,128)(2,1)S(1)} custom-call(s32[1]{0:T(128)} %bitcast.4.order_ref, bf16[16,2,200,200]{3,2,1,0:T(8,128)(2,1)} %bitcast.18, bf16[400]{0:T(512)(128)(2,1)} %energy_ref.1), custom_call_target="tpu_custom_call" | custom-call | bytes 3000000 | tf_op jit(solution)/shard_map/pallas_call | solution.py:138
  2.0 0.0 copy-start.1
  2.0 3.6 %collective-permute-start.7 = (bf16[208,3200]{1,0:T(8,128)(2,1)S(1)}, bf16[208,3200]{1,0:T(8,128)(2,1)}, u32[]{:S(2)}, u32[]{:S(2)}) collective-permute-start(bf16[208,3200]{1,0:T(8,128)(2,1)S(1)} %shard_map.82.refs_3_), channel_id=1, source_target_pairs={{0,1},{4,39},{8,9},{12,47},{16,17},{20,55},{24,25},{28,63},{1,2},{... | collective-permute-start | bytes 3993608 | tf_op jit(solution)/shard_map/ppermute | solution.py:35
  5.7 0.6 gather_fusion
  6.4 0.6 gather_fusion.1
  7.0 0.1 fusion.2
  7.2 0.0 copy-start.4
  7.2 1.8 %shard_map.84 = bf16[4,4,160,128]{3,2,1,0:T(8,128)(2,1)} custom-call(s32[2]{0:T(128)S(1)} %get-tuple-element.96.pick_ref, bf16[4,2,200,200]{3,2,1,0:T(8,128)(2,1)S(1)} %bitcast.13, bf16[4,2,200,200]{3,2,1,0:T(8,128)(2,1)S(1)} %bitcast.16), custom_call_target="tpu_custom_call" | custom-call | bytes 1500000 | tf_op jit(solution)/shard_map/pallas_call | solution.py:202
  8.9 14.2 %collective-permute-start.8 = (bf16[4,4,160,128]{3,2,1,0:T(8,128)(2,1)}, bf16[4,4,160,128]{3,2,1,0:T(8,128)(2,1)}, u32[]{:S(2)}, u32[]{:S(2)}) collective-permute-start(bf16[4,4,160,128]{3,2,1,0:T(8,128)(2,1)} %shard_map.84), channel_id=1, source_target_pairs={{0,384},{4,388},{8,392},{12,396},{16,400},{20,404},{24,408},{28,41... | collective-permute-start | bytes 1966088 | tf_op jit(solution)/shard_map/ppermute | solution.py:35
  23.2 0.6 gather_fusion.2
  23.8 0.6 gather_fusion.3
  24.4 0.1 reshape.101
  24.5 0.5 slice.13
  25.1 2.1 %shard_map.83 = bf16[4,4,160,128]{3,2,1,0:T(8,128)(2,1)} custom-call(s32[2]{0:T(128)S(1)} %get-tuple-element.95.pick_ref, bf16[4,2,200,200]{3,2,1,0:T(8,128)(2,1)S(1)} %bitcast.14, bf16[4,2,200,200]{3,2,1,0:T(8,128)(2,1)S(1)} %bitcast.17), custom_call_target="tpu_custom_call" | custom-call | bytes 1500000 | tf_op jit(solution)/shard_map/pallas_call | solution.py:202
  27.1 0.1 fusion.3
  27.2 0.1 add.70.source_ref
  27.3 0.1 add.73.source_ref
  28.1 0.0 collective-permute-done.7.refs_5_
  28.1 0.1 broadcast_in_dim.101.near_ref
  28.2 60.3 %conditional.2 = (bf16[208,3200]{1,0:T(8,128)(2,1)}, bf16[208,3200]{1,0:T(8,128)(2,1)}, bf16[208,3200]{1,0:T(8,128)(2,1)}, bf16[208,3200]{1,0:T(8,128)(2,1)}, bf...) conditional(s32[]{:T(128)} %bitcast.8, () %tuple.23, ...), branch_computations={%region_3.4_spmd, %region_4.5_spmd} | conditional | flops 1 | bytes 36682572 | solution.py:67
  28.2 3.4 %collective-permute-start = (bf16[208,3200]{1,0:T(8,128)(2,1)}, bf16[208,3200]{1,0:T(8,128)(2,1)}, u32[]{:S(2)}, u32[]{:S(2)}) collective-permute-start(bf16[208,3200]{1,0:T(8,128)(2,1)} %get-tuple-element.29.in_ref), channel_id=1, source_target_pairs={{0,8},{4,28},{8,16},{12,4},{16,24},{20,12},{24,0},{28,20},{1,9},{5... | collective-permute-start | bytes 3993608 | tf_op jit(solution)/shard_map/cond/branch_1_fun/ppermute | solution.py:35
  31.6 2.0 %branch_1_fun.5 = bf16[208,1664]{1,0:T(8,128)(2,1)} custom-call(s32[1]{0:T(128)} %bitcast.1.core_ref, bf16[208,3200]{1,0:T(8,128)(2,1)} %get-tuple-element.29.in_ref), custom_call_target="tpu_custom_call" | custom-call | bytes 1400000 | tf_op jit(solution)/shard_map/cond/branch_1_fun/pallas_call | solution.py:118
  33.6 3.5 %collective-permute-start.3 = (bf16[208,1664]{1,0:T(8,128)(2,1)}, bf16[208,1664]{1,0:T(8,128)(2,1)}, u32[]{:S(2)}, u32[]{:S(2)}) collective-permute-start(bf16[208,1664]{1,0:T(8,128)(2,1)} %branch_1_fun.5), channel_id=1, source_target_pairs={{0,1},{4,39},{8,9},{12,47},{16,17},{20,55},{24,25},{28,63},{1,2},{... | collective-permute-start | bytes 2076680 | tf_op jit(solution)/shard_map/cond/branch_1_fun/ppermute | solution.py:35
  37.1 5.2 %all-to-all-start = ((bf16[4,4,160,128]{3,2,1,0:T(8,128)(2,1)}), bf16[4,4,160,128]{3,2,1,0:T(8,128)(2,1)S(1)}, u32[]{:S(2)}, u32[]{:S(2)}) async-start(bf16[4,4,160,128]{3,2,1,0:T(8,128)(2,1)} %get-tuple-element.32), calls=%async_computation | async-start | bytes 1310720 | tf_op jit(solution)/shard_map/cond/branch_1_fun/all_to_all | solution.py:56
  42.3 6.5 %collective-permute-done.3 = bf16[208,1664]{1,0:T(8,128)(2,1)} collective-permute-done((bf16[208,1664]{1,0:T(8,128)(2,1)}, bf16[208,1664]{1,0:T(8,128)(2,1)}, u32[]{:S(2)}, u32[]{:S(2)}) %collective-permute-start.3) | collective-permute-done | bytes 692256 | tf_op jit(solution)/shard_map/cond/branch_1_fun/ppermute | solution.py:35
  48.7 5.6 %collective-permute-start.4 = (bf16[208,1664]{1,0:T(8,128)(2,1)}, bf16[208,1664]{1,0:T(8,128)(2,1)}, u32[]{:S(2)}, u32[]{:S(2)}) collective-permute-start(bf16[208,1664]{1,0:T(8,128)(2,1)} %collective-permute-done.3), channel_id=1, source_target_pairs={{0,8},{4,28},{8,16},{12,4},{16,24},{20,12},{24,0},{28,20},{1,9},{5... | collective-permute-start | bytes 2076680 | tf_op jit(solution)/shard_map/cond/branch_1_fun/ppermute | solution.py:35
  54.3 3.6 %collective-permute-start.1 = (bf16[208,3200]{1,0:T(8,128)(2,1)}, bf16[208,3200]{1,0:T(8,128)(2,1)}, u32[]{:S(2)}, u32[]{:S(2)}) collective-permute-start(bf16[208,3200]{1,0:T(8,128)(2,1)} %get-tuple-element.29.in_ref), channel_id=1, source_target_pairs={{0,4},{4,0},{8,12},{12,8},{16,20},{20,16},{24,28},{28,24},{1,5},{5... | collective-permute-start | bytes 3993608 | tf_op jit(solution)/shard_map/cond/branch_1_fun/ppermute | solution.py:35
  58.0 0.0 collective-permute-done
  58.0 1.9 %collective-permute-start.2 = (bf16[208,3200]{1,0:T(8,128)(2,1)}, bf16[208,3200]{1,0:T(8,128)(2,1)}, u32[]{:S(2)}, u32[]{:S(2)}) collective-permute-start(bf16[208,3200]{1,0:T(8,128)(2,1)} %collective-permute-done), channel_id=1, source_target_pairs={{0,4},{4,0},{8,12},{12,8},{16,20},{20,16},{24,28},{28,24},{1,5},{5... | collective-permute-start | bytes 3993608 | tf_op jit(solution)/shard_map/cond/branch_1_fun/ppermute | solution.py:35
  59.9 0.1 all-to-all-done.in_ref
  60.0 1.4 %branch_1_fun.6 = bf16[4,4,160,128]{3,2,1,0:T(8,128)(2,1)} custom-call(s32[2]{0:T(128)S(1)} %get-tuple-element.31.step_ref, bf16[4,4,160,128]{3,2,1,0:T(8,128)(2,1)S(1)} %all-to-all-done.in_ref), custom_call_target="tpu_custom_call" | custom-call | bytes 1300000 | tf_op jit(solution)/shard_map/cond/branch_1_fun/pallas_call | solution.py:95
  61.4 9.0 %all-to-all-start.1 = ((bf16[4,4,160,128]{3,2,1,0:T(8,128)(2,1)}), bf16[4,4,160,128]{3,2,1,0:T(8,128)(2,1)}, u32[]{:S(2)}, u32[]{:S(2)}) async-start(bf16[4,4,160,128]{3,2,1,0:T(8,128)(2,1)} %branch_1_fun.6), calls=%async_computation.1 | async-start | bytes 1310720 | tf_op jit(solution)/shard_map/cond/branch_1_fun/all_to_all | solution.py:56
  70.4 1.9 %collective-permute-start.5 = (bf16[208,1664]{1,0:T(8,128)(2,1)}, bf16[208,1664]{1,0:T(8,128)(2,1)}, u32[]{:S(2)}, u32[]{:S(2)}) collective-permute-start(bf16[208,1664]{1,0:T(8,128)(2,1)} %collective-permute-done.3), channel_id=1, source_target_pairs={{0,4},{4,0},{8,12},{12,8},{16,20},{20,16},{24,28},{28,24},{1,5},{5... | collective-permute-start | bytes 2076680 | tf_op jit(solution)/shard_map/cond/branch_1_fun/ppermute | solution.py:35
  72.3 0.0 collective-permute-done.4
  72.3 2.4 %collective-permute-start.6 = (bf16[208,1664]{1,0:T(8,128)(2,1)}, bf16[208,1664]{1,0:T(8,128)(2,1)}, u32[]{:S(2)}, u32[]{:S(2)}) collective-permute-start(bf16[208,1664]{1,0:T(8,128)(2,1)} %collective-permute-done.4), channel_id=1, source_target_pairs={{0,4},{4,0},{8,12},{12,8},{16,20},{20,16},{24,28},{28,24},{1,5},{5... | collective-permute-start | bytes 2076680 | tf_op jit(solution)/shard_map/cond/branch_1_fun/ppermute | solution.py:35
  74.7 3.0 %branch_1_fun.4 = bf16[208,3200]{1,0:T(8,128)(2,1)} custom-call(s32[1]{0:T(128)} %bitcast.order_ref, bf16[16,2,200,200]{3,2,1,0:T(8,128)(2,1)} %get-tuple-element.27.slab_ref, bf16[400]{0:T(512)(128)(2,1)S(1)} %get-tuple-element.28.energy_ref), custom_call_target="tpu_custom_call" | custom-call | bytes 3000000 | tf_op jit(solution)/shard_map/cond/branch_1_fun/pallas_call | solution.py:138
  77.7 0.0 collective-permute-done.1
  77.7 0.0 collective-permute-done.5
  77.7 10.8 %all-to-all-done.1 = bf16[4,4,160,128]{3,2,1,0:T(8,128)(2,1)} async-done(((bf16[4,4,160,128]{3,2,1,0:T(8,128)(2,1)}), bf16[4,4,160,128]{3,2,1,0:T(8,128)(2,1)}, u32[]{:S(2)}, u32[]{:S(2)}) %all-to-all-start.1) | async-done | bytes 655392 | tf_op jit(solution)/shard_map/cond/branch_1_fun/all_to_all | solution.py:56
  88.5 0.0 collective-permute-done.6
  88.5 12.7 %shard_map.85 = (bf16[4,2,160,128]{3,2,1,0:T(8,128)(2,1)}, f32[8,8,200]{2,1,0:T(8,128)S(1)}) custom-call(s32[4]{0:T(128)S(1)} %add.70.source_ref, s32[2]{0:T(128)S(1)} %get-tuple-element.67.flip_ref, s32[1]{0:T(128)} %bitcast.9.core_ref, bf16[16,2,200,200]{3,2,1,0:T(8,128)(2,1)} %bitcast.20, bf16[4,4,160,128]{3,2,1,0:T(8,128)(2,1)} %collective-permute-done.8.refs_1_, ...), custom_call_target="tpu_custom_call" | custom-call | flops 2048000000 | bytes 10000000 | tf_op jit(solution)/shard_map/pallas_call | solution.py:304
  101.2 8.2 %collective-permute-start.9 = (bf16[4,2,160,128]{3,2,1,0:T(8,128)(2,1)}, bf16[4,2,160,128]{3,2,1,0:T(8,128)(2,1)S(1)}, u32[]{:S(2)}, u32[]{:S(2)}) collective-permute-start(bf16[4,2,160,128]{3,2,1,0:T(8,128)(2,1)} %get-tuple-element.90), channel_id=1, source_target_pairs={{0,384},{4,388},{8,392},{12,396},{16,400},{20,404},{24,408},{28,41... | collective-permute-start | bytes 983048 | tf_op jit(solution)/shard_map/ppermute | solution.py:35
  109.4 26.5 %conditional.3 = (bf16[4,2,160,128]{3,2,1,0:T(8,128)(2,1)S(1)}) conditional(s32[]{:T(128)} %bitcast.8, () %tuple.22, (bf16[4,2,160,128]{3,2,1,0:T(8,128)(2,1)}, s32[2]{0:T(128)S(1)}) %tuple.26), branch_computations={%region_6.7_spmd, %region_7.8_spmd} | conditional | bytes 2610728 | solution.py:67
  109.4 13.5 %all_to_all.16.in_ref = bf16[4,2,160,128]{3,2,1,0:T(8,128)(2,1)S(1)} all-to-all(bf16[4,2,160,128]{3,2,1,0:T(8,128)(2,1)} %get-tuple-element.34), channel_id=1, replica_groups=mesh['pair'=192,'virt'=4] {'virt'}, dimensions={0} | all-to-all | bytes 655360 | tf_op jit(solution)/shard_map/cond/branch_1_fun/all_to_all | solution.py:56
  122.9 0.6 branch_1_fun.7
  123.5 12.3 %all_to_all.17 = bf16[4,2,160,128]{3,2,1,0:T(8,128)(2,1)S(1)} all-to-all(bf16[4,2,160,128]{3,2,1,0:T(8,128)(2,1)S(1)} %branch_1_fun.7), channel_id=1, replica_groups=mesh['pair'=192,'virt'=4] {'virt'}, dimensions={0} | all-to-all | bytes 655360 | tf_op jit(solution)/shard_map/cond/branch_1_fun/all_to_all | solution.py:56
  135.8 0.0 collective-permute-done.9.mirror_ref
  135.8 3.2 %shard_map.86 = bf16[4,2,200,200]{3,2,1,0:T(8,128)(2,1)} custom-call(s32[4]{0:T(128)S(1)} %compare_convert_fusion.1.kept_ref, s32[4]{0:T(128)S(1)} %get-tuple-element.99.at_ref, s32[4]{0:T(128)S(1)} %get-tuple-element.101.flip_ref, s32[8]{0:T(128)S(1)} %add.73.source_ref, f32[4]{0:T(128)S(1)} %add.67.pair_ref, bf16[4,2,200,200]{3,2,1,0:T(8,128)(2,1)S(1)} %bitcast.15, ...), custom_call_target="tpu_custom_call" | custom-call | tf_op jit(solution)/shard_map/pallas_call | solution.py:362
  (22 shorter events, 0.1 us)
Async XLA Ops:
  0.0 5.7 %copy-start = (s32[200]{0:T(256)S(1)}, s32[200]{0:T(256)}, u32[]{:S(2)}) copy-start(s32[200]{0:T(256)} %param.17) | copy-start | bytes 2404
  0.0 5.7 %copy-start.5 = (s32[4,2]{0,1:T(2,128)S(1)}, s32[4,2]{0,1:T(2,128)}, u32[]{:S(2)}) copy-start(s32[4,2]{0,1:T(2,128)} %param.15) | copy-start | bytes 100
  0.0 7.0 %copy-start.6 = (s32[4]{0:T(128)S(1)}, s32[4]{0:T(128)}, u32[]{:S(2)}) copy-start(s32[4]{0:T(128)} %param.16) | copy-start | bytes 52
  0.0 7.1 %copy-start.2 = (bf16[4,400,200]{2,1,0:T(8,128)(2,1)S(1)}, bf16[4,400,200]{2,1,0:T(8,128)(2,1)}, u32[]{:S(2)}) copy-start(bf16[4,400,200]{2,1,0:T(8,128)(2,1)} %param.13) | copy-start | bytes 1920004
  2.0 5.1 %copy-start.1 = (bf16[4,400,200]{2,1,0:T(8,128)(2,1)S(1)}, bf16[4,400,200]{2,1,0:T(8,128)(2,1)}, u32[]{:S(2)}) copy-start(bf16[4,400,200]{2,1,0:T(8,128)(2,1)} %param.12) | copy-start | bytes 1920004
  2.0 26.0 %collective-permute-start.7 = (bf16[208,3200]{1,0:T(8,128)(2,1)S(1)}, bf16[208,3200]{1,0:T(8,128)(2,1)}, u32[]{:S(2)}, u32[]{:S(2)}) collective-permute-start(bf16[208,3200]{1,0:T(8,128)(2,1)S(1)} %shard_map.82.refs_3_), channel_id=1, source_target_pairs={{0,1},{4,39},{8,9},{12,47},{16,17},{20,55},{24,25},{28,63},{1,2},{... | collective-permute-start | bytes 3993608 | tf_op jit(solution)/shard_map/ppermute | solution.py:35
  6.4 16.8 %copy-start.3 = (f32[200]{0:T(256)S(1)}, f32[200]{0:T(256)}, u32[]{:S(2)}) copy-start(f32[200]{0:T(256)} %param.18) | copy-start | bytes 2404
  7.2 17.3 %copy-start.4 = (bf16[400]{0:T(512)(128)(2,1)S(1)}, bf16[400]{0:T(512)(128)(2,1)}, u32[]{:S(2)}) copy-start(bf16[400]{0:T(512)(128)(2,1)} %energy_ref.1) | copy-start | bytes 2404
  8.9 79.5 %collective-permute-start.8 = (bf16[4,4,160,128]{3,2,1,0:T(8,128)(2,1)}, bf16[4,4,160,128]{3,2,1,0:T(8,128)(2,1)}, u32[]{:S(2)}, u32[]{:S(2)}) collective-permute-start(bf16[4,4,160,128]{3,2,1,0:T(8,128)(2,1)} %shard_map.84), channel_id=1, source_target_pairs={{0,384},{4,388},{8,392},{12,396},{16,400},{20,404},{24,408},{28,41... | collective-permute-start | bytes 1966088 | tf_op jit(solution)/shard_map/ppermute | solution.py:35
  28.2 29.8 %collective-permute-start = (bf16[208,3200]{1,0:T(8,128)(2,1)}, bf16[208,3200]{1,0:T(8,128)(2,1)}, u32[]{:S(2)}, u32[]{:S(2)}) collective-permute-start(bf16[208,3200]{1,0:T(8,128)(2,1)} %get-tuple-element.29.in_ref), channel_id=1, source_target_pairs={{0,8},{4,28},{8,16},{12,4},{16,24},{20,12},{24,0},{28,20},{1,9},{5... | collective-permute-start | bytes 3993608 | tf_op jit(solution)/shard_map/cond/branch_1_fun/ppermute | solution.py:35
  33.6 15.1 %collective-permute-start.3 = (bf16[208,1664]{1,0:T(8,128)(2,1)}, bf16[208,1664]{1,0:T(8,128)(2,1)}, u32[]{:S(2)}, u32[]{:S(2)}) collective-permute-start(bf16[208,1664]{1,0:T(8,128)(2,1)} %branch_1_fun.5), channel_id=1, source_target_pairs={{0,1},{4,39},{8,9},{12,47},{16,17},{20,55},{24,25},{28,63},{1,2},{... | collective-permute-start | bytes 2076680 | tf_op jit(solution)/shard_map/cond/branch_1_fun/ppermute | solution.py:35
  37.1 22.9 %all-to-all-start = ((bf16[4,4,160,128]{3,2,1,0:T(8,128)(2,1)}), bf16[4,4,160,128]{3,2,1,0:T(8,128)(2,1)S(1)}, u32[]{:S(2)}, u32[]{:S(2)}) async-start(bf16[4,4,160,128]{3,2,1,0:T(8,128)(2,1)} %get-tuple-element.32), calls=%async_computation | async-start | bytes 1310720 | tf_op jit(solution)/shard_map/cond/branch_1_fun/all_to_all | solution.py:56
  48.7 23.6 %collective-permute-start.4 = (bf16[208,1664]{1,0:T(8,128)(2,1)}, bf16[208,1664]{1,0:T(8,128)(2,1)}, u32[]{:S(2)}, u32[]{:S(2)}) collective-permute-start(bf16[208,1664]{1,0:T(8,128)(2,1)} %collective-permute-done.3), channel_id=1, source_target_pairs={{0,8},{4,28},{8,16},{12,4},{16,24},{20,12},{24,0},{28,20},{1,9},{5... | collective-permute-start | bytes 2076680 | tf_op jit(solution)/shard_map/cond/branch_1_fun/ppermute | solution.py:35
  54.3 23.3 %collective-permute-start.1 = (bf16[208,3200]{1,0:T(8,128)(2,1)}, bf16[208,3200]{1,0:T(8,128)(2,1)}, u32[]{:S(2)}, u32[]{:S(2)}) collective-permute-start(bf16[208,3200]{1,0:T(8,128)(2,1)} %get-tuple-element.29.in_ref), channel_id=1, source_target_pairs={{0,4},{4,0},{8,12},{12,8},{16,20},{20,16},{24,28},{28,24},{1,5},{5... | collective-permute-start | bytes 3993608 | tf_op jit(solution)/shard_map/cond/branch_1_fun/ppermute | solution.py:35
  58.0 30.5 %collective-permute-start.2 = (bf16[208,3200]{1,0:T(8,128)(2,1)}, bf16[208,3200]{1,0:T(8,128)(2,1)}, u32[]{:S(2)}, u32[]{:S(2)}) collective-permute-start(bf16[208,3200]{1,0:T(8,128)(2,1)} %collective-permute-done), channel_id=1, source_target_pairs={{0,4},{4,0},{8,12},{12,8},{16,20},{20,16},{24,28},{28,24},{1,5},{5... | collective-permute-start | bytes 3993608 | tf_op jit(solution)/shard_map/cond/branch_1_fun/ppermute | solution.py:35
  61.4 27.1 %all-to-all-start.1 = ((bf16[4,4,160,128]{3,2,1,0:T(8,128)(2,1)}), bf16[4,4,160,128]{3,2,1,0:T(8,128)(2,1)}, u32[]{:S(2)}, u32[]{:S(2)}) async-start(bf16[4,4,160,128]{3,2,1,0:T(8,128)(2,1)} %branch_1_fun.6), calls=%async_computation.1 | async-start | bytes 1310720 | tf_op jit(solution)/shard_map/cond/branch_1_fun/all_to_all | solution.py:56
  70.4 7.3 %collective-permute-start.5 = (bf16[208,1664]{1,0:T(8,128)(2,1)}, bf16[208,1664]{1,0:T(8,128)(2,1)}, u32[]{:S(2)}, u32[]{:S(2)}) collective-permute-start(bf16[208,1664]{1,0:T(8,128)(2,1)} %collective-permute-done.3), channel_id=1, source_target_pairs={{0,4},{4,0},{8,12},{12,8},{16,20},{20,16},{24,28},{28,24},{1,5},{5... | collective-permute-start | bytes 2076680 | tf_op jit(solution)/shard_map/cond/branch_1_fun/ppermute | solution.py:35
  72.3 16.2 %collective-permute-start.6 = (bf16[208,1664]{1,0:T(8,128)(2,1)}, bf16[208,1664]{1,0:T(8,128)(2,1)}, u32[]{:S(2)}, u32[]{:S(2)}) collective-permute-start(bf16[208,1664]{1,0:T(8,128)(2,1)} %collective-permute-done.4), channel_id=1, source_target_pairs={{0,4},{4,0},{8,12},{12,8},{16,20},{20,16},{24,28},{28,24},{1,5},{5... | collective-permute-start | bytes 2076680 | tf_op jit(solution)/shard_map/cond/branch_1_fun/ppermute | solution.py:35
  101.2 34.6 %collective-permute-start.9 = (bf16[4,2,160,128]{3,2,1,0:T(8,128)(2,1)}, bf16[4,2,160,128]{3,2,1,0:T(8,128)(2,1)S(1)}, u32[]{:S(2)}, u32[]{:S(2)}) collective-permute-start(bf16[4,2,160,128]{3,2,1,0:T(8,128)(2,1)} %get-tuple-element.90), channel_id=1, source_target_pairs={{0,384},{4,388},{8,392},{12,396},{16,400},{20,404},{24,408},{28,41... | collective-permute-start | bytes 983048 | tf_op jit(solution)/shard_map/ppermute | solution.py:35

commit v8 on v6

--- a/solution.py
+++ b/solution.py
@@ -1,3 +1,5 @@
+import functools
+
 import jax
 import jax.numpy as jnp
 from jax import lax
@@ -147,32 +149,28 @@
     return jnp.pad(tile, ((0, 56), (0, 56))).T[0:W, 0:W]
 
 
-def tiles_kernel(pick_ref, amp_ref, int_ref, *refs):
-    *outs, unit = refs
+def tiles_kernel(turn, pick_ref, amp_ref, int_ref, out_ref, unit):
     unit[3 * W : UNIT, :] = jnp.zeros((UNIT - 3 * W, 128), F32)
     j = pl.program_id(0)
     for kind, ref in enumerate((amp_ref, int_ref)):
         for block in range(2):
-            put_tile(unit, block, ref[0, block].astype(F32))
+            tile = ref[0, block].astype(F32)
+            put_tile(unit, block, turned(tile) if turn else tile)
         for i in range(4):
-            piece = unit[i * PIECE : (i + 1) * PIECE, :].astype(BF)
-            if len(outs) == 2:
-                outs[kind][i, j] = piece
-            else:
-                outs[0][i, 2 * kind + j] = piece
-
-
-def pack_tiles(pick, amplitudes, integrals, arrays):
+            out_ref[i, 2 * kind + j] = unit[i * PIECE : (i + 1) * PIECE, :].astype(BF)
+
+
+def pack_tiles(pick, amplitudes, integrals, turn):
     tile = pl.BlockSpec((1, 2, W, W), lambda j, pick: (pick[j], 0, 0, 0))
-    shape = (4, 4 // arrays, PIECE, 128)
+    shape = (4, 4, PIECE, 128)
     return pl.pallas_call(
-        tiles_kernel,
-        out_shape=[jax.ShapeDtypeStruct(shape, BF)] * arrays,
+        functools.partial(tiles_kernel, turn),
+        out_shape=jax.ShapeDtypeStruct(shape, BF),
         grid_spec=pltpu.PrefetchScalarGridSpec(
             num_scalar_prefetch=1,
             grid=(2,),
             in_specs=[tile, tile],
-            out_specs=[pl.BlockSpec(shape, lambda j, pick: (0, 0, 0, 0))] * arrays,
+            out_specs=pl.BlockSpec(shape, lambda j, pick: (0, 0, 0, 0)),
             scratch_shapes=[pltpu.VMEM((UNIT, 128), F32)],
         ),
         compiler_params=params("arbitrary"),
@@ -180,26 +178,50 @@
     )(pick, amplitudes, integrals)
 
 
-def half_kernel(flip_ref, slab_ref, local_ref, cross_ref, half_ref, int_ref):
+def half_kernel(flip_ref, slab_ref, local_ref, cross_ref, half_ref, int_ref, *refs):
+    local, cross, slab, unit_sem, slab_sem = refs
+    copies = []
+    for i in range(4):
+        copies.append(pltpu.make_async_copy(local_ref.at[i], local.at[i], unit_sem.at[0, i]))
+        copies.append(pltpu.make_async_copy(cross_ref.at[i], cross.at[i], unit_sem.at[1, i]))
+    parts = [
+        [
+            pltpu.make_async_copy(
+                slab_ref.at[pl.ds(4 * i, 4), b], slab.at[b, pl.ds(4 * i, 4)], slab_sem.at[b, i]
+            )
+            for i in range(4)
+        ]
+        for b in range(2)
+    ]
+    for copy in (*copies, *parts[0], *parts[1]):
+        copy.start()
+    for copy in copies:
+        copy.wait()
+
     @pl.loop(0, 2)
     def _(j):
         straight = flip_ref[j] == 0
 
         def sums(at):
-            local, cross = whole_unit(at, local_ref), whole_unit(at, cross_ref)
-            tiles = [get_tile(cross, b) for b in range(2)]
+            here, there = whole_unit(at, local), whole_unit(at, cross)
+            tiles = [get_tile(there, b) for b in range(2)]
             return [
-                get_tile(local, b) + turned(jnp.where(straight, tiles[b], tiles[1 - b]))
-                for b in range(2)
+                get_tile(here, b) + jnp.where(straight, tiles[b], tiles[1 - b]) for b in range(2)
             ]
 
         for b, tile in enumerate(sums(2 + j)):
             int_ref[2 * j + b] = tile
         for b, tile in enumerate(sums(j)):
             both = tile.astype(BF)
+
+            @pl.when(j == 0)
+            def _():
+                for copy in parts[b]:
+                    copy.wait()
+
             for q in range(NQ):
                 half_ref[2 * j + b, :, q * W : (q + 1) * W] = jnp.dot(
-                    slab_ref[q, b], both, preferred_element_type=F32
+                    slab[b, q], both, preferred_element_type=F32
                 ).astype(BF)
 
 
@@ -207,59 +229,85 @@
     return pl.pallas_call(
         half_kernel,
         out_shape=(pltpu.VMEM((4, W, DEEP), BF), pltpu.VMEM((4, W, W), F32)),
-        in_specs=[SCALARS] + [WHOLE] * 3,
+        in_specs=[SCALARS] + [pl.BlockSpec(memory_space=pl.ANY)] * 3,
         out_specs=[WHOLE, WHOLE],
+        scratch_shapes=[
+            pltpu.VMEM((4, 4, PIECE, 128), BF),
+            pltpu.VMEM((4, 4, PIECE, 128), BF),
+            pltpu.VMEM((2, NQ, W, W), BF),
+            pltpu.SemaphoreType.DMA((2, 4)),
+            pltpu.SemaphoreType.DMA((2, 4)),
+        ],
         compiler_params=params(),
         cost_estimate=cost(8 * NQ * W**3, 4_000_000),
     )(flip, slab, local, cross)
 
 
+CHUNKS = ((0, 64), (64, 48), (112, 48), (160, 48))
+
+
 def ladder_kernel(source_ref, core_ref, half_ref, int_ref, *refs):
-    full, (near, near_x, far, far_x), (out_ref, table_ref, unit, sums) = (
-        refs[:6], refs[6:10], refs[10:]
-    )
-    even = core_ref[0] == 0
-    odd = core_ref[0] != 0
+    full, (near, near_x, far, far_x), (out_ref, table_ref, *refs) = refs[:6], refs[6:10], refs[10:]
+    right, rows, unit, right_sem, row_sem = refs
+    even, odd = core_ref[0] == 0, core_ref[0] != 0
     split = ((even, near, far), (even, near_x, far_x), (odd, far, near), (odd, far_x, near_x))
-    dims = (((1,), (1,)), ((), ()))
-
-    @pl.loop(0, 4)
-    def _(t):
+
+    for t in range(4):
         for r in range(6):
 
             @pl.when(source_ref[t] == r)
             def _():
-                sums[t] = lax.dot_general(
-                    half_ref[t], full[r][0:W, :], dims, preferred_element_type=F32
-                )
+                for i, chunk in enumerate(CHUNKS):
+                    here = pl.ds(*chunk)
+                    pltpu.make_async_copy(
+                        full[r].at[here], right.at[t, here], right_sem.at[t, i]
+                    ).start()
 
         for r, (on, low, high) in enumerate(split):
 
             @pl.when(jnp.logical_and(on, source_ref[t] == 6 + r % 2))
             def _():
-                sums[t] = lax.dot_general(
-                    half_ref[t, :, 0:PART], low[0:W, :], dims, preferred_element_type=F32
-                ) + lax.dot_general(
-                    half_ref[t, :, PART:DEEP],
-                    high[0:W, 2 * PART - DEEP : PART],
-                    dims,
-                    preferred_element_type=F32,
-                )
-
+                for i, chunk in enumerate(CHUNKS):
+                    here = pl.ds(*chunk)
+                    pltpu.make_async_copy(
+                        low.at[here], right.at[t, here, pl.ds(0, PART)], right_sem.at[t, i]
+                    ).start()
+                    pltpu.make_async_copy(
+                        high.at[here, pl.ds(2 * PART - DEEP, DEEP - PART)],
+                        right.at[t, here, pl.ds(PART, DEEP - PART)],
+                        right_sem.at[t, i],
+                    ).start()
+
+    corner = (pl.ds(TALL - 16, 16), pl.ds(0, 256))
     for r in range(6):
-        table_ref[r] = full[r][W:TALL, 0:W].astype(F32)
+        pltpu.make_async_copy(full[r].at[corner], rows.at[r], row_sem.at[r]).start()
     for r, (on, low, _) in enumerate(split):
 
         @pl.when(on)
         def _():
-            table_ref[6 + r % 2] = low[W:TALL, 0:W].astype(F32)
+            pltpu.make_async_copy(low.at[corner], rows.at[6 + r % 2], row_sem.at[6 + r % 2]).start()
 
     unit[3 * W : UNIT, :] = jnp.zeros((UNIT - 3 * W, 128), F32)
-    for j in range(2):
+
+    @pl.loop(0, 2)
+    def _(j):
         for b in range(2):
-            put_tile(unit, b, int_ref[2 * j + b] + sums[2 * j + b])
+            t = 2 * j + b
+            for i, chunk in enumerate(CHUNKS):
+                here = pl.ds(*chunk)
+                pltpu.make_async_copy(
+                    full[0].at[here], right.at[t, here], right_sem.at[t, i]
+                ).wait()
+            ladder = lax.dot_general(
+                half_ref[t], right[t, 0:W, :], (((1,), (1,)), ((), ())), preferred_element_type=F32
+            )
+            put_tile(unit, b, int_ref[t] + ladder)
         for i in range(4):
             out_ref[i, j] = unit[i * PIECE : (i + 1) * PIECE, :].astype(BF)
+
+    for r in range(8):
+        pltpu.make_async_copy(full[0].at[corner], rows.at[r], row_sem.at[r]).wait()
+        table_ref[r] = rows[r].astype(F32)[8:16, 0:W]
 
 
 def symmetric_units(source, core, half_done, integrals, full, parts):
@@ -269,12 +317,18 @@
             jax.ShapeDtypeStruct((4, 2, PIECE, 128), BF),
             jax.ShapeDtypeStruct((8, TALL - W, W), F32),
         ),
-        in_specs=[SCALARS, SCALARS] + [WHOLE] * 12,
+        in_specs=[SCALARS] * 2 + [WHOLE] * 2 + [pl.BlockSpec(memory_space=pl.ANY)] * 10,
         out_specs=[WHOLE] * 2,
-        scratch_shapes=[pltpu.VMEM((UNIT, 128), F32), pltpu.VMEM((4, W, W), F32)],
+        scratch_shapes=[
+            pltpu.VMEM((4, TALL, DEEP), BF),
+            pltpu.VMEM((8, 16, 256), BF),
+            pltpu.VMEM((UNIT, 128), F32),
+            pltpu.SemaphoreType.DMA((4, 4)),
+            pltpu.SemaphoreType.DMA((8,)),
+        ],
         compiler_params=params(),
-        cost_estimate=cost(8 * NQ * W**3, 3_000_000),
-    )(source, core, *in_vmem(half_done, integrals, *full, *parts))
+        cost_estimate=cost(8 * NQ * W**3, 6_000_000),
+    )(source, core, *in_vmem(half_done, integrals), *full, *parts)
 
 
 def update_kernel(
@@ -285,7 +339,7 @@
 
     def finish(block, symmetric):
         far = table_ref[source_ref[2 * p + block], 0:1, :]
-        denominator = pair_ref[p] - near_ref[block] - far
+        denominator = pair_ref[p] - near_ref[block, :, 0:1] - far
         old = amp_ref[0, block].astype(F32)
         out_ref[0, block] = (old + symmetric / denominator).astype(BF)
 
@@ -320,7 +374,7 @@
                 pl.BlockSpec((4, 1, PIECE, 128), pick),
                 pl.BlockSpec((4, 1, PIECE, 128), pick),
                 pl.BlockSpec((8, TALL - W, W), fixed),
-                pl.BlockSpec((2, W, 1), fixed),
+                pl.BlockSpec((2, W, 128), fixed),
             ],
             out_specs=pl.BlockSpec((1, 2, W, W), here),
         ),
@@ -354,14 +408,14 @@
 
     one = pack_slab(slab, virt_energy, parity[None])
     y_one = along_y(one)
-    local = to_mirror(pack_tiles(send, amp, ints, 1)[0])
-    kept_tiles = pack_tiles(keep, amp, ints, 1)[0]
+    local = to_mirror(pack_tiles(send, amp, ints, False))
+    kept_tiles = pack_tiles(keep, amp, ints, True)
 
     irrep = jnp.bitwise_xor(occ_irrep[pair_list[:, 0]], occ_irrep[pair_list[:, 1]])
     step, flip = jnp.right_shift(irrep, 1), jnp.bitwise_and(irrep, 1)
     keep_step, keep_flip = among(step, upper), among(flip, upper)
     pair_energy = occ_energy[pair_list[:, 0]] + occ_energy[pair_list[:, 1]]
-    near = virt_energy.astype(F32).reshape(2, W, 1)
+    near = jnp.broadcast_to(virt_energy.astype(F32).reshape(2, W, 1), (2, W, 128))
 
     def sources(step, flip):
         apart = jnp.bitwise_and(jnp.bitwise_xor(virt, step) - virt, 3)[:, None]
@@ -399,7 +453,8 @@
         keep_source, core[None], half_done, both_ints, full, parts
     )
     mirrored = to_mirror(result)
-    crossed = as_unit(ready, lambda x: exchange(reorder(exchange(x), keep_step)), result)
+    scattered = exchange(result)
+    crossed = as_unit(ready, lambda x: exchange(reorder(x, keep_step)), scattered)
     new = update(
         kept, at, flip, source, pair_energy, amp, crossed, mirrored, table, near
     )

time: 133 us -> 134 us (level)
  the two profiles are of different devices: /device:TPU:56 before, /device:TPU:120 now
where the time goes in v8:
time: 134 us; the launch traced here: 133 us
  starting transfers between devices  60.7 us (45%)
  Pallas kernels  25.9 us (19%)
  waiting for transfers between devices  23.7 us (18%)
  blocking collectives  13.4 us (10%)
  local copies, waits for them, and re-layouts  7.71 us (6%)
    ppermute x10, starting transfers between devices, permute(): return lax.ppermute(value, ('pair', 'virt'), pairs)  41 us
    ppermute x10, waiting for transfers between devices, permute(): return lax.ppermute(value, ('pair', 'virt'), pairs)  21.1 us
    all_to_all x3, starting transfers between devices, exchange(): return lax.all_to_all(units, 'virt', 0, 0, tiled=True)  19.7 us
    all_to_all x1, blocking collectives, exchange(): return lax.all_to_all(units, 'virt', 0, 0, tiled=True)  13.4 us
    pallas_call x1, Pallas kernels, first_half(): pl.pallas_call(half_kernel, out_shape=(pltpu.VMEM((4, W, DEEP), BF), pltp...  7.12 us
    pallas_call x1, Pallas kernels, symmetric_units(): pl.pallas_call(ladder_kernel, out_shape=(jax.ShapeDtypeStruct((4, 2, PIEC...  6.8 us
    pallas_call x2, Pallas kernels, pack_slab(): pl.pallas_call(pack_kernel, out_shape=jax.ShapeDtypeStruct((TALL, DEEP),...  4.94 us
    pallas_call x2, Pallas kernels, pack_tiles(): pl.pallas_call(functools.partial(tiles_kernel, turn), out_shape=jax.Shape...  3.87 us
  transfers between devices with their start and end apart: 13, of which 4 were waited for; matrix products, arithmetic and copies ran while one was open for 6% of the time, Pallas kernels for 11%

profile of v8, /device:TPU:120, one launch (start us, length us, event | category | flops | bytes accessed | tf_op | source)
XLA Modules:
  0.0 132.8 jit_solution(6498638952865030383)
XLA Ops:
  0.0 2.0 %shard_map.82.refs_0_ = bf16[208,3200]{1,0:T(8,128)(2,1)S(1)} custom-call(s32[1]{0:T(128)} %bitcast.5.order_ref, bf16[16,2,200,200]{3,2,1,0:T(8,128)(2,1)} %bitcast.23, bf16[400]{0:T(512)(128)(2,1)} %energy_ref.1), custom_call_target="tpu_custom_call" | custom-call | bytes 3000000 | tf_op jit(solution)/shard_map/pallas_call | solution.py:102
  2.0 0.0 copy-start.1
  2.0 2.1 %collective-permute-start.6 = (bf16[208,3200]{1,0:T(8,128)(2,1)S(1)}, bf16[208,3200]{1,0:T(8,128)(2,1)}, u32[]{:S(2)}, u32[]{:S(2)}) collective-permute-start(bf16[208,3200]{1,0:T(8,128)(2,1)S(1)} %shard_map.82.refs_0_), channel_id=1, source_target_pairs={{0,1},{4,39},{8,9},{12,47},{16,17},{20,55},{24,25},{28,63},{1,2},{... | collective-permute-start | bytes 3993608 | tf_op jit(solution)/shard_map/ppermute | solution.py:35
  4.2 0.6 gather_fusion.2
  4.8 0.6 gather_fusion.3
  5.5 0.1 fusion.8
  5.6 0.0 copy-start.4
  5.6 1.8 %shard_map.84 = bf16[4,4,160,128]{3,2,1,0:T(8,128)(2,1)} custom-call(s32[2]{0:T(128)S(1)} %get-tuple-element.96.pick_ref, bf16[4,2,200,200]{3,2,1,0:T(8,128)(2,1)S(1)} %bitcast.18, bf16[4,2,200,200]{3,2,1,0:T(8,128)(2,1)S(1)} %bitcast.21), custom_call_target="tpu_custom_call" | custom-call | bytes 1500000 | tf_op jit(solution)/shard_map/pallas_call | solution.py:166
  7.4 14.2 %collective-permute-start.7 = (bf16[4,4,160,128]{3,2,1,0:T(8,128)(2,1)}, bf16[4,4,160,128]{3,2,1,0:T(8,128)(2,1)}, u32[]{:S(2)}, u32[]{:S(2)}) collective-permute-start(bf16[4,4,160,128]{3,2,1,0:T(8,128)(2,1)} %shard_map.84), channel_id=1, source_target_pairs={{0,384},{4,388},{8,392},{12,396},{16,400},{20,404},{24,408},{28,41... | collective-permute-start | bytes 1966088 | tf_op jit(solution)/shard_map/ppermute | solution.py:35
  21.6 0.6 gather_fusion.4
  22.3 0.6 gather_fusion.5
  22.9 0.1 reshape.181
  23.0 0.5 slice.13
  23.5 2.1 %shard_map.83 = bf16[4,4,160,128]{3,2,1,0:T(8,128)(2,1)} custom-call(s32[2]{0:T(128)S(1)} %get-tuple-element.95.pick_ref, bf16[4,2,200,200]{3,2,1,0:T(8,128)(2,1)S(1)} %bitcast.19, bf16[4,2,200,200]{3,2,1,0:T(8,128)(2,1)S(1)} %bitcast.22), custom_call_target="tpu_custom_call" | custom-call | bytes 1500000 | tf_op jit(solution)/shard_map/pallas_call | solution.py:166
  25.6 0.1 fusion.9
  25.7 0.1 add.95.source_ref
  25.8 0.1 add.98.source_ref
  26.5 0.0 collective-permute-done.6.refs_2_
  26.5 0.1 broadcast_in_dim.116.near_ref
  26.6 49.2 %conditional.2 = (bf16[208,3200]{1,0:T(8,128)(2,1)}, bf16[208,3200]{1,0:T(8,128)(2,1)}, bf16[208,3200]{1,0:T(8,128)(2,1)}, bf16[208,3200]{1,0:T(8,128)(2,1)}, bf...) conditional(s32[]{:T(128)} %bitcast.9, () %tuple.23, ...), branch_computations={%region_3.4_spmd, %region_4.5_spmd} | conditional | flops 153 | bytes 33909204 | solution.py:72
  26.7 3.4 %collective-permute-start = (bf16[208,3200]{1,0:T(8,128)(2,1)}, bf16[208,3200]{1,0:T(8,128)(2,1)}, u32[]{:S(2)}, u32[]{:S(2)}) collective-permute-start(bf16[208,3200]{1,0:T(8,128)(2,1)} %get-tuple-element.29), channel_id=1, source_target_pairs={{0,8},{4,28},{8,16},{12,4},{16,24},{20,12},{24,0},{28,20},{1,9},{5... | collective-permute-start | bytes 3993608 | tf_op jit(solution)/shard_map/cond/branch_1_fun/ppermute | solution.py:35
  30.1 7.0 %all-to-all-start = ((bf16[4,4,160,128]{3,2,1,0:T(8,128)(2,1)}), bf16[4,4,160,128]{3,2,1,0:T(8,128)(2,1)S(1)}, u32[]{:S(2)}, u32[]{:S(2)}) async-start(bf16[4,4,160,128]{3,2,1,0:T(8,128)(2,1)} %get-tuple-element.31), calls=%async_computation | async-start | bytes 1310720 | tf_op jit(solution)/shard_map/cond/branch_1_fun/all_to_all | solution.py:56
  37.1 2.0 %constant_dynamic-slice_fusion = bf16[208,1664]{1,0:T(8,128)(2,1)} fusion(bf16[208,3200]{1,0:T(8,128)(2,1)} %get-tuple-element.29, s32[]{:T(128)S(6)} %select_n.91), kind=kLoop, calls=%fused_computation.11 | loop fusion | bytes 1384452 | tf_op jit(solution)/shard_map/cond/branch_1_fun/dynamic_slice | solution.py:438
  39.1 2.3 %collective-permute-start.3 = (bf16[208,1664]{1,0:T(8,128)(2,1)}, bf16[208,1664]{1,0:T(8,128)(2,1)}, u32[]{:S(2)}, u32[]{:S(2)}) collective-permute-start(bf16[208,1664]{1,0:T(8,128)(2,1)} %constant_dynamic-slice_fusion), channel_id=1, source_target_pairs={{0,1},{4,39},{8,9},{12,47},{16,17},{20,55},{24,25},{28,63},{1,2},{... | collective-permute-start | bytes 2076680 | tf_op jit(solution)/shard_map/cond/branch_1_fun/ppermute | solution.py:35
  41.4 1.9 %collective-permute-start.1 = (bf16[208,3200]{1,0:T(8,128)(2,1)}, bf16[208,3200]{1,0:T(8,128)(2,1)}, u32[]{:S(2)}, u32[]{:S(2)}) collective-permute-start(bf16[208,3200]{1,0:T(8,128)(2,1)} %get-tuple-element.29), channel_id=1, source_target_pairs={{0,4},{4,0},{8,12},{12,8},{16,20},{20,16},{24,28},{28,24},{1,5},{5... | collective-permute-start | bytes 3993608 | tf_op jit(solution)/shard_map/cond/branch_1_fun/ppermute | solution.py:35
  43.3 4.6 %collective-permute-done = bf16[208,3200]{1,0:T(8,128)(2,1)} collective-permute-done((bf16[208,3200]{1,0:T(8,128)(2,1)}, bf16[208,3200]{1,0:T(8,128)(2,1)}, u32[]{:S(2)}, u32[]{:S(2)}) %collective-permute-start) | collective-permute-done | bytes 1331232 | tf_op jit(solution)/shard_map/cond/branch_1_fun/ppermute | solution.py:35
  47.9 1.9 %collective-permute-start.2 = (bf16[208,3200]{1,0:T(8,128)(2,1)}, bf16[208,3200]{1,0:T(8,128)(2,1)}, u32[]{:S(2)}, u32[]{:S(2)}) collective-permute-start(bf16[208,3200]{1,0:T(8,128)(2,1)} %collective-permute-done), channel_id=1, source_target_pairs={{0,4},{4,0},{8,12},{12,8},{16,20},{20,16},{24,28},{28,24},{1,5},{5... | collective-permute-start | bytes 3993608 | tf_op jit(solution)/shard_map/cond/branch_1_fun/ppermute | solution.py:35
  49.8 0.1 pad_add_fusion
  49.9 0.1 reshape.183
  50.0 2.6 %all-to-all-done = bf16[4,4,160,128]{3,2,1,0:T(8,128)(2,1)S(1)} async-done(((bf16[4,4,160,128]{3,2,1,0:T(8,128)(2,1)}), bf16[4,4,160,128]{3,2,1,0:T(8,128)(2,1)S(1)}, u32[]{:S(2)}, u32[]{:S(2)}) %all-to-all-start) | async-done | bytes 655392 | tf_op jit(solution)/shard_map/cond/branch_1_fun/all_to_all | solution.py:56
  52.6 1.5 %gather_fusion = bf16[16,160,128]{2,1,0:T(8,128)(2,1)} fusion(bf16[4,4,160,128]{3,2,1,0:T(8,128)(2,1)S(1)} %all-to-all-done, s32[16]{0:T(128)S(1)} %reshape.183), kind=kCustom, calls=%fused_computation | custom fusion | bytes 1310848 | tf_op jit(solution)/shard_map/cond/branch_1_fun/gather | solution.py:61
  54.1 7.3 %all-to-all-start.1 = ((bf16[4,4,160,128]{3,2,1,0:T(8,128)(2,1)}), bf16[4,4,160,128]{3,2,1,0:T(8,128)(2,1)}, u32[]{:S(2)}, u32[]{:S(2)}) async-start(bf16[4,4,160,128]{3,2,1,0:T(8,128)(2,1)} %bitcast.26), calls=%async_computation.1 | async-start | bytes 1310720 | tf_op jit(solution)/shard_map/cond/branch_1_fun/all_to_all | solution.py:56
  61.4 0.0 collective-permute-done.3
  61.4 1.9 %collective-permute-start.4 = (bf16[208,1664]{1,0:T(8,128)(2,1)}, bf16[208,1664]{1,0:T(8,128)(2,1)}, u32[]{:S(2)}, u32[]{:S(2)}) collective-permute-start(bf16[208,1664]{1,0:T(8,128)(2,1)} %collective-permute-done.3), channel_id=1, source_target_pairs={{0,8},{4,28},{8,16},{12,4},{16,24},{20,12},{24,0},{28,20},{1,9},{5... | collective-permute-start | bytes 2076680 | tf_op jit(solution)/shard_map/cond/branch_1_fun/ppermute | solution.py:35
  63.3 1.9 %collective-permute-start.5 = (bf16[208,1664]{1,0:T(8,128)(2,1)}, bf16[208,1664]{1,0:T(8,128)(2,1)}, u32[]{:S(2)}, u32[]{:S(2)}) collective-permute-start(bf16[208,1664]{1,0:T(8,128)(2,1)} %collective-permute-done.3), channel_id=1, source_target_pairs={{0,4},{4,0},{8,12},{12,8},{16,20},{20,16},{24,28},{28,24},{1,5},{5... | collective-permute-start | bytes 2076680 | tf_op jit(solution)/shard_map/cond/branch_1_fun/ppermute | solution.py:35
  65.3 3.0 %branch_1_fun.1 = bf16[208,3200]{1,0:T(8,128)(2,1)} custom-call(s32[1]{0:T(128)} %bitcast.order_ref, bf16[16,2,200,200]{3,2,1,0:T(8,128)(2,1)} %get-tuple-element.27.slab_ref, bf16[400]{0:T(512)(128)(2,1)S(1)} %get-tuple-element.28.energy_ref), custom_call_target="tpu_custom_call" | custom-call | bytes 3000000 | tf_op jit(solution)/shard_map/cond/branch_1_fun/pallas_call | solution.py:102
  68.2 7.6 %collective-permute-done.4 = bf16[208,1664]{1,0:T(8,128)(2,1)} collective-permute-done((bf16[208,1664]{1,0:T(8,128)(2,1)}, bf16[208,1664]{1,0:T(8,128)(2,1)}, u32[]{:S(2)}, u32[]{:S(2)}) %collective-permute-start.4) | collective-permute-done | bytes 692256 | tf_op jit(solution)/shard_map/cond/branch_1_fun/ppermute | solution.py:35
  75.8 1.9 %collective-permute-start.8 = (bf16[208,1664]{1,0:T(8,128)(2,1)}, bf16[208,1664]{1,0:T(8,128)(2,1)S(1)}, u32[]{:S(2)}, u32[]{:S(2)}) collective-permute-start(bf16[208,1664]{1,0:T(8,128)(2,1)} %get-tuple-element.88.refs_7_), channel_id=1, source_target_pairs={{0,4},{4,0},{8,12},{12,8},{16,20},{20,16},{24,28},{28,24},{1,5},{5... | collective-permute-start | bytes 2076680 | tf_op jit(solution)/shard_map/ppermute | solution.py:35
  77.8 7.1 %shard_map.85 = (bf16[4,200,3200]{2,1,0:T(8,128)(2,1)S(1)}, f32[4,200,200]{2,1,0:T(8,128)S(1)}) custom-call(s32[2]{0:T(128)S(1)} %get-tuple-element.68.flip_ref, bf16[16,2,200,200]{3,2,1,0:T(8,128)(2,1)} %bitcast.25, bf16[4,4,160,128]{3,2,1,0:T(8,128)(2,1)} %collective-permute-done.7.local_ref, bf16[4,4,160,128]{3,2,1,0:T(8,128)(2,1)} %get-tuple-element.80.cross_ref), custom_call_target="tpu_custom_call" | custom-call | flops 1024000000 | bytes 4000000 | tf_op jit(solution)/shard_map/pallas_call | solution.py:229
  84.9 6.8 %shard_map.86 = (bf16[4,2,160,128]{3,2,1,0:T(8,128)(2,1)}, f32[8,8,200]{2,1,0:T(8,128)S(1)}) custom-call(s32[4]{0:T(128)S(1)} %add.95.source_ref, s32[1]{0:T(128)} %bitcast.10.core_ref, bf16[4,200,3200]{2,1,0:T(8,128)(2,1)S(1)} %get-tuple-element.81.half_ref, f32[4,200,200]{2,1,0:T(8,128)S(1)} %get-tuple-element.82.int_ref, ...), custom_call_target="tpu_custom_call" | custom-call | flops 1024000000 | bytes 6000000 | tf_op jit(solution)/shard_map/pallas_call | solution.py:314
  91.7 5.3 %all-to-all-start.3 = ((bf16[4,2,160,128]{3,2,1,0:T(8,128)(2,1)}), bf16[4,2,160,128]{3,2,1,0:T(8,128)(2,1)S(1)}, u32[]{:S(2)}, u32[]{:S(2)}) async-start(bf16[4,2,160,128]{3,2,1,0:T(8,128)(2,1)} %get-tuple-element.90), calls=%async_computation.3 | async-start | bytes 655360 | tf_op jit(solution)/shard_map/all_to_all | solution.py:56
  97.0 9.5 %collective-permute-start.9 = (bf16[4,2,160,128]{3,2,1,0:T(8,128)(2,1)}, bf16[4,2,160,128]{3,2,1,0:T(8,128)(2,1)S(1)}, u32[]{:S(2)}, u32[]{:S(2)}) collective-permute-start(bf16[4,2,160,128]{3,2,1,0:T(8,128)(2,1)} %get-tuple-element.90), channel_id=1, source_target_pairs={{0,384},{4,388},{8,392},{12,396},{16,400},{20,404},{24,408},{28,41... | collective-permute-start | bytes 983048 | tf_op jit(solution)/shard_map/ppermute | solution.py:35
  106.5 14.1 %conditional.3 = (bf16[4,2,160,128]{3,2,1,0:T(8,128)(2,1)S(1)}) conditional(s32[]{:T(128)} %bitcast.9, () %tuple.22, (s32[2]{0:T(128)S(1)}, bf16[4,2,160,128]{3,2,1,0:T(8,128)(2,1)S(1)}) %tuple.26), branch_computations={%region_6.7_spmd, %region_7.8_spmd} | conditional | flops 72 | bytes 1310896 | solution.py:72
  106.6 0.1 reshape.189
  106.7 0.6 gather_fusion.1
  107.3 13.4 %all_to_all.17 = bf16[4,2,160,128]{3,2,1,0:T(8,128)(2,1)S(1)} all-to-all(bf16[4,2,160,128]{3,2,1,0:T(8,128)(2,1)S(1)} %bitcast.27), channel_id=1, replica_groups=mesh['pair'=192,'virt'=4] {'virt'}, dimensions={0} | all-to-all | bytes 655360 | tf_op jit(solution)/shard_map/cond/branch_1_fun/all_to_all | solution.py:56
  120.7 8.9 %collective-permute-done.9.mirror_ref = bf16[4,2,160,128]{3,2,1,0:T(8,128)(2,1)S(1)} collective-permute-done((bf16[4,2,160,128]{3,2,1,0:T(8,128)(2,1)}, bf16[4,2,160,128]{3,2,1,0:T(8,128)(2,1)S(1)}, u32[]{:S(2)}, u32[]{:S(2)}) %collective-permute-start.9) | collective-permute-done | bytes 327712 | tf_op jit(solution)/shard_map/ppermute | solution.py:35
  129.6 3.2 %shard_map.87 = bf16[4,2,200,200]{3,2,1,0:T(8,128)(2,1)} custom-call(s32[4]{0:T(128)S(1)} %compare_convert_fusion.1.kept_ref, s32[4]{0:T(128)S(1)} %get-tuple-element.99.at_ref, s32[4]{0:T(128)S(1)} %get-tuple-element.101.flip_ref, s32[8]{0:T(128)S(1)} %add.98.source_ref, f32[4]{0:T(128)S(1)} %add.92.pair_ref, bf16[4,2,200,200]{3,2,1,0:T(8,128)(2,1)S(1)} %bitcast.20, ...), custom_call_target="tpu_custom_call" | custom-call | tf_op jit(solution)/shard_map/pallas_call | solution.py:366
  (29 shorter events, 0.1 us)
Async XLA Ops:
  0.0 4.2 %copy-start = (s32[200]{0:T(256)S(1)}, s32[200]{0:T(256)}, u32[]{:S(2)}) copy-start(s32[200]{0:T(256)} %param.17) | copy-start | bytes 2404
  0.0 4.1 %copy-start.5 = (s32[4,2]{0,1:T(2,128)S(1)}, s32[4,2]{0,1:T(2,128)}, u32[]{:S(2)}) copy-start(s32[4,2]{0,1:T(2,128)} %param.15) | copy-start | bytes 100
  0.0 5.5 %copy-start.6 = (s32[4]{0:T(128)S(1)}, s32[4]{0:T(128)}, u32[]{:S(2)}) copy-start(s32[4]{0:T(128)} %param.16) | copy-start | bytes 52
  0.0 5.6 %copy-start.2 = (bf16[4,400,200]{2,1,0:T(8,128)(2,1)S(1)}, bf16[4,400,200]{2,1,0:T(8,128)(2,1)}, u32[]{:S(2)}) copy-start(bf16[4,400,200]{2,1,0:T(8,128)(2,1)} %param.13) | copy-start | bytes 1920004
  2.0 3.6 %copy-start.1 = (bf16[4,400,200]{2,1,0:T(8,128)(2,1)S(1)}, bf16[4,400,200]{2,1,0:T(8,128)(2,1)}, u32[]{:S(2)}) copy-start(bf16[4,400,200]{2,1,0:T(8,128)(2,1)} %param.12) | copy-start | bytes 1920004
  2.0 24.5 %collective-permute-start.6 = (bf16[208,3200]{1,0:T(8,128)(2,1)S(1)}, bf16[208,3200]{1,0:T(8,128)(2,1)}, u32[]{:S(2)}, u32[]{:S(2)}) collective-permute-start(bf16[208,3200]{1,0:T(8,128)(2,1)S(1)} %shard_map.82.refs_0_), channel_id=1, source_target_pairs={{0,1},{4,39},{8,9},{12,47},{16,17},{20,55},{24,25},{28,63},{1,2},{... | collective-permute-start | bytes 3993608 | tf_op jit(solution)/shard_map/ppermute | solution.py:35
  4.8 16.8 %copy-start.3 = (f32[200]{0:T(256)S(1)}, f32[200]{0:T(256)}, u32[]{:S(2)}) copy-start(f32[200]{0:T(256)} %param.18) | copy-start | bytes 2404
  5.6 17.3 %copy-start.4 = (bf16[400]{0:T(512)(128)(2,1)S(1)}, bf16[400]{0:T(512)(128)(2,1)}, u32[]{:S(2)}) copy-start(bf16[400]{0:T(512)(128)(2,1)} %energy_ref.1) | copy-start | bytes 2404
  7.4 68.5 %collective-permute-start.7 = (bf16[4,4,160,128]{3,2,1,0:T(8,128)(2,1)}, bf16[4,4,160,128]{3,2,1,0:T(8,128)(2,1)}, u32[]{:S(2)}, u32[]{:S(2)}) collective-permute-start(bf16[4,4,160,128]{3,2,1,0:T(8,128)(2,1)} %shard_map.84), channel_id=1, source_target_pairs={{0,384},{4,388},{8,392},{12,396},{16,400},{20,404},{24,408},{28,41... | collective-permute-start | bytes 1966088 | tf_op jit(solution)/shard_map/ppermute | solution.py:35
  26.7 21.2 %collective-permute-start = (bf16[208,3200]{1,0:T(8,128)(2,1)}, bf16[208,3200]{1,0:T(8,128)(2,1)}, u32[]{:S(2)}, u32[]{:S(2)}) collective-permute-start(bf16[208,3200]{1,0:T(8,128)(2,1)} %get-tuple-element.29), channel_id=1, source_target_pairs={{0,8},{4,28},{8,16},{12,4},{16,24},{20,12},{24,0},{28,20},{1,9},{5... | collective-permute-start | bytes 3993608 | tf_op jit(solution)/shard_map/cond/branch_1_fun/ppermute | solution.py:35
  30.1 22.6 %all-to-all-start = ((bf16[4,4,160,128]{3,2,1,0:T(8,128)(2,1)}), bf16[4,4,160,128]{3,2,1,0:T(8,128)(2,1)S(1)}, u32[]{:S(2)}, u32[]{:S(2)}) async-start(bf16[4,4,160,128]{3,2,1,0:T(8,128)(2,1)} %get-tuple-element.31), calls=%async_computation | async-start | bytes 1310720 | tf_op jit(solution)/shard_map/cond/branch_1_fun/all_to_all | solution.py:56
  39.1 22.3 %collective-permute-start.3 = (bf16[208,1664]{1,0:T(8,128)(2,1)}, bf16[208,1664]{1,0:T(8,128)(2,1)}, u32[]{:S(2)}, u32[]{:S(2)}) collective-permute-start(bf16[208,1664]{1,0:T(8,128)(2,1)} %constant_dynamic-slice_fusion), channel_id=1, source_target_pairs={{0,1},{4,39},{8,9},{12,47},{16,17},{20,55},{24,25},{28,63},{1,2},{... | collective-permute-start | bytes 2076680 | tf_op jit(solution)/shard_map/cond/branch_1_fun/ppermute | solution.py:35
  41.4 26.8 %collective-permute-start.1 = (bf16[208,3200]{1,0:T(8,128)(2,1)}, bf16[208,3200]{1,0:T(8,128)(2,1)}, u32[]{:S(2)}, u32[]{:S(2)}) collective-permute-start(bf16[208,3200]{1,0:T(8,128)(2,1)} %get-tuple-element.29), channel_id=1, source_target_pairs={{0,4},{4,0},{8,12},{12,8},{16,20},{20,16},{24,28},{28,24},{1,5},{5... | collective-permute-start | bytes 3993608 | tf_op jit(solution)/shard_map/cond/branch_1_fun/ppermute | solution.py:35
  47.9 27.9 %collective-permute-start.2 = (bf16[208,3200]{1,0:T(8,128)(2,1)}, bf16[208,3200]{1,0:T(8,128)(2,1)}, u32[]{:S(2)}, u32[]{:S(2)}) collective-permute-start(bf16[208,3200]{1,0:T(8,128)(2,1)} %collective-permute-done), channel_id=1, source_target_pairs={{0,4},{4,0},{8,12},{12,8},{16,20},{20,16},{24,28},{28,24},{1,5},{5... | collective-permute-start | bytes 3993608 | tf_op jit(solution)/shard_map/cond/branch_1_fun/ppermute | solution.py:35
  54.1 21.7 %all-to-all-start.1 = ((bf16[4,4,160,128]{3,2,1,0:T(8,128)(2,1)}), bf16[4,4,160,128]{3,2,1,0:T(8,128)(2,1)}, u32[]{:S(2)}, u32[]{:S(2)}) async-start(bf16[4,4,160,128]{3,2,1,0:T(8,128)(2,1)} %bitcast.26), calls=%async_computation.1 | async-start | bytes 1310720 | tf_op jit(solution)/shard_map/cond/branch_1_fun/all_to_all | solution.py:56
  61.4 14.4 %collective-permute-start.4 = (bf16[208,1664]{1,0:T(8,128)(2,1)}, bf16[208,1664]{1,0:T(8,128)(2,1)}, u32[]{:S(2)}, u32[]{:S(2)}) collective-permute-start(bf16[208,1664]{1,0:T(8,128)(2,1)} %collective-permute-done.3), channel_id=1, source_target_pairs={{0,8},{4,28},{8,16},{12,4},{16,24},{20,12},{24,0},{28,20},{1,9},{5... | collective-permute-start | bytes 2076680 | tf_op jit(solution)/shard_map/cond/branch_1_fun/ppermute | solution.py:35
  63.3 12.5 %collective-permute-start.5 = (bf16[208,1664]{1,0:T(8,128)(2,1)}, bf16[208,1664]{1,0:T(8,128)(2,1)}, u32[]{:S(2)}, u32[]{:S(2)}) collective-permute-start(bf16[208,1664]{1,0:T(8,128)(2,1)} %collective-permute-done.3), channel_id=1, source_target_pairs={{0,4},{4,0},{8,12},{12,8},{16,20},{20,16},{24,28},{28,24},{1,5},{5... | collective-permute-start | bytes 2076680 | tf_op jit(solution)/shard_map/cond/branch_1_fun/ppermute | solution.py:35
  75.8 9.1 %collective-permute-start.8 = (bf16[208,1664]{1,0:T(8,128)(2,1)}, bf16[208,1664]{1,0:T(8,128)(2,1)S(1)}, u32[]{:S(2)}, u32[]{:S(2)}) collective-permute-start(bf16[208,1664]{1,0:T(8,128)(2,1)} %get-tuple-element.88.refs_7_), channel_id=1, source_target_pairs={{0,4},{4,0},{8,12},{12,8},{16,20},{20,16},{24,28},{28,24},{1,5},{5... | collective-permute-start | bytes 2076680 | tf_op jit(solution)/shard_map/ppermute | solution.py:35
  91.7 14.8 %all-to-all-start.3 = ((bf16[4,2,160,128]{3,2,1,0:T(8,128)(2,1)}), bf16[4,2,160,128]{3,2,1,0:T(8,128)(2,1)S(1)}, u32[]{:S(2)}, u32[]{:S(2)}) async-start(bf16[4,2,160,128]{3,2,1,0:T(8,128)(2,1)} %get-tuple-element.90), calls=%async_computation.3 | async-start | bytes 655360 | tf_op jit(solution)/shard_map/all_to_all | solution.py:56
  97.0 32.6 %collective-permute-start.9 = (bf16[4,2,160,128]{3,2,1,0:T(8,128)(2,1)}, bf16[4,2,160,128]{3,2,1,0:T(8,128)(2,1)S(1)}, u32[]{:S(2)}, u32[]{:S(2)}) collective-permute-start(bf16[4,2,160,128]{3,2,1,0:T(8,128)(2,1)} %get-tuple-element.90), channel_id=1, source_target_pairs={{0,384},{4,388},{8,392},{12,396},{16,400},{20,404},{24,408},{28,41... | collective-permute-start | bytes 983048 | tf_op jit(solution)/shard_map/ppermute | solution.py:35

commit v9 on v6

--- a/solution.py
+++ b/solution.py
@@ -1,3 +1,5 @@
+import functools
+
 import jax
 import jax.numpy as jnp
 from jax import lax
@@ -147,71 +149,63 @@
     return jnp.pad(tile, ((0, 56), (0, 56))).T[0:W, 0:W]
 
 
-def tiles_kernel(pick_ref, amp_ref, int_ref, *refs):
-    *outs, unit = refs
+def tiles_kernel(turn, pick_ref, flip_ref, amp_ref, int_ref, out_ref, unit):
     unit[3 * W : UNIT, :] = jnp.zeros((UNIT - 3 * W, 128), F32)
     j = pl.program_id(0)
     for kind, ref in enumerate((amp_ref, int_ref)):
+        tiles = [ref[0, block].astype(F32) for block in range(2)]
+        if turn:
+            straight = flip_ref[j] == 0
+            tiles = [turned(jnp.where(straight, tiles[b], tiles[1 - b])) for b in range(2)]
         for block in range(2):
-            put_tile(unit, block, ref[0, block].astype(F32))
+            put_tile(unit, block, tiles[block])
         for i in range(4):
-            piece = unit[i * PIECE : (i + 1) * PIECE, :].astype(BF)
-            if len(outs) == 2:
-                outs[kind][i, j] = piece
-            else:
-                outs[0][i, 2 * kind + j] = piece
-
-
-def pack_tiles(pick, amplitudes, integrals, arrays):
-    tile = pl.BlockSpec((1, 2, W, W), lambda j, pick: (pick[j], 0, 0, 0))
-    shape = (4, 4 // arrays, PIECE, 128)
+            out_ref[i, 2 * kind + j] = unit[i * PIECE : (i + 1) * PIECE, :].astype(BF)
+
+
+def pack_tiles(pick, flip, amplitudes, integrals, turn):
+    tile = pl.BlockSpec((1, 2, W, W), lambda j, pick, flip: (pick[j], 0, 0, 0))
+    shape = (4, 4, PIECE, 128)
     return pl.pallas_call(
-        tiles_kernel,
-        out_shape=[jax.ShapeDtypeStruct(shape, BF)] * arrays,
+        functools.partial(tiles_kernel, turn),
+        out_shape=jax.ShapeDtypeStruct(shape, BF),
         grid_spec=pltpu.PrefetchScalarGridSpec(
-            num_scalar_prefetch=1,
+            num_scalar_prefetch=2,
             grid=(2,),
             in_specs=[tile, tile],
-            out_specs=[pl.BlockSpec(shape, lambda j, pick: (0, 0, 0, 0))] * arrays,
+            out_specs=pl.BlockSpec(shape, lambda j, pick, flip: (0, 0, 0, 0)),
             scratch_shapes=[pltpu.VMEM((UNIT, 128), F32)],
         ),
         compiler_params=params("arbitrary"),
         cost_estimate=cost(0, 1_500_000),
-    )(pick, amplitudes, integrals)
-
-
-def half_kernel(flip_ref, slab_ref, local_ref, cross_ref, half_ref, int_ref):
+    )(pick, flip, amplitudes, integrals)
+
+
+def half_kernel(slab_ref, local_ref, cross_ref, half_ref, int_ref):
+    for i in range(4):
+        for j in range(2):
+            int_ref[i, j] = local_ref[i, 2 + j].astype(F32) + cross_ref[i, 2 + j].astype(F32)
+
     @pl.loop(0, 2)
     def _(j):
-        straight = flip_ref[j] == 0
-
-        def sums(at):
-            local, cross = whole_unit(at, local_ref), whole_unit(at, cross_ref)
-            tiles = [get_tile(cross, b) for b in range(2)]
-            return [
-                get_tile(local, b) + turned(jnp.where(straight, tiles[b], tiles[1 - b]))
-                for b in range(2)
-            ]
-
-        for b, tile in enumerate(sums(2 + j)):
-            int_ref[2 * j + b] = tile
-        for b, tile in enumerate(sums(j)):
-            both = tile.astype(BF)
+        unit = whole_unit(j, local_ref) + whole_unit(j, cross_ref)
+        for b in range(2):
+            both = get_tile(unit, b).astype(BF)
             for q in range(NQ):
                 half_ref[2 * j + b, :, q * W : (q + 1) * W] = jnp.dot(
                     slab_ref[q, b], both, preferred_element_type=F32
                 ).astype(BF)
 
 
-def first_half(flip, slab, local, cross):
+def first_half(slab, local, cross):
     return pl.pallas_call(
         half_kernel,
-        out_shape=(pltpu.VMEM((4, W, DEEP), BF), pltpu.VMEM((4, W, W), F32)),
-        in_specs=[SCALARS] + [WHOLE] * 3,
-        out_specs=[WHOLE, WHOLE],
+        out_shape=(pltpu.VMEM((4, W, DEEP), BF), pltpu.VMEM((4, 2, PIECE, 128), F32)),
+        in_specs=[WHOLE] * 3,
+        out_specs=[WHOLE] * 2,
         compiler_params=params(),
         cost_estimate=cost(8 * NQ * W**3, 4_000_000),
-    )(flip, slab, local, cross)
+    )(slab, local, cross)
 
 
 def ladder_kernel(source_ref, core_ref, half_ref, int_ref, *refs):
@@ -257,9 +251,9 @@
     unit[3 * W : UNIT, :] = jnp.zeros((UNIT - 3 * W, 128), F32)
     for j in range(2):
         for b in range(2):
-            put_tile(unit, b, int_ref[2 * j + b] + sums[2 * j + b])
+            put_tile(unit, b, sums[2 * j + b])
         for i in range(4):
-            out_ref[i, j] = unit[i * PIECE : (i + 1) * PIECE, :].astype(BF)
+            out_ref[i, j] = (unit[i * PIECE : (i + 1) * PIECE, :] + int_ref[i, j]).astype(BF)
 
 
 def symmetric_units(source, core, half_done, integrals, full, parts):
@@ -285,7 +279,7 @@
 
     def finish(block, symmetric):
         far = table_ref[source_ref[2 * p + block], 0:1, :]
-        denominator = pair_ref[p] - near_ref[block] - far
+        denominator = pair_ref[p] - near_ref[block, :, 0:1] - far
         old = amp_ref[0, block].astype(F32)
         out_ref[0, block] = (old + symmetric / denominator).astype(BF)
 
@@ -320,7 +314,7 @@
                 pl.BlockSpec((4, 1, PIECE, 128), pick),
                 pl.BlockSpec((4, 1, PIECE, 128), pick),
                 pl.BlockSpec((8, TALL - W, W), fixed),
-                pl.BlockSpec((2, W, 1), fixed),
+                pl.BlockSpec((2, W, 128), fixed),
             ],
             out_specs=pl.BlockSpec((1, 2, W, W), here),
         ),
@@ -354,14 +348,14 @@
 
     one = pack_slab(slab, virt_energy, parity[None])
     y_one = along_y(one)
-    local = to_mirror(pack_tiles(send, amp, ints, 1)[0])
-    kept_tiles = pack_tiles(keep, amp, ints, 1)[0]
+    local = to_mirror(pack_tiles(send, send, amp, ints, False))
 
     irrep = jnp.bitwise_xor(occ_irrep[pair_list[:, 0]], occ_irrep[pair_list[:, 1]])
     step, flip = jnp.right_shift(irrep, 1), jnp.bitwise_and(irrep, 1)
     keep_step, keep_flip = among(step, upper), among(flip, upper)
+    kept_tiles = pack_tiles(keep, keep_flip, amp, ints, True)
     pair_energy = occ_energy[pair_list[:, 0]] + occ_energy[pair_list[:, 1]]
-    near = virt_energy.astype(F32).reshape(2, W, 1)
+    near = jnp.broadcast_to(virt_energy.astype(F32).reshape(2, W, 1), (2, W, 128))
 
     def sources(step, flip):
         apart = jnp.bitwise_and(jnp.bitwise_xor(virt, step) - virt, 3)[:, None]
@@ -394,12 +388,13 @@
     full = (one, two, y_one, x_one, y_swap, x_swap)
     parts = (y_far, x_far, y_far_swap, swap_cores(x_far))
 
-    half_done, both_ints = first_half(keep_flip, slab, local, cross)
+    half_done, both_ints = first_half(slab, local, cross)
     result, table = symmetric_units(
         keep_source, core[None], half_done, both_ints, full, parts
     )
     mirrored = to_mirror(result)
-    crossed = as_unit(ready, lambda x: exchange(reorder(exchange(x), keep_step)), result)
+    scattered = exchange(result)
+    crossed = as_unit(ready, lambda x: exchange(reorder(x, keep_step)), scattered)
     new = update(
         kept, at, flip, source, pair_energy, amp, crossed, mirrored, table, near
     )

time: 133 us -> 132 us (level)
  the two profiles are of different devices: /device:TPU:56 before, /device:TPU:248 now
where the time goes in v9:
time: 132 us; the launch traced here: 131 us
  starting transfers between devices  57.2 us (43%)
  waiting for transfers between devices  26.5 us (20%)
  Pallas kernels  21.7 us (16%)
  blocking collectives  12.8 us (10%)
  local copies, waits for them, and re-layouts  9.38 us (7%)
  other arithmetic  2.75 us (2%)
    ppermute x10, starting transfers between devices, permute(): return lax.ppermute(value, ('pair', 'virt'), pairs)  37.5 us
    ppermute x10, waiting for transfers between devices, permute(): return lax.ppermute(value, ('pair', 'virt'), pairs)  23.4 us
    all_to_all x3, starting transfers between devices, exchange(): return lax.all_to_all(units, 'virt', 0, 0, tiled=True)  19.8 us
    all_to_all x1, blocking collectives, exchange(): return lax.all_to_all(units, 'virt', 0, 0, tiled=True)  12.8 us
    pallas_call x1, Pallas kernels, symmetric_units(): pl.pallas_call(ladder_kernel, out_shape=(jax.ShapeDtypeStruct((4, 2, PIEC...  5.86 us
    pallas_call x1, Pallas kernels, first_half(): pl.pallas_call(half_kernel, out_shape=(pltpu.VMEM((4, W, DEEP), BF), pltp...  4.87 us
    pallas_call x2, Pallas kernels, pack_tiles(): pl.pallas_call(functools.partial(tiles_kernel, turn), out_shape=jax.Shape...  3.92 us
    pallas_call x2, Pallas kernels, pack_slab(): pl.pallas_call(pack_kernel, out_shape=jax.ShapeDtypeStruct((TALL, DEEP),...  3.88 us
  transfers between devices with their start and end apart: 13, of which 5 were waited for; matrix products, arithmetic and copies ran while one was open for 9% of the time, Pallas kernels for 8%

profile of v9, /device:TPU:248, one launch (start us, length us, event | category | flops | bytes accessed | tf_op | source)
XLA Modules:
  0.0 131.5 jit_solution(1345346593127222704)
XLA Ops:
  0.0 2.0 %shard_map.82.refs_0_ = bf16[208,3200]{1,0:T(8,128)(2,1)S(1)} custom-call(s32[1]{0:T(128)} %bitcast.5.order_ref, bf16[16,2,200,200]{3,2,1,0:T(8,128)(2,1)} %bitcast.23, bf16[400]{0:T(512)(128)(2,1)} %energy_ref.1), custom_call_target="tpu_custom_call" | custom-call | bytes 3000000 | tf_op jit(solution)/shard_map/pallas_call | solution.py:102
  2.0 2.1 %collective-permute-start.6 = (bf16[208,3200]{1,0:T(8,128)(2,1)S(1)}, bf16[208,3200]{1,0:T(8,128)(2,1)}, u32[]{:S(2)}, u32[]{:S(2)}) collective-permute-start(bf16[208,3200]{1,0:T(8,128)(2,1)S(1)} %shard_map.82.refs_0_), channel_id=1, source_target_pairs={{0,1},{4,39},{8,9},{12,47},{16,17},{20,55},{24,25},{28,63},{1,2},{... | collective-permute-start | bytes 3993608 | tf_op jit(solution)/shard_map/ppermute | solution.py:35
  4.2 0.6 gather_fusion.2
  4.8 0.6 gather_fusion.3
  5.5 0.6 broadcast_and_fusion.1
  6.1 0.1 fusion.8
  6.2 1.8 %shard_map.84 = bf16[4,4,160,128]{3,2,1,0:T(8,128)(2,1)} custom-call(s32[2]{0:T(128)S(1)} %get-tuple-element.94.pick_ref.flip_ref, s32[2]{0:T(128)S(1)} %get-tuple-element.94.pick_ref.flip_ref, bf16[4,2,200,200]{3,2,1,0:T(8,128)(2,1)S(1)} %bitcast.18, bf16[4,2,200,200]{3,2,1,0:T(8,128)(2,1)S(1)} %bitcast.21), custom_call_target="tpu_custom_call" | custom-call | bytes 1500000 | tf_op jit(solution)/shard_map/pallas_call | solution.py:169
  7.9 12.4 %collective-permute-start.7 = (bf16[4,4,160,128]{3,2,1,0:T(8,128)(2,1)}, bf16[4,4,160,128]{3,2,1,0:T(8,128)(2,1)}, u32[]{:S(2)}, u32[]{:S(2)}) collective-permute-start(bf16[4,4,160,128]{3,2,1,0:T(8,128)(2,1)} %shard_map.84), channel_id=1, source_target_pairs={{0,384},{4,388},{8,392},{12,396},{16,400},{20,404},{24,408},{28,41... | collective-permute-start | bytes 1966088 | tf_op jit(solution)/shard_map/ppermute | solution.py:35
  20.4 0.6 gather_fusion.4
  21.0 0.6 gather_fusion.5
  21.7 0.1 reshape.181
  21.8 0.6 slice.13
  22.4 2.2 %shard_map.83 = bf16[4,4,160,128]{3,2,1,0:T(8,128)(2,1)} custom-call(s32[2]{0:T(128)S(1)} %get-tuple-element.93.pick_ref, s32[2]{0:T(128)S(1)} %get-tuple-element.92.flip_ref, bf16[4,2,200,200]{3,2,1,0:T(8,128)(2,1)S(1)} %bitcast.19, bf16[4,2,200,200]{3,2,1,0:T(8,128)(2,1)S(1)} %bitcast.22), custom_call_target="tpu_custom_call" | custom-call | bytes 1500000 | tf_op jit(solution)/shard_map/pallas_call | solution.py:169
  24.6 0.6 add.95.source_ref
  25.2 0.6 add.98.source_ref
  26.5 0.6 add.92.pair_ref
  27.1 0.8 broadcast_in_dim.116.near_ref
  27.9 49.1 %conditional.2 = (bf16[208,3200]{1,0:T(8,128)(2,1)S(1)}, bf16[208,3200]{1,0:T(8,128)(2,1)}, bf16[208,3200]{1,0:T(8,128)(2,1)}, bf16[208,3200]{1,0:T(8,128)(2,1)}...) conditional(s32[]{:T(128)} %bitcast.9, () %tuple.23, ...), branch_computations={%region_3.4_spmd, %region_4.5_spmd} | conditional | flops 153 | bytes 33909204 | solution.py:72
  27.9 3.4 %collective-permute-start = (bf16[208,3200]{1,0:T(8,128)(2,1)}, bf16[208,3200]{1,0:T(8,128)(2,1)}, u32[]{:S(2)}, u32[]{:S(2)}) collective-permute-start(bf16[208,3200]{1,0:T(8,128)(2,1)} %get-tuple-element.29), channel_id=1, source_target_pairs={{0,8},{4,28},{8,16},{12,4},{16,24},{20,12},{24,0},{28,20},{1,9},{5... | collective-permute-start | bytes 3993608 | tf_op jit(solution)/shard_map/cond/branch_1_fun/ppermute | solution.py:35
  31.3 7.0 %all-to-all-start = ((bf16[4,4,160,128]{3,2,1,0:T(8,128)(2,1)}), bf16[4,4,160,128]{3,2,1,0:T(8,128)(2,1)S(1)}, u32[]{:S(2)}, u32[]{:S(2)}) async-start(bf16[4,4,160,128]{3,2,1,0:T(8,128)(2,1)} %get-tuple-element.31), calls=%async_computation | async-start | bytes 1310720 | tf_op jit(solution)/shard_map/cond/branch_1_fun/all_to_all | solution.py:56
  38.3 1.1 constant_dynamic-slice_fusion
  39.5 2.3 %collective-permute-start.3 = (bf16[208,1664]{1,0:T(8,128)(2,1)S(1)}, bf16[208,1664]{1,0:T(8,128)(2,1)}, u32[]{:S(2)}, u32[]{:S(2)}) collective-permute-start(bf16[208,1664]{1,0:T(8,128)(2,1)S(1)} %constant_dynamic-slice_fusion), channel_id=1, source_target_pairs={{0,1},{4,39},{8,9},{12,47},{16,17},{20,55},{24,25},{28,63},{1,2},{... | collective-permute-start | bytes 2076680 | tf_op jit(solution)/shard_map/cond/branch_1_fun/ppermute | solution.py:35
  41.8 1.9 %collective-permute-start.1 = (bf16[208,3200]{1,0:T(8,128)(2,1)}, bf16[208,3200]{1,0:T(8,128)(2,1)}, u32[]{:S(2)}, u32[]{:S(2)}) collective-permute-start(bf16[208,3200]{1,0:T(8,128)(2,1)} %get-tuple-element.29), channel_id=1, source_target_pairs={{0,4},{4,0},{8,12},{12,8},{16,20},{20,16},{24,28},{28,24},{1,5},{5... | collective-permute-start | bytes 3993608 | tf_op jit(solution)/shard_map/cond/branch_1_fun/ppermute | solution.py:35
  43.7 5.4 %collective-permute-done = bf16[208,3200]{1,0:T(8,128)(2,1)} collective-permute-done((bf16[208,3200]{1,0:T(8,128)(2,1)}, bf16[208,3200]{1,0:T(8,128)(2,1)}, u32[]{:S(2)}, u32[]{:S(2)}) %collective-permute-start) | collective-permute-done | bytes 1331232 | tf_op jit(solution)/shard_map/cond/branch_1_fun/ppermute | solution.py:35
  49.1 1.9 %collective-permute-start.2 = (bf16[208,3200]{1,0:T(8,128)(2,1)}, bf16[208,3200]{1,0:T(8,128)(2,1)}, u32[]{:S(2)}, u32[]{:S(2)}) collective-permute-start(bf16[208,3200]{1,0:T(8,128)(2,1)} %collective-permute-done), channel_id=1, source_target_pairs={{0,4},{4,0},{8,12},{12,8},{16,20},{20,16},{24,28},{28,24},{1,5},{5... | collective-permute-start | bytes 3993608 | tf_op jit(solution)/shard_map/cond/branch_1_fun/ppermute | solution.py:35
  51.1 0.1 reshape.183
  51.2 2.6 %all-to-all-done = bf16[4,4,160,128]{3,2,1,0:T(8,128)(2,1)S(1)} async-done(((bf16[4,4,160,128]{3,2,1,0:T(8,128)(2,1)}), bf16[4,4,160,128]{3,2,1,0:T(8,128)(2,1)S(1)}, u32[]{:S(2)}, u32[]{:S(2)}) %all-to-all-start) | async-done | bytes 655392 | tf_op jit(solution)/shard_map/cond/branch_1_fun/all_to_all | solution.py:56
  53.8 1.5 %gather_fusion = bf16[16,160,128]{2,1,0:T(8,128)(2,1)} fusion(bf16[4,4,160,128]{3,2,1,0:T(8,128)(2,1)S(1)} %all-to-all-done, s32[16]{0:T(128)S(1)} %reshape.183), kind=kCustom, calls=%fused_computation | custom fusion | bytes 1310848 | tf_op jit(solution)/shard_map/cond/branch_1_fun/gather | solution.py:61
  55.3 7.3 %all-to-all-start.1 = ((bf16[4,4,160,128]{3,2,1,0:T(8,128)(2,1)}), bf16[4,4,160,128]{3,2,1,0:T(8,128)(2,1)}, u32[]{:S(2)}, u32[]{:S(2)}) async-start(bf16[4,4,160,128]{3,2,1,0:T(8,128)(2,1)} %bitcast.1), calls=%async_computation.1 | async-start | bytes 1310720 | tf_op jit(solution)/shard_map/cond/branch_1_fun/all_to_all | solution.py:56
  62.6 1.9 %collective-permute-start.4 = (bf16[208,1664]{1,0:T(8,128)(2,1)}, bf16[208,1664]{1,0:T(8,128)(2,1)}, u32[]{:S(2)}, u32[]{:S(2)}) collective-permute-start(bf16[208,1664]{1,0:T(8,128)(2,1)} %collective-permute-done.3), channel_id=1, source_target_pairs={{0,8},{4,28},{8,16},{12,4},{16,24},{20,12},{24,0},{28,20},{1,9},{5... | collective-permute-start | bytes 2076680 | tf_op jit(solution)/shard_map/cond/branch_1_fun/ppermute | solution.py:35
  64.5 1.9 %collective-permute-start.5 = (bf16[208,1664]{1,0:T(8,128)(2,1)}, bf16[208,1664]{1,0:T(8,128)(2,1)}, u32[]{:S(2)}, u32[]{:S(2)}) collective-permute-start(bf16[208,1664]{1,0:T(8,128)(2,1)} %collective-permute-done.3), channel_id=1, source_target_pairs={{0,4},{4,0},{8,12},{12,8},{16,20},{20,16},{24,28},{28,24},{1,5},{5... | collective-permute-start | bytes 2076680 | tf_op jit(solution)/shard_map/cond/branch_1_fun/ppermute | solution.py:35
  66.5 1.9 %branch_1_fun.1 = bf16[208,3200]{1,0:T(8,128)(2,1)S(1)} custom-call(s32[1]{0:T(128)} %bitcast.order_ref, bf16[16,2,200,200]{3,2,1,0:T(8,128)(2,1)} %get-tuple-element.27.slab_ref, bf16[400]{0:T(512)(128)(2,1)S(1)} %get-tuple-element.28.energy_ref), custom_call_target="tpu_custom_call" | custom-call | bytes 3000000 | tf_op jit(solution)/shard_map/cond/branch_1_fun/pallas_call | solution.py:102
  68.4 8.6 %collective-permute-done.4 = bf16[208,1664]{1,0:T(8,128)(2,1)} collective-permute-done((bf16[208,1664]{1,0:T(8,128)(2,1)}, bf16[208,1664]{1,0:T(8,128)(2,1)}, u32[]{:S(2)}, u32[]{:S(2)}) %collective-permute-start.4) | collective-permute-done | bytes 692256 | tf_op jit(solution)/shard_map/cond/branch_1_fun/ppermute | solution.py:35
  77.0 1.9 %collective-permute-start.8 = (bf16[208,1664]{1,0:T(8,128)(2,1)}, bf16[208,1664]{1,0:T(8,128)(2,1)S(1)}, u32[]{:S(2)}, u32[]{:S(2)}) collective-permute-start(bf16[208,1664]{1,0:T(8,128)(2,1)} %get-tuple-element.86.refs_7_), channel_id=1, source_target_pairs={{0,4},{4,0},{8,12},{12,8},{16,20},{20,16},{24,28},{28,24},{1,5},{5... | collective-permute-start | bytes 2076680 | tf_op jit(solution)/shard_map/ppermute | solution.py:35
  79.0 4.9 %shard_map.85 = (bf16[4,200,3200]{2,1,0:T(8,128)(2,1)S(1)}, f32[4,2,160,128]{3,2,1,0:T(8,128)S(1)}) custom-call(bf16[16,2,200,200]{3,2,1,0:T(8,128)(2,1)} %bitcast.25, bf16[4,4,160,128]{3,2,1,0:T(8,128)(2,1)} %collective-permute-done.7.local_ref, bf16[4,4,160,128]{3,2,1,0:T(8,128)(2,1)} %get-tuple-element.78.cross_ref), custom_call_target="tpu_custom_call" | custom-call | flops 1024000000 | bytes 4000000 | tf_op jit(solution)/shard_map/pallas_call | solution.py:201
  83.9 5.9 %shard_map.86 = (bf16[4,2,160,128]{3,2,1,0:T(8,128)(2,1)S(1)}, f32[8,8,200]{2,1,0:T(8,128)S(1)}) custom-call(s32[4]{0:T(128)S(1)} %copy-done.7, s32[1]{0:T(128)} %bitcast.10.core_ref, bf16[4,200,3200]{2,1,0:T(8,128)(2,1)S(1)} %get-tuple-element.79.half_ref, f32[4,2,160,128]{3,2,1,0:T(8,128)S(1)} %get-tuple-element.80.int_ref, ...), custom_call_target="tpu_custom_call" | custom-call | flops 1024000000 | bytes 3000000 | tf_op jit(solution)/shard_map/pallas_call | solution.py:260
  89.7 0.7 copy-done.4
  90.5 5.4 %all-to-all-start.3 = ((bf16[4,2,160,128]{3,2,1,0:T(8,128)(2,1)}), bf16[4,2,160,128]{3,2,1,0:T(8,128)(2,1)S(1)}, u32[]{:S(2)}, u32[]{:S(2)}) async-start(bf16[4,2,160,128]{3,2,1,0:T(8,128)(2,1)} %copy-done.4), calls=%async_computation.3 | async-start | bytes 655360 | tf_op jit(solution)/shard_map/all_to_all | solution.py:56
  95.9 7.8 %collective-permute-start.9 = (bf16[4,2,160,128]{3,2,1,0:T(8,128)(2,1)}, bf16[4,2,160,128]{3,2,1,0:T(8,128)(2,1)S(1)}, u32[]{:S(2)}, u32[]{:S(2)}) collective-permute-start(bf16[4,2,160,128]{3,2,1,0:T(8,128)(2,1)} %copy-done.4), channel_id=1, source_target_pairs={{0,384},{4,388},{8,392},{12,396},{16,400},{20,404},{24,408},{28,41... | collective-permute-start | bytes 983048 | tf_op jit(solution)/shard_map/ppermute | solution.py:35
  103.6 0.7 compare_convert_fusion.1.kept_ref
  104.3 0.4 all-to-all-done.3
  104.7 14.1 %conditional.3 = (bf16[4,2,160,128]{3,2,1,0:T(8,128)(2,1)S(1)}) conditional(s32[]{:T(128)} %bitcast.9, () %tuple.22, (s32[2]{0:T(128)}, bf16[4,2,160,128]{3,2,1,0:T(8,128)(2,1)S(1)}) %tuple.43), branch_computations={%region_6.7_spmd, %region_7.8_spmd} | conditional | flops 72 | bytes 1310896 | solution.py:72
  104.7 0.6 fusion.5
  105.3 0.1 reshape.189
  105.4 0.6 gather_fusion.1
  106.0 12.8 %all_to_all.17 = bf16[4,2,160,128]{3,2,1,0:T(8,128)(2,1)S(1)} all-to-all(bf16[4,2,160,128]{3,2,1,0:T(8,128)(2,1)S(1)} %bitcast.26), channel_id=1, replica_groups=mesh['pair'=192,'virt'=4] {'virt'}, dimensions={0} | all-to-all | bytes 655360 | tf_op jit(solution)/shard_map/cond/branch_1_fun/all_to_all | solution.py:56
  118.8 9.4 %collective-permute-done.9.mirror_ref = bf16[4,2,160,128]{3,2,1,0:T(8,128)(2,1)S(1)} collective-permute-done((bf16[4,2,160,128]{3,2,1,0:T(8,128)(2,1)}, bf16[4,2,160,128]{3,2,1,0:T(8,128)(2,1)S(1)}, u32[]{:S(2)}, u32[]{:S(2)}) %collective-permute-start.9) | collective-permute-done | bytes 327712 | tf_op jit(solution)/shard_map/ppermute | solution.py:35
  128.2 3.2 %shard_map.87 = bf16[4,2,200,200]{3,2,1,0:T(8,128)(2,1)} custom-call(s32[4]{0:T(128)S(1)} %compare_convert_fusion.1.kept_ref, s32[4]{0:T(128)S(1)} %copy-done.6, s32[4]{0:T(128)S(1)} %get-tuple-element.99.flip_ref, s32[8]{0:T(128)S(1)} %copy-done.5, f32[4]{0:T(128)S(1)} %copy-done.8, bf16[4,2,200,200]{3,2,1,0:T(8,128)(2,1)S(1)} %bitcast.20, ...), custom_call_target="tpu_custom_call" | custom-call | tf_op jit(solution)/shard_map/pallas_call | solution.py:306
  (45 shorter events, 0.3 us)
Async XLA Ops:
  0.0 4.2 %copy-start = (s32[200]{0:T(256)S(1)}, s32[200]{0:T(256)}, u32[]{:S(2)}) copy-start(s32[200]{0:T(256)} %param.17) | copy-start | bytes 2404
  0.0 4.1 %copy-start.13 = (s32[4,2]{0,1:T(2,128)S(1)}, s32[4,2]{0,1:T(2,128)}, u32[]{:S(2)}) copy-start(s32[4,2]{0,1:T(2,128)} %param.15) | copy-start | bytes 100
  0.0 5.5 %copy-start.14 = (s32[4]{0:T(128)S(1)}, s32[4]{0:T(128)}, u32[]{:S(2)}) copy-start(s32[4]{0:T(128)} %param.16) | copy-start | bytes 52
  0.0 6.2 %copy-start.2 = (bf16[4,400,200]{2,1,0:T(8,128)(2,1)S(1)}, bf16[4,400,200]{2,1,0:T(8,128)(2,1)}, u32[]{:S(2)}) copy-start(bf16[4,400,200]{2,1,0:T(8,128)(2,1)} %param.13) | copy-start | bytes 1920004
  2.0 4.2 %copy-start.1 = (bf16[4,400,200]{2,1,0:T(8,128)(2,1)S(1)}, bf16[4,400,200]{2,1,0:T(8,128)(2,1)}, u32[]{:S(2)}) copy-start(bf16[4,400,200]{2,1,0:T(8,128)(2,1)} %param.12) | copy-start | bytes 1920004
  2.0 25.1 %collective-permute-start.6 = (bf16[208,3200]{1,0:T(8,128)(2,1)S(1)}, bf16[208,3200]{1,0:T(8,128)(2,1)}, u32[]{:S(2)}, u32[]{:S(2)}) collective-permute-start(bf16[208,3200]{1,0:T(8,128)(2,1)S(1)} %shard_map.82.refs_0_), channel_id=1, source_target_pairs={{0,1},{4,39},{8,9},{12,47},{16,17},{20,55},{24,25},{28,63},{1,2},{... | collective-permute-start | bytes 3993608 | tf_op jit(solution)/shard_map/ppermute | solution.py:35
  4.8 15.6 %copy-start.9 = (f32[200]{0:T(256)S(1)}, f32[200]{0:T(256)}, u32[]{:S(2)}) copy-start(f32[200]{0:T(256)} %param.18) | copy-start | bytes 2404
  6.1 15.0 %copy-start.12 = (s32[4]{0:T(128)}, s32[4]{0:T(128)S(1)}, u32[]{:S(2)}) copy-start(s32[4]{0:T(128)S(1)} %get-tuple-element.98) | copy-start | bytes 52
  6.2 21.7 %copy-start.11 = (s32[2]{0:T(128)}, s32[2]{0:T(128)S(1)}, u32[]{:S(2)}) copy-start(s32[2]{0:T(128)S(1)} %get-tuple-element.65) | copy-start | bytes 28
  6.2 15.5 %copy-start.10 = (bf16[400]{0:T(512)(128)(2,1)S(1)}, bf16[400]{0:T(512)(128)(2,1)}, u32[]{:S(2)}) copy-start(bf16[400]{0:T(512)(128)(2,1)} %energy_ref.1) | copy-start | bytes 2404
  7.9 69.1 %collective-permute-start.7 = (bf16[4,4,160,128]{3,2,1,0:T(8,128)(2,1)}, bf16[4,4,160,128]{3,2,1,0:T(8,128)(2,1)}, u32[]{:S(2)}, u32[]{:S(2)}) collective-permute-start(bf16[4,4,160,128]{3,2,1,0:T(8,128)(2,1)} %shard_map.84), channel_id=1, source_target_pairs={{0,384},{4,388},{8,392},{12,396},{16,400},{20,404},{24,408},{28,41... | collective-permute-start | bytes 1966088 | tf_op jit(solution)/shard_map/ppermute | solution.py:35
  27.9 21.2 %collective-permute-start = (bf16[208,3200]{1,0:T(8,128)(2,1)}, bf16[208,3200]{1,0:T(8,128)(2,1)}, u32[]{:S(2)}, u32[]{:S(2)}) collective-permute-start(bf16[208,3200]{1,0:T(8,128)(2,1)} %get-tuple-element.29), channel_id=1, source_target_pairs={{0,8},{4,28},{8,16},{12,4},{16,24},{20,12},{24,0},{28,20},{1,9},{5... | collective-permute-start | bytes 3993608 | tf_op jit(solution)/shard_map/cond/branch_1_fun/ppermute | solution.py:35
  31.3 22.6 %all-to-all-start = ((bf16[4,4,160,128]{3,2,1,0:T(8,128)(2,1)}), bf16[4,4,160,128]{3,2,1,0:T(8,128)(2,1)S(1)}, u32[]{:S(2)}, u32[]{:S(2)}) async-start(bf16[4,4,160,128]{3,2,1,0:T(8,128)(2,1)} %get-tuple-element.31), calls=%async_computation | async-start | bytes 1310720 | tf_op jit(solution)/shard_map/cond/branch_1_fun/all_to_all | solution.py:56
  39.5 23.1 %collective-permute-start.3 = (bf16[208,1664]{1,0:T(8,128)(2,1)S(1)}, bf16[208,1664]{1,0:T(8,128)(2,1)}, u32[]{:S(2)}, u32[]{:S(2)}) collective-permute-start(bf16[208,1664]{1,0:T(8,128)(2,1)S(1)} %constant_dynamic-slice_fusion), channel_id=1, source_target_pairs={{0,1},{4,39},{8,9},{12,47},{16,17},{20,55},{24,25},{28,63},{1,2},{... | collective-permute-start | bytes 2076680 | tf_op jit(solution)/shard_map/cond/branch_1_fun/ppermute | solution.py:35
  41.8 26.6 %collective-permute-start.1 = (bf16[208,3200]{1,0:T(8,128)(2,1)}, bf16[208,3200]{1,0:T(8,128)(2,1)}, u32[]{:S(2)}, u32[]{:S(2)}) collective-permute-start(bf16[208,3200]{1,0:T(8,128)(2,1)} %get-tuple-element.29), channel_id=1, source_target_pairs={{0,4},{4,0},{8,12},{12,8},{16,20},{20,16},{24,28},{28,24},{1,5},{5... | collective-permute-start | bytes 3993608 | tf_op jit(solution)/shard_map/cond/branch_1_fun/ppermute | solution.py:35
  49.1 27.9 %collective-permute-start.2 = (bf16[208,3200]{1,0:T(8,128)(2,1)}, bf16[208,3200]{1,0:T(8,128)(2,1)}, u32[]{:S(2)}, u32[]{:S(2)}) collective-permute-start(bf16[208,3200]{1,0:T(8,128)(2,1)} %collective-permute-done), channel_id=1, source_target_pairs={{0,4},{4,0},{8,12},{12,8},{16,20},{20,16},{24,28},{28,24},{1,5},{5... | collective-permute-start | bytes 3993608 | tf_op jit(solution)/shard_map/cond/branch_1_fun/ppermute | solution.py:35
  55.3 21.7 %all-to-all-start.1 = ((bf16[4,4,160,128]{3,2,1,0:T(8,128)(2,1)}), bf16[4,4,160,128]{3,2,1,0:T(8,128)(2,1)}, u32[]{:S(2)}, u32[]{:S(2)}) async-start(bf16[4,4,160,128]{3,2,1,0:T(8,128)(2,1)} %bitcast.1), calls=%async_computation.1 | async-start | bytes 1310720 | tf_op jit(solution)/shard_map/cond/branch_1_fun/all_to_all | solution.py:56
  62.6 14.4 %collective-permute-start.4 = (bf16[208,1664]{1,0:T(8,128)(2,1)}, bf16[208,1664]{1,0:T(8,128)(2,1)}, u32[]{:S(2)}, u32[]{:S(2)}) collective-permute-start(bf16[208,1664]{1,0:T(8,128)(2,1)} %collective-permute-done.3), channel_id=1, source_target_pairs={{0,8},{4,28},{8,16},{12,4},{16,24},{20,12},{24,0},{28,20},{1,9},{5... | collective-permute-start | bytes 2076680 | tf_op jit(solution)/shard_map/cond/branch_1_fun/ppermute | solution.py:35
  64.5 12.5 %collective-permute-start.5 = (bf16[208,1664]{1,0:T(8,128)(2,1)}, bf16[208,1664]{1,0:T(8,128)(2,1)}, u32[]{:S(2)}, u32[]{:S(2)}) collective-permute-start(bf16[208,1664]{1,0:T(8,128)(2,1)} %collective-permute-done.3), channel_id=1, source_target_pairs={{0,4},{4,0},{8,12},{12,8},{16,20},{20,16},{24,28},{28,24},{1,5},{5... | collective-permute-start | bytes 2076680 | tf_op jit(solution)/shard_map/cond/branch_1_fun/ppermute | solution.py:35
  77.0 6.8 %copy-start.7 = (s32[4]{0:T(128)S(1)}, s32[4]{0:T(128)}, u32[]{:S(2)}) copy-start(s32[4]{0:T(128)} %add.95.source_ref) | copy-start | bytes 52
  77.0 6.8 %collective-permute-start.8 = (bf16[208,1664]{1,0:T(8,128)(2,1)}, bf16[208,1664]{1,0:T(8,128)(2,1)S(1)}, u32[]{:S(2)}, u32[]{:S(2)}) collective-permute-start(bf16[208,1664]{1,0:T(8,128)(2,1)} %get-tuple-element.86.refs_7_), channel_id=1, source_target_pairs={{0,4},{4,0},{8,12},{12,8},{16,20},{20,16},{24,28},{28,24},{1,5},{5... | collective-permute-start | bytes 2076680 | tf_op jit(solution)/shard_map/ppermute | solution.py:35
  89.7 0.7 copy-start.4
  90.5 37.8 %copy-start.3 = (f32[2,200,128]{2,1,0:T(8,128)S(1)}, f32[2,200,128]{2,1,0:T(8,128)}, u32[]{:S(2)}) copy-start(f32[2,200,128]{2,1,0:T(8,128)} %broadcast_in_dim.116.near_ref) | copy-start | bytes 614404
  90.5 37.8 %copy-start.5 = (s32[8]{0:T(128)S(1)}, s32[8]{0:T(128)}, u32[]{:S(2)}) copy-start(s32[8]{0:T(128)} %add.98.source_ref) | copy-start | bytes 100
  90.5 37.8 %copy-start.6 = (s32[4]{0:T(128)S(1)}, s32[4]{0:T(128)}, u32[]{:S(2)}) copy-start(s32[4]{0:T(128)} %get-tuple-element.97.at_ref) | copy-start | bytes 52
  90.5 37.8 %copy-start.8 = (f32[4]{0:T(128)S(1)}, f32[4]{0:T(128)}, u32[]{:S(2)}) copy-start(f32[4]{0:T(128)} %add.92.pair_ref) | copy-start | bytes 52
  90.5 14.2 %all-to-all-start.3 = ((bf16[4,2,160,128]{3,2,1,0:T(8,128)(2,1)}), bf16[4,2,160,128]{3,2,1,0:T(8,128)(2,1)S(1)}, u32[]{:S(2)}, u32[]{:S(2)}) async-start(bf16[4,2,160,128]{3,2,1,0:T(8,128)(2,1)} %copy-done.4), calls=%async_computation.3 | async-start | bytes 655360 | tf_op jit(solution)/shard_map/all_to_all | solution.py:56
  95.9 32.4 %collective-permute-start.9 = (bf16[4,2,160,128]{3,2,1,0:T(8,128)(2,1)}, bf16[4,2,160,128]{3,2,1,0:T(8,128)(2,1)S(1)}, u32[]{:S(2)}, u32[]{:S(2)}) collective-permute-start(bf16[4,2,160,128]{3,2,1,0:T(8,128)(2,1)} %copy-done.4), channel_id=1, source_target_pairs={{0,384},{4,388},{8,392},{12,396},{16,400},{20,404},{24,408},{28,41... | collective-permute-start | bytes 983048 | tf_op jit(solution)/shard_map/ppermute | solution.py:35

commit v10 on v9

--- a/solution.py
+++ b/solution.py
@@ -90,9 +90,10 @@
 SCALARS = pl.BlockSpec(memory_space=pltpu.SMEM)
 
 
-def pack_kernel(order_ref, slab_ref, energy_ref, out_ref):
+def pack_kernel(order_ref, *refs):
+    *slab_refs, energy_ref, out_ref = refs
     for q in range(NQ):
-        out_ref[0:W, q * W : (q + 1) * W] = slab_ref[q, 0]
+        out_ref[0:W, q * W : (q + 1) * W] = slab_refs[q // 4][q % 4, 0]
     both = jnp.broadcast_to(energy_ref[...].reshape(1, 2 * W), (TALL - W, 2 * W))
     out_ref[W:TALL, 0:W] = jnp.where(order_ref[0] == 0, both[:, 0:W], both[:, W : 2 * W])
     out_ref[W:TALL, W:DEEP] = jnp.zeros((TALL - W, DEEP - W), BF)
@@ -106,14 +107,15 @@
             num_scalar_prefetch=1,
             grid=(1,),
             in_specs=[
-                pl.BlockSpec((NQ, 1, W, W), lambda i, order: (0, order[0], 0, 0)),
-                pl.BlockSpec((2 * W,), lambda i, order: (0,)),
-            ],
+                pl.BlockSpec((4, 1, W, W), lambda i, order, part=part: (part, order[0], 0, 0))
+                for part in range(4)
+            ]
+            + [pl.BlockSpec((2 * W,), lambda i, order: (0,))],
             out_specs=pl.BlockSpec((TALL, DEEP), lambda i, order: (0, 0)),
         ),
         compiler_params=params("arbitrary"),
         cost_estimate=cost(0, 3_000_000),
-    )(block, slab, energy)
+    )(block, slab, slab, slab, slab, energy)
 
 
 def put_tile(unit_ref, block, tile):
@@ -354,8 +356,6 @@
     step, flip = jnp.right_shift(irrep, 1), jnp.bitwise_and(irrep, 1)
     keep_step, keep_flip = among(step, upper), among(flip, upper)
     kept_tiles = pack_tiles(keep, keep_flip, amp, ints, True)
-    pair_energy = occ_energy[pair_list[:, 0]] + occ_energy[pair_list[:, 1]]
-    near = jnp.broadcast_to(virt_energy.astype(F32).reshape(2, W, 1), (2, W, 128))
 
     def sources(step, flip):
         apart = jnp.bitwise_and(jnp.bitwise_xor(virt, step) - virt, 3)[:, None]
@@ -364,26 +364,31 @@
         start = jnp.where(apart == 0, 0, jnp.where(apart == 2, 6, side))
         return (start + second).reshape(-1)
 
-    keep_source, source = sources(keep_step, keep_flip), sources(step, flip)
     ready = pair_list[0, 0] >= 0
-    (
-        y_one, kept_tiles, keep_step, keep_flip, pair_energy, near, keep_source, source
-    ) = together(
-        y_one, kept_tiles, keep_step, keep_flip, pair_energy, near, keep_source, source
-    )
-
-    def bring(y_one, kept_tiles, keep_step, slab, virt_energy):
+    y_one, kept_tiles, keep_step = together(y_one, kept_tiles, keep_step)
+
+    def bring(y_one, kept_tiles, keep_step, keep_flip, step, flip, slab, virt_energy):
         scattered = exchange(kept_tiles)
+        y_part = lax.dynamic_slice(y_one, (0, core * (DEEP - PART)), (TALL, PART))
         x_one = along_x(y_one)
-        y_far = along_y(lax.dynamic_slice(y_one, (0, core * (DEEP - PART)), (TALL, PART)))
+        y_far = along_y(y_part)
+        scalars = (
+            occ_energy[pair_list[:, 0]] + occ_energy[pair_list[:, 1]],
+            jnp.broadcast_to(virt_energy.astype(F32).reshape(2, W, 1), (2, W, 128)),
+            sources(keep_step, keep_flip),
+            sources(step, flip),
+        )
         cross = exchange(reorder(scattered, jnp.concatenate([keep_step, keep_step])))
         two = pack_slab(slab, virt_energy, 1 - parity[None])
         return (
             two, x_one, swap_cores(y_one), swap_cores(x_one),
-            y_far, along_x(y_far), swap_cores(y_far), cross,
+            y_far, along_x(y_far), swap_cores(y_far), cross, *scalars,
         )
 
-    brought = as_unit(ready, bring, y_one, kept_tiles, keep_step, slab, virt_energy)
+    brought = as_unit(
+        ready, bring, y_one, kept_tiles, keep_step, keep_flip, step, flip, slab, virt_energy
+    )
+    *brought, pair_energy, near, keep_source, source = brought
     two, x_one, y_swap, x_swap, y_far, x_far, y_far_swap, cross, local = together(*brought, local)
     full = (one, two, y_one, x_one, y_swap, x_swap)
     parts = (y_far, x_far, y_far_swap, swap_cores(x_far))

time: 132 us -> 132 us (level)
  the two profiles are of different devices: /device:TPU:248 before, /device:TPU:120 now
where the time goes in v10:
time: 132 us; the launch traced here: 131 us
  starting transfers between devices  62.9 us (48%)
  waiting for transfers between devices  21.9 us (17%)
  Pallas kernels  21.6 us (16%)
  blocking collectives  12.9 us (10%)
  local copies, waits for them, and re-layouts  9.13 us (7%)
  other arithmetic  1.82 us (1%)
    ppermute x10, starting transfers between devices, permute(): return lax.ppermute(value, ('pair', 'virt'), pairs)  43.1 us
    all_to_all x3, starting transfers between devices, exchange(): return lax.all_to_all(units, 'virt', 0, 0, tiled=True)  19.7 us
    ppermute x10, waiting for transfers between devices, permute(): return lax.ppermute(value, ('pair', 'virt'), pairs)  19.2 us
    all_to_all x1, blocking collectives, exchange(): return lax.all_to_all(units, 'virt', 0, 0, tiled=True)  12.9 us
    pallas_call x1, Pallas kernels, symmetric_units(): pl.pallas_call(ladder_kernel, out_shape=(jax.ShapeDtypeStruct((4, 2, PIEC...  5.88 us
    pallas_call x1, Pallas kernels, first_half(): pl.pallas_call(half_kernel, out_shape=(pltpu.VMEM((4, W, DEEP), BF), pltp...  4.87 us
    pallas_call x2, Pallas kernels, pack_tiles(): pl.pallas_call(functools.partial(tiles_kernel, turn), out_shape=jax.Shape...  3.9 us
    pallas_call x2, Pallas kernels, pack_slab(): pl.pallas_call(pack_kernel, out_shape=jax.ShapeDtypeStruct((TALL, DEEP),...  3.76 us
  transfers between devices with their start and end apart: 13, of which 4 were waited for; matrix products, arithmetic and copies ran while one was open for 7% of the time, Pallas kernels for 8%

profile of v10, /device:TPU:120, one launch (start us, length us, event | category | flops | bytes accessed | tf_op | source)
XLA Modules:
  0.0 131.3 jit_solution(13106754592583952118)
XLA Ops:
  0.0 1.9 %shard_map.83.refs_0_ = bf16[208,3200]{1,0:T(8,128)(2,1)S(1)} custom-call(s32[1]{0:T(128)} %bitcast.9.order_ref, bf16[16,2,200,200]{3,2,1,0:T(8,128)(2,1)} %bitcast.27, bf16[16,2,200,200]{3,2,1,0:T(8,128)(2,1)} %bitcast.28, bf16[16,2,200,200]{3,2,1,0:T(8,128)(2,1)} %bitcast.29, bf16[16,2,200,200]{3,2,1,0:T(8,128)(2,1)} %bitcast.30, bf16[400]{0:T(512)(128)(2,1)} %refs_4_.1), custom_call_target="tpu_custom_call" | custom-call | bytes 3000000 | tf_op jit(solution)/shard_map/pallas_call | solution.py:103
  2.0 2.1 %collective-permute-start.6 = (bf16[208,3200]{1,0:T(8,128)(2,1)S(1)}, bf16[208,3200]{1,0:T(8,128)(2,1)}, u32[]{:S(2)}, u32[]{:S(2)}) collective-permute-start(bf16[208,3200]{1,0:T(8,128)(2,1)S(1)} %shard_map.83.refs_0_), channel_id=1, source_target_pairs={{0,1},{4,39},{8,9},{12,47},{16,17},{20,55},{24,25},{28,63},{1,2},{... | collective-permute-start | bytes 3993608 | tf_op jit(solution)/shard_map/ppermute | solution.py:35
  4.1 0.6 gather_fusion.4
  4.7 0.6 gather_fusion.5
  5.4 0.2 fusion.12
  5.7 1.8 %shard_map.85 = bf16[4,4,160,128]{3,2,1,0:T(8,128)(2,1)} custom-call(s32[2]{0:T(128)S(1)} %get-tuple-element.117.pick_ref.flip_ref, s32[2]{0:T(128)S(1)} %get-tuple-element.117.pick_ref.flip_ref, bf16[4,2,200,200]{3,2,1,0:T(8,128)(2,1)S(1)} %bitcast.22, bf16[4,2,200,200]{3,2,1,0:T(8,128)(2,1)S(1)} %bitcast.25), custom_call_target="tpu_custom_call" | custom-call | bytes 1500000 | tf_op jit(solution)/shard_map/pallas_call | solution.py:171
  7.5 14.4 %collective-permute-start.7 = (bf16[4,4,160,128]{3,2,1,0:T(8,128)(2,1)}, bf16[4,4,160,128]{3,2,1,0:T(8,128)(2,1)}, u32[]{:S(2)}, u32[]{:S(2)}) collective-permute-start(bf16[4,4,160,128]{3,2,1,0:T(8,128)(2,1)} %shard_map.85), channel_id=1, source_target_pairs={{0,384},{4,388},{8,392},{12,396},{16,400},{20,404},{24,408},{28,41... | collective-permute-start | bytes 1966088 | tf_op jit(solution)/shard_map/ppermute | solution.py:35
  21.9 0.5 slice.17
  23.0 2.1 %shard_map.84 = bf16[4,4,160,128]{3,2,1,0:T(8,128)(2,1)} custom-call(s32[2]{0:T(128)S(1)} %get-tuple-element.116.pick_ref, s32[2]{0:T(128)S(1)} %get-tuple-element.115.flip_ref, bf16[4,2,200,200]{3,2,1,0:T(8,128)(2,1)S(1)} %bitcast.23, bf16[4,2,200,200]{3,2,1,0:T(8,128)(2,1)S(1)} %bitcast.26), custom_call_target="tpu_custom_call" | custom-call | bytes 1500000 | tf_op jit(solution)/shard_map/pallas_call | solution.py:171
  25.1 49.3 %conditional.2 = (bf16[208,3200]{1,0:T(8,128)(2,1)S(1)}, bf16[208,3200]{1,0:T(8,128)(2,1)}, bf16[208,3200]{1,0:T(8,128)(2,1)}, bf16[208,3200]{1,0:T(8,128)(2,1)}...) conditional(s32[]{:T(128)} %bitcast.7, () %tuple.21, ...), branch_computations={%region_3.4_spmd, %region_4.5_spmd} | conditional | flops 2337 | bytes 34126756 | solution.py:72
  25.2 3.4 %collective-permute-start = (bf16[208,3200]{1,0:T(8,128)(2,1)}, bf16[208,3200]{1,0:T(8,128)(2,1)}, u32[]{:S(2)}, u32[]{:S(2)}) collective-permute-start(bf16[208,3200]{1,0:T(8,128)(2,1)} %get-tuple-element.44), channel_id=1, source_target_pairs={{0,8},{4,28},{8,16},{12,4},{16,24},{20,12},{24,0},{28,20},{1,9},{5... | collective-permute-start | bytes 3993608 | tf_op jit(solution)/shard_map/cond/branch_1_fun/ppermute | solution.py:35
  28.6 7.0 %all-to-all-start = ((bf16[4,4,160,128]{3,2,1,0:T(8,128)(2,1)}), bf16[4,4,160,128]{3,2,1,0:T(8,128)(2,1)S(1)}, u32[]{:S(2)}, u32[]{:S(2)}) async-start(bf16[4,4,160,128]{3,2,1,0:T(8,128)(2,1)} %get-tuple-element.46), calls=%async_computation | async-start | bytes 1310720 | tf_op jit(solution)/shard_map/cond/branch_1_fun/all_to_all | solution.py:56
  35.6 2.0 %constant_dynamic-slice_fusion = bf16[208,1664]{1,0:T(8,128)(2,1)} fusion(bf16[208,3200]{1,0:T(8,128)(2,1)} %get-tuple-element.44, s32[]{:T(128)S(6)} %select_n.71), kind=kLoop, calls=%fused_computation.27 | loop fusion | bytes 1384452 | tf_op jit(solution)/shard_map/cond/branch_1_fun/dynamic_slice | solution.py:372
  37.6 2.3 %collective-permute-start.3 = (bf16[208,1664]{1,0:T(8,128)(2,1)}, bf16[208,1664]{1,0:T(8,128)(2,1)}, u32[]{:S(2)}, u32[]{:S(2)}) collective-permute-start(bf16[208,1664]{1,0:T(8,128)(2,1)} %constant_dynamic-slice_fusion), channel_id=1, source_target_pairs={{0,1},{4,39},{8,9},{12,47},{16,17},{20,55},{24,25},{28,63},{1,2},{... | collective-permute-start | bytes 2076680 | tf_op jit(solution)/shard_map/cond/branch_1_fun/ppermute | solution.py:35
  39.9 1.9 %collective-permute-start.1 = (bf16[208,3200]{1,0:T(8,128)(2,1)}, bf16[208,3200]{1,0:T(8,128)(2,1)}, u32[]{:S(2)}, u32[]{:S(2)}) collective-permute-start(bf16[208,3200]{1,0:T(8,128)(2,1)} %get-tuple-element.44), channel_id=1, source_target_pairs={{0,4},{4,0},{8,12},{12,8},{16,20},{20,16},{24,28},{28,24},{1,5},{5... | collective-permute-start | bytes 3993608 | tf_op jit(solution)/shard_map/cond/branch_1_fun/ppermute | solution.py:35
  41.8 4.6 %collective-permute-done = bf16[208,3200]{1,0:T(8,128)(2,1)} collective-permute-done((bf16[208,3200]{1,0:T(8,128)(2,1)}, bf16[208,3200]{1,0:T(8,128)(2,1)}, u32[]{:S(2)}, u32[]{:S(2)}) %collective-permute-start) | collective-permute-done | bytes 1331232 | tf_op jit(solution)/shard_map/cond/branch_1_fun/ppermute | solution.py:35
  46.4 1.9 %collective-permute-start.2 = (bf16[208,3200]{1,0:T(8,128)(2,1)}, bf16[208,3200]{1,0:T(8,128)(2,1)}, u32[]{:S(2)}, u32[]{:S(2)}) collective-permute-start(bf16[208,3200]{1,0:T(8,128)(2,1)} %collective-permute-done), channel_id=1, source_target_pairs={{0,4},{4,0},{8,12},{12,8},{16,20},{20,16},{24,28},{28,24},{1,5},{5... | collective-permute-start | bytes 3993608 | tf_op jit(solution)/shard_map/cond/branch_1_fun/ppermute | solution.py:35
  48.3 0.1 compare_select_fusion.5
  48.4 0.1 reshape.162
  48.5 2.6 %all-to-all-done = bf16[4,4,160,128]{3,2,1,0:T(8,128)(2,1)S(1)} async-done(((bf16[4,4,160,128]{3,2,1,0:T(8,128)(2,1)}), bf16[4,4,160,128]{3,2,1,0:T(8,128)(2,1)S(1)}, u32[]{:S(2)}, u32[]{:S(2)}) %all-to-all-start) | async-done | bytes 655392 | tf_op jit(solution)/shard_map/cond/branch_1_fun/all_to_all | solution.py:56
  51.1 1.5 %gather_fusion = bf16[16,160,128]{2,1,0:T(8,128)(2,1)} fusion(bf16[4,4,160,128]{3,2,1,0:T(8,128)(2,1)S(1)} %all-to-all-done, s32[16]{0:T(128)S(1)} %reshape.162), kind=kCustom, calls=%fused_computation | custom fusion | bytes 1310848 | tf_op jit(solution)/shard_map/cond/branch_1_fun/gather | solution.py:61
  52.6 7.3 %all-to-all-start.1 = ((bf16[4,4,160,128]{3,2,1,0:T(8,128)(2,1)}), bf16[4,4,160,128]{3,2,1,0:T(8,128)(2,1)}, u32[]{:S(2)}, u32[]{:S(2)}) async-start(bf16[4,4,160,128]{3,2,1,0:T(8,128)(2,1)} %bitcast.1), calls=%async_computation.1 | async-start | bytes 1310720 | tf_op jit(solution)/shard_map/cond/branch_1_fun/all_to_all | solution.py:56
  59.9 1.9 %collective-permute-start.4 = (bf16[208,1664]{1,0:T(8,128)(2,1)}, bf16[208,1664]{1,0:T(8,128)(2,1)}, u32[]{:S(2)}, u32[]{:S(2)}) collective-permute-start(bf16[208,1664]{1,0:T(8,128)(2,1)} %collective-permute-done.3), channel_id=1, source_target_pairs={{0,8},{4,28},{8,16},{12,4},{16,24},{20,12},{24,0},{28,20},{1,9},{5... | collective-permute-start | bytes 2076680 | tf_op jit(solution)/shard_map/cond/branch_1_fun/ppermute | solution.py:35
  61.9 1.9 %collective-permute-start.5 = (bf16[208,1664]{1,0:T(8,128)(2,1)}, bf16[208,1664]{1,0:T(8,128)(2,1)}, u32[]{:S(2)}, u32[]{:S(2)}) collective-permute-start(bf16[208,1664]{1,0:T(8,128)(2,1)} %collective-permute-done.3), channel_id=1, source_target_pairs={{0,4},{4,0},{8,12},{12,8},{16,20},{20,16},{24,28},{28,24},{1,5},{5... | collective-permute-start | bytes 2076680 | tf_op jit(solution)/shard_map/cond/branch_1_fun/ppermute | solution.py:35
  63.8 0.6 gather_fusion.1
  64.4 0.6 gather_fusion.2
  65.1 0.1 reshape.160
  65.2 0.1 fusion.3
  65.3 0.1 add.83
  65.4 0.1 add.86
  65.5 1.8 %branch_1_fun.1 = bf16[208,3200]{1,0:T(8,128)(2,1)S(1)} custom-call(s32[1]{0:T(128)} %bitcast.order_ref, bf16[16,2,200,200]{3,2,1,0:T(8,128)(2,1)} %get-tuple-element.42.refs_0_.refs_1_.refs_2_.refs_3_, bf16[16,2,200,200]{3,2,1,0:T(8,128)(2,1)} %get-tuple-element.42.refs_0_.refs_1_.refs_2_.refs_3_, ...), custom_call_target="tpu_custom_call" | custom-call | bytes 3000000 | tf_op jit(solution)/shard_map/cond/branch_1_fun/pallas_call | solution.py:103
  67.4 7.0 %collective-permute-done.4 = bf16[208,1664]{1,0:T(8,128)(2,1)} collective-permute-done((bf16[208,1664]{1,0:T(8,128)(2,1)}, bf16[208,1664]{1,0:T(8,128)(2,1)}, u32[]{:S(2)}, u32[]{:S(2)}) %collective-permute-start.4) | collective-permute-done | bytes 692256 | tf_op jit(solution)/shard_map/cond/branch_1_fun/ppermute | solution.py:35
  74.3 0.1 broadcast_in_dim.73
  74.5 0.7 copy-done.5
  75.2 1.9 %collective-permute-start.8 = (bf16[208,1664]{1,0:T(8,128)(2,1)}, bf16[208,1664]{1,0:T(8,128)(2,1)S(1)}, u32[]{:S(2)}, u32[]{:S(2)}) collective-permute-start(bf16[208,1664]{1,0:T(8,128)(2,1)} %get-tuple-element.107.refs_7_), channel_id=1, source_target_pairs={{0,4},{4,0},{8,12},{12,8},{16,20},{20,16},{24,28},{28,24},{1,5},{5... | collective-permute-start | bytes 2076680 | tf_op jit(solution)/shard_map/ppermute | solution.py:35
  77.1 4.9 %shard_map.86 = (bf16[4,200,3200]{2,1,0:T(8,128)(2,1)S(1)}, f32[4,2,160,128]{3,2,1,0:T(8,128)S(1)}) custom-call(bf16[16,2,200,200]{3,2,1,0:T(8,128)(2,1)} %bitcast.32, bf16[4,4,160,128]{3,2,1,0:T(8,128)(2,1)} %collective-permute-done.7.local_ref, bf16[4,4,160,128]{3,2,1,0:T(8,128)(2,1)} %get-tuple-element.99.cross_ref), custom_call_target="tpu_custom_call" | custom-call | flops 1024000000 | bytes 4000000 | tf_op jit(solution)/shard_map/pallas_call | solution.py:203
  82.0 5.9 %shard_map.87 = (bf16[4,2,160,128]{3,2,1,0:T(8,128)(2,1)S(1)}, f32[8,8,200]{2,1,0:T(8,128)S(1)}) custom-call(s32[4]{0:T(128)} %copy-done.13, s32[1]{0:T(128)} %bitcast.12.core_ref, bf16[4,200,3200]{2,1,0:T(8,128)(2,1)S(1)} %get-tuple-element.100.half_ref, f32[4,2,160,128]{3,2,1,0:T(8,128)S(1)} %get-tuple-element.101.int_ref, ...), custom_call_target="tpu_custom_call" | custom-call | flops 1024000000 | bytes 3000000 | tf_op jit(solution)/shard_map/pallas_call | solution.py:262
  87.9 0.7 copy-done.3
  88.6 5.4 %all-to-all-start.3 = ((bf16[4,2,160,128]{3,2,1,0:T(8,128)(2,1)}), bf16[4,2,160,128]{3,2,1,0:T(8,128)(2,1)S(1)}, u32[]{:S(2)}, u32[]{:S(2)}) async-start(bf16[4,2,160,128]{3,2,1,0:T(8,128)(2,1)} %copy-done.3), calls=%async_computation.3 | async-start | bytes 655360 | tf_op jit(solution)/shard_map/all_to_all | solution.py:56
  94.0 11.5 %collective-permute-start.9 = (bf16[4,2,160,128]{3,2,1,0:T(8,128)(2,1)}, bf16[4,2,160,128]{3,2,1,0:T(8,128)(2,1)S(1)}, u32[]{:S(2)}, u32[]{:S(2)}) collective-permute-start(bf16[4,2,160,128]{3,2,1,0:T(8,128)(2,1)} %copy-done.3), channel_id=1, source_target_pairs={{0,384},{4,388},{8,392},{12,396},{16,400},{20,404},{24,408},{28,41... | collective-permute-start | bytes 983048 | tf_op jit(solution)/shard_map/ppermute | solution.py:35
  105.5 0.6 compare_convert_fusion.1.kept_ref
  106.1 14.3 %conditional.3 = (bf16[4,2,160,128]{3,2,1,0:T(8,128)(2,1)S(1)}) conditional(s32[]{:T(128)} %bitcast.7, () %tuple.24, (s32[2]{0:T(128)}, bf16[4,2,160,128]{3,2,1,0:T(8,128)(2,1)S(1)}) %tuple.45), branch_computations={%region_6.7_spmd, %region_7.8_spmd} | conditional | flops 72 | bytes 1310896 | solution.py:72
  106.1 0.7 fusion.8
  106.8 0.1 reshape.184
  106.9 0.6 gather_fusion.3
  107.5 12.9 %all_to_all.17 = bf16[4,2,160,128]{3,2,1,0:T(8,128)(2,1)S(1)} all-to-all(bf16[4,2,160,128]{3,2,1,0:T(8,128)(2,1)S(1)} %bitcast.33), channel_id=1, replica_groups=mesh['pair'=192,'virt'=4] {'virt'}, dimensions={0} | all-to-all | bytes 655360 | tf_op jit(solution)/shard_map/cond/branch_1_fun/all_to_all | solution.py:56
  120.4 7.7 %collective-permute-done.9.mirror_ref = bf16[4,2,160,128]{3,2,1,0:T(8,128)(2,1)S(1)} collective-permute-done((bf16[4,2,160,128]{3,2,1,0:T(8,128)(2,1)}, bf16[4,2,160,128]{3,2,1,0:T(8,128)(2,1)S(1)}, u32[]{:S(2)}, u32[]{:S(2)}) %collective-permute-start.9) | collective-permute-done | bytes 327712 | tf_op jit(solution)/shard_map/ppermute | solution.py:35
  128.1 3.2 %shard_map.88 = bf16[4,2,200,200]{3,2,1,0:T(8,128)(2,1)} custom-call(s32[4]{0:T(128)S(1)} %compare_convert_fusion.1.kept_ref, s32[4]{0:T(128)S(1)} %get-tuple-element.120.at_ref, s32[4]{0:T(128)S(1)} %copy-done.10, s32[8]{0:T(128)S(1)} %copy-done.17, f32[4]{0:T(128)S(1)} %copy-done.15, bf16[4,2,200,200]{3,2,1,0:T(8,128)(2,1)S(1)} %bitcast.24, ...), custom_call_target="tpu_custom_call" | custom-call | tf_op jit(solution)/shard_map/pallas_call | solution.py:308
  (57 shorter events, 0.2 us)
Async XLA Ops:
  0.0 4.1 %copy-start = (s32[200]{0:T(256)S(1)}, s32[200]{0:T(256)}, u32[]{:S(2)}) copy-start(s32[200]{0:T(256)} %param.17) | copy-start | bytes 2404
  0.0 4.0 %copy-start.11 = (s32[4,2]{0,1:T(2,128)S(1)}, s32[4,2]{0,1:T(2,128)}, u32[]{:S(2)}) copy-start(s32[4,2]{0,1:T(2,128)} %param.15) | copy-start | bytes 100
  0.0 5.4 %copy-start.18 = (s32[4]{0:T(128)S(1)}, s32[4]{0:T(128)}, u32[]{:S(2)}) copy-start(s32[4]{0:T(128)} %param.16) | copy-start | bytes 52
  0.0 5.6 %copy-start.2 = (bf16[4,400,200]{2,1,0:T(8,128)(2,1)S(1)}, bf16[4,400,200]{2,1,0:T(8,128)(2,1)}, u32[]{:S(2)}) copy-start(bf16[4,400,200]{2,1,0:T(8,128)(2,1)} %param.13) | copy-start | bytes 1920004
  1.9 3.7 %copy-start.1 = (bf16[4,400,200]{2,1,0:T(8,128)(2,1)S(1)}, bf16[4,400,200]{2,1,0:T(8,128)(2,1)}, u32[]{:S(2)}) copy-start(bf16[4,400,200]{2,1,0:T(8,128)(2,1)} %param.12) | copy-start | bytes 1920004
  2.0 23.1 %collective-permute-start.6 = (bf16[208,3200]{1,0:T(8,128)(2,1)S(1)}, bf16[208,3200]{1,0:T(8,128)(2,1)}, u32[]{:S(2)}, u32[]{:S(2)}) collective-permute-start(bf16[208,3200]{1,0:T(8,128)(2,1)S(1)} %shard_map.83.refs_0_), channel_id=1, source_target_pairs={{0,1},{4,39},{8,9},{12,47},{16,17},{20,55},{24,25},{28,63},{1,2},{... | collective-permute-start | bytes 3993608 | tf_op jit(solution)/shard_map/ppermute | solution.py:35
  5.4 19.7 %copy-start.9 = (s32[4]{0:T(128)}, s32[4]{0:T(128)S(1)}, u32[]{:S(2)}) copy-start(s32[4]{0:T(128)S(1)} %broadcast_and_fusion.flip_ref) | copy-start | bytes 52
  5.4 19.7 %copy-start.12 = (s32[4]{0:T(128)}, s32[4]{0:T(128)S(1)}, u32[]{:S(2)}) copy-start(s32[4]{0:T(128)S(1)} %get-tuple-element.121) | copy-start | bytes 52
  5.6 19.5 %copy-start.8 = (s32[2]{0:T(128)}, s32[2]{0:T(128)S(1)}, u32[]{:S(2)}) copy-start(s32[2]{0:T(128)S(1)} %get-tuple-element.86) | copy-start | bytes 28
  7.5 17.6 %copy-start.4 = (f32[200]{0:T(256)S(1)}, f32[200]{0:T(256)}, u32[]{:S(2)}) copy-start(f32[200]{0:T(256)} %param.18) | copy-start | bytes 2404
  7.5 17.6 %copy-start.7 = (bf16[400]{0:T(512)(128)(2,1)S(1)}, bf16[400]{0:T(512)(128)(2,1)}, u32[]{:S(2)}) copy-start(bf16[400]{0:T(512)(128)(2,1)} %refs_4_.1) | copy-start | bytes 2404
  7.5 67.0 %collective-permute-start.7 = (bf16[4,4,160,128]{3,2,1,0:T(8,128)(2,1)}, bf16[4,4,160,128]{3,2,1,0:T(8,128)(2,1)}, u32[]{:S(2)}, u32[]{:S(2)}) collective-permute-start(bf16[4,4,160,128]{3,2,1,0:T(8,128)(2,1)} %shard_map.85), channel_id=1, source_target_pairs={{0,384},{4,388},{8,392},{12,396},{16,400},{20,404},{24,408},{28,41... | collective-permute-start | bytes 1966088 | tf_op jit(solution)/shard_map/ppermute | solution.py:35
  25.2 21.2 %collective-permute-start = (bf16[208,3200]{1,0:T(8,128)(2,1)}, bf16[208,3200]{1,0:T(8,128)(2,1)}, u32[]{:S(2)}, u32[]{:S(2)}) collective-permute-start(bf16[208,3200]{1,0:T(8,128)(2,1)} %get-tuple-element.44), channel_id=1, source_target_pairs={{0,8},{4,28},{8,16},{12,4},{16,24},{20,12},{24,0},{28,20},{1,9},{5... | collective-permute-start | bytes 3993608 | tf_op jit(solution)/shard_map/cond/branch_1_fun/ppermute | solution.py:35
  28.6 22.6 %all-to-all-start = ((bf16[4,4,160,128]{3,2,1,0:T(8,128)(2,1)}), bf16[4,4,160,128]{3,2,1,0:T(8,128)(2,1)S(1)}, u32[]{:S(2)}, u32[]{:S(2)}) async-start(bf16[4,4,160,128]{3,2,1,0:T(8,128)(2,1)} %get-tuple-element.46), calls=%async_computation | async-start | bytes 1310720 | tf_op jit(solution)/shard_map/cond/branch_1_fun/all_to_all | solution.py:56
  37.6 22.3 %collective-permute-start.3 = (bf16[208,1664]{1,0:T(8,128)(2,1)}, bf16[208,1664]{1,0:T(8,128)(2,1)}, u32[]{:S(2)}, u32[]{:S(2)}) collective-permute-start(bf16[208,1664]{1,0:T(8,128)(2,1)} %constant_dynamic-slice_fusion), channel_id=1, source_target_pairs={{0,1},{4,39},{8,9},{12,47},{16,17},{20,55},{24,25},{28,63},{1,2},{... | collective-permute-start | bytes 2076680 | tf_op jit(solution)/shard_map/cond/branch_1_fun/ppermute | solution.py:35
  39.9 27.5 %collective-permute-start.1 = (bf16[208,3200]{1,0:T(8,128)(2,1)}, bf16[208,3200]{1,0:T(8,128)(2,1)}, u32[]{:S(2)}, u32[]{:S(2)}) collective-permute-start(bf16[208,3200]{1,0:T(8,128)(2,1)} %get-tuple-element.44), channel_id=1, source_target_pairs={{0,4},{4,0},{8,12},{12,8},{16,20},{20,16},{24,28},{28,24},{1,5},{5... | collective-permute-start | bytes 3993608 | tf_op jit(solution)/shard_map/cond/branch_1_fun/ppermute | solution.py:35
  46.4 27.9 %collective-permute-start.2 = (bf16[208,3200]{1,0:T(8,128)(2,1)}, bf16[208,3200]{1,0:T(8,128)(2,1)}, u32[]{:S(2)}, u32[]{:S(2)}) collective-permute-start(bf16[208,3200]{1,0:T(8,128)(2,1)} %collective-permute-done), channel_id=1, source_target_pairs={{0,4},{4,0},{8,12},{12,8},{16,20},{20,16},{24,28},{28,24},{1,5},{5... | collective-permute-start | bytes 3993608 | tf_op jit(solution)/shard_map/cond/branch_1_fun/ppermute | solution.py:35
  52.6 21.7 %all-to-all-start.1 = ((bf16[4,4,160,128]{3,2,1,0:T(8,128)(2,1)}), bf16[4,4,160,128]{3,2,1,0:T(8,128)(2,1)}, u32[]{:S(2)}, u32[]{:S(2)}) async-start(bf16[4,4,160,128]{3,2,1,0:T(8,128)(2,1)} %bitcast.1), calls=%async_computation.1 | async-start | bytes 1310720 | tf_op jit(solution)/shard_map/cond/branch_1_fun/all_to_all | solution.py:56
  59.9 14.4 %collective-permute-start.4 = (bf16[208,1664]{1,0:T(8,128)(2,1)}, bf16[208,1664]{1,0:T(8,128)(2,1)}, u32[]{:S(2)}, u32[]{:S(2)}) collective-permute-start(bf16[208,1664]{1,0:T(8,128)(2,1)} %collective-permute-done.3), channel_id=1, source_target_pairs={{0,8},{4,28},{8,16},{12,4},{16,24},{20,12},{24,0},{28,20},{1,9},{5... | collective-permute-start | bytes 2076680 | tf_op jit(solution)/shard_map/cond/branch_1_fun/ppermute | solution.py:35
  61.9 12.5 %collective-permute-start.5 = (bf16[208,1664]{1,0:T(8,128)(2,1)}, bf16[208,1664]{1,0:T(8,128)(2,1)}, u32[]{:S(2)}, u32[]{:S(2)}) collective-permute-start(bf16[208,1664]{1,0:T(8,128)(2,1)} %collective-permute-done.3), channel_id=1, source_target_pairs={{0,4},{4,0},{8,12},{12,8},{16,20},{20,16},{24,28},{28,24},{1,5},{5... | collective-permute-start | bytes 2076680 | tf_op jit(solution)/shard_map/cond/branch_1_fun/ppermute | solution.py:35
  74.5 0.7 copy-start.5
  74.5 7.5 %copy-start.13 = (s32[4]{0:T(128)}, s32[4]{0:T(128)S(1)}, u32[]{:S(2)}) copy-start(s32[4]{0:T(128)S(1)} %get-tuple-element.89.source_ref) | copy-start | bytes 52
  74.5 7.5 %copy-start.14 = (f32[4]{0:T(128)}, f32[4]{0:T(128)S(1)}, u32[]{:S(2)}) copy-start(f32[4]{0:T(128)S(1)} %get-tuple-element.88.pair_ref) | copy-start | bytes 52
  74.5 7.5 %copy-start.16 = (s32[8]{0:T(128)}, s32[8]{0:T(128)S(1)}, u32[]{:S(2)}) copy-start(s32[8]{0:T(128)S(1)} %get-tuple-element.87.source_ref) | copy-start | bytes 100
  75.2 6.8 %collective-permute-start.8 = (bf16[208,1664]{1,0:T(8,128)(2,1)}, bf16[208,1664]{1,0:T(8,128)(2,1)S(1)}, u32[]{:S(2)}, u32[]{:S(2)}) collective-permute-start(bf16[208,1664]{1,0:T(8,128)(2,1)} %get-tuple-element.107.refs_7_), channel_id=1, source_target_pairs={{0,4},{4,0},{8,12},{12,8},{16,20},{20,16},{24,28},{28,24},{1,5},{5... | collective-permute-start | bytes 2076680 | tf_op jit(solution)/shard_map/ppermute | solution.py:35
  87.9 0.7 copy-start.3
  88.6 39.5 %copy-start.6 = (f32[2,200,128]{2,1,0:T(8,128)S(1)}, f32[2,200,128]{2,1,0:T(8,128)}, u32[]{:S(2)}) copy-start(f32[2,200,128]{2,1,0:T(8,128)} %copy-done.5) | copy-start | bytes 614404
  88.6 39.5 %copy-start.10 = (s32[4]{0:T(128)S(1)}, s32[4]{0:T(128)}, u32[]{:S(2)}) copy-start(s32[4]{0:T(128)} %copy-done.9) | copy-start | bytes 52
  88.6 39.5 %copy-start.15 = (f32[4]{0:T(128)S(1)}, f32[4]{0:T(128)}, u32[]{:S(2)}) copy-start(f32[4]{0:T(128)} %copy-done.14) | copy-start | bytes 52
  88.6 39.5 %copy-start.17 = (s32[8]{0:T(128)S(1)}, s32[8]{0:T(128)}, u32[]{:S(2)}) copy-start(s32[8]{0:T(128)} %copy-done.16) | copy-start | bytes 100
  88.6 17.5 %all-to-all-start.3 = ((bf16[4,2,160,128]{3,2,1,0:T(8,128)(2,1)}), bf16[4,2,160,128]{3,2,1,0:T(8,128)(2,1)S(1)}, u32[]{:S(2)}, u32[]{:S(2)}) async-start(bf16[4,2,160,128]{3,2,1,0:T(8,128)(2,1)} %copy-done.3), calls=%async_computation.3 | async-start | bytes 655360 | tf_op jit(solution)/shard_map/all_to_all | solution.py:56
  94.0 34.1 %collective-permute-start.9 = (bf16[4,2,160,128]{3,2,1,0:T(8,128)(2,1)}, bf16[4,2,160,128]{3,2,1,0:T(8,128)(2,1)S(1)}, u32[]{:S(2)}, u32[]{:S(2)}) collective-permute-start(bf16[4,2,160,128]{3,2,1,0:T(8,128)(2,1)} %copy-done.3), channel_id=1, source_target_pairs={{0,384},{4,388},{8,392},{12,396},{16,400},{20,404},{24,408},{28,41... | collective-permute-start | bytes 983048 | tf_op jit(solution)/shard_map/ppermute | solution.py:35

commit v11 on v10

--- a/solution.py
+++ b/solution.py
@@ -374,7 +374,6 @@
         y_far = along_y(y_part)
         scalars = (
             occ_energy[pair_list[:, 0]] + occ_energy[pair_list[:, 1]],
-            jnp.broadcast_to(virt_energy.astype(F32).reshape(2, W, 1), (2, W, 128)),
             sources(keep_step, keep_flip),
             sources(step, flip),
         )
@@ -388,7 +387,7 @@
     brought = as_unit(
         ready, bring, y_one, kept_tiles, keep_step, keep_flip, step, flip, slab, virt_energy
     )
-    *brought, pair_energy, near, keep_source, source = brought
+    *brought, pair_energy, keep_source, source = brought
     two, x_one, y_swap, x_swap, y_far, x_far, y_far_swap, cross, local = together(*brought, local)
     full = (one, two, y_one, x_one, y_swap, x_swap)
     parts = (y_far, x_far, y_far_swap, swap_cores(x_far))
@@ -398,8 +397,13 @@
         keep_source, core[None], half_done, both_ints, full, parts
     )
     mirrored = to_mirror(result)
-    scattered = exchange(result)
-    crossed = as_unit(ready, lambda x: exchange(reorder(x, keep_step)), scattered)
+
+    def finish(result, keep_step, virt_energy):
+        scattered = exchange(result)
+        near = jnp.broadcast_to(virt_energy.astype(F32).reshape(2, W, 1), (2, W, 128))
+        return exchange(reorder(scattered, keep_step)), near
+
+    crossed, near = as_unit(ready, finish, result, keep_step, virt_energy)
     new = update(
         kept, at, flip, source, pair_energy, amp, crossed, mirrored, table, near
     )

time: 132 us -> 135 us (1.023)
  the two profiles are of different devices: /device:TPU:120 before, /device:TPU:64 now
where the time goes in v11:
time: 135 us; the launch traced here: 134 us
  starting transfers between devices  63.2 us (47%)
  waiting for transfers between devices  37.6 us (28%)
  Pallas kernels  23.6 us (17%)
  local copies, waits for them, and re-layouts  7.65 us (6%)
    ppermute x10, starting transfers between devices, permute(): return lax.ppermute(value, ('pair', 'virt'), pairs)  45.4 us
    all_to_all x4, waiting for transfers between devices, exchange(): return lax.all_to_all(units, 'virt', 0, 0, tiled=True)  26.3 us
    all_to_all x4, starting transfers between devices, exchange(): return lax.all_to_all(units, 'virt', 0, 0, tiled=True)  17.8 us
    ppermute x10, waiting for transfers between devices, permute(): return lax.ppermute(value, ('pair', 'virt'), pairs)  11.3 us
    pallas_call x1, Pallas kernels, symmetric_units(): pl.pallas_call(ladder_kernel, out_shape=(jax.ShapeDtypeStruct((4, 2, PIEC...  6.59 us
    pallas_call x1, Pallas kernels, first_half(): pl.pallas_call(half_kernel, out_shape=(pltpu.VMEM((4, W, DEEP), BF), pltp...  4.87 us
    pallas_call x1, Pallas kernels, update(): pl.pallas_call(update_kernel, out_shape=jax.ShapeDtypeStruct((pairs, 2, W...  4.5 us
    pallas_call x2, Pallas kernels, pack_tiles(): pl.pallas_call(functools.partial(tiles_kernel, turn), out_shape=jax.Shape...  3.9 us
  transfers between devices with their start and end apart: 14, of which 6 were waited for; matrix products, arithmetic and copies ran while one was open for 6% of the time, Pallas kernels for 8%

profile of v11, /device:TPU:64, one launch (start us, length us, event | category | flops | bytes accessed | tf_op | source)
XLA Modules:
  0.0 134.4 jit_solution(11231784670031797693)
XLA Ops:
  0.0 1.9 %shard_map.83.refs_0_ = bf16[208,3200]{1,0:T(8,128)(2,1)S(1)} custom-call(s32[1]{0:T(128)} %bitcast.9.order_ref, bf16[16,2,200,200]{3,2,1,0:T(8,128)(2,1)} %bitcast.27, bf16[16,2,200,200]{3,2,1,0:T(8,128)(2,1)} %bitcast.28, bf16[16,2,200,200]{3,2,1,0:T(8,128)(2,1)} %bitcast.29, bf16[16,2,200,200]{3,2,1,0:T(8,128)(2,1)} %bitcast.30, bf16[400]{0:T(512)(128)(2,1)} %refs_4_.1), custom_call_target="tpu_custom_call" | custom-call | bytes 3000000 | tf_op jit(solution)/shard_map/pallas_call | solution.py:103
  2.0 3.6 %collective-permute-start.6 = (bf16[208,3200]{1,0:T(8,128)(2,1)S(1)}, bf16[208,3200]{1,0:T(8,128)(2,1)}, u32[]{:S(2)}, u32[]{:S(2)}) collective-permute-start(bf16[208,3200]{1,0:T(8,128)(2,1)S(1)} %shard_map.83.refs_0_), channel_id=1, source_target_pairs={{0,1},{4,39},{8,9},{12,47},{16,17},{20,55},{24,25},{28,63},{1,2},{... | collective-permute-start | bytes 3993608 | tf_op jit(solution)/shard_map/ppermute | solution.py:35
  5.6 0.6 gather_fusion.4
  6.3 0.6 gather_fusion.5
  7.0 0.2 fusion.12
  7.2 1.8 %shard_map.85 = bf16[4,4,160,128]{3,2,1,0:T(8,128)(2,1)} custom-call(s32[2]{0:T(128)S(1)} %get-tuple-element.119.pick_ref.flip_ref, s32[2]{0:T(128)S(1)} %get-tuple-element.119.pick_ref.flip_ref, bf16[4,2,200,200]{3,2,1,0:T(8,128)(2,1)S(1)} %bitcast.22, bf16[4,2,200,200]{3,2,1,0:T(8,128)(2,1)S(1)} %bitcast.25), custom_call_target="tpu_custom_call" | custom-call | bytes 1500000 | tf_op jit(solution)/shard_map/pallas_call | solution.py:171
  9.0 14.4 %collective-permute-start.7 = (bf16[4,4,160,128]{3,2,1,0:T(8,128)(2,1)}, bf16[4,4,160,128]{3,2,1,0:T(8,128)(2,1)}, u32[]{:S(2)}, u32[]{:S(2)}) collective-permute-start(bf16[4,4,160,128]{3,2,1,0:T(8,128)(2,1)} %shard_map.85), channel_id=1, source_target_pairs={{0,384},{4,388},{8,392},{12,396},{16,400},{20,404},{24,408},{28,41... | collective-permute-start | bytes 1966088 | tf_op jit(solution)/shard_map/ppermute | solution.py:35
  23.4 0.5 slice.17
  24.6 2.1 %shard_map.84 = bf16[4,4,160,128]{3,2,1,0:T(8,128)(2,1)} custom-call(s32[2]{0:T(128)S(1)} %get-tuple-element.118.pick_ref, s32[2]{0:T(128)S(1)} %get-tuple-element.117.flip_ref, bf16[4,2,200,200]{3,2,1,0:T(8,128)(2,1)S(1)} %bitcast.23, bf16[4,2,200,200]{3,2,1,0:T(8,128)(2,1)S(1)} %bitcast.26), custom_call_target="tpu_custom_call" | custom-call | bytes 1500000 | tf_op jit(solution)/shard_map/pallas_call | solution.py:171
  26.7 49.4 %conditional.2 = (bf16[208,3200]{1,0:T(8,128)(2,1)S(1)}, bf16[208,3200]{1,0:T(8,128)(2,1)}, bf16[208,3200]{1,0:T(8,128)(2,1)}, bf16[208,3200]{1,0:T(8,128)(2,1)}...) conditional(s32[]{:T(128)} %bitcast.7, () %tuple.23, ...), branch_computations={%region_3.4_spmd, %region_4.5_spmd} | conditional | flops 2337 | bytes 33917948 | solution.py:72
  26.7 3.4 %collective-permute-start = (bf16[208,3200]{1,0:T(8,128)(2,1)}, bf16[208,3200]{1,0:T(8,128)(2,1)}, u32[]{:S(2)}, u32[]{:S(2)}) collective-permute-start(bf16[208,3200]{1,0:T(8,128)(2,1)} %get-tuple-element.43), channel_id=1, source_target_pairs={{0,8},{4,28},{8,16},{12,4},{16,24},{20,12},{24,0},{28,20},{1,9},{5... | collective-permute-start | bytes 3993608 | tf_op jit(solution)/shard_map/cond/branch_1_fun/ppermute | solution.py:35
  30.1 6.1 %all-to-all-start = ((bf16[4,4,160,128]{3,2,1,0:T(8,128)(2,1)}), bf16[4,4,160,128]{3,2,1,0:T(8,128)(2,1)S(1)}, u32[]{:S(2)}, u32[]{:S(2)}) async-start(bf16[4,4,160,128]{3,2,1,0:T(8,128)(2,1)} %get-tuple-element.45), calls=%async_computation | async-start | bytes 1310720 | tf_op jit(solution)/shard_map/cond/branch_1_fun/all_to_all | solution.py:56
  36.2 1.1 constant_dynamic-slice_fusion
  37.4 3.9 %collective-permute-start.3 = (bf16[208,1664]{1,0:T(8,128)(2,1)S(1)}, bf16[208,1664]{1,0:T(8,128)(2,1)}, u32[]{:S(2)}, u32[]{:S(2)}) collective-permute-start(bf16[208,1664]{1,0:T(8,128)(2,1)S(1)} %constant_dynamic-slice_fusion), channel_id=1, source_target_pairs={{0,1},{4,39},{8,9},{12,47},{16,17},{20,55},{24,25},{28,63},{1,2},{... | collective-permute-start | bytes 2076680 | tf_op jit(solution)/shard_map/cond/branch_1_fun/ppermute | solution.py:35
  41.3 2.2 %collective-permute-start.1 = (bf16[208,3200]{1,0:T(8,128)(2,1)}, bf16[208,3200]{1,0:T(8,128)(2,1)}, u32[]{:S(2)}, u32[]{:S(2)}) collective-permute-start(bf16[208,3200]{1,0:T(8,128)(2,1)} %get-tuple-element.43), channel_id=1, source_target_pairs={{0,4},{4,0},{8,12},{12,8},{16,20},{20,16},{24,28},{28,24},{1,5},{5... | collective-permute-start | bytes 3993608 | tf_op jit(solution)/shard_map/cond/branch_1_fun/ppermute | solution.py:35
  43.6 4.4 %collective-permute-done = bf16[208,3200]{1,0:T(8,128)(2,1)} collective-permute-done((bf16[208,3200]{1,0:T(8,128)(2,1)}, bf16[208,3200]{1,0:T(8,128)(2,1)}, u32[]{:S(2)}, u32[]{:S(2)}) %collective-permute-start) | collective-permute-done | bytes 1331232 | tf_op jit(solution)/shard_map/cond/branch_1_fun/ppermute | solution.py:35
  48.0 1.9 %collective-permute-start.2 = (bf16[208,3200]{1,0:T(8,128)(2,1)}, bf16[208,3200]{1,0:T(8,128)(2,1)}, u32[]{:S(2)}, u32[]{:S(2)}) collective-permute-start(bf16[208,3200]{1,0:T(8,128)(2,1)} %collective-permute-done), channel_id=1, source_target_pairs={{0,4},{4,0},{8,12},{12,8},{16,20},{20,16},{24,28},{28,24},{1,5},{5... | collective-permute-start | bytes 3993608 | tf_op jit(solution)/shard_map/cond/branch_1_fun/ppermute | solution.py:35
  49.9 0.1 compare_select_fusion.5
  50.0 0.1 reshape.162
  50.1 4.5 %all-to-all-done = bf16[4,4,160,128]{3,2,1,0:T(8,128)(2,1)S(1)} async-done(((bf16[4,4,160,128]{3,2,1,0:T(8,128)(2,1)}), bf16[4,4,160,128]{3,2,1,0:T(8,128)(2,1)S(1)}, u32[]{:S(2)}, u32[]{:S(2)}) %all-to-all-start) | async-done | bytes 655392 | tf_op jit(solution)/shard_map/cond/branch_1_fun/all_to_all | solution.py:56
  54.6 1.5 %gather_fusion = bf16[16,160,128]{2,1,0:T(8,128)(2,1)} fusion(bf16[4,4,160,128]{3,2,1,0:T(8,128)(2,1)S(1)} %all-to-all-done, s32[16]{0:T(128)S(1)} %reshape.162), kind=kCustom, calls=%fused_computation | custom fusion | bytes 1310848 | tf_op jit(solution)/shard_map/cond/branch_1_fun/gather | solution.py:61
  56.1 4.2 %all-to-all-start.1 = ((bf16[4,4,160,128]{3,2,1,0:T(8,128)(2,1)}), bf16[4,4,160,128]{3,2,1,0:T(8,128)(2,1)}, u32[]{:S(2)}, u32[]{:S(2)}) async-start(bf16[4,4,160,128]{3,2,1,0:T(8,128)(2,1)} %bitcast.1), calls=%async_computation.1 | async-start | bytes 1310720 | tf_op jit(solution)/shard_map/cond/branch_1_fun/all_to_all | solution.py:56
  60.3 2.1 %collective-permute-start.4 = (bf16[208,1664]{1,0:T(8,128)(2,1)}, bf16[208,1664]{1,0:T(8,128)(2,1)}, u32[]{:S(2)}, u32[]{:S(2)}) collective-permute-start(bf16[208,1664]{1,0:T(8,128)(2,1)} %collective-permute-done.3), channel_id=1, source_target_pairs={{0,8},{4,28},{8,16},{12,4},{16,24},{20,12},{24,0},{28,20},{1,9},{5... | collective-permute-start | bytes 2076680 | tf_op jit(solution)/shard_map/cond/branch_1_fun/ppermute | solution.py:35
  62.4 1.9 %collective-permute-start.5 = (bf16[208,1664]{1,0:T(8,128)(2,1)}, bf16[208,1664]{1,0:T(8,128)(2,1)}, u32[]{:S(2)}, u32[]{:S(2)}) collective-permute-start(bf16[208,1664]{1,0:T(8,128)(2,1)} %collective-permute-done.3), channel_id=1, source_target_pairs={{0,4},{4,0},{8,12},{12,8},{16,20},{20,16},{24,28},{28,24},{1,5},{5... | collective-permute-start | bytes 2076680 | tf_op jit(solution)/shard_map/cond/branch_1_fun/ppermute | solution.py:35
  64.3 0.6 gather_fusion.1
  64.9 0.6 gather_fusion.2
  65.6 0.1 fusion.3
  65.7 0.1 add.83
  65.8 0.1 convert_add_fusion
  65.8 0.1 add.86
  65.9 1.8 %branch_1_fun.1 = bf16[208,3200]{1,0:T(8,128)(2,1)S(1)} custom-call(s32[1]{0:T(128)} %bitcast.order_ref, bf16[16,2,200,200]{3,2,1,0:T(8,128)(2,1)} %get-tuple-element.41.refs_0_.refs_1_.refs_2_.refs_3_, bf16[16,2,200,200]{3,2,1,0:T(8,128)(2,1)} %get-tuple-element.41.refs_0_.refs_1_.refs_2_.refs_3_, ...), custom_call_target="tpu_custom_call" | custom-call | bytes 3000000 | tf_op jit(solution)/shard_map/cond/branch_1_fun/pallas_call | solution.py:103
  67.8 6.9 %collective-permute-done.4 = bf16[208,1664]{1,0:T(8,128)(2,1)} collective-permute-done((bf16[208,1664]{1,0:T(8,128)(2,1)}, bf16[208,1664]{1,0:T(8,128)(2,1)}, u32[]{:S(2)}, u32[]{:S(2)}) %collective-permute-start.4) | collective-permute-done | bytes 692256 | tf_op jit(solution)/shard_map/cond/branch_1_fun/ppermute | solution.py:35
  74.7 1.5 %all-to-all-done.1 = bf16[4,4,160,128]{3,2,1,0:T(8,128)(2,1)} async-done(((bf16[4,4,160,128]{3,2,1,0:T(8,128)(2,1)}), bf16[4,4,160,128]{3,2,1,0:T(8,128)(2,1)}, u32[]{:S(2)}, u32[]{:S(2)}) %all-to-all-start.1) | async-done | bytes 655392 | tf_op jit(solution)/shard_map/cond/branch_1_fun/all_to_all | solution.py:56
  76.2 1.9 %collective-permute-start.8 = (bf16[208,1664]{1,0:T(8,128)(2,1)}, bf16[208,1664]{1,0:T(8,128)(2,1)S(1)}, u32[]{:S(2)}, u32[]{:S(2)}) collective-permute-start(bf16[208,1664]{1,0:T(8,128)(2,1)} %get-tuple-element.108.refs_7_), channel_id=1, source_target_pairs={{0,4},{4,0},{8,12},{12,8},{16,20},{20,16},{24,28},{28,24},{1,5},{5... | collective-permute-start | bytes 2076680 | tf_op jit(solution)/shard_map/ppermute | solution.py:35
  78.1 4.9 %shard_map.86 = (bf16[4,200,3200]{2,1,0:T(8,128)(2,1)S(1)}, f32[4,2,160,128]{3,2,1,0:T(8,128)S(1)}) custom-call(bf16[16,2,200,200]{3,2,1,0:T(8,128)(2,1)} %bitcast.32, bf16[4,4,160,128]{3,2,1,0:T(8,128)(2,1)} %collective-permute-done.7.local_ref, bf16[4,4,160,128]{3,2,1,0:T(8,128)(2,1)} %get-tuple-element.100.cross_ref), custom_call_target="tpu_custom_call" | custom-call | flops 1024000000 | bytes 4000000 | tf_op jit(solution)/shard_map/pallas_call | solution.py:203
  83.0 6.6 %shard_map.87 = (bf16[4,2,160,128]{3,2,1,0:T(8,128)(2,1)}, f32[8,8,200]{2,1,0:T(8,128)S(1)}) custom-call(s32[4]{0:T(128)} %copy-done.12, s32[1]{0:T(128)} %bitcast.12.core_ref, bf16[4,200,3200]{2,1,0:T(8,128)(2,1)S(1)} %get-tuple-element.101.half_ref, f32[4,2,160,128]{3,2,1,0:T(8,128)S(1)} %get-tuple-element.102.int_ref, ...), custom_call_target="tpu_custom_call" | custom-call | flops 1024000000 | bytes 3000000 | tf_op jit(solution)/shard_map/pallas_call | solution.py:262
  89.6 10.0 %collective-permute-start.9 = (bf16[4,2,160,128]{3,2,1,0:T(8,128)(2,1)}, bf16[4,2,160,128]{3,2,1,0:T(8,128)(2,1)S(1)}, u32[]{:S(2)}, u32[]{:S(2)}) collective-permute-start(bf16[4,2,160,128]{3,2,1,0:T(8,128)(2,1)} %get-tuple-element.110), channel_id=1, source_target_pairs={{0,384},{4,388},{8,392},{12,396},{16,400},{20,404},{24,408},{28,41... | collective-permute-start | bytes 983048 | tf_op jit(solution)/shard_map/ppermute | solution.py:35
  99.7 30.2 %conditional.3 = (bf16[4,2,160,128]{3,2,1,0:T(8,128)(2,1)}, f32[2,200,128]{2,1,0:T(8,128)S(1)}) conditional(s32[]{:T(128)} %bitcast.7, () %tuple.26, (bf16[4,2,160,128]{3,2,1,0:T(8,128)(2,1)}, s32[2]{0:T(128)}, bf16[400]{0:T(512)(128)(2,1)}) %tuple.47), branch_computations={%region_6.7_spmd, %region_7.8_spmd} | conditional | flops 72 | bytes 2833716 | solution.py:72
  99.7 3.5 %all-to-all-start.2 = ((bf16[4,2,160,128]{3,2,1,0:T(8,128)(2,1)}), bf16[4,2,160,128]{3,2,1,0:T(8,128)(2,1)S(1)}, u32[]{:S(2)}, u32[]{:S(2)}) async-start(bf16[4,2,160,128]{3,2,1,0:T(8,128)(2,1)} %get-tuple-element.53), calls=%async_computation.2 | async-start | bytes 655360 | tf_op jit(solution)/shard_map/cond/branch_1_fun/all_to_all | solution.py:56
  103.2 0.6 fusion.8
  103.8 0.1 reshape.184
  103.9 10.2 %all-to-all-done.2 = bf16[4,2,160,128]{3,2,1,0:T(8,128)(2,1)S(1)} async-done(((bf16[4,2,160,128]{3,2,1,0:T(8,128)(2,1)}), bf16[4,2,160,128]{3,2,1,0:T(8,128)(2,1)S(1)}, u32[]{:S(2)}, u32[]{:S(2)}) %all-to-all-start.2) | async-done | bytes 327712 | tf_op jit(solution)/shard_map/cond/branch_1_fun/all_to_all | solution.py:56
  114.1 1.3 gather_fusion.3
  115.4 4.1 %all-to-all-start.3 = ((bf16[4,2,160,128]{3,2,1,0:T(8,128)(2,1)}), bf16[4,2,160,128]{3,2,1,0:T(8,128)(2,1)}, u32[]{:S(2)}, u32[]{:S(2)}) async-start(bf16[4,2,160,128]{3,2,1,0:T(8,128)(2,1)} %bitcast.4), calls=%async_computation.3 | async-start | bytes 655360 | tf_op jit(solution)/shard_map/cond/branch_1_fun/all_to_all | solution.py:56
  119.5 0.1 reshape.160
  119.6 10.1 %all-to-all-done.3 = bf16[4,2,160,128]{3,2,1,0:T(8,128)(2,1)} async-done(((bf16[4,2,160,128]{3,2,1,0:T(8,128)(2,1)}), bf16[4,2,160,128]{3,2,1,0:T(8,128)(2,1)}, u32[]{:S(2)}, u32[]{:S(2)}) %all-to-all-start.3) | async-done | bytes 327712 | tf_op jit(solution)/shard_map/cond/branch_1_fun/all_to_all | solution.py:56
  129.7 0.1 broadcast_in_dim.75
  129.9 4.5 %shard_map.88 = bf16[4,2,200,200]{3,2,1,0:T(8,128)(2,1)} custom-call(s32[4]{0:T(128)S(1)} %compare_convert_fusion.1.kept_ref, s32[4]{0:T(128)S(1)} %get-tuple-element.122.at_ref, s32[4]{0:T(128)S(1)} %copy-done.8, s32[8]{0:T(128)S(1)} %copy-done.16, f32[4]{0:T(128)S(1)} %copy-done.14, bf16[4,2,200,200]{3,2,1,0:T(8,128)(2,1)S(1)} %bitcast.24, ...), custom_call_target="tpu_custom_call" | custom-call | tf_op jit(solution)/shard_map/pallas_call | solution.py:308
  (56 shorter events, 0.2 us)
Async XLA Ops:
  0.0 5.6 %copy-start = (s32[200]{0:T(256)S(1)}, s32[200]{0:T(256)}, u32[]{:S(2)}) copy-start(s32[200]{0:T(256)} %param.17) | copy-start | bytes 2404
  0.0 5.6 %copy-start.9 = (s32[4,2]{0,1:T(2,128)S(1)}, s32[4,2]{0,1:T(2,128)}, u32[]{:S(2)}) copy-start(s32[4,2]{0,1:T(2,128)} %param.15) | copy-start | bytes 100
  0.0 6.9 %copy-start.17 = (s32[4]{0:T(128)S(1)}, s32[4]{0:T(128)}, u32[]{:S(2)}) copy-start(s32[4]{0:T(128)} %param.16) | copy-start | bytes 52
  0.0 7.2 %copy-start.2 = (bf16[4,400,200]{2,1,0:T(8,128)(2,1)S(1)}, bf16[4,400,200]{2,1,0:T(8,128)(2,1)}, u32[]{:S(2)}) copy-start(bf16[4,400,200]{2,1,0:T(8,128)(2,1)} %param.13) | copy-start | bytes 1920004
  1.9 5.3 %copy-start.1 = (bf16[4,400,200]{2,1,0:T(8,128)(2,1)S(1)}, bf16[4,400,200]{2,1,0:T(8,128)(2,1)}, u32[]{:S(2)}) copy-start(bf16[4,400,200]{2,1,0:T(8,128)(2,1)} %param.12) | copy-start | bytes 1920004
  2.0 24.7 %collective-permute-start.6 = (bf16[208,3200]{1,0:T(8,128)(2,1)S(1)}, bf16[208,3200]{1,0:T(8,128)(2,1)}, u32[]{:S(2)}, u32[]{:S(2)}) collective-permute-start(bf16[208,3200]{1,0:T(8,128)(2,1)S(1)} %shard_map.83.refs_0_), channel_id=1, source_target_pairs={{0,1},{4,39},{8,9},{12,47},{16,17},{20,55},{24,25},{28,63},{1,2},{... | collective-permute-start | bytes 3993608 | tf_op jit(solution)/shard_map/ppermute | solution.py:35
  6.9 19.7 %copy-start.7 = (s32[4]{0:T(128)}, s32[4]{0:T(128)S(1)}, u32[]{:S(2)}) copy-start(s32[4]{0:T(128)S(1)} %broadcast_and_fusion.flip_ref) | copy-start | bytes 52
  7.0 19.7 %copy-start.10 = (s32[4]{0:T(128)}, s32[4]{0:T(128)S(1)}, u32[]{:S(2)}) copy-start(s32[4]{0:T(128)S(1)} %get-tuple-element.123) | copy-start | bytes 52
  7.2 19.5 %copy-start.6 = (s32[2]{0:T(128)}, s32[2]{0:T(128)S(1)}, u32[]{:S(2)}) copy-start(s32[2]{0:T(128)S(1)} %get-tuple-element.87) | copy-start | bytes 28
  9.0 17.6 %copy-start.3 = (f32[200]{0:T(256)S(1)}, f32[200]{0:T(256)}, u32[]{:S(2)}) copy-start(f32[200]{0:T(256)} %param.18) | copy-start | bytes 2404
  9.0 17.6 %copy-start.4 = (bf16[400]{0:T(512)(128)(2,1)S(1)}, bf16[400]{0:T(512)(128)(2,1)}, u32[]{:S(2)}) copy-start(bf16[400]{0:T(512)(128)(2,1)} %refs_4_.1) | copy-start | bytes 2404
  9.0 67.1 %collective-permute-start.7 = (bf16[4,4,160,128]{3,2,1,0:T(8,128)(2,1)}, bf16[4,4,160,128]{3,2,1,0:T(8,128)(2,1)}, u32[]{:S(2)}, u32[]{:S(2)}) collective-permute-start(bf16[4,4,160,128]{3,2,1,0:T(8,128)(2,1)} %shard_map.85), channel_id=1, source_target_pairs={{0,384},{4,388},{8,392},{12,396},{16,400},{20,404},{24,408},{28,41... | collective-permute-start | bytes 1966088 | tf_op jit(solution)/shard_map/ppermute | solution.py:35
  26.7 21.2 %collective-permute-start = (bf16[208,3200]{1,0:T(8,128)(2,1)}, bf16[208,3200]{1,0:T(8,128)(2,1)}, u32[]{:S(2)}, u32[]{:S(2)}) collective-permute-start(bf16[208,3200]{1,0:T(8,128)(2,1)} %get-tuple-element.43), channel_id=1, source_target_pairs={{0,8},{4,28},{8,16},{12,4},{16,24},{20,12},{24,0},{28,20},{1,9},{5... | collective-permute-start | bytes 3993608 | tf_op jit(solution)/shard_map/cond/branch_1_fun/ppermute | solution.py:35
  30.1 24.4 %all-to-all-start = ((bf16[4,4,160,128]{3,2,1,0:T(8,128)(2,1)}), bf16[4,4,160,128]{3,2,1,0:T(8,128)(2,1)S(1)}, u32[]{:S(2)}, u32[]{:S(2)}) async-start(bf16[4,4,160,128]{3,2,1,0:T(8,128)(2,1)} %get-tuple-element.45), calls=%async_computation | async-start | bytes 1310720 | tf_op jit(solution)/shard_map/cond/branch_1_fun/all_to_all | solution.py:56
  37.4 22.9 %collective-permute-start.3 = (bf16[208,1664]{1,0:T(8,128)(2,1)S(1)}, bf16[208,1664]{1,0:T(8,128)(2,1)}, u32[]{:S(2)}, u32[]{:S(2)}) collective-permute-start(bf16[208,1664]{1,0:T(8,128)(2,1)S(1)} %constant_dynamic-slice_fusion), channel_id=1, source_target_pairs={{0,1},{4,39},{8,9},{12,47},{16,17},{20,55},{24,25},{28,63},{1,2},{... | collective-permute-start | bytes 2076680 | tf_op jit(solution)/shard_map/cond/branch_1_fun/ppermute | solution.py:35
  41.3 26.4 %collective-permute-start.1 = (bf16[208,3200]{1,0:T(8,128)(2,1)}, bf16[208,3200]{1,0:T(8,128)(2,1)}, u32[]{:S(2)}, u32[]{:S(2)}) collective-permute-start(bf16[208,3200]{1,0:T(8,128)(2,1)} %get-tuple-element.43), channel_id=1, source_target_pairs={{0,4},{4,0},{8,12},{12,8},{16,20},{20,16},{24,28},{28,24},{1,5},{5... | collective-permute-start | bytes 3993608 | tf_op jit(solution)/shard_map/cond/branch_1_fun/ppermute | solution.py:35
  48.0 28.2 %collective-permute-start.2 = (bf16[208,3200]{1,0:T(8,128)(2,1)}, bf16[208,3200]{1,0:T(8,128)(2,1)}, u32[]{:S(2)}, u32[]{:S(2)}) collective-permute-start(bf16[208,3200]{1,0:T(8,128)(2,1)} %collective-permute-done), channel_id=1, source_target_pairs={{0,4},{4,0},{8,12},{12,8},{16,20},{20,16},{24,28},{28,24},{1,5},{5... | collective-permute-start | bytes 3993608 | tf_op jit(solution)/shard_map/cond/branch_1_fun/ppermute | solution.py:35
  56.1 20.1 %all-to-all-start.1 = ((bf16[4,4,160,128]{3,2,1,0:T(8,128)(2,1)}), bf16[4,4,160,128]{3,2,1,0:T(8,128)(2,1)}, u32[]{:S(2)}, u32[]{:S(2)}) async-start(bf16[4,4,160,128]{3,2,1,0:T(8,128)(2,1)} %bitcast.1), calls=%async_computation.1 | async-start | bytes 1310720 | tf_op jit(solution)/shard_map/cond/branch_1_fun/all_to_all | solution.py:56
  60.3 14.4 %collective-permute-start.4 = (bf16[208,1664]{1,0:T(8,128)(2,1)}, bf16[208,1664]{1,0:T(8,128)(2,1)}, u32[]{:S(2)}, u32[]{:S(2)}) collective-permute-start(bf16[208,1664]{1,0:T(8,128)(2,1)} %collective-permute-done.3), channel_id=1, source_target_pairs={{0,8},{4,28},{8,16},{12,4},{16,24},{20,12},{24,0},{28,20},{1,9},{5... | collective-permute-start | bytes 2076680 | tf_op jit(solution)/shard_map/cond/branch_1_fun/ppermute | solution.py:35
  62.4 12.3 %collective-permute-start.5 = (bf16[208,1664]{1,0:T(8,128)(2,1)}, bf16[208,1664]{1,0:T(8,128)(2,1)}, u32[]{:S(2)}, u32[]{:S(2)}) collective-permute-start(bf16[208,1664]{1,0:T(8,128)(2,1)} %collective-permute-done.3), channel_id=1, source_target_pairs={{0,4},{4,0},{8,12},{12,8},{16,20},{20,16},{24,28},{28,24},{1,5},{5... | collective-permute-start | bytes 2076680 | tf_op jit(solution)/shard_map/cond/branch_1_fun/ppermute | solution.py:35
  76.1 6.8 %copy-start.12 = (s32[4]{0:T(128)}, s32[4]{0:T(128)S(1)}, u32[]{:S(2)}) copy-start(s32[4]{0:T(128)S(1)} %get-tuple-element.90.source_ref) | copy-start | bytes 52
  76.1 6.8 %copy-start.13 = (f32[4]{0:T(128)}, f32[4]{0:T(128)S(1)}, u32[]{:S(2)}) copy-start(f32[4]{0:T(128)S(1)} %get-tuple-element.89.pair_ref) | copy-start | bytes 52
  76.1 6.8 %copy-start.15 = (s32[8]{0:T(128)}, s32[8]{0:T(128)S(1)}, u32[]{:S(2)}) copy-start(s32[8]{0:T(128)S(1)} %get-tuple-element.88.source_ref) | copy-start | bytes 100
  76.2 6.8 %collective-permute-start.8 = (bf16[208,1664]{1,0:T(8,128)(2,1)}, bf16[208,1664]{1,0:T(8,128)(2,1)S(1)}, u32[]{:S(2)}, u32[]{:S(2)}) collective-permute-start(bf16[208,1664]{1,0:T(8,128)(2,1)} %get-tuple-element.108.refs_7_), channel_id=1, source_target_pairs={{0,4},{4,0},{8,12},{12,8},{16,20},{20,16},{24,28},{28,24},{1,5},{5... | collective-permute-start | bytes 2076680 | tf_op jit(solution)/shard_map/ppermute | solution.py:35
  83.0 16.6 %copy-start.11 = (s32[4]{0:T(128)S(1)}, s32[4]{0:T(128)}, u32[]{:S(2)}) copy-start(s32[4]{0:T(128)} %copy-done.10) | copy-start | bytes 52
  89.6 40.2 %collective-permute-start.9 = (bf16[4,2,160,128]{3,2,1,0:T(8,128)(2,1)}, bf16[4,2,160,128]{3,2,1,0:T(8,128)(2,1)S(1)}, u32[]{:S(2)}, u32[]{:S(2)}) collective-permute-start(bf16[4,2,160,128]{3,2,1,0:T(8,128)(2,1)} %get-tuple-element.110), channel_id=1, source_target_pairs={{0,384},{4,388},{8,392},{12,396},{16,400},{20,404},{24,408},{28,41... | collective-permute-start | bytes 983048 | tf_op jit(solution)/shard_map/ppermute | solution.py:35
  99.6 30.2 %copy-start.8 = (s32[4]{0:T(128)S(1)}, s32[4]{0:T(128)}, u32[]{:S(2)}) copy-start(s32[4]{0:T(128)} %copy-done.7) | copy-start | bytes 52
  99.6 30.2 %copy-start.14 = (f32[4]{0:T(128)S(1)}, f32[4]{0:T(128)}, u32[]{:S(2)}) copy-start(f32[4]{0:T(128)} %copy-done.13) | copy-start | bytes 52
  99.6 30.2 %copy-start.16 = (s32[8]{0:T(128)S(1)}, s32[8]{0:T(128)}, u32[]{:S(2)}) copy-start(s32[8]{0:T(128)} %copy-done.15) | copy-start | bytes 100
  99.7 19.8 %copy-start.5 = (bf16[400]{0:T(512)(128)(2,1)S(1)}, bf16[400]{0:T(512)(128)(2,1)}, u32[]{:S(2)}) copy-start(bf16[400]{0:T(512)(128)(2,1)} %get-tuple-element.55) | copy-start | bytes 2404 | tf_op jit(solution)/shard_map/cond
  99.7 14.4 %all-to-all-start.2 = ((bf16[4,2,160,128]{3,2,1,0:T(8,128)(2,1)}), bf16[4,2,160,128]{3,2,1,0:T(8,128)(2,1)S(1)}, u32[]{:S(2)}, u32[]{:S(2)}) async-start(bf16[4,2,160,128]{3,2,1,0:T(8,128)(2,1)} %get-tuple-element.53), calls=%async_computation.2 | async-start | bytes 655360 | tf_op jit(solution)/shard_map/cond/branch_1_fun/all_to_all | solution.py:56
  115.4 14.3 %all-to-all-start.3 = ((bf16[4,2,160,128]{3,2,1,0:T(8,128)(2,1)}), bf16[4,2,160,128]{3,2,1,0:T(8,128)(2,1)}, u32[]{:S(2)}, u32[]{:S(2)}) async-start(bf16[4,2,160,128]{3,2,1,0:T(8,128)(2,1)} %bitcast.4), calls=%async_computation.3 | async-start | bytes 655360 | tf_op jit(solution)/shard_map/cond/branch_1_fun/all_to_all | solution.py:56

commit v12 on v10

--- a/solution.py
+++ b/solution.py
@@ -374,7 +374,6 @@
         y_far = along_y(y_part)
         scalars = (
             occ_energy[pair_list[:, 0]] + occ_energy[pair_list[:, 1]],
-            jnp.broadcast_to(virt_energy.astype(F32).reshape(2, W, 1), (2, W, 128)),
             sources(keep_step, keep_flip),
             sources(step, flip),
         )
@@ -388,7 +387,7 @@
     brought = as_unit(
         ready, bring, y_one, kept_tiles, keep_step, keep_flip, step, flip, slab, virt_energy
     )
-    *brought, pair_energy, near, keep_source, source = brought
+    *brought, pair_energy, keep_source, source = brought
     two, x_one, y_swap, x_swap, y_far, x_far, y_far_swap, cross, local = together(*brought, local)
     full = (one, two, y_one, x_one, y_swap, x_swap)
     parts = (y_far, x_far, y_far_swap, swap_cores(x_far))
@@ -400,6 +399,7 @@
     mirrored = to_mirror(result)
     scattered = exchange(result)
     crossed = as_unit(ready, lambda x: exchange(reorder(x, keep_step)), scattered)
+    near = jnp.broadcast_to(virt_energy.astype(F32).reshape(2, W, 1), (2, W, 128))
     new = update(
         kept, at, flip, source, pair_energy, amp, crossed, mirrored, table, near
     )

time: 132 us -> 131 us (level)
  no operation moved by 1% of the time
where the time goes in v12:
time: 131 us
  starting transfers between devices  62.9 us (48%)
  waiting for transfers between devices  22.1 us (17%)
  Pallas kernels  21.6 us (16%)
  blocking collectives  12.9 us (10%)
  local copies, waits for them, and re-layouts  8.31 us (6%)
  other arithmetic  1.76 us (1%)
    ppermute x10, starting transfers between devices, permute(): return lax.ppermute(value, ('pair', 'virt'), pairs)  43.1 us
    all_to_all x3, starting transfers between devices, exchange(): return lax.all_to_all(units, 'virt', 0, 0, tiled=True)  19.7 us
    ppermute x10, waiting for transfers between devices, permute(): return lax.ppermute(value, ('pair', 'virt'), pairs)  19.4 us
    all_to_all x1, blocking collectives, exchange(): return lax.all_to_all(units, 'virt', 0, 0, tiled=True)  12.9 us
    pallas_call x1, Pallas kernels, symmetric_units(): pl.pallas_call(ladder_kernel, out_shape=(jax.ShapeDtypeStruct((4, 2, PIEC...  5.88 us
    pallas_call x1, Pallas kernels, first_half(): pl.pallas_call(half_kernel, out_shape=(pltpu.VMEM((4, W, DEEP), BF), pltp...  4.86 us
    pallas_call x2, Pallas kernels, pack_tiles(): pl.pallas_call(functools.partial(tiles_kernel, turn), out_shape=jax.Shape...  3.92 us
    pallas_call x2, Pallas kernels, pack_slab(): pl.pallas_call(pack_kernel, out_shape=jax.ShapeDtypeStruct((TALL, DEEP),...  3.76 us
  transfers between devices with their start and end apart: 13, of which 4 were waited for; matrix products, arithmetic and copies ran while one was open for 7% of the time, Pallas kernels for 8%

profile of v12, /device:TPU:120, one launch (start us, length us, event | category | flops | bytes accessed | tf_op | source)
XLA Modules:
  0.0 130.6 jit_solution(12461663232352603331)
XLA Ops:
  0.0 1.9 %shard_map.83.refs_0_ = bf16[208,3200]{1,0:T(8,128)(2,1)S(1)} custom-call(s32[1]{0:T(128)} %bitcast.9.order_ref, bf16[16,2,200,200]{3,2,1,0:T(8,128)(2,1)} %bitcast.27, bf16[16,2,200,200]{3,2,1,0:T(8,128)(2,1)} %bitcast.28, bf16[16,2,200,200]{3,2,1,0:T(8,128)(2,1)} %bitcast.29, bf16[16,2,200,200]{3,2,1,0:T(8,128)(2,1)} %bitcast.30, bf16[400]{0:T(512)(128)(2,1)} %refs_4_.1), custom_call_target="tpu_custom_call" | custom-call | bytes 3000000 | tf_op jit(solution)/shard_map/pallas_call | solution.py:103
  2.0 2.1 %collective-permute-start.6 = (bf16[208,3200]{1,0:T(8,128)(2,1)S(1)}, bf16[208,3200]{1,0:T(8,128)(2,1)}, u32[]{:S(2)}, u32[]{:S(2)}) collective-permute-start(bf16[208,3200]{1,0:T(8,128)(2,1)S(1)} %shard_map.83.refs_0_), channel_id=1, source_target_pairs={{0,1},{4,39},{8,9},{12,47},{16,17},{20,55},{24,25},{28,63},{1,2},{... | collective-permute-start | bytes 3993608 | tf_op jit(solution)/shard_map/ppermute | solution.py:35
  4.1 0.6 gather_fusion.4
  4.7 0.6 gather_fusion.5
  5.4 0.2 fusion.12
  5.7 1.8 %shard_map.85 = bf16[4,4,160,128]{3,2,1,0:T(8,128)(2,1)} custom-call(s32[2]{0:T(128)S(1)} %get-tuple-element.115.pick_ref.flip_ref, s32[2]{0:T(128)S(1)} %get-tuple-element.115.pick_ref.flip_ref, bf16[4,2,200,200]{3,2,1,0:T(8,128)(2,1)S(1)} %bitcast.22, bf16[4,2,200,200]{3,2,1,0:T(8,128)(2,1)S(1)} %bitcast.25), custom_call_target="tpu_custom_call" | custom-call | bytes 1500000 | tf_op jit(solution)/shard_map/pallas_call | solution.py:171
  7.5 14.4 %collective-permute-start.7 = (bf16[4,4,160,128]{3,2,1,0:T(8,128)(2,1)}, bf16[4,4,160,128]{3,2,1,0:T(8,128)(2,1)}, u32[]{:S(2)}, u32[]{:S(2)}) collective-permute-start(bf16[4,4,160,128]{3,2,1,0:T(8,128)(2,1)} %shard_map.85), channel_id=1, source_target_pairs={{0,384},{4,388},{8,392},{12,396},{16,400},{20,404},{24,408},{28,41... | collective-permute-start | bytes 1966088 | tf_op jit(solution)/shard_map/ppermute | solution.py:35
  21.9 0.5 slice.17
  23.0 2.1 %shard_map.84 = bf16[4,4,160,128]{3,2,1,0:T(8,128)(2,1)} custom-call(s32[2]{0:T(128)S(1)} %get-tuple-element.114.pick_ref, s32[2]{0:T(128)S(1)} %get-tuple-element.113.flip_ref, bf16[4,2,200,200]{3,2,1,0:T(8,128)(2,1)S(1)} %bitcast.23, bf16[4,2,200,200]{3,2,1,0:T(8,128)(2,1)S(1)} %bitcast.26), custom_call_target="tpu_custom_call" | custom-call | bytes 1500000 | tf_op jit(solution)/shard_map/pallas_call | solution.py:171
  25.2 49.2 %conditional.2 = (bf16[208,3200]{1,0:T(8,128)(2,1)S(1)}, bf16[208,3200]{1,0:T(8,128)(2,1)}, bf16[208,3200]{1,0:T(8,128)(2,1)}, bf16[208,3200]{1,0:T(8,128)(2,1)}...) conditional(s32[]{:T(128)} %bitcast.7, () %tuple.21, ...), branch_computations={%region_3.4_spmd, %region_4.5_spmd} | conditional | flops 2337 | bytes 33917948 | solution.py:72
  25.2 3.4 %collective-permute-start = (bf16[208,3200]{1,0:T(8,128)(2,1)}, bf16[208,3200]{1,0:T(8,128)(2,1)}, u32[]{:S(2)}, u32[]{:S(2)}) collective-permute-start(bf16[208,3200]{1,0:T(8,128)(2,1)} %get-tuple-element.44), channel_id=1, source_target_pairs={{0,8},{4,28},{8,16},{12,4},{16,24},{20,12},{24,0},{28,20},{1,9},{5... | collective-permute-start | bytes 3993608 | tf_op jit(solution)/shard_map/cond/branch_1_fun/ppermute | solution.py:35
  28.6 7.1 %all-to-all-start = ((bf16[4,4,160,128]{3,2,1,0:T(8,128)(2,1)}), bf16[4,4,160,128]{3,2,1,0:T(8,128)(2,1)S(1)}, u32[]{:S(2)}, u32[]{:S(2)}) async-start(bf16[4,4,160,128]{3,2,1,0:T(8,128)(2,1)} %get-tuple-element.46), calls=%async_computation | async-start | bytes 1310720 | tf_op jit(solution)/shard_map/cond/branch_1_fun/all_to_all | solution.py:56
  35.6 1.1 constant_dynamic-slice_fusion
  36.8 2.3 %collective-permute-start.3 = (bf16[208,1664]{1,0:T(8,128)(2,1)S(1)}, bf16[208,1664]{1,0:T(8,128)(2,1)}, u32[]{:S(2)}, u32[]{:S(2)}) collective-permute-start(bf16[208,1664]{1,0:T(8,128)(2,1)S(1)} %constant_dynamic-slice_fusion), channel_id=1, source_target_pairs={{0,1},{4,39},{8,9},{12,47},{16,17},{20,55},{24,25},{28,63},{1,2},{... | collective-permute-start | bytes 2076680 | tf_op jit(solution)/shard_map/cond/branch_1_fun/ppermute | solution.py:35
  39.1 1.9 %collective-permute-start.1 = (bf16[208,3200]{1,0:T(8,128)(2,1)}, bf16[208,3200]{1,0:T(8,128)(2,1)}, u32[]{:S(2)}, u32[]{:S(2)}) collective-permute-start(bf16[208,3200]{1,0:T(8,128)(2,1)} %get-tuple-element.44), channel_id=1, source_target_pairs={{0,4},{4,0},{8,12},{12,8},{16,20},{20,16},{24,28},{28,24},{1,5},{5... | collective-permute-start | bytes 3993608 | tf_op jit(solution)/shard_map/cond/branch_1_fun/ppermute | solution.py:35
  41.0 5.4 %collective-permute-done = bf16[208,3200]{1,0:T(8,128)(2,1)} collective-permute-done((bf16[208,3200]{1,0:T(8,128)(2,1)}, bf16[208,3200]{1,0:T(8,128)(2,1)}, u32[]{:S(2)}, u32[]{:S(2)}) %collective-permute-start) | collective-permute-done | bytes 1331232 | tf_op jit(solution)/shard_map/cond/branch_1_fun/ppermute | solution.py:35
  46.4 1.9 %collective-permute-start.2 = (bf16[208,3200]{1,0:T(8,128)(2,1)}, bf16[208,3200]{1,0:T(8,128)(2,1)}, u32[]{:S(2)}, u32[]{:S(2)}) collective-permute-start(bf16[208,3200]{1,0:T(8,128)(2,1)} %collective-permute-done), channel_id=1, source_target_pairs={{0,4},{4,0},{8,12},{12,8},{16,20},{20,16},{24,28},{28,24},{1,5},{5... | collective-permute-start | bytes 3993608 | tf_op jit(solution)/shard_map/cond/branch_1_fun/ppermute | solution.py:35
  48.3 0.1 compare_select_fusion.5
  48.4 0.1 reshape.162
  48.5 2.6 %all-to-all-done = bf16[4,4,160,128]{3,2,1,0:T(8,128)(2,1)S(1)} async-done(((bf16[4,4,160,128]{3,2,1,0:T(8,128)(2,1)}), bf16[4,4,160,128]{3,2,1,0:T(8,128)(2,1)S(1)}, u32[]{:S(2)}, u32[]{:S(2)}) %all-to-all-start) | async-done | bytes 655392 | tf_op jit(solution)/shard_map/cond/branch_1_fun/all_to_all | solution.py:56
  51.2 1.5 %gather_fusion = bf16[16,160,128]{2,1,0:T(8,128)(2,1)} fusion(bf16[4,4,160,128]{3,2,1,0:T(8,128)(2,1)S(1)} %all-to-all-done, s32[16]{0:T(128)S(1)} %reshape.162), kind=kCustom, calls=%fused_computation | custom fusion | bytes 1310848 | tf_op jit(solution)/shard_map/cond/branch_1_fun/gather | solution.py:61
  52.6 7.3 %all-to-all-start.1 = ((bf16[4,4,160,128]{3,2,1,0:T(8,128)(2,1)}), bf16[4,4,160,128]{3,2,1,0:T(8,128)(2,1)}, u32[]{:S(2)}, u32[]{:S(2)}) async-start(bf16[4,4,160,128]{3,2,1,0:T(8,128)(2,1)} %bitcast.1), calls=%async_computation.1 | async-start | bytes 1310720 | tf_op jit(solution)/shard_map/cond/branch_1_fun/all_to_all | solution.py:56
  59.9 1.9 %collective-permute-start.4 = (bf16[208,1664]{1,0:T(8,128)(2,1)}, bf16[208,1664]{1,0:T(8,128)(2,1)}, u32[]{:S(2)}, u32[]{:S(2)}) collective-permute-start(bf16[208,1664]{1,0:T(8,128)(2,1)} %collective-permute-done.3), channel_id=1, source_target_pairs={{0,8},{4,28},{8,16},{12,4},{16,24},{20,12},{24,0},{28,20},{1,9},{5... | collective-permute-start | bytes 2076680 | tf_op jit(solution)/shard_map/cond/branch_1_fun/ppermute | solution.py:35
  61.9 1.9 %collective-permute-start.5 = (bf16[208,1664]{1,0:T(8,128)(2,1)}, bf16[208,1664]{1,0:T(8,128)(2,1)}, u32[]{:S(2)}, u32[]{:S(2)}) collective-permute-start(bf16[208,1664]{1,0:T(8,128)(2,1)} %collective-permute-done.3), channel_id=1, source_target_pairs={{0,4},{4,0},{8,12},{12,8},{16,20},{20,16},{24,28},{28,24},{1,5},{5... | collective-permute-start | bytes 2076680 | tf_op jit(solution)/shard_map/cond/branch_1_fun/ppermute | solution.py:35
  63.8 0.6 gather_fusion.1
  64.5 0.6 gather_fusion.2
  65.1 0.1 fusion.3
  65.2 0.1 add.83
  65.3 0.1 convert_add_fusion
  65.3 0.1 add.86
  65.4 1.8 %branch_1_fun.1 = bf16[208,3200]{1,0:T(8,128)(2,1)S(1)} custom-call(s32[1]{0:T(128)} %bitcast.order_ref, bf16[16,2,200,200]{3,2,1,0:T(8,128)(2,1)} %get-tuple-element.42.refs_0_.refs_1_.refs_2_.refs_3_, bf16[16,2,200,200]{3,2,1,0:T(8,128)(2,1)} %get-tuple-element.42.refs_0_.refs_1_.refs_2_.refs_3_, ...), custom_call_target="tpu_custom_call" | custom-call | bytes 3000000 | tf_op jit(solution)/shard_map/cond/branch_1_fun/pallas_call | solution.py:103
  67.3 7.1 %collective-permute-done.4 = bf16[208,1664]{1,0:T(8,128)(2,1)} collective-permute-done((bf16[208,1664]{1,0:T(8,128)(2,1)}, bf16[208,1664]{1,0:T(8,128)(2,1)}, u32[]{:S(2)}, u32[]{:S(2)}) %collective-permute-start.4) | collective-permute-done | bytes 692256 | tf_op jit(solution)/shard_map/cond/branch_1_fun/ppermute | solution.py:35
  74.4 1.9 %collective-permute-start.8 = (bf16[208,1664]{1,0:T(8,128)(2,1)}, bf16[208,1664]{1,0:T(8,128)(2,1)S(1)}, u32[]{:S(2)}, u32[]{:S(2)}) collective-permute-start(bf16[208,1664]{1,0:T(8,128)(2,1)} %get-tuple-element.106.refs_7_), channel_id=1, source_target_pairs={{0,4},{4,0},{8,12},{12,8},{16,20},{20,16},{24,28},{28,24},{1,5},{5... | collective-permute-start | bytes 2076680 | tf_op jit(solution)/shard_map/ppermute | solution.py:35
  76.3 4.9 %shard_map.86 = (bf16[4,200,3200]{2,1,0:T(8,128)(2,1)S(1)}, f32[4,2,160,128]{3,2,1,0:T(8,128)S(1)}) custom-call(bf16[16,2,200,200]{3,2,1,0:T(8,128)(2,1)} %bitcast.32, bf16[4,4,160,128]{3,2,1,0:T(8,128)(2,1)} %collective-permute-done.7.local_ref, bf16[4,4,160,128]{3,2,1,0:T(8,128)(2,1)} %get-tuple-element.98.cross_ref), custom_call_target="tpu_custom_call" | custom-call | flops 1024000000 | bytes 4000000 | tf_op jit(solution)/shard_map/pallas_call | solution.py:203
  81.2 5.9 %shard_map.87 = (bf16[4,2,160,128]{3,2,1,0:T(8,128)(2,1)S(1)}, f32[8,8,200]{2,1,0:T(8,128)S(1)}) custom-call(s32[4]{0:T(128)} %copy-done.11, s32[1]{0:T(128)} %bitcast.12.core_ref, bf16[4,200,3200]{2,1,0:T(8,128)(2,1)S(1)} %get-tuple-element.99.half_ref, f32[4,2,160,128]{3,2,1,0:T(8,128)S(1)} %get-tuple-element.100.int_ref, ...), custom_call_target="tpu_custom_call" | custom-call | flops 1024000000 | bytes 3000000 | tf_op jit(solution)/shard_map/pallas_call | solution.py:262
  87.1 0.7 copy-done.3
  87.9 5.4 %all-to-all-start.3 = ((bf16[4,2,160,128]{3,2,1,0:T(8,128)(2,1)}), bf16[4,2,160,128]{3,2,1,0:T(8,128)(2,1)S(1)}, u32[]{:S(2)}, u32[]{:S(2)}) async-start(bf16[4,2,160,128]{3,2,1,0:T(8,128)(2,1)} %copy-done.3), calls=%async_computation.3 | async-start | bytes 655360 | tf_op jit(solution)/shard_map/all_to_all | solution.py:56
  93.2 11.4 %collective-permute-start.9 = (bf16[4,2,160,128]{3,2,1,0:T(8,128)(2,1)}, bf16[4,2,160,128]{3,2,1,0:T(8,128)(2,1)S(1)}, u32[]{:S(2)}, u32[]{:S(2)}) collective-permute-start(bf16[4,2,160,128]{3,2,1,0:T(8,128)(2,1)} %copy-done.3), channel_id=1, source_target_pairs={{0,384},{4,388},{8,392},{12,396},{16,400},{20,404},{24,408},{28,41... | collective-permute-start | bytes 983048 | tf_op jit(solution)/shard_map/ppermute | solution.py:35
  104.7 0.8 reshape.161
  105.4 0.6 compare_convert_fusion.1.kept_ref
  106.1 14.3 %conditional.3 = (bf16[4,2,160,128]{3,2,1,0:T(8,128)(2,1)S(1)}) conditional(s32[]{:T(128)} %bitcast.7, () %tuple.24, (s32[2]{0:T(128)}, bf16[4,2,160,128]{3,2,1,0:T(8,128)(2,1)S(1)}) %tuple.45), branch_computations={%region_6.7_spmd, %region_7.8_spmd} | conditional | flops 72 | bytes 1310896 | solution.py:72
  106.1 0.6 fusion.8
  106.7 0.1 reshape.184
  106.8 0.6 gather_fusion.3
  107.4 12.9 %all_to_all.17 = bf16[4,2,160,128]{3,2,1,0:T(8,128)(2,1)S(1)} all-to-all(bf16[4,2,160,128]{3,2,1,0:T(8,128)(2,1)S(1)} %bitcast.33), channel_id=1, replica_groups=mesh['pair'=192,'virt'=4] {'virt'}, dimensions={0} | all-to-all | bytes 655360 | tf_op jit(solution)/shard_map/cond/branch_1_fun/all_to_all | solution.py:56
  120.3 6.9 %collective-permute-done.9.mirror_ref = bf16[4,2,160,128]{3,2,1,0:T(8,128)(2,1)S(1)} collective-permute-done((bf16[4,2,160,128]{3,2,1,0:T(8,128)(2,1)}, bf16[4,2,160,128]{3,2,1,0:T(8,128)(2,1)S(1)}, u32[]{:S(2)}, u32[]{:S(2)}) %collective-permute-start.9) | collective-permute-done | bytes 327712 | tf_op jit(solution)/shard_map/ppermute | solution.py:35
  127.3 0.1 broadcast_in_dim.118.near_ref
  127.4 3.2 %shard_map.88 = bf16[4,2,200,200]{3,2,1,0:T(8,128)(2,1)} custom-call(s32[4]{0:T(128)S(1)} %compare_convert_fusion.1.kept_ref, s32[4]{0:T(128)S(1)} %get-tuple-element.118.at_ref, s32[4]{0:T(128)S(1)} %copy-done.8, s32[8]{0:T(128)S(1)} %copy-done.15, f32[4]{0:T(128)S(1)} %copy-done.13, bf16[4,2,200,200]{3,2,1,0:T(8,128)(2,1)S(1)} %bitcast.24, ...), custom_call_target="tpu_custom_call" | custom-call | tf_op jit(solution)/shard_map/pallas_call | solution.py:308
  (53 shorter events, 0.2 us)
Async XLA Ops:
  0.0 4.1 %copy-start = (s32[200]{0:T(256)S(1)}, s32[200]{0:T(256)}, u32[]{:S(2)}) copy-start(s32[200]{0:T(256)} %param.17) | copy-start | bytes 2404
  0.0 4.0 %copy-start.9 = (s32[4,2]{0,1:T(2,128)S(1)}, s32[4,2]{0,1:T(2,128)}, u32[]{:S(2)}) copy-start(s32[4,2]{0,1:T(2,128)} %param.15) | copy-start | bytes 100
  0.0 5.4 %copy-start.16 = (s32[4]{0:T(128)S(1)}, s32[4]{0:T(128)}, u32[]{:S(2)}) copy-start(s32[4]{0:T(128)} %param.16) | copy-start | bytes 52
  0.0 5.6 %copy-start.2 = (bf16[4,400,200]{2,1,0:T(8,128)(2,1)S(1)}, bf16[4,400,200]{2,1,0:T(8,128)(2,1)}, u32[]{:S(2)}) copy-start(bf16[4,400,200]{2,1,0:T(8,128)(2,1)} %param.13) | copy-start | bytes 1920004
  1.9 3.7 %copy-start.1 = (bf16[4,400,200]{2,1,0:T(8,128)(2,1)S(1)}, bf16[4,400,200]{2,1,0:T(8,128)(2,1)}, u32[]{:S(2)}) copy-start(bf16[4,400,200]{2,1,0:T(8,128)(2,1)} %param.12) | copy-start | bytes 1920004
  2.0 23.2 %collective-permute-start.6 = (bf16[208,3200]{1,0:T(8,128)(2,1)S(1)}, bf16[208,3200]{1,0:T(8,128)(2,1)}, u32[]{:S(2)}, u32[]{:S(2)}) collective-permute-start(bf16[208,3200]{1,0:T(8,128)(2,1)S(1)} %shard_map.83.refs_0_), channel_id=1, source_target_pairs={{0,1},{4,39},{8,9},{12,47},{16,17},{20,55},{24,25},{28,63},{1,2},{... | collective-permute-start | bytes 3993608 | tf_op jit(solution)/shard_map/ppermute | solution.py:35
  5.4 19.8 %copy-start.7 = (s32[4]{0:T(128)}, s32[4]{0:T(128)S(1)}, u32[]{:S(2)}) copy-start(s32[4]{0:T(128)S(1)} %broadcast_and_fusion.flip_ref) | copy-start | bytes 52
  5.4 19.7 %copy-start.10 = (s32[4]{0:T(128)}, s32[4]{0:T(128)S(1)}, u32[]{:S(2)}) copy-start(s32[4]{0:T(128)S(1)} %get-tuple-element.119) | copy-start | bytes 52
  5.6 19.5 %copy-start.6 = (s32[2]{0:T(128)}, s32[2]{0:T(128)S(1)}, u32[]{:S(2)}) copy-start(s32[2]{0:T(128)S(1)} %get-tuple-element.85) | copy-start | bytes 28
  7.5 17.6 %copy-start.4 = (f32[200]{0:T(256)S(1)}, f32[200]{0:T(256)}, u32[]{:S(2)}) copy-start(f32[200]{0:T(256)} %param.18) | copy-start | bytes 2404
  7.5 17.6 %copy-start.5 = (bf16[400]{0:T(512)(128)(2,1)S(1)}, bf16[400]{0:T(512)(128)(2,1)}, u32[]{:S(2)}) copy-start(bf16[400]{0:T(512)(128)(2,1)} %refs_4_.1) | copy-start | bytes 2404
  7.5 66.9 %collective-permute-start.7 = (bf16[4,4,160,128]{3,2,1,0:T(8,128)(2,1)}, bf16[4,4,160,128]{3,2,1,0:T(8,128)(2,1)}, u32[]{:S(2)}, u32[]{:S(2)}) collective-permute-start(bf16[4,4,160,128]{3,2,1,0:T(8,128)(2,1)} %shard_map.85), channel_id=1, source_target_pairs={{0,384},{4,388},{8,392},{12,396},{16,400},{20,404},{24,408},{28,41... | collective-permute-start | bytes 1966088 | tf_op jit(solution)/shard_map/ppermute | solution.py:35
  25.2 21.2 %collective-permute-start = (bf16[208,3200]{1,0:T(8,128)(2,1)}, bf16[208,3200]{1,0:T(8,128)(2,1)}, u32[]{:S(2)}, u32[]{:S(2)}) collective-permute-start(bf16[208,3200]{1,0:T(8,128)(2,1)} %get-tuple-element.44), channel_id=1, source_target_pairs={{0,8},{4,28},{8,16},{12,4},{16,24},{20,12},{24,0},{28,20},{1,9},{5... | collective-permute-start | bytes 3993608 | tf_op jit(solution)/shard_map/cond/branch_1_fun/ppermute | solution.py:35
  28.6 22.6 %all-to-all-start = ((bf16[4,4,160,128]{3,2,1,0:T(8,128)(2,1)}), bf16[4,4,160,128]{3,2,1,0:T(8,128)(2,1)S(1)}, u32[]{:S(2)}, u32[]{:S(2)}) async-start(bf16[4,4,160,128]{3,2,1,0:T(8,128)(2,1)} %get-tuple-element.46), calls=%async_computation | async-start | bytes 1310720 | tf_op jit(solution)/shard_map/cond/branch_1_fun/all_to_all | solution.py:56
  36.8 23.2 %collective-permute-start.3 = (bf16[208,1664]{1,0:T(8,128)(2,1)S(1)}, bf16[208,1664]{1,0:T(8,128)(2,1)}, u32[]{:S(2)}, u32[]{:S(2)}) collective-permute-start(bf16[208,1664]{1,0:T(8,128)(2,1)S(1)} %constant_dynamic-slice_fusion), channel_id=1, source_target_pairs={{0,1},{4,39},{8,9},{12,47},{16,17},{20,55},{24,25},{28,63},{1,2},{... | collective-permute-start | bytes 2076680 | tf_op jit(solution)/shard_map/cond/branch_1_fun/ppermute | solution.py:35
  39.1 28.2 %collective-permute-start.1 = (bf16[208,3200]{1,0:T(8,128)(2,1)}, bf16[208,3200]{1,0:T(8,128)(2,1)}, u32[]{:S(2)}, u32[]{:S(2)}) collective-permute-start(bf16[208,3200]{1,0:T(8,128)(2,1)} %get-tuple-element.44), channel_id=1, source_target_pairs={{0,4},{4,0},{8,12},{12,8},{16,20},{20,16},{24,28},{28,24},{1,5},{5... | collective-permute-start | bytes 3993608 | tf_op jit(solution)/shard_map/cond/branch_1_fun/ppermute | solution.py:35
  46.4 27.9 %collective-permute-start.2 = (bf16[208,3200]{1,0:T(8,128)(2,1)}, bf16[208,3200]{1,0:T(8,128)(2,1)}, u32[]{:S(2)}, u32[]{:S(2)}) collective-permute-start(bf16[208,3200]{1,0:T(8,128)(2,1)} %collective-permute-done), channel_id=1, source_target_pairs={{0,4},{4,0},{8,12},{12,8},{16,20},{20,16},{24,28},{28,24},{1,5},{5... | collective-permute-start | bytes 3993608 | tf_op jit(solution)/shard_map/cond/branch_1_fun/ppermute | solution.py:35
  52.6 21.7 %all-to-all-start.1 = ((bf16[4,4,160,128]{3,2,1,0:T(8,128)(2,1)}), bf16[4,4,160,128]{3,2,1,0:T(8,128)(2,1)}, u32[]{:S(2)}, u32[]{:S(2)}) async-start(bf16[4,4,160,128]{3,2,1,0:T(8,128)(2,1)} %bitcast.1), calls=%async_computation.1 | async-start | bytes 1310720 | tf_op jit(solution)/shard_map/cond/branch_1_fun/all_to_all | solution.py:56
  59.9 14.4 %collective-permute-start.4 = (bf16[208,1664]{1,0:T(8,128)(2,1)}, bf16[208,1664]{1,0:T(8,128)(2,1)}, u32[]{:S(2)}, u32[]{:S(2)}) collective-permute-start(bf16[208,1664]{1,0:T(8,128)(2,1)} %collective-permute-done.3), channel_id=1, source_target_pairs={{0,8},{4,28},{8,16},{12,4},{16,24},{20,12},{24,0},{28,20},{1,9},{5... | collective-permute-start | bytes 2076680 | tf_op jit(solution)/shard_map/cond/branch_1_fun/ppermute | solution.py:35
  61.9 12.5 %collective-permute-start.5 = (bf16[208,1664]{1,0:T(8,128)(2,1)}, bf16[208,1664]{1,0:T(8,128)(2,1)}, u32[]{:S(2)}, u32[]{:S(2)}) collective-permute-start(bf16[208,1664]{1,0:T(8,128)(2,1)} %collective-permute-done.3), channel_id=1, source_target_pairs={{0,4},{4,0},{8,12},{12,8},{16,20},{20,16},{24,28},{28,24},{1,5},{5... | collective-permute-start | bytes 2076680 | tf_op jit(solution)/shard_map/cond/branch_1_fun/ppermute | solution.py:35
  74.4 6.8 %copy-start.11 = (s32[4]{0:T(128)}, s32[4]{0:T(128)S(1)}, u32[]{:S(2)}) copy-start(s32[4]{0:T(128)S(1)} %get-tuple-element.88.source_ref) | copy-start | bytes 52
  74.4 6.8 %copy-start.12 = (f32[4]{0:T(128)}, f32[4]{0:T(128)S(1)}, u32[]{:S(2)}) copy-start(f32[4]{0:T(128)S(1)} %get-tuple-element.87.pair_ref) | copy-start | bytes 52
  74.4 6.8 %copy-start.14 = (s32[8]{0:T(128)}, s32[8]{0:T(128)S(1)}, u32[]{:S(2)}) copy-start(s32[8]{0:T(128)S(1)} %get-tuple-element.86.source_ref) | copy-start | bytes 100
  74.4 6.8 %collective-permute-start.8 = (bf16[208,1664]{1,0:T(8,128)(2,1)}, bf16[208,1664]{1,0:T(8,128)(2,1)S(1)}, u32[]{:S(2)}, u32[]{:S(2)}) collective-permute-start(bf16[208,1664]{1,0:T(8,128)(2,1)} %get-tuple-element.106.refs_7_), channel_id=1, source_target_pairs={{0,4},{4,0},{8,12},{12,8},{16,20},{20,16},{24,28},{28,24},{1,5},{5... | collective-permute-start | bytes 2076680 | tf_op jit(solution)/shard_map/ppermute | solution.py:35
  87.1 0.7 copy-start.3
  87.9 39.5 %copy-start.8 = (s32[4]{0:T(128)S(1)}, s32[4]{0:T(128)}, u32[]{:S(2)}) copy-start(s32[4]{0:T(128)} %copy-done.7) | copy-start | bytes 52
  87.9 39.5 %copy-start.13 = (f32[4]{0:T(128)S(1)}, f32[4]{0:T(128)}, u32[]{:S(2)}) copy-start(f32[4]{0:T(128)} %copy-done.12) | copy-start | bytes 52
  87.9 39.5 %copy-start.15 = (s32[8]{0:T(128)S(1)}, s32[8]{0:T(128)}, u32[]{:S(2)}) copy-start(s32[8]{0:T(128)} %copy-done.14) | copy-start | bytes 100
  87.9 18.2 %all-to-all-start.3 = ((bf16[4,2,160,128]{3,2,1,0:T(8,128)(2,1)}), bf16[4,2,160,128]{3,2,1,0:T(8,128)(2,1)S(1)}, u32[]{:S(2)}, u32[]{:S(2)}) async-start(bf16[4,2,160,128]{3,2,1,0:T(8,128)(2,1)} %copy-done.3), calls=%async_computation.3 | async-start | bytes 655360 | tf_op jit(solution)/shard_map/all_to_all | solution.py:56
  93.2 34.0 %collective-permute-start.9 = (bf16[4,2,160,128]{3,2,1,0:T(8,128)(2,1)}, bf16[4,2,160,128]{3,2,1,0:T(8,128)(2,1)S(1)}, u32[]{:S(2)}, u32[]{:S(2)}) collective-permute-start(bf16[4,2,160,128]{3,2,1,0:T(8,128)(2,1)} %copy-done.3), channel_id=1, source_target_pairs={{0,384},{4,388},{8,392},{12,396},{16,400},{20,404},{24,408},{28,41... | collective-permute-start | bytes 983048 | tf_op jit(solution)/shard_map/ppermute | solution.py:35
